TPU v7x, 32 devices: a whole 2x2x4 slice. The times are simulated.
32 devices in a mesh: dp: 8 (over y, x, core), mp: 4 (over z).
Axes of the slice: x: 2, y: 2, z: 4, core: 2. Of those that a mesh axis runs over, the one named last changes fastest.
Arguments:
- block_input: float32 [8, 8192, 512], P('dp', 'mp'), may hold values from -6 to 6
- ln_gain: float32 [512], replicated, may hold values from 0.1 to 1.9
- ln_bias: float32 [512], replicated, may hold values from -3 to 3
- nu_log: float32 [256], P('mp'), may hold values from -9 to -2.5
- theta_log: float32 [256], P('mp'), may hold values from -4.6 to 1
- gamma_log: float32 [256], P('mp'), may hold values from -4.9 to -0.2
- in_weight: bfloat16 [512, 2, 256], P(None, None, 'mp'), may hold values from -0.25 to 0.25
- out_weight: bfloat16 [2, 256, 512], P(None, 'mp'), may hold values from -0.25 to 0.25
- skip: float32 [512], replicated, may hold values from -4 to 4
- glu_weight: bfloat16 [512, 2, 512], P(None, None, 'mp'), may hold values from -0.25 to 0.25
- glu_bias: bfloat16 [2, 512], P(None, 'mp'), may hold values from -3 to 3
- out_cotangent: float32 [8, 8192, 512], P('dp', 'mp'), may hold values from -6 to 6
Outputs:
- block_output: float32 [8, 8192, 512], P('dp', 'mp')
- grad_input: float32 [8, 8192, 512], P('dp', 'mp')
- grad_ln_gain: float32 [512], replicated
- grad_ln_bias: float32 [512], replicated
- grad_nu_log: float32 [256], P('mp')
- grad_theta_log: float32 [256], P('mp')
- grad_gamma_log: float32 [256], P('mp')
- grad_in_weight: float32 [512, 2, 256], P(None, None, 'mp')
- grad_out_weight: float32 [2, 256, 512], P(None, 'mp')
- grad_skip: float32 [512], replicated
- grad_glu_weight: float32 [512, 2, 512], P(None, None, 'mp')
- grad_glu_bias: float32 [2, 512], P(None, 'mp')
All inputs are finite; a program needn't handle non-finite values.
Results may differ from a plain program's by a relative error of at most 0.011.
Values may be sent and summed in bfloat16 or wider, within the bound.
No kernel may reach another device: no remote copies, remote signals or barrier semaphores. Data moves between devices by JAX's collectives and lax.ppermute only.
A program may use at most 192 MiB of HBM per device.

v0:
```python
from functools import partial

import jax
import jax.numpy as jnp
from jax import lax
from jax.sharding import PartitionSpec as P

EPS = 1e-05


def combine_pair(earlier, later):
    ar1, ai1, br1, bi1 = earlier
    ar2, ai2, br2, bi2 = later
    return (
        ar2 * ar1 - ai2 * ai1,
        ar2 * ai1 + ai2 * ar1,
        ar2 * br1 - ai2 * bi1 + br2,
        ar2 * bi1 + ai2 * br1 + bi2,
    )


def recurrence_full(lam_re, lam_im, src_re, src_im):
    power_re = jnp.broadcast_to(lam_re, src_re.shape)
    power_im = jnp.broadcast_to(lam_im, src_re.shape)
    return lax.associative_scan(combine_pair, (power_re, power_im, src_re, src_im), axis=0)


def normalize(rows, gain, bias):
    mean = jnp.mean(rows, -1, keepdims=True)
    centred = rows - mean
    var = jnp.mean(centred * centred, -1, keepdims=True)
    return centred * lax.rsqrt(var + EPS) * gain + bias


def decay(nu_log, theta_log):
    radius = jnp.exp(-jnp.exp(nu_log))
    turn = jnp.exp(theta_log)
    return (radius * jnp.cos(turn), radius * jnp.sin(turn))


def gated(hidden, pre):
    return pre[:, :hidden] * jax.nn.sigmoid(pre[:, hidden:])


def times_transposed(left, right):
    return lax.dot_general(
        left, right, (((1,), (1,)), ((), ())), preferred_element_type=jnp.float32
    )


def on_device(
    block_input,
    ln_gain,
    ln_bias,
    nu_log,
    theta_log,
    gamma_log,
    in_weight,
    out_weight,
    skip,
    glu_weight,
    glu_bias,
    out_cotangent,
):
    width = block_input.shape[2]
    tokens = block_input.shape[1]
    rows = block_input.reshape(tokens, width)
    cot = out_cotangent.reshape(tokens, width)
    normed, norm_back = jax.vjp(normalize, rows, ln_gain, ln_bias)
    normed_low = normed.astype(jnp.bfloat16)
    states = nu_log.shape[0]
    normed_in = lax.all_gather(normed_low, "mp", axis=0, tiled=True)
    b_flat = in_weight.reshape(width, 2 * states)
    gamma = jnp.exp(gamma_log)
    (lam_re, lam_im), decay_back = jax.vjp(decay, nu_log, theta_log)
    drive = jnp.dot(normed_in, b_flat, preferred_element_type=jnp.float32)
    drive_re = drive[:, :states]
    drive_im = drive[:, states:]
    scanned = recurrence_full(lam_re, lam_im, drive_re * gamma, drive_im * gamma)
    state_re, state_im = (scanned[2], scanned[3])
    first_re = jnp.zeros((states,), jnp.float32)
    first_im = jnp.zeros((states,), jnp.float32)
    state_low = jnp.concatenate([state_re, state_im], 1).astype(jnp.bfloat16)
    c_stack = jnp.concatenate([out_weight[0], -out_weight[1]], 0)
    part = state_low
    mixed = lax.psum_scatter(
        jnp.dot(part, c_stack, preferred_element_type=jnp.float32),
        "mp",
        scatter_dimension=0,
        tiled=True,
    )
    lru_out = mixed + skip * normed
    act, gelu_back = jax.vjp(partial(jax.nn.gelu, approximate=False), lru_out)
    act_low = act.astype(jnp.bfloat16)
    cot_low = cot.astype(jnp.bfloat16)
    hidden = glu_weight.shape[2]
    act_all = lax.all_gather(act_low, "mp", axis=0, tiled=True)
    w_flat = glu_weight.reshape(width, 2 * hidden)
    pre = jnp.dot(act_all, w_flat, preferred_element_type=jnp.float32) + glu_bias.reshape(
        2 * hidden
    ).astype(jnp.float32)
    branch, glu_back = jax.vjp(partial(gated, hidden), pre)
    branch_rows = lax.all_to_all(
        branch.astype(jnp.bfloat16), "mp", split_axis=0, concat_axis=1, tiled=True
    )
    cot_cols = lax.all_to_all(cot_low, "mp", split_axis=1, concat_axis=0, tiled=True)
    grad_pre = glu_back(cot_cols.astype(jnp.float32))[0].astype(jnp.bfloat16)
    grad_glu_weight = jnp.einsum(
        "ld,lk->dk", act_all, grad_pre, preferred_element_type=jnp.float32
    ).reshape(width, 2, hidden)
    grad_glu_bias = jnp.sum(grad_pre.astype(jnp.float32), 0).reshape(2, hidden)
    part = lax.slice_in_dim(grad_pre, 0, lax.axis_size("mp") * tokens, axis=0)
    grad_act = lax.psum_scatter(
        times_transposed(part, w_flat), "mp", scatter_dimension=0, tiled=True
    )
    block_output = rows + branch_rows.astype(jnp.float32)
    grad_lru = gelu_back(grad_act)[0]
    skip_local = jnp.sum(grad_lru * normed, 0)
    grad_lru_low = grad_lru.astype(jnp.bfloat16)
    grad_mixed = lax.all_gather(grad_lru_low, "mp", axis=0, tiled=True)
    grad_c_stack = jnp.einsum(
        "ls,ld->sd", state_low, grad_mixed, preferred_element_type=jnp.float32
    )
    grad_out_weight = jnp.stack([grad_c_stack[:states], -grad_c_stack[states:]], 0)
    grad_state = times_transposed(grad_mixed, c_stack)
    back = recurrence_full(lam_re, -lam_im, grad_state[::-1, :states], grad_state[::-1, states:])
    adjoint_re = back[2][::-1]
    adjoint_im = back[3][::-1]
    prev_re = jnp.concatenate([first_re[None, :], state_re[:-1]], 0)
    prev_im = jnp.concatenate([first_im[None, :], state_im[:-1]], 0)
    grad_lam_re = jnp.sum(adjoint_re * prev_re + adjoint_im * prev_im, 0)
    grad_lam_im = jnp.sum(adjoint_im * prev_re - adjoint_re * prev_im, 0)
    grad_nu_log, grad_theta_log = decay_back((grad_lam_re, grad_lam_im))
    grad_gamma_log = jnp.sum(adjoint_re * drive_re + adjoint_im * drive_im, 0) * gamma
    grad_drive = jnp.concatenate([adjoint_re * gamma, adjoint_im * gamma], 1).astype(jnp.bfloat16)
    grad_in_weight = jnp.einsum(
        "ld,lk->dk", normed_in, grad_drive, preferred_element_type=jnp.float32
    ).reshape(width, 2, states)
    part = grad_drive
    grad_from_lru = lax.psum_scatter(
        times_transposed(part, b_flat).astype(jnp.bfloat16), "mp", scatter_dimension=0, tiled=True
    ).astype(jnp.float32)
    grad_normed = grad_from_lru + grad_lru * skip
    grad_rows, gain_local, bias_local = norm_back(grad_normed)
    grad_input = (cot + grad_rows).reshape(block_input.shape)
    grad_ln_gain, grad_ln_bias, grad_skip = lax.psum(
        (gain_local, bias_local, skip_local), ("dp", "mp")
    )
    (
        grad_nu_log,
        grad_theta_log,
        grad_gamma_log,
        grad_in_weight,
        grad_out_weight,
        grad_glu_weight,
        grad_glu_bias,
    ) = lax.psum(
        (
            grad_nu_log,
            grad_theta_log,
            grad_gamma_log,
            grad_in_weight,
            grad_out_weight,
            grad_glu_weight,
            grad_glu_bias,
        ),
        "dp",
    )
    return (
        block_output.reshape(block_input.shape),
        grad_input,
        grad_ln_gain,
        grad_ln_bias,
        grad_nu_log,
        grad_theta_log,
        grad_gamma_log,
        grad_in_weight,
        grad_out_weight,
        grad_skip,
        grad_glu_weight,
        grad_glu_bias,
    )


def solution(mesh):
    in_specs = (
        P("dp", "mp", None),
        P(),
        P(),
        P("mp"),
        P("mp"),
        P("mp"),
        P(None, None, "mp"),
        P(None, "mp", None),
        P(),
        P(None, None, "mp"),
        P(None, "mp"),
        P("dp", "mp", None),
    )
    out_specs = (
        P("dp", "mp", None),
        P("dp", "mp", None),
        P(),
        P(),
        P("mp"),
        P("mp"),
        P("mp"),
        P(None, None, "mp"),
        P(None, "mp", None),
        P(),
        P(None, None, "mp"),
        P(None, "mp"),
    )
    return jax.shard_map(
        on_device, mesh=mesh, in_specs=in_specs, out_specs=out_specs, check_vma=False
    )
```

profile of v0, /device:TPU:0, one launch (start us, length us, event | category | flops | bytes accessed | tf_op | source)
XLA Modules:
  0.0 2074.6 jit_solution(4038759254359928557)
XLA Ops:
  18.2 149.7 %all-gather.4.cloned.1.call-done = bf16[8192,512]{1,0:T(8,128)(2,1)} async-done(((bf16[2048,512]{1,0:T(8,128)(2,1)}), bf16[8192,512]{1,0:T(8,128)(2,1)}) %all-gather.4.cloned.1.call-update) | async-done | bytes 8388624 | tf_op jit(solution)/shard_map/all_gather | solution.py:72
  179.6 11.4 slice.1339
  361.1 16.5 pad.374
  379.1 16.4 pad.372
  395.5 16.6 pad.373
  436.9 278.6 %reduce-scatter.4.cloned.1.call-done = f32[2048,512]{1,0:T(8,128)} async-done(((f32[8192,512]{1,0:T(8,128)}), f32[2048,512]{1,0:T(8,128)}) %reduce-scatter.4.cloned.1.call-update) | async-done | bytes 4194320 | tf_op jit(solution)/shard_map/reduce_scatter | solution.py:86
  715.6 14.1 multiply_convert_fusion.3
  741.8 183.1 %all-gather.6.cloned.1.call-done = bf16[8192,512]{1,0:T(8,128)(2,1)} async-done(((bf16[2048,512]{1,0:T(8,128)(2,1)}), bf16[8192,512]{1,0:T(8,128)(2,1)}) %all-gather.6.cloned.1.call-update) | async-done | bytes 8388624 | tf_op jit(solution)/shard_map/all_gather | solution.py:97
  951.4 278.6 %reduce-scatter.6.cloned.1.call-done = f32[2048,512]{1,0:T(8,128)} async-done(((f32[8192,512]{1,0:T(8,128)}), f32[2048,512]{1,0:T(8,128)}) %reduce-scatter.6.cloned.1.call-update) | async-done | bytes 4194320 | tf_op jit(solution)/shard_map/reduce_scatter | solution.py:113
  1247.2 140.5 %all-gather.8.cloned.1.call-done = bf16[8192,512]{1,0:T(8,128)(2,1)} async-done(((bf16[2048,512]{1,0:T(8,128)(2,1)}), bf16[8192,512]{1,0:T(8,128)(2,1)}) %all-gather.8.cloned.1.call-update) | async-done | bytes 8388624 | tf_op jit(solution)/shard_map/all_gather | solution.py:120
  1398.7 11.3 slice.1519
  1453.3 11.2 slice.1352
  1464.5 16.6 slice.1349
  1491.2 16.6 slice.1353
  1590.8 17.1 slice.1523
  1665.1 16.6 pad.428
  1683.2 16.5 pad.426
  1714.4 32.6 %rev.8 = f32[8192,64]{1,0:T(8,128)} reverse(f32[8192,64]{1,0:T(8,128)} %add.1226), dimensions={0} | reverse | bytes 4194304 | tf_op jit(solution)/shard_map/rev | solution.py:127
  1761.6 32.4 %rev.9 = f32[8192,64]{1,0:T(8,128)} reverse(f32[8192,64]{1,0:T(8,128)} %add.1229), dimensions={0} | reverse | bytes 4194304 | tf_op jit(solution)/shard_map/rev | solution.py:128
  1794.1 12.6 subtract_reduce_fusion
  1832.4 90.7 %all-to-all-done = bf16[4,2048,128]{2,1,0:T(8,128)(2,1)S(1)} async-done(((bf16[4,2048,128]{2,1,0:T(8,128)(2,1)}), bf16[4,2048,128]{2,1,0:T(8,128)(2,1)S(1)}, u32[]{:S(2)}, u32[]{:S(2)}) %all-to-all-start) | async-done | bytes 2097184 | tf_op jit(solution)/shard_map/all_to_all | solution.py:103
  1955.2 15.1 all-reduce.109
  1970.4 25.8 %reduce-scatter.8.cloned.1.call-done = bf16[2048,512]{1,0:T(8,128)(2,1)} async-done(((bf16[8192,512]{1,0:T(8,128)(2,1)}), bf16[2048,512]{1,0:T(8,128)(2,1)}) %reduce-scatter.8.cloned.1.call-update) | async-done | bytes 2097168 | tf_op jit(solution)/shard_map/reduce_scatter | solution.py:140
  2006.4 45.8 %all-reduce.108 = (f32[512]{0:T(512)}, f32[512]{0:T(512)}, f32[512]{0:T(512)}) all-reduce(f32[512]{0:T(512)S(1)} %get-tuple-element.14, f32[512]{0:T(512)S(1)} %get-tuple-element.18, f32[512]{0:T(512)S(1)} %get-tuple-element.16), channel_id=1, replica_groups=mesh['dp'=8,'mp'=4] {'dp','mp'}, use_global_device_ids=true, to_apply=%region_8.0 | all-reduce | flops 1536 | bytes 12288 | tf_op jit(solution)/shard_map/psum | solution.py:146
  (808 shorter events, 590.8 us)
Async XLA Ops:
  7.2 160.6 %all-gather.4.cloned.1.call-start = ((), (), s32[]{:S(2)}) async-start(), calls=%async_computation.5 | async-start | bytes 10485760 | tf_op jit(solution)/shard_map/all_gather | solution.py:72
  9.8 705.7 %copy-start.57 = (f32[2048]{0:T(1024)}, f32[2048]{0:T(1024)S(1)}, u32[]{:S(2)}) copy-start(f32[2048]{0:T(1024)S(1)} %broadcast_multiply_fusion) | copy-start | bytes 24580
  13.5 702.1 %copy-start.59 = (f32[2048]{0:T(1024)}, f32[2048]{0:T(1024)S(1)}, u32[]{:S(2)}) copy-start(f32[2048]{0:T(1024)S(1)} %fusion.22) | copy-start | bytes 24580
  15.4 700.2 %reduce-scatter.4.cloned.1.call-start = ((), (), s32[]{:S(2)}) async-start(), calls=%async_computation.6 | async-start | bytes 20971520 | tf_op jit(solution)/shard_map/reduce_scatter | solution.py:86
  16.2 266.3 %copy-start.75 = (f32[64]{0:T(128)}, f32[64]{0:T(128)S(1)}, u32[]{:S(2)}) copy-start(f32[64]{0:T(128)S(1)} %get-tuple-element.51) | copy-start | bytes 772
  16.9 265.6 %copy-start.130 = (f32[64]{0:T(128)}, f32[64]{0:T(128)S(1)}, u32[]{:S(2)}) copy-start(f32[64]{0:T(128)S(1)} %get-tuple-element.78) | copy-start | bytes 772
  16.9 275.7 %copy-start.95 = (f32[64]{0:T(128)}, f32[64]{0:T(128)S(1)}, u32[]{:S(2)}) copy-start(f32[64]{0:T(128)S(1)} %get-tuple-element.76) | copy-start | bytes 772
  16.9 275.7 %copy-start.96 = (f32[64]{0:T(128)}, f32[64]{0:T(128)S(1)}, u32[]{:S(2)}) copy-start(f32[64]{0:T(128)S(1)} %get-tuple-element.77) | copy-start | bytes 772
  16.9 281.5 %copy-start.126 = (f32[64]{0:T(128)}, f32[64]{0:T(128)S(1)}, u32[]{:S(2)}) copy-start(f32[64]{0:T(128)S(1)} %get-tuple-element.74) | copy-start | bytes 772
  16.9 281.5 %copy-start.127 = (f32[64]{0:T(128)}, f32[64]{0:T(128)S(1)}, u32[]{:S(2)}) copy-start(f32[64]{0:T(128)S(1)} %get-tuple-element.75) | copy-start | bytes 772
  16.9 282.7 %copy-start.87 = (f32[64]{0:T(128)}, f32[64]{0:T(128)S(1)}, u32[]{:S(2)}) copy-start(f32[64]{0:T(128)S(1)} %get-tuple-element.72) | copy-start | bytes 772
  16.9 282.7 %copy-start.89 = (f32[64]{0:T(128)}, f32[64]{0:T(128)S(1)}, u32[]{:S(2)}) copy-start(f32[64]{0:T(128)S(1)} %get-tuple-element.73) | copy-start | bytes 772
  16.9 282.9 %copy-start.122 = (f32[64]{0:T(128)}, f32[64]{0:T(128)S(1)}, u32[]{:S(2)}) copy-start(f32[64]{0:T(128)S(1)} %get-tuple-element.70) | copy-start | bytes 772
  16.9 282.9 %copy-start.123 = (f32[64]{0:T(128)}, f32[64]{0:T(128)S(1)}, u32[]{:S(2)}) copy-start(f32[64]{0:T(128)S(1)} %get-tuple-element.71) | copy-start | bytes 772
  436.8 278.7 %copy-start.65 = (f32[512]{0:T(512)S(1)}, f32[512]{0:T(512)}, u32[]{:S(2)}) copy-start(f32[512]{0:T(512)} %param.13) | copy-start | bytes 6148
  436.8 278.7 %copy-start.68 = (f32[512]{0:T(512)S(1)}, f32[512]{0:T(512)}, u32[]{:S(2)}) copy-start(f32[512]{0:T(512)} %param.14) | copy-start | bytes 6148
  436.8 278.7 %copy-start.70 = (f32[512]{0:T(512)S(1)}, f32[512]{0:T(512)}, u32[]{:S(2)}) copy-start(f32[512]{0:T(512)} %param.20) | copy-start | bytes 6148
  436.9 488.0 %all-gather.6.cloned.1.call-start = ((), (), s32[]{:S(2)}) async-start(), calls=%async_computation.7 | async-start | bytes 10485760 | tf_op jit(solution)/shard_map/all_gather | solution.py:97
  737.4 196.5 %all-to-all-start.1 = ((bf16[2048,4,128]{2,0,1:T(8,128)(2,1)}), bf16[2048,4,128]{2,0,1:T(8,128)(2,1)S(1)}, u32[]{:S(2)}, u32[]{:S(2)}) async-start(bf16[2048,4,128]{2,0,1:T(8,128)(2,1)} %copy.144), calls=%async_computation.2 | async-start | bytes 4194304 | tf_op jit(solution)/shard_map/all_to_all | solution.py:106
  741.8 488.1 %reduce-scatter.6.cloned.1.call-start = ((), (), s32[]{:S(2)}) async-start(), calls=%async_computation.8 | async-start | bytes 20971520 | tf_op jit(solution)/shard_map/reduce_scatter | solution.py:113
  951.3 436.3 %all-gather.8.cloned.1.call-start = ((), (), s32[]{:S(2)}) async-start(), calls=%async_computation.9 | async-start | bytes 10485760 | tf_op jit(solution)/shard_map/all_gather | solution.py:120
  1237.1 759.1 %reduce-scatter.8.cloned.1.call-start = ((), (), s32[]{:S(2)}) async-start(), calls=%async_computation.10 | async-start | bytes 10485760 | tf_op jit(solution)/shard_map/reduce_scatter | solution.py:140
  1814.3 108.7 %all-to-all-start = ((bf16[4,2048,128]{2,1,0:T(8,128)(2,1)}), bf16[4,2048,128]{2,1,0:T(8,128)(2,1)S(1)}, u32[]{:S(2)}, u32[]{:S(2)}) async-start(bf16[4,2048,128]{2,1,0:T(8,128)(2,1)} %bitcast.9), calls=%async_computation.1 | async-start | bytes 4194304 | tf_op jit(solution)/shard_map/all_to_all | solution.py:103
  1817.9 244.5 %all-reduce.113.cloned.1.call-start = ((), (), s32[]{:S(2)}) async-start(), calls=%async_computation.11 | async-start | bytes 2097152 | tf_op jit(solution)/shard_map/psum | solution.py:157
  (144 other events, 2862.1 us)
Sparse Core Ops, SparseCore 0:
  15.5 152.3 all-gather.3
  437.0 278.5 reduce-scatter.3
  729.8 195.0 all-gather.5
  951.4 278.4 reduce-scatter.5
  1237.2 150.3 all-gather.7
  1814.4 181.6 reduce-scatter.7
  2000.7 61.7 all-reduce.112
where the time goes:
time: 2090 us; the launch traced here: 2070 us
  waiting for transfers between devices  1150 us (55%)
  local copies, waits for them, and re-layouts  601 us (29%)
  other arithmetic  176 us (8%)
  blocking collectives  60.9 us (3%)
  matrix products  59.9 us (3%)
    slice x189, local copies, waits for them, and re-layouts, recurrence_full(): lax.associative_scan(combine_pair, (power_re, power_im, src_re, src_im),...  307 us
    reduce_scatter x1, waiting for transfers between devices, on_device(): lax.psum_scatter(jnp.dot(part, c_stack, preferred_element_type=jnp.float3...  279 us
    reduce_scatter x1, waiting for transfers between devices, on_device(): lax.psum_scatter(times_transposed(part, w_flat), 'mp', scatter_dimension=...  279 us
    all_gather x1, waiting for transfers between devices, on_device(): act_all = lax.all_gather(act_low, 'mp', axis=0, tiled=True)  183 us
    pad x96, local copies, waits for them, and re-layouts, recurrence_full(): lax.associative_scan(combine_pair, (power_re, power_im, src_re, src_im),...  175 us
    all_gather x1, waiting for transfers between devices, on_device(): normed_in = lax.all_gather(normed_low, 'mp', axis=0, tiled=True)  150 us
    all_gather x1, waiting for transfers between devices, on_device(): grad_mixed = lax.all_gather(grad_lru_low, 'mp', axis=0, tiled=True)  140 us
    all_to_all x1, waiting for transfers between devices, on_device(): lax.all_to_all(branch.astype(jnp.bfloat16), 'mp', split_axis=0, concat_ax...  90.7 us
  transfers between devices with their start and end apart: 9, of which 8 were waited for; matrix products, arithmetic and copies ran while one was open for 4% of the time, Pallas kernels for 0%

commit v1 on v0

v1 whole, which is shorter than its diff:
```python
from functools import partial

import jax
import jax.numpy as jnp
from jax import lax
from jax.experimental import pallas as pl
from jax.experimental.pallas import tpu as pltpu
from jax.sharding import PartitionSpec as P

EPS = 1e-05
F32 = jnp.float32
BF16 = jnp.bfloat16
CHUNKS = 16
STEP_ROWS = 256
PARAM_ROWS = 16
VMEM_LIMIT = 56 * 1024 * 1024
INV_SQRT2 = 0.7071067811865476
INV_SQRT_2PI = 0.3989422804014327


def nt(a, b):
    return lax.dot_general(a, b, (((1,), (1,)), ((), ())), preferred_element_type=F32)


def nn(a, b):
    return lax.dot_general(a, b, (((1,), (0,)), ((), ())), preferred_element_type=F32)


def tn(a, b):
    return lax.dot_general(a, b, (((0,), (0,)), ((), ())), preferred_element_type=F32)


def cmul(ar, ai, br, bi):
    return ar * br - ai * bi, ar * bi + ai * br


def cpower(re, im, log2):
    for _ in range(log2):
        re, im = cmul(re, im, re, im)
    return re, im


def log2_of(n):
    return n.bit_length() - 1


def assemble(dst, dst_row, own, other, src_row, rows, me, core, slots, negate_second):
    for slot in range(slots):
        for part in range(2):
            place = pl.ds(dst_row + (part * slots + slot) * rows, rows)
            mine = own[me ^ slot, pl.ds(src_row, rows), :]
            theirs = other[me ^ slot, pl.ds(src_row, rows), :]
            value = jnp.where(core == part, mine, theirs)
            dst[place, :] = -value if negate_second and part == 1 else value


def forward_first(
    chunk, mp, idx, x_ref, gain_ref, bias_ref, own_ref, other_ref,
    xhat_ref, rstd_ref, src_ref, wt_ref, par_ref, ends_ref, last_ref, h_ref, norm_ref, drive_ref,
):
    step = pl.program_id(0)
    width = x_ref.shape[2]
    states = width // 2
    per = x_ref.shape[1]
    ns = states // mp

    @pl.when(step == 0)
    def _():
        me, core = idx[0], idx[1]
        assemble(wt_ref, 0, own_ref, other_ref, 0, ns, me, core, mp, False)
        total = own_ref[0, 2 * 0 + ns : ns + PARAM_ROWS, :].astype(F32)
        for s in range(1, mp):
            total = total + own_ref[s, ns : ns + PARAM_ROWS, :].astype(F32)
        lam = total[0:1] + total[1:2] + total[2:3]
        gam = total[3:4] + total[4:5] + total[5:6]
        re, im = lam[:, :states], lam[:, states:]
        lre, lim = cpower(re, im, log2_of(chunk))
        tre, tim = cpower(lre, lim, log2_of(CHUNKS))
        par_ref[0:1, :] = lam
        par_ref[1:2, :] = gam
        par_ref[2:3, :] = jnp.concatenate([lre, lim], 1)
        par_ref[3:5, :] = total[6:8]
        pre, pim = jnp.ones_like(tre), jnp.zeros_like(tim)
        for s in range(mp):
            par_ref[8 + s : 9 + s, :] = jnp.concatenate([pre, pim], 1)
            pre, pim = cmul(pre, pim, tre, tim)
        h_ref[...] = jnp.zeros_like(h_ref)

    x = jnp.swapaxes(x_ref[...], 0, 1).reshape(per * CHUNKS, width)
    gain, bias = gain_ref[...], bias_ref[...]
    for r in range(0, per * CHUNKS, 16):
        rows = x[r : r + 16]
        mean = jnp.mean(rows, -1, keepdims=True)
        cen = rows - mean
        var = jnp.mean(cen * cen, -1, keepdims=True)
        rstd = lax.rsqrt(var + EPS)
        xhat = cen * rstd
        xhat_ref[r : r + 16, :] = xhat
        rstd_ref[r : r + 16, :] = jnp.broadcast_to(rstd, (16, 128))
        norm_ref[r : r + 16, :] = (xhat * gain + bias).astype(BF16)
    drive_ref[...] = nt(norm_ref[...], wt_ref[...])
    gam = par_ref[1:2, :]
    lre, lim = par_ref[0:1, :states], par_ref[0:1, states:]
    hre, him = h_ref[:, :states], h_ref[:, states:]
    for k in range(per):
        rows = pl.ds(k * CHUNKS, CHUNKS)
        src = drive_ref[rows, :] * gam
        src_ref[rows, :] = src
        hre, him = (
            src[:, :states] + lre * hre - lim * him,
            src[:, states:] + lre * him + lim * hre,
        )
    h_ref[:, :states] = hre
    h_ref[:, states:] = him

    @pl.when(step == pl.num_programs(0) - 1)
    def _():
        ends_ref[...] = h_ref[...]
        pre, pim = par_ref[2:3, :states], par_ref[2:3, states:]
        re, im = h_ref[0:1, :states], h_ref[0:1, states:]
        for c in range(1, CHUNKS):
            mre, mim = cmul(pre, pim, re, im)
            re, im = mre + h_ref[c : c + 1, :states], mim + h_ref[c : c + 1, states:]
        last_ref[...] = jnp.broadcast_to(jnp.concatenate([re, im], 1), last_ref.shape)


def gelu_parts(v):
    cdf = 0.5 * (1.0 + lax.erf(v * INV_SQRT2))
    pdf = jnp.exp(-0.5 * v * v) * INV_SQRT_2PI
    return v * cdf, cdf + v * pdf


def middle(
    mp, idx, x_ref, cot_ref, xhat_ref, src_ref, par_ref, ends_ref, gain_ref, bias_ref, skip_ref, own_ref, other_ref,
    *rest,
):
    others = rest[: mp - 1]
    (
        y_ref, state_ref, glru_ref, gs_ref, gglu_ref, gout_ref, adj_ref, first_ref, vec_ref,
        w_ref, h_ref, p_ref, mix_ref, act_ref, slope_ref, pre_ref, gpre_ref, gmix_ref, br_ref,
    ) = rest[mp - 1 :]
    step = pl.program_id(0)
    width = x_ref.shape[2]
    states = width // 2
    per = x_ref.shape[1]
    rows_all = per * CHUNKS
    ns = states // mp
    hid = width // mp
    me, core = idx[0], idx[1]

    @pl.when(step == 0)
    def _():
        assemble(w_ref, 0, own_ref, other_ref, 0, ns, me, core, mp, True)
        assemble(w_ref, width, own_ref, other_ref, ns, hid, me, core, mp, False)
        re = jnp.zeros((1, states), F32)
        im = jnp.zeros((1, states), F32)
        for s in range(1, mp):
            j = me ^ s
            power = jnp.maximum(me - 1 - j, 0)
            row = par_ref[pl.ds(8 + power, 1), :]
            sre, sim = cmul(row[:, :states], row[:, states:], others[s - 1][0:1, :states], others[s - 1][0:1, states:])
            keep = (j < me).astype(F32)
            re, im = re + keep * sre, im + keep * sim
        lre, lim = par_ref[2:3, :states], par_ref[2:3, states:]
        for c in range(CHUNKS):
            h_ref[c : c + 1, :states] = re
            h_ref[c : c + 1, states:] = im
            mre, mim = cmul(lre, lim, re, im)
            re, im = mre + ends_ref[c : c + 1, :states], mim + ends_ref[c : c + 1, states:]
        p_ref[:, :states] = jnp.ones((8, states), F32)
        p_ref[:, states:] = jnp.zeros((8, states), F32)
        adj_ref[...] = jnp.zeros_like(adj_ref)
        gglu_ref[...] = jnp.zeros_like(gglu_ref)
        gout_ref[...] = jnp.zeros_like(gout_ref)
        vec_ref[...] = jnp.zeros_like(vec_ref)

    lre, lim = par_ref[0:1, :states], par_ref[0:1, states:]
    hre, him = h_ref[:, :states], h_ref[:, states:]
    for k in range(per):
        rows = pl.ds(k * CHUNKS, CHUNKS)
        hre, him = (
            src_ref[rows, :states] + lre * hre - lim * him,
            src_ref[rows, states:] + lre * him + lim * hre,
        )
        state_ref[rows, :states] = hre.astype(BF16)
        state_ref[rows, states:] = him.astype(BF16)
    h_ref[:, :states] = hre
    h_ref[:, states:] = him

    mix_ref[...] = nn(state_ref[...], w_ref[0:width, :])
    for r in range(0, rows_all, 16):
        for c in range(0, width, 128):
            cols = slice(c, c + 128)
            normed = xhat_ref[r : r + 16, cols] * gain_ref[:, cols] + bias_ref[:, cols]
            lru = mix_ref[r : r + 16, cols] + skip_ref[:, cols] * normed
            act, slope = gelu_parts(lru)
            act_ref[r : r + 16, cols] = act.astype(BF16)
            slope_ref[r : r + 16, cols] = slope
    pre_ref[...] = nt(act_ref[...], w_ref[width:, :])
    cot = jnp.swapaxes(cot_ref[...], 0, 1).reshape(rows_all, width)
    for c in range(0, width, 128):
        cols = slice(c, c + 128)
        gate_cols = slice(width + c, width + c + 128)
        sum_value = jnp.zeros((16, 128), F32)
        sum_gate = jnp.zeros((16, 128), F32)
        for r in range(0, rows_all, 16):
            value = pre_ref[r : r + 16, cols] + par_ref[3:4, cols]
            gate = pre_ref[r : r + 16, gate_cols] + par_ref[4:5, cols]
            sig = 0.5 * jnp.tanh(0.5 * gate) + 0.5
            branch = value * sig
            br_ref[r : r + 16, cols] = branch.astype(BF16).astype(F32)
            g = cot[r : r + 16, cols].astype(BF16).astype(F32)
            g_value = (g * sig).astype(BF16)
            g_gate = (g * branch * (1.0 - sig)).astype(BF16)
            gpre_ref[r : r + 16, cols] = g_value
            gpre_ref[r : r + 16, gate_cols] = g_gate
            sum_value = sum_value + g_value.astype(F32)
            sum_gate = sum_gate + g_gate.astype(F32)
        vec_ref[1:2, cols] += jnp.sum(sum_value, 0, keepdims=True)
        vec_ref[2:3, cols] += jnp.sum(sum_gate, 0, keepdims=True)
    y_ref[...] = x_ref[...] + jnp.swapaxes(br_ref[...].reshape(per, CHUNKS, width), 0, 1)
    gglu_ref[...] += tn(gpre_ref[...], act_ref[...])
    mix_ref[...] = nn(gpre_ref[...], w_ref[width:, :])
    for c in range(0, width, 128):
        cols = slice(c, c + 128)
        total = jnp.zeros((16, 128), F32)
        for r in range(0, rows_all, 16):
            normed = xhat_ref[r : r + 16, cols] * gain_ref[:, cols] + bias_ref[:, cols]
            g_lru = mix_ref[r : r + 16, cols] * slope_ref[r : r + 16, cols]
            glru_ref[r : r + 16, cols] = g_lru
            gmix_ref[r : r + 16, cols] = g_lru.astype(BF16)
            total = total + g_lru * normed
        vec_ref[0:1, cols] += jnp.sum(total, 0, keepdims=True)
    gout_ref[...] += tn(state_ref[...], gmix_ref[...])
    gs_ref[...] = nt(gmix_ref[...], w_ref[0:width, :])
    pre, pim = p_ref[:, :states], p_ref[:, states:]
    are = [adj_ref[c : c + 8, :states] for c in range(0, CHUNKS, 8)]
    aim = [adj_ref[c : c + 8, states:] for c in range(0, CHUNKS, 8)]
    for k in range(per):
        for n, c in enumerate(range(0, CHUNKS, 8)):
            rows = pl.ds(k * CHUNKS + c, 8)
            gre, gim = gs_ref[rows, :states], gs_ref[rows, states:]
            mre, mim = cmul(pre, pim, gre, gim)
            are[n], aim[n] = are[n] + mre, aim[n] + mim
        pre, pim = pre * lre + pim * lim, pim * lre - pre * lim
    for n, c in enumerate(range(0, CHUNKS, 8)):
        adj_ref[c : c + 8, :states] = are[n]
        adj_ref[c : c + 8, states:] = aim[n]
    p_ref[:, :states] = pre
    p_ref[:, states:] = pim

    @pl.when(step == pl.num_programs(0) - 1)
    def _():
        lre, lim = par_ref[2:3, :states], -par_ref[2:3, states:]
        last = CHUNKS - 1
        re, im = adj_ref[last : last + 1, :states], adj_ref[last : last + 1, states:]
        for c in range(CHUNKS - 2, -1, -1):
            mre, mim = cmul(lre, lim, re, im)
            re, im = mre + adj_ref[c : c + 1, :states], mim + adj_ref[c : c + 1, states:]
        first_ref[...] = jnp.broadcast_to(jnp.concatenate([re, im], 1), first_ref.shape)


def backward_last(
    mp, idx, cot_ref, xhat_ref, rstd_ref, src_ref, state_ref, glru_ref, gs_ref, par_ref, adj_ref,
    gain_ref, bias_ref, skip_ref, wt_ref, *rest,
):
    others = rest[: mp - 1]
    (gx_ref, gin_ref, vec_ref, h_ref, norm_ref, gdrive_ref, gn_ref, dx_ref, lam_ref) = rest[mp - 1 :]
    step = pl.program_id(0)
    width = cot_ref.shape[2]
    states = width // 2
    per = cot_ref.shape[1]
    rows_all = per * CHUNKS
    me = idx[0]

    @pl.when(step == 0)
    def _():
        re = jnp.zeros((1, states), F32)
        im = jnp.zeros((1, states), F32)
        for s in range(1, mp):
            j = me ^ s
            power = jnp.maximum(j - me - 1, 0)
            row = par_ref[pl.ds(8 + power, 1), :]
            sre, sim = cmul(row[:, :states], -row[:, states:], others[s - 1][0:1, :states], others[s - 1][0:1, states:])
            keep = (j > me).astype(F32)
            re, im = re + keep * sre, im + keep * sim
        lre, lim = par_ref[2:3, :states], -par_ref[2:3, states:]
        for c in range(CHUNKS - 1, -1, -1):
            h_ref[c : c + 1, :states] = re
            h_ref[c : c + 1, states:] = im
            mre, mim = cmul(lre, lim, re, im)
            re, im = mre + adj_ref[c : c + 1, :states], mim + adj_ref[c : c + 1, states:]
        gin_ref[...] = jnp.zeros_like(gin_ref)
        vec_ref[...] = jnp.zeros_like(vec_ref)
        lam_ref[...] = jnp.zeros_like(lam_ref)

    lre, lim = par_ref[0:1, :states], par_ref[0:1, states:]
    gam = par_ref[1:2, :states]
    hre, him = h_ref[:, :states], h_ref[:, states:]
    sre, sim = lam_ref[:, :states], lam_ref[:, states : 2 * states]
    sgam = lam_ref[:, 2 * states :]
    for k in range(per - 1, -1, -1):
        rows = pl.ds(k * CHUNKS, CHUNKS)
        tre, tim = state_ref[rows, :states].astype(F32), state_ref[rows, states:].astype(F32)
        sre = sre + (hre * tre + him * tim)
        sim = sim + (him * tre - hre * tim)
        hre, him = (
            gs_ref[rows, :states] + lre * hre + lim * him,
            gs_ref[rows, states:] + lre * him - lim * hre,
        )
        sgam = sgam + (hre * src_ref[rows, :states] + him * src_ref[rows, states:])
        gdrive_ref[rows, :states] = (hre * gam).astype(BF16)
        gdrive_ref[rows, states:] = (him * gam).astype(BF16)
    h_ref[:, :states] = hre
    h_ref[:, states:] = him
    lam_ref[:, :states] = sre
    lam_ref[:, states : 2 * states] = sim
    lam_ref[:, 2 * states :] = sgam

    for r in range(0, rows_all, 16):
        norm_ref[r : r + 16, :] = (xhat_ref[r : r + 16, :] * gain_ref[...] + bias_ref[...]).astype(BF16)
    gin_ref[...] += tn(gdrive_ref[...], norm_ref[...])
    gn_ref[...] = nn(gdrive_ref[...], wt_ref[...])
    sum_gain = jnp.zeros((16, width), F32)
    sum_bias = jnp.zeros((16, width), F32)
    for r in range(0, rows_all, 16):
        rows = slice(r, r + 16)
        xhat = xhat_ref[rows, :]
        g = gn_ref[rows, :] + skip_ref[...] * glru_ref[rows, :]
        sum_gain = sum_gain + g * xhat
        sum_bias = sum_bias + g
        gh = g * gain_ref[...]
        first = jnp.mean(gh, -1, keepdims=True)
        second = jnp.mean(gh * xhat, -1, keepdims=True)
        dx_ref[rows, :] = rstd_ref[rows, 0:1] * (gh - first - xhat * second)
    vec_ref[0:1, :] += jnp.sum(sum_gain, 0, keepdims=True)
    vec_ref[1:2, :] += jnp.sum(sum_bias, 0, keepdims=True)
    gx_ref[...] = cot_ref[...] + jnp.swapaxes(dx_ref[...].reshape(per, CHUNKS, width), 0, 1)

    @pl.when(step == pl.num_programs(0) - 1)
    def _():
        total = jnp.sum(lam_ref[...], 0, keepdims=True)
        vec_ref[2:3, :] = total[:, :width]
        vec_ref[3:4, :] = jnp.concatenate([total[:, 2 * states :], jnp.zeros((1, states), F32)], 1)


def whole(shape):
    return pl.BlockSpec(shape, lambda i, idx: (0,) * len(shape))


def call(kernel, grid, in_specs, out_specs, out_shape, scratch, flops):
    return pl.pallas_call(
        kernel,
        grid_spec=pltpu.PrefetchScalarGridSpec(
            num_scalar_prefetch=1, grid=grid, in_specs=in_specs, out_specs=out_specs, scratch_shapes=scratch
        ),
        out_shape=out_shape,
        compiler_params=pltpu.CompilerParams(vmem_limit_bytes=VMEM_LIMIT),
        cost_estimate=pl.CostEstimate(flops=flops, bytes_accessed=16 * 1024 * 1024, transcendentals=0),
    )


def xor_pairs(n, s):
    return [(i, i ^ s) for i in range(n)]


def from_each(value, axis, n):
    return [value] + [lax.ppermute(value, axis, xor_pairs(n, s)) for s in range(1, n)]


def tree_sum(parts):
    parts = list(parts)
    while len(parts) > 1:
        parts = [parts[i] + parts[i + 1] for i in range(0, len(parts), 2)]
    return parts[0]


def high_low(v):
    high = lax.reduce_precision(v, 8, 7)
    low = lax.reduce_precision(v - high, 8, 7)
    return high, low


def on_device(
    block_input, ln_gain, ln_bias, nu_log, theta_log, gamma_log, in_weight, out_weight, skip, glu_weight, glu_bias,
    out_cotangent,
):
    mp = lax.axis_size("mp")
    dp = lax.axis_size("dp")
    me = lax.axis_index("mp")
    dpi = lax.axis_index("dp")
    core = dpi & 1
    idx = jnp.stack([me, core]).astype(jnp.int32)
    tokens, width = block_input.shape[1:]
    ns = nu_log.shape[0]
    states = ns * mp
    hid = glu_weight.shape[2]
    chunk = tokens // CHUNKS
    per = STEP_ROWS // CHUNKS
    steps = chunk // per
    x = block_input.reshape(CHUNKS, chunk, width)
    cot = out_cotangent.reshape(CHUNKS, chunk, width)
    gain, bias, skp = ln_gain[None], ln_bias[None], skip[None]

    def decay(nu, theta):
        radius = jnp.exp(-jnp.exp(nu))
        turn = jnp.exp(theta)
        return radius * jnp.cos(turn), radius * jnp.sin(turn)

    (lam_re, lam_im), decay_back = jax.vjp(decay, nu_log, theta_log)
    gamma = jnp.exp(gamma_log)

    here = (jnp.arange(mp) == me).astype(F32)[:, None]

    def placed(v):
        return (here * v[None]).reshape(-1)

    def thirds(v):
        high, rest = high_low(v)
        return [high, rest, lax.reduce_precision(v - high - rest, 8, 7)]

    lam_row = jnp.concatenate([placed(lam_re), placed(lam_im)])
    gam_row = jnp.concatenate([placed(gamma), placed(gamma)])
    bias_rows = [placed(glu_bias[p].astype(F32)) for p in range(2)]
    params = jnp.stack(thirds(lam_row) + thirds(gam_row) + bias_rows).astype(BF16)
    params = jnp.pad(params, ((0, PARAM_ROWS - params.shape[0]), (0, 0)))

    in_part = lax.dynamic_index_in_dim(in_weight, core, 1, keepdims=False).T
    out_part = lax.dynamic_index_in_dim(out_weight, core, 0, keepdims=False)
    glu_part = lax.dynamic_index_in_dim(glu_weight, core, 1, keepdims=False).T
    first_own = jnp.stack(from_each(jnp.concatenate([in_part, params]), "mp", mp))
    first_other = lax.ppermute(first_own, "dp", xor_pairs(dp, 1))
    second_own = jnp.stack(from_each(jnp.concatenate([out_part, glu_part]), "mp", mp))
    second_other = lax.ppermute(second_own, "dp", xor_pairs(dp, 1))

    chunked = pl.BlockSpec((CHUNKS, per, width), lambda i, idx: (0, i, 0))
    rowed = pl.BlockSpec((STEP_ROWS, width), lambda i, idx: (i, 0))
    narrow = pl.BlockSpec((STEP_ROWS, 128), lambda i, idx: (i, 0))
    vector = whole((1, width))
    big = jax.ShapeDtypeStruct((tokens, width), F32)
    big_low = jax.ShapeDtypeStruct((tokens, width), BF16)

    def shape(*dims):
        return jax.ShapeDtypeStruct(dims, F32)

    product = 2 * tokens * width * width
    npar = 8 + mp
    xhat, rstd, src, wt, par, ends, last = call(
        partial(forward_first, chunk, mp),
        (steps,),
        [chunked, vector, vector, whole(first_own.shape), whole(first_own.shape)],
        [rowed, narrow, rowed, whole((width, width)), whole((npar, width)), whole((CHUNKS, width)), whole((8, width))],
        [big, shape(tokens, 128), big, jax.ShapeDtypeStruct((width, width), BF16), shape(npar, width),
         shape(CHUNKS, width), shape(8, width)],
        [pltpu.VMEM((CHUNKS, width), F32), pltpu.VMEM((STEP_ROWS, width), BF16), pltpu.VMEM((STEP_ROWS, width), F32)],
        product,
    )(idx, x, gain, bias, first_own, first_other)

    lasts = from_each(last, "mp", mp)[1:]
    small = whole((8, width))
    y, state, glru, gs, gglu, gout, adj, first, vec_mid = call(
        partial(middle, mp),
        (steps,),
        [chunked, chunked, rowed, rowed, whole((npar, width)), whole((CHUNKS, width)), vector, vector, vector,
         whole(second_own.shape), whole(second_own.shape)] + [small] * (mp - 1),
        [chunked, rowed, rowed, rowed, whole((2 * width, width)), whole((width, width)), whole((CHUNKS, width)), small,
         small],
        [shape(CHUNKS, chunk, width), big_low, big, big, shape(2 * width, width), shape(width, width),
         shape(CHUNKS, width), shape(8, width), shape(8, width)],
        [
            pltpu.VMEM((3 * width, width), BF16),
            pltpu.VMEM((CHUNKS, width), F32),
            pltpu.VMEM((8, width), F32),
            pltpu.VMEM((STEP_ROWS, width), F32),
            pltpu.VMEM((STEP_ROWS, width), BF16),
            pltpu.VMEM((STEP_ROWS, width), F32),
            pltpu.VMEM((STEP_ROWS, 2 * width), F32),
            pltpu.VMEM((STEP_ROWS, 2 * width), BF16),
            pltpu.VMEM((STEP_ROWS, width), BF16),
            pltpu.VMEM((STEP_ROWS, width), F32),
        ],
        9 * product,
    )(idx, x, cot, xhat, src, par, ends, gain, bias, skp, second_own, second_other, *lasts)

    firsts = from_each(first, "mp", mp)[1:]

    def back(i, idx):
        return (steps - 1 - i, 0)

    rowed_back = pl.BlockSpec((STEP_ROWS, width), back)
    narrow_back = pl.BlockSpec((STEP_ROWS, 128), back)
    chunked_back = pl.BlockSpec((CHUNKS, per, width), lambda i, idx: (0, steps - 1 - i, 0))
    gx, gin, vec_last = call(
        partial(backward_last, mp),
        (steps,),
        [chunked_back, rowed_back, narrow_back, rowed_back, rowed_back, rowed_back, rowed_back, whole((npar, width)),
         whole((CHUNKS, width)), vector, vector, vector, whole((width, width))] + [small] * (mp - 1),
        [chunked_back, whole((width, width)), small],
        [shape(CHUNKS, chunk, width), shape(width, width), shape(8, width)],
        [
            pltpu.VMEM((CHUNKS, width), F32),
            pltpu.VMEM((STEP_ROWS, width), BF16),
            pltpu.VMEM((STEP_ROWS, width), BF16),
            pltpu.VMEM((STEP_ROWS, width), F32),
            pltpu.VMEM((STEP_ROWS, width), F32),
            pltpu.VMEM((CHUNKS, 3 * states), F32),
        ],
        2 * product,
    )(idx, cot, xhat, rstd, src, state, glru, gs, par, adj, gain, bias, skp, wt, *firsts)

    vec = jnp.concatenate([vec_mid[0:3], vec_last[0:4], jnp.zeros((1, width), F32)])
    grads = jnp.concatenate(
        [gin.reshape(2, mp, ns, width), gout.reshape(2, mp, ns, width), gglu.reshape(2, mp, hid, width)], 2
    )

    def exchange(send, vec, axis, perm):
        high, low = high_low(vec)
        buffer = jnp.concatenate([send.reshape(-1, width).astype(BF16), high.astype(BF16), low.astype(BF16)])
        got = lax.ppermute(buffer, axis, perm)
        n = got.shape[0] - 16
        return got[:n].astype(F32).reshape(send.shape), (
            got[n : n + 8].astype(F32) + got[n + 8 :].astype(F32)
        ), high + low

    bits = log2_of(dp)
    rows = grads
    for b in range(bits):
        bit = (dpi >> b) & 1
        if b > 0:
            half = rows.shape[1] // 2
            rows = rows.reshape(mp, 2, half, width).swapaxes(0, 1)
        keep = lax.dynamic_index_in_dim(rows, bit, 0, keepdims=False)
        send = lax.dynamic_index_in_dim(rows, 1 - bit, 0, keepdims=False)
        got, vec_got, vec_own = exchange(send, vec, "dp", xor_pairs(dp, 1 << b))
        rows, vec = keep + got, vec_own + vec_got
    pieces = [lax.dynamic_index_in_dim(rows, me, 0, keepdims=False)]
    vecs = []
    for s in range(1, mp):
        send = lax.dynamic_index_in_dim(rows, me ^ s, 0, keepdims=False)
        got, vec_got, vec_own = exchange(send, vec, "mp", xor_pairs(mp, s))
        pieces.append(got)
        vecs.append(vec_got)
    vec = tree_sum([vec_own] + vecs)
    piece = tree_sum(pieces).astype(BF16)
    for b in range(bits - 1, -1, -1):
        bit = (dpi >> b) & 1
        other = lax.ppermute(piece, "dp", xor_pairs(dp, 1 << b))
        piece = jnp.where(bit == 0, jnp.stack([piece, other]), jnp.stack([other, piece]))
        if b > 0:
            piece = piece.reshape(-1, width)
    total = piece.astype(F32)

    grad_in_weight = total[:, :ns].transpose(2, 0, 1)
    grad_out = total[:, ns : 2 * ns]
    grad_out_weight = jnp.stack([grad_out[0], -grad_out[1]])
    grad_glu_weight = total[:, 2 * ns :].transpose(2, 0, 1)
    grad_skip = vec[0]
    grad_glu_bias = lax.dynamic_slice_in_dim(vec[1:3], me * hid, hid, 1)
    grad_lam = lax.dynamic_slice_in_dim(vec[5].reshape(2, states), me * ns, ns, 1)
    grad_nu_log, grad_theta_log = decay_back((grad_lam[0], grad_lam[1]))
    grad_gamma_log = lax.dynamic_slice_in_dim(vec[6], me * ns, ns, 0)
    return (
        y.reshape(block_input.shape),
        gx.reshape(block_input.shape),
        vec[3],
        vec[4],
        grad_nu_log,
        grad_theta_log,
        grad_gamma_log,
        grad_in_weight,
        grad_out_weight,
        grad_skip,
        grad_glu_weight,
        grad_glu_bias,
    )


def solution(mesh):
    in_specs = (
        P("dp", "mp", None), P(), P(), P("mp"), P("mp"), P("mp"), P(None, None, "mp"), P(None, "mp", None), P(),
        P(None, None, "mp"), P(None, "mp"), P("dp", "mp", None),
    )
    out_specs = (
        P("dp", "mp", None), P("dp", "mp", None), P(), P(), P("mp"), P("mp"), P("mp"), P(None, None, "mp"),
        P(None, "mp", None), P(), P(None, None, "mp"), P(None, "mp"),
    )
    return jax.shard_map(on_device, mesh=mesh, in_specs=in_specs, out_specs=out_specs, check_vma=False)
```

time: 2090 us -> 160 us (0.08)
  waiting for transfers between devices: 1150 us -> 52.2 us
  local copies, waits for them, and re-layouts: 601 us -> 13.7 us
  other arithmetic: 176 us -> 6.46 us
  blocking collectives: 60.9 us -> 0 us
  matrix products: 59.9 us -> 0 us
  Pallas kernels: 0 us -> 52.6 us
  starting transfers between devices: 8.27 us -> 32.8 us
    reduce_scatter x3 -> x0, waiting for transfers between devices: 583 us -> none  [the longest x1 279 us: on_device(): lax.psum_scatter(jnp.dot(part, c_stack, preferred_element_type=jnp.float3...]
    all_gather x3 -> x0, waiting for transfers between devices: 473 us -> none  [the longest x1 183 us: on_device(): act_all = lax.all_gather(act_low, 'mp', axis=0, tiled=True)]
    slice x190 -> x7, local copies, waits for them, and re-layouts: 312 us -> 2.16 us  [the longest x1 0.72 us: on_device(): vec_last[0:4]]
    pad x96 -> x0, local copies, waits for them, and re-layouts: 175 us -> none  [recurrence_full(): lax.associative_scan(combine_pair, (power_re, power_im, src_re, src_im),...]
    all_to_all x2 -> x0, waiting for transfers between devices: 90.7 us -> none  [the longest x1 90.7 us: on_device(): lax.all_to_all(branch.astype(jnp.bfloat16), 'mp', split_axis=0, concat_ax...]
    add x104 -> x4, other arithmetic: 81.5 us -> 0.59 us  [the longest x3 0.57 us: on_device(): rows, vec = (keep + got, vec_own + vec_got)]
    rev x2 -> x0, local copies, waits for them, and re-layouts: 65.1 us -> none  [the longest x1 32.6 us: on_device(): adjoint_re = back[2][::-1]]
    psum x2 -> x0, blocking collectives: 60.9 us -> none  [the longest x1 45.8 us: on_device(): lax.psum((gain_local, bias_local, skip_local), ('dp', 'mp'))]
  transfers between devices with their start and end apart: 9 -> 23, of which waited for: 8 -> 18; matrix products, arithmetic and copies ran while one was open for 4% -> 5% of each run, Pallas kernels for 0% -> 7%
where the time goes in v1:
time: 160 us; the launch traced here: 159 us
  Pallas kernels  52.6 us (33%)
  waiting for transfers between devices  52.2 us (33%)
  starting transfers between devices  32.8 us (20%)
  local copies, waits for them, and re-layouts  13.7 us (9%)
  other arithmetic  6.46 us (4%)
    pallas_call x1, Pallas kernels, on_device(): call(partial(middle, mp), (steps,), [chunked, chunked, rowed, rowed, whol...  26.3 us
    ppermute x6, waiting for transfers between devices, exchange(): got = lax.ppermute(buffer, axis, perm)  24.9 us
    ppermute x12, starting transfers between devices, from_each(): lax.ppermute(value, axis, xor_pairs(n, s))  21.8 us
    ppermute x12, waiting for transfers between devices, from_each(): lax.ppermute(value, axis, xor_pairs(n, s))  20.9 us
    pallas_call x1, Pallas kernels, on_device(): call(partial(backward_last, mp), (steps,), [chunked_back, rowed_back, nar...  15.8 us
    pallas_call x1, Pallas kernels, on_device(): call(partial(forward_first, chunk, mp), (steps,), [chunked, vector, vecto...  10.6 us
    ppermute x6, starting transfers between devices, exchange(): got = lax.ppermute(buffer, axis, perm)  7.6 us
    ppermute x3, waiting for transfers between devices, on_device(): other = lax.ppermute(piece, 'dp', xor_pairs(dp, 1 << b))  5.3 us
  transfers between devices with their start and end apart: 23, of which 18 were waited for; matrix products, arithmetic and copies ran while one was open for 5% of the time, Pallas kernels for 7%

profile of v1, /device:TPU:0, one launch (start us, length us, event | category | flops | bytes accessed | tf_op | source)
XLA Modules:
  0.0 158.8 jit_solution(3909534150134965936)
XLA Ops:
  2.1 4.1 %collective-permute-start.5 = (bf16[192,512]{1,0:T(8,128)(2,1)S(1)}, bf16[192,512]{1,0:T(8,128)(2,1)S(1)}, u32[]{:S(2)}, u32[]{:S(2)}) collective-permute-start(bf16[192,512]{1,0:T(8,128)(2,1)S(1)} %get-tuple-element.86), channel_id=1, source_target_pairs={{0,2},{1,3},{2,0},{3,1},{4,6},{5,7},{6,4},{7,5},{8,10},{9,11},{10,... | collective-permute-start | bytes 589832 | tf_op jit(solution)/shard_map/ppermute | solution.py:368
  10.3 6.7 %collective-permute-done.5 = bf16[192,512]{1,0:T(8,128)(2,1)S(1)} collective-permute-done((bf16[192,512]{1,0:T(8,128)(2,1)S(1)}, bf16[192,512]{1,0:T(8,128)(2,1)S(1)}, u32[]{:S(2)}, u32[]{:S(2)}) %collective-permute-start.5) | collective-permute-done | bytes 196640 | tf_op jit(solution)/shard_map/ppermute | solution.py:368
  17.0 3.7 %collective-permute-done.6 = bf16[192,512]{1,0:T(8,128)(2,1)S(1)} collective-permute-done((bf16[192,512]{1,0:T(8,128)(2,1)S(1)}, bf16[192,512]{1,0:T(8,128)(2,1)S(1)}, u32[]{:S(2)}, u32[]{:S(2)}) %collective-permute-start.6) | collective-permute-done | bytes 196640 | tf_op jit(solution)/shard_map/ppermute | solution.py:368
  21.0 5.7 %collective-permute-start.1 = (bf16[80,512]{1,0:T(8,128)(2,1)S(1)}, bf16[80,512]{1,0:T(8,128)(2,1)S(1)}, u32[]{:S(2)}, u32[]{:S(2)}) collective-permute-start(bf16[80,512]{1,0:T(8,128)(2,1)S(1)} %get-tuple-element.88), channel_id=1, source_target_pairs={{0,2},{1,3},{2,0},{3,1},{4,6},{5,7},{6,4},{7,5},{8,10},{9,11},{10,... | collective-permute-start | bytes 245768 | tf_op jit(solution)/shard_map/ppermute | solution.py:368
  28.3 5.3 %collective-permute-done.1 = bf16[80,512]{1,0:T(8,128)(2,1)S(1)} collective-permute-done((bf16[80,512]{1,0:T(8,128)(2,1)S(1)}, bf16[80,512]{1,0:T(8,128)(2,1)S(1)}, u32[]{:S(2)}, u32[]{:S(2)}) %collective-permute-start.1) | collective-permute-done | bytes 81952 | tf_op jit(solution)/shard_map/ppermute | solution.py:368
  37.0 10.6 %shard_map.211 = (f32[2048,512]{1,0:T(8,128)}, f32[2048,128]{1,0:T(8,128)}, f32[2048,512]{1,0:T(8,128)}, bf16[512,512]{1,0:T(8,128)(2,1)}, f32[12,512]{1,0:T(8,1...) custom-call(s32[2]{0:T(128)} %pad_add_fusion.idx, f32[16,128,512]{2,1,0:T(8,128)} %bitcast.124, f32[1,512]{1,0:T(1,128)} %bitcast.150, ...), custom_call_target="tpu_custom_call" | custom-call | flops 1073741824 | bytes 16777216 | tf_op jit(solution)/shard_map/pallas_call | solution.py:448
  47.6 2.4 %collective-permute-start.10 = (f32[8,512]{1,0:T(8,128)}, f32[8,512]{1,0:T(8,128)S(1)}, u32[]{:S(2)}, u32[]{:S(2)}) collective-permute-start(f32[8,512]{1,0:T(8,128)} %get-tuple-element.35), channel_id=1, source_target_pairs={{0,3},{1,2},{2,1},{3,0},{4,7},{5,6},{6,5},{7,4},{8,11},{9,10},{10,... | collective-permute-start | bytes 49160 | tf_op jit(solution)/shard_map/ppermute | solution.py:368
  50.3 1.8 %collective-permute-start.8 = (f32[8,512]{1,0:T(8,128)}, f32[8,512]{1,0:T(8,128)S(1)}, u32[]{:S(2)}, u32[]{:S(2)}) collective-permute-start(f32[8,512]{1,0:T(8,128)} %get-tuple-element.35), channel_id=1, source_target_pairs={{0,1},{1,0},{2,3},{3,2},{4,5},{5,4},{6,7},{7,6},{8,9},{9,8},{10,11... | collective-permute-start | bytes 49160 | tf_op jit(solution)/shard_map/ppermute | solution.py:368
  55.8 26.3 %shard_map.212 = (f32[16,128,512]{2,1,0:T(8,128)}, bf16[2048,512]{1,0:T(8,128)(2,1)}, f32[2048,512]{1,0:T(8,128)}, f32[2048,512]{1,0:T(8,128)}, f32[1024,512]{1,...) custom-call(s32[2]{0:T(128)} %pad_add_fusion.idx, ...), custom_call_target="tpu_custom_call" | custom-call | flops 9663676416 | bytes 16777216 | tf_op jit(solution)/shard_map/pallas_call | solution.py:461
  82.1 1.7 %collective-permute-start.13 = (f32[8,512]{1,0:T(8,128)}, f32[8,512]{1,0:T(8,128)S(1)}, u32[]{:S(2)}, u32[]{:S(2)}) collective-permute-start(f32[8,512]{1,0:T(8,128)} %get-tuple-element.43), channel_id=1, source_target_pairs={{0,3},{1,2},{2,1},{3,0},{4,7},{5,6},{6,5},{7,4},{8,11},{9,10},{10,... | collective-permute-start | bytes 49160 | tf_op jit(solution)/shard_map/ppermute | solution.py:368
  84.8 1.8 %collective-permute-start.11 = (f32[8,512]{1,0:T(8,128)}, f32[8,512]{1,0:T(8,128)S(1)}, u32[]{:S(2)}, u32[]{:S(2)}) collective-permute-start(f32[8,512]{1,0:T(8,128)} %get-tuple-element.43), channel_id=1, source_target_pairs={{0,1},{1,0},{2,3},{3,2},{4,5},{5,4},{6,7},{7,6},{8,9},{9,8},{10,11... | collective-permute-start | bytes 49160 | tf_op jit(solution)/shard_map/ppermute | solution.py:368
  89.4 15.8 %shard_map.213 = (f32[16,128,512]{2,1,0:T(8,128)}, f32[512,512]{1,0:T(8,128)}, f32[8,512]{1,0:T(8,128)}) custom-call(s32[2]{0:T(128)} %pad_add_fusion.idx, f32[16,128,512]{2,1,0:T(8,128)} %bitcast.127, f32[2048,512]{1,0:T(8,128)} %get-tuple-element.31.xhat_ref, f32[2048,128]{1,0:T(8,128)} %get-tuple-element.37.rstd_ref, ...), custom_call_target="tpu_custom_call" | custom-call | flops 2147483648 | bytes 16777216 | tf_op jit(solution)/shard_map/pallas_call | solution.py:493
  105.9 1.7 %pad_maximum_fusion = f32[2,4,256,512]{3,2,1,0:T(8,128)S(1)} fusion(f32[2,4,128,512]{3,2,1,0:T(8,128)S(1)} %bitcast.130, f32[2,4,64,512]{3,2,1,0:T(8,128)S(1)} %bitcast.135, f32[2,4,64,512]{3,2,1,0:T(8,128)} %bitcast.136), kind=kLoop, calls=%fused_computation | loop fusion | flops 2097152 | bytes 8388608 | tf_op jit(solution)/shard_map/concatenate | solution.py:512
  107.9 1.7 %copy-done.2 = f32[2,4,256,512]{3,2,1,0:T(8,128)} copy-done((f32[2,4,256,512]{3,2,1,0:T(8,128)}, f32[2,4,256,512]{3,2,1,0:T(8,128)S(1)}, u32[]{:S(2)}) %copy-start.2) | copy-done | bytes 4194328
  109.6 1.8 %constant_dynamic-slice_fusion.4 = f32[1,4,256,512]{3,2,1,0:T(8,128)S(1)} fusion(f32[2,4,256,512]{3,2,1,0:T(8,128)} %copy-done.2, s32[]{:T(128)S(6)} %select_n.105), kind=kLoop, calls=%fused_computation.75 | loop fusion | bytes 4194308 | tf_op jit(solution)/shard_map/jit(dynamic_index_in_dim)/dynamic_slice | solution.py:532
  114.5 12.8 %collective-permute-done.15 = bf16[528,512]{1,0:T(8,128)(2,1)S(1)} collective-permute-done((bf16[528,512]{1,0:T(8,128)(2,1)S(1)}, bf16[528,512]{1,0:T(8,128)(2,1)S(1)}, u32[]{:S(2)}, u32[]{:S(2)}) %collective-permute-start.15) | collective-permute-done | bytes 540704 | tf_op jit(solution)/shard_map/ppermute | solution.py:519
  127.6 1.6 %collective-permute-start.16 = (bf16[272,512]{1,0:T(8,128)(2,1)S(1)}, bf16[272,512]{1,0:T(8,128)(2,1)S(1)}, u32[]{:S(2)}, u32[]{:S(2)}) collective-permute-start(bf16[272,512]{1,0:T(8,128)(2,1)S(1)} %pad_maximum_fusion.5), channel_id=1, source_target_pairs={{0,16},{4,20},{8,24},{12,28},{16,0},{20,4},{24,8},{28,12},{1,17},{... | collective-permute-start | bytes 835592 | tf_op jit(solution)/shard_map/ppermute | solution.py:519
  129.2 6.3 %collective-permute-done.16 = bf16[272,512]{1,0:T(8,128)(2,1)S(1)} collective-permute-done((bf16[272,512]{1,0:T(8,128)(2,1)S(1)}, bf16[272,512]{1,0:T(8,128)(2,1)S(1)}, u32[]{:S(2)}, u32[]{:S(2)}) %collective-permute-start.16) | collective-permute-done | bytes 278560 | tf_op jit(solution)/shard_map/ppermute | solution.py:519
  135.8 1.7 %collective-permute-start.17 = (bf16[80,512]{1,0:T(8,128)(2,1)S(1)}, bf16[80,512]{1,0:T(8,128)(2,1)S(1)}, u32[]{:S(2)}, u32[]{:S(2)}) collective-permute-start(bf16[80,512]{1,0:T(8,128)(2,1)S(1)} %get-tuple-element.96), channel_id=1, source_target_pairs={{0,1},{1,0},{2,3},{3,2},{4,5},{5,4},{6,7},{7,6},{8,9},{9,8},{10,11... | collective-permute-start | bytes 245768 | tf_op jit(solution)/shard_map/ppermute | solution.py:519
  138.6 1.6 %collective-permute-start.19 = (bf16[80,512]{1,0:T(8,128)(2,1)S(1)}, bf16[80,512]{1,0:T(8,128)(2,1)S(1)}, u32[]{:S(2)}, u32[]{:S(2)}) collective-permute-start(bf16[80,512]{1,0:T(8,128)(2,1)S(1)} %get-tuple-element.98), channel_id=1, source_target_pairs={{0,3},{1,2},{2,1},{3,0},{4,7},{5,6},{6,5},{7,4},{8,11},{9,10},{10,... | collective-permute-start | bytes 245768 | tf_op jit(solution)/shard_map/ppermute | solution.py:519
  141.4 3.7 %collective-permute-done.18 = bf16[80,512]{1,0:T(8,128)(2,1)S(1)} collective-permute-done((bf16[80,512]{1,0:T(8,128)(2,1)S(1)}, bf16[80,512]{1,0:T(8,128)(2,1)S(1)}, u32[]{:S(2)}, u32[]{:S(2)}) %collective-permute-start.18) | collective-permute-done | bytes 81952 | tf_op jit(solution)/shard_map/ppermute | solution.py:519
  145.2 1.6 %collective-permute-start.20 = (bf16[64,512]{1,0:T(8,128)(2,1)S(1)}, bf16[64,512]{1,0:T(8,128)(2,1)S(1)}, u32[]{:S(2)}, u32[]{:S(2)}) collective-permute-start(bf16[64,512]{1,0:T(8,128)(2,1)S(1)} %fusion.3), channel_id=1, source_target_pairs={{0,16},{4,20},{8,24},{12,28},{16,0},{20,4},{24,8},{28,12},{1,17},{... | collective-permute-start | bytes 196616 | tf_op jit(solution)/shard_map/ppermute | solution.py:547
  147.4 2.1 %collective-permute-done.20 = bf16[64,512]{1,0:T(8,128)(2,1)S(1)} collective-permute-done((bf16[64,512]{1,0:T(8,128)(2,1)S(1)}, bf16[64,512]{1,0:T(8,128)(2,1)S(1)}, u32[]{:S(2)}, u32[]{:S(2)}) %collective-permute-start.20) | collective-permute-done | bytes 65568 | tf_op jit(solution)/shard_map/ppermute | solution.py:547
  151.7 2.8 %collective-permute-done.21 = bf16[128,512]{1,0:T(8,128)(2,1)S(1)} collective-permute-done((bf16[128,512]{1,0:T(8,128)(2,1)S(1)}, bf16[128,512]{1,0:T(8,128)(2,1)S(1)}, u32[]{:S(2)}, u32[]{:S(2)}) %collective-permute-start.21) | collective-permute-done | bytes 131104 | tf_op jit(solution)/shard_map/ppermute | solution.py:547
  (129 shorter events, 32.5 us)
Async XLA Ops:
  2.1 15.0 %collective-permute-start.5 = (bf16[192,512]{1,0:T(8,128)(2,1)S(1)}, bf16[192,512]{1,0:T(8,128)(2,1)S(1)}, u32[]{:S(2)}, u32[]{:S(2)}) collective-permute-start(bf16[192,512]{1,0:T(8,128)(2,1)S(1)} %get-tuple-element.86), channel_id=1, source_target_pairs={{0,2},{1,3},{2,0},{3,1},{4,6},{5,7},{6,4},{7,5},{8,10},{9,11},{10,... | collective-permute-start | bytes 589832 | tf_op jit(solution)/shard_map/ppermute | solution.py:368
  6.2 10.9 %collective-permute-start.4 = (bf16[192,512]{1,0:T(8,128)(2,1)S(1)}, bf16[192,512]{1,0:T(8,128)(2,1)S(1)}, u32[]{:S(2)}, u32[]{:S(2)}) collective-permute-start(bf16[192,512]{1,0:T(8,128)(2,1)S(1)} %get-tuple-element.86), channel_id=1, source_target_pairs={{0,1},{1,0},{2,3},{3,2},{4,5},{5,4},{6,7},{7,6},{8,9},{9,8},{10,11... | collective-permute-start | bytes 589832 | tf_op jit(solution)/shard_map/ppermute | solution.py:368
  7.8 13.0 %collective-permute-start.6 = (bf16[192,512]{1,0:T(8,128)(2,1)S(1)}, bf16[192,512]{1,0:T(8,128)(2,1)S(1)}, u32[]{:S(2)}, u32[]{:S(2)}) collective-permute-start(bf16[192,512]{1,0:T(8,128)(2,1)S(1)} %get-tuple-element.86), channel_id=1, source_target_pairs={{0,3},{1,2},{2,1},{3,0},{4,7},{5,6},{6,5},{7,4},{8,11},{9,10},{10,... | collective-permute-start | bytes 589832 | tf_op jit(solution)/shard_map/ppermute | solution.py:368
  20.8 34.0 %collective-permute-start.7 = (bf16[4,192,512]{2,1,0:T(8,128)(2,1)S(1)}, bf16[4,192,512]{2,1,0:T(8,128)(2,1)S(1)}, u32[]{:S(2)}, u32[]{:S(2)}) collective-permute-start(bf16[4,192,512]{2,1,0:T(8,128)(2,1)S(1)} %pad_maximum_fusion.2.own_ref), channel_id=1, source_target_pairs={{0,4},{4,0},{8,12},{12,8},{16,20},{20,16},{24,28},{28,24},{1,5},{5... | collective-permute-start | bytes 2359304 | tf_op jit(solution)/shard_map/ppermute | solution.py:434
  21.0 12.6 %collective-permute-start.1 = (bf16[80,512]{1,0:T(8,128)(2,1)S(1)}, bf16[80,512]{1,0:T(8,128)(2,1)S(1)}, u32[]{:S(2)}, u32[]{:S(2)}) collective-permute-start(bf16[80,512]{1,0:T(8,128)(2,1)S(1)} %get-tuple-element.88), channel_id=1, source_target_pairs={{0,2},{1,3},{2,0},{3,1},{4,6},{5,7},{6,4},{7,5},{8,10},{9,11},{10,... | collective-permute-start | bytes 245768 | tf_op jit(solution)/shard_map/ppermute | solution.py:368
  26.7 7.8 %collective-permute-start = (bf16[80,512]{1,0:T(8,128)(2,1)S(1)}, bf16[80,512]{1,0:T(8,128)(2,1)S(1)}, u32[]{:S(2)}, u32[]{:S(2)}) collective-permute-start(bf16[80,512]{1,0:T(8,128)(2,1)S(1)} %get-tuple-element.88), channel_id=1, source_target_pairs={{0,1},{1,0},{2,3},{3,2},{4,5},{5,4},{6,7},{7,6},{8,9},{9,8},{10,11... | collective-permute-start | bytes 245768 | tf_op jit(solution)/shard_map/ppermute | solution.py:368
  26.7 7.8 %collective-permute-start.2 = (bf16[80,512]{1,0:T(8,128)(2,1)S(1)}, bf16[80,512]{1,0:T(8,128)(2,1)S(1)}, u32[]{:S(2)}, u32[]{:S(2)}) collective-permute-start(bf16[80,512]{1,0:T(8,128)(2,1)S(1)} %get-tuple-element.88), channel_id=1, source_target_pairs={{0,3},{1,2},{2,1},{3,0},{4,7},{5,6},{6,5},{7,4},{8,11},{9,10},{10,... | collective-permute-start | bytes 245768 | tf_op jit(solution)/shard_map/ppermute | solution.py:368
  34.6 1.7 %collective-permute-start.3 = (bf16[4,80,512]{2,1,0:T(8,128)(2,1)S(1)}, bf16[4,80,512]{2,1,0:T(8,128)(2,1)S(1)}, u32[]{:S(2)}, u32[]{:S(2)}) collective-permute-start(bf16[4,80,512]{2,1,0:T(8,128)(2,1)S(1)} %pad_maximum_fusion.4.own_ref), channel_id=1, source_target_pairs={{0,4},{4,0},{8,12},{12,8},{16,20},{20,16},{24,28},{28,24},{1,5},{5... | collective-permute-start | bytes 983048 | tf_op jit(solution)/shard_map/ppermute | solution.py:432
  47.6 5.8 %collective-permute-start.10 = (f32[8,512]{1,0:T(8,128)}, f32[8,512]{1,0:T(8,128)S(1)}, u32[]{:S(2)}, u32[]{:S(2)}) collective-permute-start(f32[8,512]{1,0:T(8,128)} %get-tuple-element.35), channel_id=1, source_target_pairs={{0,3},{1,2},{2,1},{3,0},{4,7},{5,6},{6,5},{7,4},{8,11},{9,10},{10,... | collective-permute-start | bytes 49160 | tf_op jit(solution)/shard_map/ppermute | solution.py:368
  50.0 4.8 %collective-permute-start.9 = (f32[8,512]{1,0:T(8,128)}, f32[8,512]{1,0:T(8,128)S(1)}, u32[]{:S(2)}, u32[]{:S(2)}) collective-permute-start(f32[8,512]{1,0:T(8,128)} %get-tuple-element.35), channel_id=1, source_target_pairs={{0,2},{1,3},{2,0},{3,1},{4,6},{5,7},{6,4},{7,5},{8,10},{9,11},{10,... | collective-permute-start | bytes 49160 | tf_op jit(solution)/shard_map/ppermute | solution.py:368
  50.3 4.6 %collective-permute-start.8 = (f32[8,512]{1,0:T(8,128)}, f32[8,512]{1,0:T(8,128)S(1)}, u32[]{:S(2)}, u32[]{:S(2)}) collective-permute-start(f32[8,512]{1,0:T(8,128)} %get-tuple-element.35), channel_id=1, source_target_pairs={{0,1},{1,0},{2,3},{3,2},{4,5},{5,4},{6,7},{7,6},{8,9},{9,8},{10,11... | collective-permute-start | bytes 49160 | tf_op jit(solution)/shard_map/ppermute | solution.py:368
  82.1 5.8 %collective-permute-start.13 = (f32[8,512]{1,0:T(8,128)}, f32[8,512]{1,0:T(8,128)S(1)}, u32[]{:S(2)}, u32[]{:S(2)}) collective-permute-start(f32[8,512]{1,0:T(8,128)} %get-tuple-element.43), channel_id=1, source_target_pairs={{0,3},{1,2},{2,1},{3,0},{4,7},{5,6},{6,5},{7,4},{8,11},{9,10},{10,... | collective-permute-start | bytes 49160 | tf_op jit(solution)/shard_map/ppermute | solution.py:368
  83.8 4.9 %collective-permute-start.12 = (f32[8,512]{1,0:T(8,128)}, f32[8,512]{1,0:T(8,128)S(1)}, u32[]{:S(2)}, u32[]{:S(2)}) collective-permute-start(f32[8,512]{1,0:T(8,128)} %get-tuple-element.43), channel_id=1, source_target_pairs={{0,2},{1,3},{2,0},{3,1},{4,6},{5,7},{6,4},{7,5},{8,10},{9,11},{10,... | collective-permute-start | bytes 49160 | tf_op jit(solution)/shard_map/ppermute | solution.py:368
  84.8 4.1 %collective-permute-start.11 = (f32[8,512]{1,0:T(8,128)}, f32[8,512]{1,0:T(8,128)S(1)}, u32[]{:S(2)}, u32[]{:S(2)}) collective-permute-start(f32[8,512]{1,0:T(8,128)} %get-tuple-element.43), channel_id=1, source_target_pairs={{0,1},{1,0},{2,3},{3,2},{4,5},{5,4},{6,7},{7,6},{8,9},{9,8},{10,11... | collective-permute-start | bytes 49160 | tf_op jit(solution)/shard_map/ppermute | solution.py:368
  109.6 2.7 %collective-permute-start.14 = (bf16[1040,512]{1,0:T(8,128)(2,1)S(1)}, bf16[1040,512]{1,0:T(8,128)(2,1)S(1)}, u32[]{:S(2)}, u32[]{:S(2)}) collective-permute-start(bf16[1040,512]{1,0:T(8,128)(2,1)S(1)} %pad_maximum_fusion.1), channel_id=1, source_target_pairs={{0,4},{4,0},{8,12},{12,8},{16,20},{20,16},{24,28},{28,24},{1,5},{5... | collective-permute-start | bytes 3194888 | tf_op jit(solution)/shard_map/ppermute | solution.py:519
  112.9 14.4 %collective-permute-start.15 = (bf16[528,512]{1,0:T(8,128)(2,1)S(1)}, bf16[528,512]{1,0:T(8,128)(2,1)S(1)}, u32[]{:S(2)}, u32[]{:S(2)}) collective-permute-start(bf16[528,512]{1,0:T(8,128)(2,1)S(1)} %pad_maximum_fusion.3), channel_id=1, source_target_pairs={{0,8},{4,12},{8,0},{12,4},{16,24},{20,28},{24,16},{28,20},{1,9},{5... | collective-permute-start | bytes 1622024 | tf_op jit(solution)/shard_map/ppermute | solution.py:519
  127.6 27.6 %copy-start.12 = (f32[64]{0:T(128)S(1)}, f32[64]{0:T(128)}, u32[]{:S(2)}) copy-start(f32[64]{0:T(128)} %param.16) | copy-start | bytes 772
  127.6 7.9 %collective-permute-start.16 = (bf16[272,512]{1,0:T(8,128)(2,1)S(1)}, bf16[272,512]{1,0:T(8,128)(2,1)S(1)}, u32[]{:S(2)}, u32[]{:S(2)}) collective-permute-start(bf16[272,512]{1,0:T(8,128)(2,1)S(1)} %pad_maximum_fusion.5), channel_id=1, source_target_pairs={{0,16},{4,20},{8,24},{12,28},{16,0},{20,4},{24,8},{28,12},{1,17},{... | collective-permute-start | bytes 835592 | tf_op jit(solution)/shard_map/ppermute | solution.py:519
  135.8 5.6 %collective-permute-start.17 = (bf16[80,512]{1,0:T(8,128)(2,1)S(1)}, bf16[80,512]{1,0:T(8,128)(2,1)S(1)}, u32[]{:S(2)}, u32[]{:S(2)}) collective-permute-start(bf16[80,512]{1,0:T(8,128)(2,1)S(1)} %get-tuple-element.96), channel_id=1, source_target_pairs={{0,1},{1,0},{2,3},{3,2},{4,5},{5,4},{6,7},{7,6},{8,9},{9,8},{10,11... | collective-permute-start | bytes 245768 | tf_op jit(solution)/shard_map/ppermute | solution.py:519
  137.5 7.6 %collective-permute-start.18 = (bf16[80,512]{1,0:T(8,128)(2,1)S(1)}, bf16[80,512]{1,0:T(8,128)(2,1)S(1)}, u32[]{:S(2)}, u32[]{:S(2)}) collective-permute-start(bf16[80,512]{1,0:T(8,128)(2,1)S(1)} %get-tuple-element.97), channel_id=1, source_target_pairs={{0,2},{1,3},{2,0},{3,1},{4,6},{5,7},{6,4},{7,5},{8,10},{9,11},{10,... | collective-permute-start | bytes 245768 | tf_op jit(solution)/shard_map/ppermute | solution.py:519
  138.6 6.5 %collective-permute-start.19 = (bf16[80,512]{1,0:T(8,128)(2,1)S(1)}, bf16[80,512]{1,0:T(8,128)(2,1)S(1)}, u32[]{:S(2)}, u32[]{:S(2)}) collective-permute-start(bf16[80,512]{1,0:T(8,128)(2,1)S(1)} %get-tuple-element.98), channel_id=1, source_target_pairs={{0,3},{1,2},{2,1},{3,0},{4,7},{5,6},{6,5},{7,4},{8,11},{9,10},{10,... | collective-permute-start | bytes 245768 | tf_op jit(solution)/shard_map/ppermute | solution.py:519
  145.2 4.3 %collective-permute-start.20 = (bf16[64,512]{1,0:T(8,128)(2,1)S(1)}, bf16[64,512]{1,0:T(8,128)(2,1)S(1)}, u32[]{:S(2)}, u32[]{:S(2)}) collective-permute-start(bf16[64,512]{1,0:T(8,128)(2,1)S(1)} %fusion.3), channel_id=1, source_target_pairs={{0,16},{4,20},{8,24},{12,28},{16,0},{20,4},{24,8},{28,12},{1,17},{... | collective-permute-start | bytes 196616 | tf_op jit(solution)/shard_map/ppermute | solution.py:547
  149.5 5.0 %collective-permute-start.21 = (bf16[128,512]{1,0:T(8,128)(2,1)S(1)}, bf16[128,512]{1,0:T(8,128)(2,1)S(1)}, u32[]{:S(2)}, u32[]{:S(2)}) collective-permute-start(bf16[128,512]{1,0:T(8,128)(2,1)S(1)} %bitcast.137), channel_id=1, source_target_pairs={{0,8},{4,12},{8,0},{12,4},{16,24},{20,28},{24,16},{28,20},{1,9},{5... | collective-permute-start | bytes 393224 | tf_op jit(solution)/shard_map/ppermute | solution.py:547
  154.6 1.6 %collective-permute-start.22 = (bf16[256,512]{1,0:T(8,128)(2,1)S(1)}, bf16[256,512]{1,0:T(8,128)(2,1)S(1)}, u32[]{:S(2)}, u32[]{:S(2)}) collective-permute-start(bf16[256,512]{1,0:T(8,128)(2,1)S(1)} %bitcast.133), channel_id=1, source_target_pairs={{0,4},{4,0},{8,12},{12,8},{16,20},{20,16},{24,28},{28,24},{1,5},{5... | collective-permute-start | bytes 786440 | tf_op jit(solution)/shard_map/ppermute | solution.py:547
  (17 other events, 121.4 us)

commit v2 on v1

v2 whole, which is shorter than its diff:
```python
from functools import partial

import jax
import jax.numpy as jnp
from jax import lax
from jax.experimental import pallas as pl
from jax.experimental.pallas import tpu as pltpu
from jax.sharding import PartitionSpec as P

EPS = 1e-05
F32 = jnp.float32
BF16 = jnp.bfloat16
CHUNKS = 16
STEP_ROWS = 512
BLOCK = 256
PARAM_ROWS = 16
MIB = 1024 * 1024
INV_SQRT2 = 0.7071067811865476
INV_SQRT_2PI = 0.3989422804014327


def nt(a, b):
    return lax.dot_general(a, b, (((1,), (1,)), ((), ())), preferred_element_type=F32)


def nn(a, b):
    return lax.dot_general(a, b, (((1,), (0,)), ((), ())), preferred_element_type=F32)


def tn(a, b):
    return lax.dot_general(a, b, (((0,), (0,)), ((), ())), preferred_element_type=F32)


def cmul(ar, ai, br, bi):
    return ar * br - ai * bi, ar * bi + ai * br


def cpower(re, im, log2):
    for _ in range(log2):
        re, im = cmul(re, im, re, im)
    return re, im


def log2_of(n):
    return n.bit_length() - 1


def block_rows(step, block):
    return pl.ds(pl.multiple_of(step * STEP_ROWS + block * BLOCK, BLOCK), BLOCK)


def tile_rows(step, start):
    return pl.ds(pl.multiple_of(step * STEP_ROWS + start, 16), 16)


def alternate(first, second):
    i = j = 0
    while i < len(first) or j < len(second):
        if j >= len(second) or (i < len(first) and i * len(second) <= j * len(first)):
            first[i]()
            i += 1
        else:
            second[j]()
            j += 1


def run(pieces):
    for piece in pieces:
        piece()


def product_nt(out, left, right, size=256):
    def piece(n):
        out[:, n : n + size] = nt(left(), right[n : n + size, :])

    return [partial(piece, n) for n in range(0, right.shape[0], size)]


def product_nn(out, left, right, size=256):
    def piece(n):
        out[:, n : n + size] = nn(left(), right[:, n : n + size])

    return [partial(piece, n) for n in range(0, right.shape[1], size)]


def product_tn(total, left, right, size=256):
    def piece(n):
        total[n : n + size, :] += tn(left(slice(n, n + size)), right())

    return [partial(piece, n) for n in range(0, total.shape[0], size)]


def assemble(dst, own, other, first, rows, me, core, slots, negate_second):
    for slot in range(slots):
        for part in range(2):
            mine = own[me ^ slot, first : first + rows, :]
            theirs = other[me ^ slot, first : first + rows, :]
            value = jnp.where(core == part, mine, theirs)
            start = (part * slots + slot) * rows
            dst[start : start + rows, :] = -value if negate_second and part == 1 else value


def prepare(idx, x_ref, gain_ref, bias_ref, xhat_ref, norm_ref, rstd_ref):
    step = pl.program_id(0)
    width = x_ref.shape[2]
    per = x_ref.shape[1]
    gain, bias = gain_ref[...], bias_ref[...]
    for k in range(0, per, 8):
        rows = jnp.swapaxes(x_ref[:, k : k + 8, :], 0, 1).reshape(8 * CHUNKS, width)
        for r in range(0, 8 * CHUNKS, 16):
            place = tile_rows(step, k * CHUNKS + r)
            part = rows[r : r + 16]
            mean = jnp.mean(part, -1, keepdims=True)
            cen = part - mean
            var = jnp.mean(cen * cen, -1, keepdims=True)
            rstd = lax.rsqrt(var + EPS)
            xhat = cen * rstd
            xhat_ref[place, :] = xhat
            rstd_ref[place, :] = jnp.broadcast_to(rstd, (16, 128))
            norm_ref[place, :] = (xhat * gain + bias).astype(BF16)


def lower(idx, cot_ref, cotlow_ref):
    step = pl.program_id(0)
    width = cot_ref.shape[2]
    for k in range(0, cot_ref.shape[1], 8):
        rows = jnp.swapaxes(cot_ref[:, k : k + 8, :], 0, 1).reshape(8 * CHUNKS, width)
        place = pl.ds(pl.multiple_of(step * STEP_ROWS + k * CHUNKS, 128), 8 * CHUNKS)
        cotlow_ref[place, :] = rows.astype(BF16)


def first_scan(
    chunk, mp, idx, norm_ref, own_ref, other_ref,
    src_ref, wt_ref, par_ref, ends_ref, last_ref, h_ref, drive_a, drive_b,
):
    step = pl.program_id(0)
    width = norm_ref.shape[1]
    states = width // 2
    ns = states // mp

    @pl.when(step == 0)
    def _():
        me, core = idx[0], idx[1]
        assemble(wt_ref, own_ref, other_ref, 0, ns, me, core, mp, False)
        total = own_ref[0, ns : ns + PARAM_ROWS, :].astype(F32)
        for s in range(1, mp):
            total = total + own_ref[s, ns : ns + PARAM_ROWS, :].astype(F32)
        decay = total[0:1] + total[1:2] + total[2:3]
        gam = jnp.exp(total[3:4] + total[4:5] + total[5:6])
        radius = jnp.exp(-jnp.exp(decay[:, :states]))
        turn = jnp.exp(decay[:, states:])
        re, im = radius * jnp.cos(turn), radius * jnp.sin(turn)
        lre, lim = cpower(re, im, log2_of(chunk))
        tre, tim = cpower(lre, lim, log2_of(CHUNKS))
        par_ref[0:1, :] = jnp.concatenate([re, im], 1)
        par_ref[1:2, :] = gam
        par_ref[2:3, :] = jnp.concatenate([lre, lim], 1)
        par_ref[3:5, :] = total[6:8]
        par_ref[5:8, :] = jnp.zeros((3, width), F32)
        pre, pim = jnp.ones_like(tre), jnp.zeros_like(tim)
        for s in range(mp):
            par_ref[8 + s : 9 + s, :] = jnp.concatenate([pre, pim], 1)
            pre, pim = cmul(pre, pim, tre, tim)
        h_ref[...] = jnp.zeros_like(h_ref)

    gam = par_ref[1:2, :]
    lre, lim = par_ref[0:1, :states], par_ref[0:1, states:]
    h = [h_ref[:, :states], h_ref[:, states:]]

    def drive_pieces(b, drive):
        return product_nt(drive, lambda: norm_ref[block_rows(step, b), :], wt_ref)

    def scan_piece(b, drive, r):
        hre, him = h
        src = drive[r : r + CHUNKS, :] * gam
        src_ref[tile_rows(step, b * BLOCK + r), :] = src
        h[0] = src[:, :states] + lre * hre - lim * him
        h[1] = src[:, states:] + lre * him + lim * hre

    def scan_pieces(b, drive):
        return [partial(scan_piece, b, drive, r) for r in range(0, BLOCK, CHUNKS)]

    run(drive_pieces(0, drive_a))
    alternate(drive_pieces(1, drive_b), scan_pieces(0, drive_a))
    run(scan_pieces(1, drive_b))
    hre, him = h
    h_ref[:, :states] = hre
    h_ref[:, states:] = him

    @pl.when(step == pl.num_programs(0) - 1)
    def _():
        ends_ref[...] = h_ref[...]
        pre, pim = par_ref[2:3, :states], par_ref[2:3, states:]
        re, im = h_ref[0:1, :states], h_ref[0:1, states:]
        for c in range(1, CHUNKS):
            mre, mim = cmul(pre, pim, re, im)
            re, im = mre + h_ref[c : c + 1, :states], mim + h_ref[c : c + 1, states:]
        last_ref[...] = jnp.broadcast_to(jnp.concatenate([re, im], 1), last_ref.shape)


def gelu_parts(v):
    cdf = 0.5 * (1.0 + lax.erf(v * INV_SQRT2))
    pdf = jnp.exp(-0.5 * v * v) * INV_SQRT_2PI
    return v * cdf, cdf + v * pdf


def readout(mp, idx, xhat_ref, src_ref, par_ref, ends_ref, gain_ref, bias_ref, skip_ref, own_ref, other_ref, *rest):
    others = rest[: mp - 1]
    (state_ref, act_ref, slope_ref, wc_ref, h_ref, low_a, low_b, mix_a, mix_b) = rest[mp - 1 :]
    step = pl.program_id(0)
    width = xhat_ref.shape[1]
    states = width // 2
    me, core = idx[0], idx[1]

    @pl.when(step == 0)
    def _():
        assemble(wc_ref, own_ref, other_ref, 0, states // mp, me, core, mp, True)
        re = jnp.zeros((1, states), F32)
        im = jnp.zeros((1, states), F32)
        for s in range(1, mp):
            j = me ^ s
            power = jnp.maximum(me - 1 - j, 0)
            row = par_ref[pl.ds(8 + power, 1), :]
            sre, sim = cmul(row[:, :states], row[:, states:], others[s - 1][0:1, :states], others[s - 1][0:1, states:])
            keep = (j < me).astype(F32)
            re, im = re + keep * sre, im + keep * sim
        lre, lim = par_ref[2:3, :states], par_ref[2:3, states:]
        for c in range(CHUNKS):
            h_ref[c : c + 1, :states] = re
            h_ref[c : c + 1, states:] = im
            mre, mim = cmul(lre, lim, re, im)
            re, im = mre + ends_ref[c : c + 1, :states], mim + ends_ref[c : c + 1, states:]

    lre, lim = par_ref[0:1, :states], par_ref[0:1, states:]
    h = [h_ref[:, :states], h_ref[:, states:]]

    def scan_piece(b, low, r):
        hre, him = h
        rows = tile_rows(step, b * BLOCK + r)
        hre, him = (
            src_ref[rows, :states] + lre * hre - lim * him,
            src_ref[rows, states:] + lre * him + lim * hre,
        )
        low[r : r + CHUNKS, :states] = hre.astype(BF16)
        low[r : r + CHUNKS, states:] = him.astype(BF16)
        state_ref[rows, :] = low[r : r + CHUNKS, :]
        h[0], h[1] = hre, him

    def gelu_piece(b, mix, r):
        rows = tile_rows(step, b * BLOCK + r)
        for c in range(0, width, 128):
            cols = slice(c, c + 128)
            normed = xhat_ref[rows, cols] * gain_ref[:, cols] + bias_ref[:, cols]
            lru = mix[r : r + 16, cols] + skip_ref[:, cols] * normed
            act, slope = gelu_parts(lru)
            act_ref[rows, cols] = act.astype(BF16)
            slope_ref[rows, cols] = slope

    def scans(b, low):
        return [partial(scan_piece, b, low, r) for r in range(0, BLOCK, CHUNKS)]

    def mixes(low, mix):
        return product_nn(mix, lambda: low[...], wc_ref)

    def gelus(b, mix):
        return [partial(gelu_piece, b, mix, r) for r in range(0, BLOCK, 16)]

    run(scans(0, low_a))
    alternate(mixes(low_a, mix_a), scans(1, low_b))
    alternate(mixes(low_b, mix_b), gelus(0, mix_a))
    run(gelus(1, mix_b))
    h_ref[:, :states] = h[0]
    h_ref[:, states:] = h[1]


def add_branch(idx, x_ref, br_ref, y_ref):
    width = x_ref.shape[2]
    for k in range(0, x_ref.shape[1], 8):
        rows = br_ref[k * CHUNKS : (k + 8) * CHUNKS, :].astype(F32).reshape(8, CHUNKS, width)
        y_ref[:, k : k + 8, :] = x_ref[:, k : k + 8, :] + jnp.swapaxes(rows, 0, 1)


def gating(mp, idx, cotlow_ref, act_ref, par_ref, own_ref, other_ref,
           br_ref, gpre_ref, wg_ref, vec_ref, pre_a, pre_b):
    step = pl.program_id(0)
    width = act_ref.shape[1]
    core = idx[1]

    @pl.when(step == 0)
    def _():
        assemble(wg_ref, own_ref, other_ref, width // 2 // mp, width // mp, idx[0], core, mp, False)
        vec_ref[...] = jnp.zeros_like(vec_ref)

    def pre_pieces(block, pre):
        rows = pl.ds(pl.multiple_of(block * BLOCK, BLOCK), BLOCK)
        return product_nt(pre, lambda: act_ref[rows, :], wg_ref)

    @pl.when(step == 0)
    def _():
        run(pre_pieces(0, pre_a))

    sums = {}

    def gate_piece(b, pre, start, c):
        cols = slice(c, c + 128)
        gate_cols = slice(width + c, width + c + 128)
        for r in range(start, start + 64, 16):
            rows = tile_rows(step, b * BLOCK + r)
            value = pre[r : r + 16, cols] + par_ref[3:4, cols]
            gate = pre[r : r + 16, gate_cols] + par_ref[4:5, cols]
            sig = 0.5 * jnp.tanh(0.5 * gate) + 0.5
            branch = value * sig
            br_ref[b * BLOCK + r : b * BLOCK + r + 16, cols] = branch.astype(BF16)
            g = cotlow_ref[rows, cols].astype(F32)
            g_value = (g * sig).astype(BF16)
            g_gate = (g * branch * (1.0 - sig)).astype(BF16)
            gpre_ref[rows, cols] = g_value
            gpre_ref[rows, gate_cols] = g_gate
            for key, part in ((("value", c), g_value), (("gate", c), g_gate)):
                part = part.astype(F32)
                sums[key] = sums[key] + part if key in sums else part

    def gate_pieces(b, pre):
        return [
            partial(gate_piece, b, pre, start, c) for start in range(0, BLOCK, 64) for c in range(0, width, 128)
        ]

    after = jnp.minimum(2 * step + 2, act_ref.shape[0] // BLOCK - 1)
    alternate(pre_pieces(2 * step + 1, pre_b), gate_pieces(0, pre_a))
    alternate(pre_pieces(after, pre_a), gate_pieces(1, pre_b))
    for c in range(0, width, 128):
        vec_ref[1:2, c : c + 128] += jnp.sum(sums["value", c], 0, keepdims=True)
        vec_ref[2:3, c : c + 128] += jnp.sum(sums["gate", c], 0, keepdims=True)


def weight_products(idx, gpre_ref, act_ref, state_ref, gmix_ref, keep_ref, send_ref):
    core = idx[1]

    def product(left_ref, right_ref, first):
        columns = left_ref.shape[1]
        size = columns // 2
        for n in range(0, columns, 256):
            total = tn(left_ref[:, n : n + 256], right_ref[...])
            here = slice(first + n % size, first + n % size + 256)

            @pl.when(core == n // size)
            def _():
                keep_ref[here, :] = total

            @pl.when(core != n // size)
            def _():
                send_ref[here, :] = total.astype(BF16)

    product(gpre_ref, act_ref, 0)
    product(state_ref, gmix_ref, gpre_ref.shape[1] // 2)


def unmix(idx, gpre_ref, slope_ref, norm_ref, wg_ref, wc_ref, par_ref,
          gmix_ref, gs_ref, adj_ref, first_ref, vec_ref, p_ref, ga_a, ga_b, gmix_a, gmix_b, gs_a, gs_b):
    step = pl.program_id(0)
    width = norm_ref.shape[1]
    states = width // 2
    core = idx[1]

    @pl.when(step == 0)
    def _():
        p_ref[:, :states] = jnp.ones((8, states), F32)
        p_ref[:, states:] = jnp.zeros((8, states), F32)
        adj_ref[...] = jnp.zeros_like(adj_ref)
        vec_ref[...] = jnp.zeros_like(vec_ref)

    sums = {}

    def act_pieces(b, ga):
        return product_nn(ga, lambda: gpre_ref[block_rows(step, b), :], wg_ref)

    def lru_piece(b, ga, gmix, r):
        rows = tile_rows(step, b * BLOCK + r)
        for c in range(0, width, 128):
            cols = slice(c, c + 128)
            g_lru = ga[r : r + 16, cols] * slope_ref[rows, cols]
            low = g_lru.astype(BF16)
            gmix[r : r + 16, cols] = low
            gmix_ref[rows, cols] = low
            part = g_lru * norm_ref[rows, cols].astype(F32)
            sums[c] = sums[c] + part if c in sums else part

    def lru_pieces(b, ga, gmix):
        return [partial(lru_piece, b, ga, gmix, r) for r in range(0, BLOCK, 16)]

    def mix_pieces(b, gs, gmix):
        return product_nt(gs, lambda: gmix[...], wc_ref)

    lre, lim = par_ref[0:1, :states], par_ref[0:1, states:]
    power = [p_ref[:, :states], p_ref[:, states:]]
    are = [adj_ref[c : c + 8, :states] for c in range(0, CHUNKS, 8)]
    aim = [adj_ref[c : c + 8, states:] for c in range(0, CHUNKS, 8)]

    def end_piece(b, gs, r):
        pre, pim = power
        for n, c in enumerate(range(0, CHUNKS, 8)):
            gre, gim = gs[r + c : r + c + 8, :states], gs[r + c : r + c + 8, states:]
            mre, mim = cmul(pre, pim, gre, gim)
            are[n], aim[n] = are[n] + mre, aim[n] + mim
        gs_ref[tile_rows(step, b * BLOCK + r), :] = gs[r : r + CHUNKS, :]
        power[0], power[1] = pre * lre + pim * lim, pim * lre - pre * lim

    def end_pieces(b, gs):
        return [partial(end_piece, b, gs, r) for r in range(0, BLOCK, CHUNKS)]

    run(act_pieces(0, ga_a))
    alternate(act_pieces(1, ga_b), lru_pieces(0, ga_a, gmix_a))
    alternate(mix_pieces(0, gs_a, gmix_a), lru_pieces(1, ga_b, gmix_b))
    alternate(mix_pieces(1, gs_b, gmix_b), end_pieces(0, gs_a))
    run(end_pieces(1, gs_b))
    for c in range(0, width, 128):
        vec_ref[0:1, c : c + 128] += jnp.sum(sums[c], 0, keepdims=True)
    for n, c in enumerate(range(0, CHUNKS, 8)):
        adj_ref[c : c + 8, :states] = are[n]
        adj_ref[c : c + 8, states:] = aim[n]
    p_ref[:, :states] = power[0]
    p_ref[:, states:] = power[1]

    @pl.when(step == pl.num_programs(0) - 1)
    def _():
        lre, lim = par_ref[2:3, :states], -par_ref[2:3, states:]
        last = CHUNKS - 1
        re, im = adj_ref[last : last + 1, :states], adj_ref[last : last + 1, states:]
        for c in range(CHUNKS - 2, -1, -1):
            mre, mim = cmul(lre, lim, re, im)
            re, im = mre + adj_ref[c : c + 1, :states], mim + adj_ref[c : c + 1, states:]
        first_ref[...] = jnp.broadcast_to(jnp.concatenate([re, im], 1), first_ref.shape)


def adjoint_scan(mp, idx, keep_in, send_in, gs_ref, state_ref, src_ref, norm_ref, par_ref, adj_ref, *rest):
    others = rest[: mp - 1]
    (gdrive_ref, keep_ref, send_ref, vec_ref, acc_ref, h_ref, gdrive_a, gdrive_b) = rest[mp - 1 :]
    step = 0
    width = gs_ref.shape[1]
    states = width // 2
    me, core = idx[0], idx[1]

    re = jnp.zeros((1, states), F32)
    im = jnp.zeros((1, states), F32)
    for s in range(1, mp):
        j = me ^ s
        power = jnp.maximum(j - me - 1, 0)
        row = par_ref[pl.ds(8 + power, 1), :]
        sre, sim = cmul(row[:, :states], -row[:, states:], others[s - 1][0:1, :states], others[s - 1][0:1, states:])
        keep = (j > me).astype(F32)
        re, im = re + keep * sre, im + keep * sim
    lre, lim = par_ref[2:3, :states], -par_ref[2:3, states:]
    for c in range(CHUNKS - 1, -1, -1):
        h_ref[c : c + 1, :states] = re
        h_ref[c : c + 1, states:] = im
        mre, mim = cmul(lre, lim, re, im)
        re, im = mre + adj_ref[c : c + 1, :states], mim + adj_ref[c : c + 1, states:]
    acc_ref[...] = jnp.zeros_like(acc_ref)

    lre, lim = par_ref[0:1, :states], par_ref[0:1, states:]
    gam = par_ref[1:2, :states]
    h = [h_ref[:, :states], h_ref[:, states:]]
    sums = [jnp.zeros((CHUNKS, states), F32)] * 3

    def scan_piece(b, gdrive, r):
        hre, him = h
        rows = tile_rows(step, b * BLOCK + r)
        tre, tim = state_ref[rows, :states].astype(F32), state_ref[rows, states:].astype(F32)
        sums[0] = sums[0] + (hre * tre + him * tim)
        sums[1] = sums[1] + (him * tre - hre * tim)
        hre, him = (
            gs_ref[rows, :states] + lre * hre + lim * him,
            gs_ref[rows, states:] + lre * him - lim * hre,
        )
        sums[2] = sums[2] + (hre * src_ref[rows, :states] + him * src_ref[rows, states:])
        gdrive[r : r + CHUNKS, :states] = (hre * gam).astype(BF16)
        gdrive[r : r + CHUNKS, states:] = (him * gam).astype(BF16)
        gdrive_ref[rows, :] = gdrive[r : r + CHUNKS, :]
        h[0], h[1] = hre, him

    def scans(b, gdrive):
        return [partial(scan_piece, b, gdrive, r) for r in range(BLOCK - CHUNKS, -1, -CHUNKS)]

    def weight_pieces(b, gdrive):
        return product_tn(acc_ref, lambda cols: gdrive[:, cols], lambda: norm_ref[block_rows(step, b), :])

    last = gs_ref.shape[0] // BLOCK - 1
    buffers = (gdrive_a, gdrive_b)
    run(scans(last, buffers[last % 2]))
    for b in range(last - 1, -1, -1):
        alternate(weight_pieces(b + 1, buffers[(b + 1) % 2]), scans(b, buffers[b % 2]))
    run(weight_pieces(0, buffers[0]))
    first = keep_ref.shape[0] - states
    keep_ref[first:, :] = acc_ref[pl.ds(core * states, states), :]
    send_ref[first:, :] = acc_ref[pl.ds((1 - core) * states, states), :].astype(BF16)
    sre, sim, sgam = [jnp.sum(v, 0, keepdims=True) for v in sums]
    vec_ref[0:1, :] = jnp.concatenate([sre, sim], 1)
    vec_ref[1:2, :] = jnp.concatenate([sgam, jnp.zeros((1, states), F32)], 1)
    vec_ref[2:8, :] = jnp.zeros((6, width), F32)


def norm_back(idx, cot_ref, gdrive_ref, wt_ref, gmix_ref, xhat_ref, rstd_ref, gain_ref, skip_ref,
              gx_ref, vec_ref, gn_a, gn_b, dx_ref):
    step = pl.program_id(0)
    width = cot_ref.shape[2]
    per = STEP_ROWS // CHUNKS

    @pl.when(step == 0)
    def _():
        vec_ref[...] = jnp.zeros_like(vec_ref)

    def normed_pieces(block, gn):
        rows = pl.ds(pl.multiple_of(block * BLOCK, BLOCK), BLOCK)
        return product_nn(gn, lambda: gdrive_ref[rows, :], wt_ref)

    @pl.when(step == 0)
    def _():
        run(normed_pieces(0, gn_a))

    sums = [jnp.zeros((16, width), F32), jnp.zeros((16, width), F32)]

    def norm_piece(b, gn, r):
        rows = tile_rows(step, b * BLOCK + r)
        xhat = xhat_ref[rows, :]
        g = gn[r : r + 16, :] + skip_ref[...] * gmix_ref[rows, :].astype(F32)
        sums[0] = sums[0] + g * xhat
        sums[1] = sums[1] + g
        gh = g * gain_ref[...]
        first = jnp.mean(gh, -1, keepdims=True)
        second = jnp.mean(gh * xhat, -1, keepdims=True)
        rstd = jnp.concatenate([rstd_ref[rows, :]] * (width // 128), 1)
        dx_ref[b * BLOCK + r : b * BLOCK + r + 16, :] = rstd * (gh - first - xhat * second)

    def norm_pieces(b, gn):
        return [partial(norm_piece, b, gn, r) for r in range(0, BLOCK, 16)]

    def output_piece(k):
        rows = dx_ref[k * CHUNKS : (k + 8) * CHUNKS, :].reshape(8, CHUNKS, width)
        place = pl.ds(pl.multiple_of(step * per + k, 8), 8)
        gx_ref[:, k : k + 8, :] = cot_ref[:, place, :] + jnp.swapaxes(rows, 0, 1)

    after = jnp.minimum(2 * step + 2, gdrive_ref.shape[0] // BLOCK - 1)
    outputs = [partial(output_piece, k) for k in range(0, per, 8)]
    alternate(normed_pieces(2 * step + 1, gn_b), norm_pieces(0, gn_a))
    alternate(normed_pieces(after, gn_a), outputs[: len(outputs) // 2] + norm_pieces(1, gn_b) + outputs[len(outputs) // 2 :])
    vec_ref[0:1, :] += jnp.sum(sums[0], 0, keepdims=True)
    vec_ref[1:2, :] += jnp.sum(sums[1], 0, keepdims=True)


def pack_rows(idx, *refs):
    *parts, out = refs
    for i, part in enumerate(parts):
        out[i] = part[...]


def split_pieces(slots, count, hid, ns, idx, keep_ref, got_ref, skip_ref, glu_ref, norm_ref, lam_ref,
                 own_ref, vec_ref, *sends):
    place = idx[2]
    height = (hid + 2 * ns) // count
    for slot in range(slots):
        parts = ((slot * hid, hid, 0), (slots * hid + slot * ns, ns, hid), (slots * (hid + ns) + slot * ns, ns, hid + ns))
        for s in range(count):
            for first, size, low in parts:
                rows = size // count
                start = pl.multiple_of(first + (place ^ s) * rows, rows)
                piece = keep_ref[pl.ds(start, rows), :] + got_ref[pl.ds(start, rows), :].astype(F32)
                begin = slot * height + low // count
                if s == 0:
                    own_ref[begin : begin + rows, :] = piece
                else:
                    sends[s - 1][begin : begin + rows, :] = piece.astype(BF16)
    rows = [skip_ref[0:1, :], glu_ref[1:3, :], norm_ref[0:2, :], lam_ref[0:2, :], jnp.zeros((1, skip_ref.shape[1]), F32)]
    vec = jnp.concatenate(rows, 0)
    high = vec.astype(BF16)
    low = (vec - high.astype(F32)).astype(BF16)
    vec_ref[...] = high.astype(F32) + low.astype(F32)
    for send in sends:
        send[slots * height :, :] = jnp.concatenate([high.astype(F32), low.astype(F32)], 0).astype(BF16)


def call(kernel, steps, ins, outs, scratch, mib, flops, moved, in_place=None):
    def in_hbm(array, block):
        return array if block is None or array.size < 65536 else pltpu.with_memory_space_constraint(array, pltpu.HBM)

    def spec(block):
        return pl.BlockSpec(memory_space=pltpu.VMEM) if block is None else block

    return pl.pallas_call(
        kernel,
        grid_spec=pltpu.PrefetchScalarGridSpec(
            num_scalar_prefetch=1,
            grid=(steps,),
            in_specs=[spec(block) for _, block in ins[1:]],
            out_specs=[spec(block) for _, _, block in outs],
            scratch_shapes=[pltpu.VMEM(*s) for s in scratch],
        ),
        out_shape=[jax.ShapeDtypeStruct(s, t) if block is None else pltpu.HBM(s, t) for s, t, block in outs],
        input_output_aliases=in_place or {},
        compiler_params=pltpu.CompilerParams(vmem_limit_bytes=mib * MIB),
        cost_estimate=pl.CostEstimate(flops=flops, bytes_accessed=moved * MIB, transcendentals=0),
    )(*[in_hbm(a, block) for a, block in ins])


def xor_pairs(n, s):
    return [(i, i ^ s) for i in range(n)]


def from_each(value, axis, n):
    return [value] + [lax.ppermute(value, axis, xor_pairs(n, s)) for s in range(1, n)]


def tree_sum(parts):
    parts = list(parts)
    while len(parts) > 1:
        parts = [parts[i] + parts[i + 1] for i in range(0, len(parts), 2)]
    return parts[0]


def high_low(v):
    high = lax.reduce_precision(v, 8, 7)
    return high, lax.reduce_precision(v - high, 8, 7)


def scatter_sum(rows, position, count, permute, vec=None):
    width = rows.shape[-1]
    own = lax.dynamic_index_in_dim(rows, position, 0, keepdims=False)
    tail = []
    if vec is not None:
        high, low = high_low(vec)
        tail = [high.astype(BF16), low.astype(BF16)]
        vec = high + low
    got, vecs = [own], [vec]
    for s in range(1, count):
        send = lax.dynamic_index_in_dim(rows, position ^ s, 0, keepdims=False).astype(BF16)
        buffer = permute(jnp.concatenate([send.reshape(-1, width)] + tail) if tail else send, s)
        if tail:
            n = buffer.shape[0] - 2 * vec.shape[0]
            vecs.append(buffer[n : n + vec.shape[0]].astype(F32) + buffer[n + vec.shape[0] :].astype(F32))
            buffer = buffer[:n].reshape(own.shape)
        got.append(buffer.astype(F32))
    return tree_sum(got), (None if vec is None else tree_sum(vecs))


def flip(stack, position):
    n = stack.shape[0]
    for b in range(log2_of(n)):
        pairs = stack.reshape((n >> (b + 1), 2, 1 << b) + stack.shape[1:])
        pairs = jnp.where((position >> b) & 1 == 1, pairs[:, ::-1], pairs)
        stack = pairs.reshape(stack.shape)
    return stack


def on_device(
    block_input, ln_gain, ln_bias, nu_log, theta_log, gamma_log, in_weight, out_weight, skip, glu_weight, glu_bias,
    out_cotangent,
):
    mp = lax.axis_size("mp")
    dp = lax.axis_size("dp")
    plane = dp // 2
    me = lax.axis_index("mp")
    dpi = lax.axis_index("dp")
    core = dpi & 1
    place = dpi >> 1
    idx = jnp.stack([me, core, place]).astype(jnp.int32)
    tokens, width = block_input.shape[1:]
    ns = nu_log.shape[0]
    states = ns * mp
    hid = glu_weight.shape[2]
    chunk = tokens // CHUNKS
    per = STEP_ROWS // CHUNKS
    steps = tokens // STEP_ROWS
    x = block_input.reshape(CHUNKS, chunk, width)
    cot = out_cotangent.reshape(CHUNKS, chunk, width)
    gain, bias, skp = ln_gain[None], ln_bias[None], skip[None]

    def over_core(v):
        return lax.ppermute(v, "dp", xor_pairs(dp, 1))

    def over_plane(v, s):
        return lax.ppermute(v, "dp", xor_pairs(dp, 2 * s))

    def over_mp(v, s):
        return lax.ppermute(v, "mp", xor_pairs(mp, s))

    here = (jnp.arange(mp) == me).astype(F32)[:, None]

    def placed(v):
        return (here * v[None]).reshape(-1)

    def thirds(v):
        high, rest = high_low(v)
        return [high, rest, lax.reduce_precision(v - high - rest, 8, 7)]

    decay_row = jnp.concatenate([placed(nu_log), placed(theta_log)])
    gam_row = jnp.concatenate([placed(gamma_log), placed(gamma_log)])
    bias_rows = [placed(glu_bias[p].astype(F32)) for p in range(2)]
    params = jnp.stack(thirds(decay_row) + thirds(gam_row) + bias_rows).astype(BF16)
    params = jnp.pad(params, ((0, PARAM_ROWS - params.shape[0]), (0, 0)))

    def gathered(value, name):
        with jax.named_scope(name):
            return [value] + [over_mp(value, s) for s in range(1, mp)]

    def packed(parts, *earlier):
        value = parts[0]
        parts = lax.optimization_barrier(tuple(parts) + earlier)[: len(parts)]
        shape = (mp,) + value.shape
        return call(pack_rows, 1, [(idx, None)] + [(p, None) for p in parts], [(shape, value.dtype, None)], [], 1, 0, 0)[0]

    def tied(value, *earlier):
        return lax.optimization_barrier((value,) + earlier)[0]

    in_part = lax.dynamic_index_in_dim(in_weight, core, 1, keepdims=False).T
    out_part = lax.dynamic_index_in_dim(out_weight, core, 0, keepdims=False)
    glu_part = lax.dynamic_index_in_dim(glu_weight, core, 1, keepdims=False).T
    in_send = jnp.concatenate([in_part, params])
    both_part = jnp.concatenate([out_part, glu_part])
    x = tied(x, in_send, both_part)
    in_own = gathered(in_send, "gather_in")

    chunked = pl.BlockSpec((CHUNKS, per, width), lambda i, idx: (0, i, 0))
    vector = pl.BlockSpec((1, width), lambda i, idx: (0, 0))
    rowed = pl.BlockSpec((STEP_ROWS, width), lambda i, idx: (i, 0))
    big = (tokens, width)
    npar = 8 + mp
    product = 2 * tokens * width * width
    small = ((8, width), F32, None)

    def scratch(*kinds):
        return [((rows, cols), kind) for rows, cols, kind in kinds]

    xhat, norm, rstd = call(
        prepare, steps,
        [(idx, None), (x, chunked), (gain, vector), (bias, vector)],
        [(big, F32, None), (big, BF16, None), ((tokens, 128), F32, None)],
        [], 6, product, 12,
    )
    in_own = packed(in_own, norm)
    in_other = over_core(in_own)
    both_own = gathered(tied(both_part, in_own), "gather_out_glu")
    (cotlow,) = call(lower, steps, [(idx, None), (tied(cot, in_own), chunked)], [(big, BF16, None)], [], 5, 0, 8)
    norm = tied(norm, cotlow)
    src, wt, par, ends, last = call(
        partial(first_scan, chunk, mp), steps,
        [(idx, None), (norm, None), (in_own, None), (in_other, None)],
        [(big, F32, None), ((width, width), BF16, None), ((npar, width), F32, None), ((CHUNKS, width), F32, None), small],
        scratch((CHUNKS, width, F32), (BLOCK, width, F32), (BLOCK, width, F32)), 5, product, 8,
    )
    with jax.named_scope("carry"):
        lasts = [over_mp(last, s) for s in range(1, mp)]
    both_own = packed(both_own, *lasts)
    both_other = over_core(both_own)
    state, act, slope, wc = call(
        partial(readout, mp), steps,
        [(idx, None), (xhat, None), (src, None), (par, None), (ends, None), (gain, vector), (bias, vector), (skp, vector),
         (both_own, None), (both_other, None)] + [(v, None) for v in lasts],
        [(big, BF16, None), (big, BF16, None), (big, F32, None), ((width, width), BF16, None)],
        scratch((CHUNKS, width, F32), (BLOCK, width, BF16), (BLOCK, width, BF16), (BLOCK, width, F32), (BLOCK, width, F32)), 8, product, 8,
    )
    branch, gpre, wg, vec_glu = call(
        partial(gating, mp), steps,
        [(idx, None), (cotlow, None), (act, None), (par, None), (both_own, None), (both_other, None)],
        [(big, BF16, rowed), ((tokens, 2 * width), BF16, None), ((2 * width, width), BF16, None), small],
        scratch((BLOCK, 2 * width, F32), (BLOCK, 2 * width, F32)),
        10, 2 * product, 8,
    )
    gmix, gs, adj, first, vec_skip = call(
        unmix, steps,
        [(idx, None), (gpre, None), (slope, None), (norm, None), (wg, None), (wc, None), (par, None)],
        [(big, BF16, None), (big, F32, None), ((CHUNKS, width), F32, None), small, small],
        scratch((8, width, F32), (BLOCK, width, F32), (BLOCK, width, F32), (BLOCK, width, BF16),
                (BLOCK, width, BF16), (BLOCK, width, F32), (BLOCK, width, F32)),
        10, 4 * product, 8,
    )
    with jax.named_scope("carry_back"):
        firsts = [over_mp(first, s) for s in range(1, mp)]
    early_rows = mp * (hid + ns)
    half_rows = early_rows + states
    sums = [((half_rows, width), F32, None), ((half_rows, width), BF16, None)]
    keep, send = call(
        weight_products, 1,
        [(idx, None), (tied(gpre, first), None), (act, None), (state, None), (gmix, None)],
        sums, [], 12, 0, 0,
    )
    firsts[0] = tied(firsts[0], send)
    gdrive, keep, send, vec_lam = call(
        partial(adjoint_scan, mp), 1,
        [(idx, None), (keep, None), (send, None), (gs, None), (state, None), (src, None), (norm, None), (par, None),
         (adj, None)] + [(v, None) for v in firsts],
        [(big, BF16, None)] + sums + [small],
        scratch((width, width, F32), (CHUNKS, width, F32), (BLOCK, width, BF16),
                (BLOCK, width, BF16)), 8, product, 8, {1: 1, 2: 2},
    )
    with jax.named_scope("sum_core"):
        got = over_core(send)
    gx, vec_norm = call(
        norm_back, steps,
        [(idx, None), (cot, None), (gdrive, None), (wt, None), (gmix, None), (xhat, None), (rstd, None),
         (gain, vector), (skp, vector)],
        [((CHUNKS, chunk, width), F32, chunked), small],
        scratch((BLOCK, width, F32), (BLOCK, width, F32), (STEP_ROWS, width, F32)), 8, product, 8,
    )
    (y,) = call(add_branch, steps, [(idx, None), (x, chunked), (tied(branch, vec_norm), rowed)],
                [((CHUNKS, chunk, width), F32, chunked)], [], 10, 0, 0)
    keep, nu_log, theta_log, me, core, place = lax.optimization_barrier(
        (keep, nu_log, theta_log, me, core, place, vec_norm)
    )[:6]
    height = mp * (hid + 2 * ns) // plane
    if ns // plane % 16 == 0 and hid // plane % 16 == 0:
        own_piece, vec, *sends = call(
            partial(split_pieces, mp, plane, hid, ns), 1,
            [(idx, None), (keep, None), (got, None), (vec_skip, None), (vec_glu, None), (vec_norm, None), (vec_lam, None)],
            [((height, width), F32, None), small] + [((height + 16, width), BF16, None)] * (plane - 1), [], 4, 0, 0,
        )
    else:
        vec = jnp.concatenate([vec_skip[0:1], vec_glu[1:3], vec_norm[0:2], vec_lam[0:2], jnp.zeros((1, width), F32)])
        vec_high, vec_low = high_low(vec)
        vec, vec_rows = vec_high + vec_low, jnp.concatenate([vec_high, vec_low]).astype(BF16)
        both = keep + got.astype(F32)
        both = [both[: mp * hid], both[mp * hid : early_rows], both[early_rows:]]
        both = jnp.concatenate([v.reshape(mp, plane, -1, width) for v in both], 2).swapaxes(0, 1)
        sends = [lax.dynamic_index_in_dim(both, place ^ s, 0, keepdims=False) for s in range(plane)]
        sends = [v.reshape(-1, width) for v in sends]
        own_piece, sends = sends[0], [jnp.concatenate([v.astype(BF16), vec_rows]) for v in sends[1:]]
    with jax.named_scope("sum_plane"):
        pieces = [over_plane(v, s + 1) for s, v in enumerate(sends)]
    pieces[0] = tied(pieces[0], y)
    vec = tree_sum(
        [vec] + [p[height : height + 8].astype(F32) + p[height + 8 :].astype(F32) for p in pieces]
    )
    rows = tree_sum([own_piece] + [p[:height].astype(F32) for p in pieces]).reshape(mp, -1, width)
    with jax.named_scope("sum_mp"):
        piece, vec = scatter_sum(rows, me, mp, over_mp, vec)
    high, low = high_low(vec)
    with jax.named_scope("spread_plane"):
        piece = piece.astype(BF16)
        stack = jnp.stack([piece] + [over_plane(piece, s) for s in range(1, plane)])
    n = plane * piece.shape[0]
    got = over_core(jnp.concatenate([stack.reshape(n, width), high.astype(BF16), low.astype(BF16)]))
    vec = high + low + (got[n : n + 8].astype(F32) + got[n + 8 :].astype(F32))
    total = jnp.stack([flip(stack, place), flip(got[:n].reshape(stack.shape), place)])
    total = flip(total, core).astype(F32)
    nh, nr = hid // plane, ns // plane

    def part(start, size):
        return total[:, :, start : start + size].reshape(2, -1, width)

    grad_glu_weight = part(0, nh).transpose(2, 0, 1)
    grad_out = part(nh, nr)
    grad_out_weight = jnp.stack([grad_out[0], -grad_out[1]])
    grad_in_weight = part(nh + nr, nr).transpose(2, 0, 1)

    def decay(nu, theta):
        radius = jnp.exp(-jnp.exp(nu))
        turn = jnp.exp(theta)
        return radius * jnp.cos(turn), radius * jnp.sin(turn)

    _, decay_back = jax.vjp(decay, nu_log, theta_log)
    grad_glu_bias = lax.dynamic_slice_in_dim(vec[1:3], me * hid, hid, 1)
    grad_lam = lax.dynamic_slice_in_dim(vec[5].reshape(2, states), me * ns, ns, 1)
    grad_nu_log, grad_theta_log = decay_back((grad_lam[0], grad_lam[1]))
    grad_gamma_log = lax.dynamic_slice_in_dim(vec[6], me * ns, ns, 0)
    return (
        y.reshape(block_input.shape),
        gx.reshape(block_input.shape),
        vec[3],
        vec[4],
        grad_nu_log,
        grad_theta_log,
        grad_gamma_log,
        grad_in_weight,
        grad_out_weight,
        vec[0],
        grad_glu_weight,
        grad_glu_bias,
    )


def solution(mesh):
    in_specs = (
        P("dp", "mp", None), P(), P(), P("mp"), P("mp"), P("mp"), P(None, None, "mp"), P(None, "mp", None), P(),
        P(None, None, "mp"), P(None, "mp"), P("dp", "mp", None),
    )
    out_specs = (
        P("dp", "mp", None), P("dp", "mp", None), P(), P(), P("mp"), P("mp"), P("mp"), P(None, None, "mp"),
        P(None, "mp", None), P(), P(None, None, "mp"), P(None, "mp"),
    )
    return jax.shard_map(on_device, mesh=mesh, in_specs=in_specs, out_specs=out_specs, check_vma=False)
```

time: 160 us -> 119 us (0.74)
  waiting for transfers between devices: 52.2 us -> 24.4 us
  local copies, waits for them, and re-layouts: 13.7 us -> 7.47 us
  other arithmetic: 6.46 us -> 3.7 us
  Pallas kernels: 52.6 us -> 50.1 us
    ppermute x23 -> x25, waiting for transfers between devices: 52.2 us -> 24.4 us  [the longest x6 10.4 us: over_plane(): return lax.ppermute(v, 'dp', xor_pairs(dp, 2 * s))]
    unnamed x39 -> x23, local copies, waits for them, and re-layouts: 5.04 us -> 2.42 us
    pallas_call x3 -> x13, Pallas kernels: 52.6 us -> 50.1 us  [call(): pl.pallas_call(kernel, grid_spec=pltpu.PrefetchScalarGridSpec(num_scalar_...]
    dynamic_slice x1 -> x0, local copies, waits for them, and re-layouts: 1.76 us -> none  [on_device(): keep = lax.dynamic_index_in_dim(rows, bit, 0, keepdims=False)]
    concatenate x5 -> x4, other arithmetic: 1.81 us -> 0.06 us  [the longest x1 0.02 us: on_device(): jnp.concatenate([stack.reshape(n, width), high.astype(BF16), low.astype(B...]
    ppermute x23 -> x25, starting transfers between devices: 32.8 us -> 32.1 us  [the longest x15 24.7 us: over_mp(): return lax.ppermute(v, 'mp', xor_pairs(mp, s))]
  transfers between devices with their start and end apart: 23 -> 25, of which waited for: 18 -> 10; matrix products, arithmetic and copies ran while one was open for 5% -> 1% of each run, Pallas kernels for 7% -> 24%
where the time goes in v2:
time: 119 us
  Pallas kernels  50.1 us (42%)
  starting transfers between devices  32.1 us (27%)
  waiting for transfers between devices  24.4 us (21%)
  local copies, waits for them, and re-layouts  7.47 us (6%)
  other arithmetic  3.7 us (3%)
    pallas_call x13, Pallas kernels, call(): pl.pallas_call(kernel, grid_spec=pltpu.PrefetchScalarGridSpec(num_scalar_...  50.1 us
    ppermute x15, starting transfers between devices, over_mp(): return lax.ppermute(v, 'mp', xor_pairs(mp, s))  24.7 us
    ppermute x6, waiting for transfers between devices, over_plane(): return lax.ppermute(v, 'dp', xor_pairs(dp, 2 * s))  10.4 us
    ppermute x15, waiting for transfers between devices, over_mp(): return lax.ppermute(v, 'mp', xor_pairs(mp, s))  10.3 us
    ppermute x6, starting transfers between devices, over_plane(): return lax.ppermute(v, 'dp', xor_pairs(dp, 2 * s))  7.11 us
    ppermute x4, waiting for transfers between devices, over_core(): return lax.ppermute(v, 'dp', xor_pairs(dp, 1))  3.67 us
    unnamed x23, local copies, waits for them, and re-layouts  2.42 us
  transfers between devices with their start and end apart: 25, of which 10 were waited for; matrix products, arithmetic and copies ran while one was open for 1% of the time, Pallas kernels for 24%

profile of v2, /device:TPU:0, one launch (start us, length us, event | category | flops | bytes accessed | tf_op | source)
XLA Modules:
  0.0 118.8 jit_solution(11796992604600765592)
XLA Ops:
  3.4 5.1 %collective-permute-start.2 = (bf16[80,512]{1,0:T(8,128)(2,1)S(1)}, bf16[80,512]{1,0:T(8,128)(2,1)S(1)}, u32[]{:S(2)}, u32[]{:S(2)}) collective-permute-start(bf16[80,512]{1,0:T(8,128)(2,1)S(1)} %fusion.6.refs_0_), channel_id=1, source_target_pairs={{0,3},{1,2},{2,1},{3,0},{4,7},{5,6},{6,5},{7,4},{8,11},{9,10},{10,... | collective-permute-start | bytes 245768 | tf_op jit(solution)/shard_map/gather_in/ppermute | solution.py:683
  11.9 4.7 %shard_map.211 = (f32[2048,512]{1,0:T(8,128)S(1)}, bf16[2048,512]{1,0:T(8,128)(2,1)S(1)}, f32[2048,128]{1,0:T(8,128)S(1)}) custom-call(s32[3]{0:T(128)S(1)} %pad_add_fusion.idx, f32[16,128,512]{2,1,0:T(8,128)} %bitcast.113, f32[1,512]{1,0:T(1,128)S(1)} %bitcast.106, f32[1,512]{1,0:T(1,128)S(1)} %bitcast.109), custom_call_target="tpu_custom_call" | custom-call | flops 1073741824 | bytes 12582912 | tf_op jit(solution)/shard_map/pallas_call | solution.py:588
  17.3 3.8 %collective-permute-start.6 = (bf16[192,512]{1,0:T(8,128)(2,1)S(1)}, bf16[192,512]{1,0:T(8,128)(2,1)S(1)}, u32[]{:S(2)}, u32[]{:S(2)}) collective-permute-start(bf16[192,512]{1,0:T(8,128)(2,1)S(1)} %pad_maximum_fusion.4.refs_0_), channel_id=1, source_target_pairs={{0,3},{1,2},{2,1},{3,0},{4,7},{5,6},{6,5},{7,4},{8,11},{9,10},{10,... | collective-permute-start | bytes 589832 | tf_op jit(solution)/shard_map/gather_out_glu/ppermute | solution.py:683
  21.7 3.8 %shard_map.213.cotlow_ref = bf16[2048,512]{1,0:T(8,128)(2,1)S(1)} custom-call(s32[3]{0:T(128)S(1)} %pad_add_fusion.idx, f32[16,128,512]{2,1,0:T(8,128)} %bitcast.104), custom_call_target="tpu_custom_call" | custom-call | bytes 8388608 | tf_op jit(solution)/shard_map/pallas_call | solution.py:588
  25.6 2.7 %shard_map.214 = (f32[2048,512]{1,0:T(8,128)S(1)}, bf16[512,512]{1,0:T(8,128)(2,1)S(1)}, f32[12,512]{1,0:T(8,128)S(1)}, f32[16,512]{1,0:T(8,128)S(1)}, f32[8,512]{1,0:T(8,128)S(1)}) custom-call(s32[3]{0:T(128)S(1)} %pad_add_fusion.idx, bf16[2048,512]{1,0:T(8,128)(2,1)S(1)} %get-tuple-element.76.norm_ref, bf16[4,80,512]{2,1,0:T(8,128)(2,1)S(1)} %shard_map.212.own_ref, ...), custom_call_target="tpu_custom_call" | custom-call | flops 1073741824 | bytes 8388608 | tf_op jit(solution)/shard_map/pallas_call | solution.py:588
  28.4 3.8 %collective-permute-start.9 = (f32[8,512]{1,0:T(8,128)S(1)}, f32[8,512]{1,0:T(8,128)S(1)}, u32[]{:S(2)}, u32[]{:S(2)}) collective-permute-start(f32[8,512]{1,0:T(8,128)S(1)} %get-tuple-element.81), channel_id=1, source_target_pairs={{0,3},{1,2},{2,1},{3,0},{4,7},{5,6},{6,5},{7,4},{8,11},{9,10},{10,... | collective-permute-start | bytes 49160 | tf_op jit(solution)/shard_map/carry/ppermute | solution.py:683
  32.2 2.7 %collective-permute-start.7 = (f32[8,512]{1,0:T(8,128)S(1)}, f32[8,512]{1,0:T(8,128)S(1)}, u32[]{:S(2)}, u32[]{:S(2)}) collective-permute-start(f32[8,512]{1,0:T(8,128)S(1)} %get-tuple-element.81), channel_id=1, source_target_pairs={{0,1},{1,0},{2,3},{3,2},{4,5},{5,4},{6,7},{7,6},{8,9},{9,8},{10,11... | collective-permute-start | bytes 49160 | tf_op jit(solution)/shard_map/carry/ppermute | solution.py:683
  34.9 4.3 %collective-permute-done.5.refs_2_ = bf16[192,512]{1,0:T(8,128)(2,1)S(1)} collective-permute-done((bf16[192,512]{1,0:T(8,128)(2,1)S(1)}, bf16[192,512]{1,0:T(8,128)(2,1)S(1)}, u32[]{:S(2)}, u32[]{:S(2)}) %collective-permute-start.5) | collective-permute-done | bytes 196640 | tf_op jit(solution)/shard_map/gather_out_glu/ppermute | solution.py:683
  40.1 2.3 %collective-permute-done.10.other_ref = bf16[4,192,512]{2,1,0:T(8,128)(2,1)S(1)} collective-permute-done((bf16[4,192,512]{2,1,0:T(8,128)(2,1)S(1)}, bf16[4,192,512]{2,1,0:T(8,128)(2,1)S(1)}, u32[]{:S(2)}, u32[]{:S(2)}) %collective-permute-start.10) | collective-permute-done | bytes 786464 | tf_op jit(solution)/shard_map/ppermute | solution.py:677
  42.4 4.3 %shard_map.216 = (bf16[2048,512]{1,0:T(8,128)(2,1)S(1)}, bf16[2048,512]{1,0:T(8,128)(2,1)S(1)}, f32[2048,512]{1,0:T(8,128)S(1)}, bf16[512,512]{1,0:T(8,128)(2,1)S(1)}) custom-call(s32[3]{0:T(128)S(1)} %pad_add_fusion.idx, f32[2048,512]{1,0:T(8,128)S(1)} %get-tuple-element.75.xhat_ref, f32[2048,512]{1,0:T(8,128)S(1)} %get-tuple-element.77.src_ref, ...), custom_call_target="tpu_custom_call" | custom-call | flops 1073741824 | bytes 8388608 | tf_op jit(solution)/shard_map/pallas_call | solution.py:588
  46.7 7.0 %shard_map.217 = (bf16[2048,512]{1,0:T(8,128)(2,1)}, bf16[2048,1024]{1,0:T(8,128)(2,1)S(1)}, bf16[1024,512]{1,0:T(8,128)(2,1)S(1)}, f32[8,512]{1,0:T(8,128)S(1)}) custom-call(s32[3]{0:T(128)S(1)} %pad_add_fusion.idx, bf16[2048,512]{1,0:T(8,128)(2,1)S(1)} %shard_map.213.cotlow_ref, bf16[2048,512]{1,0:T(8,128)(2,1)S(1)} %get-tuple-element.86.act_ref, ...), custom_call_target="tpu_custom_call" | custom-call | flops 2147483648 | bytes 8388608 | tf_op jit(solution)/shard_map/pallas_call | solution.py:588
  53.7 5.0 %shard_map.218 = (bf16[2048,512]{1,0:T(8,128)(2,1)S(1)}, f32[2048,512]{1,0:T(8,128)S(1)}, f32[16,512]{1,0:T(8,128)S(1)}, f32[8,512]{1,0:T(8,128)S(1)}, f32[8,512]{1,0:T(8,128)S(1)}) custom-call(s32[3]{0:T(128)S(1)} %pad_add_fusion.idx, bf16[2048,1024]{1,0:T(8,128)(2,1)S(1)} %get-tuple-element.93.gpre_ref, f32[2048,512]{1,0:T(8,128)S(1)} %get-tuple-element.89.slope_ref, ...), custom_call_target="tpu_custom_call" | custom-call | flops 4294967296 | bytes 8388608 | tf_op jit(solution)/shard_map/pallas_call | solution.py:588
  59.2 2.4 %collective-permute-start.13 = (f32[8,512]{1,0:T(8,128)S(1)}, f32[8,512]{1,0:T(8,128)S(1)}, u32[]{:S(2)}, u32[]{:S(2)}) collective-permute-start(f32[8,512]{1,0:T(8,128)S(1)} %get-tuple-element.92), channel_id=1, source_target_pairs={{0,3},{1,2},{2,1},{3,0},{4,7},{5,6},{6,5},{7,4},{8,11},{9,10},{10,... | collective-permute-start | bytes 49160 | tf_op jit(solution)/shard_map/carry_back/ppermute | solution.py:683
  62.3 5.3 %shard_map.219 = (f32[1024,512]{1,0:T(8,128)S(1)}, bf16[1024,512]{1,0:T(8,128)(2,1)S(1)}) custom-call(s32[3]{0:T(128)S(1)} %pad_add_fusion.idx, bf16[2048,1024]{1,0:T(8,128)(2,1)S(1)} %get-tuple-element.93.gpre_ref, bf16[2048,512]{1,0:T(8,128)(2,1)S(1)} %get-tuple-element.86.act_ref, bf16[2048,512]{1,0:T(8,128)(2,1)S(1)} %get-tuple-element.94.state_ref, ...), custom_call_target="tpu_custom_call" | custom-call | tf_op jit(solution)/shard_map/pallas_call | solution.py:588
  67.6 3.5 %shard_map.220 = (bf16[2048,512]{1,0:T(8,128)(2,1)S(1)}, f32[1024,512]{1,0:T(8,128)S(1)}, bf16[1024,512]{1,0:T(8,128)(2,1)S(1)}, f32[8,512]{1,0:T(8,128)S(1)}) custom-call(s32[3]{0:T(128)S(1)} %pad_add_fusion.idx, f32[1024,512]{1,0:T(8,128)S(1)} %get-tuple-element.96.keep_in, ...), custom_call_target="tpu_custom_call", output_to_operand_aliasing={{1}: (1, {}), {2}: (2, {})} | custom-call | flops 1073741824 | bytes 8388608 | tf_op jit(solution)/shard_map/pallas_call | solution.py:588
  71.2 5.9 %shard_map.221 = (f32[16,128,512]{2,1,0:T(8,128)}, f32[8,512]{1,0:T(8,128)S(1)}) custom-call(s32[3]{0:T(128)S(1)} %pad_add_fusion.idx, f32[16,128,512]{2,1,0:T(8,128)S(1)} %bitcast.105, bf16[2048,512]{1,0:T(8,128)(2,1)S(1)} %get-tuple-element.101.gdrive_ref, bf16[512,512]{1,0:T(8,128)(2,1)S(1)} %get-tuple-element.102.wt_ref, ...), custom_call_target="tpu_custom_call" | custom-call | flops 1073741824 | bytes 8388608 | tf_op jit(solution)/shard_map/pallas_call | solution.py:588
  77.8 1.6 %collective-permute-start.15 = (bf16[272,512]{1,0:T(8,128)(2,1)S(1)}, bf16[272,512]{1,0:T(8,128)(2,1)S(1)}, u32[]{:S(2)}, u32[]{:S(2)}) collective-permute-start(bf16[272,512]{1,0:T(8,128)(2,1)S(1)} %get-tuple-element.114), channel_id=1, source_target_pairs={{0,8},{4,12},{8,0},{12,4},{16,24},{20,28},{24,16},{28,20},{1,9},{5... | collective-permute-start | bytes 835592 | tf_op jit(solution)/shard_map/sum_plane/ppermute | solution.py:680
  81.4 6.0 %shard_map.222 = f32[16,128,512]{2,1,0:T(8,128)} custom-call(s32[3]{0:T(128)S(1)} %pad_add_fusion.idx, f32[16,128,512]{2,1,0:T(8,128)} %bitcast.114, bf16[2048,512]{1,0:T(8,128)(2,1)} %get-tuple-element.105.br_ref), custom_call_target="tpu_custom_call" | custom-call | tf_op jit(solution)/shard_map/pallas_call | solution.py:588
  87.4 6.7 %collective-permute-done.16 = bf16[272,512]{1,0:T(8,128)(2,1)S(1)} collective-permute-done((bf16[272,512]{1,0:T(8,128)(2,1)S(1)}, bf16[272,512]{1,0:T(8,128)(2,1)S(1)}, u32[]{:S(2)}, u32[]{:S(2)}) %collective-permute-start.16) | collective-permute-done | bytes 278560 | tf_op jit(solution)/shard_map/sum_plane/ppermute | solution.py:680
  95.7 1.7 %collective-permute-start.19 = (bf16[80,512]{1,0:T(8,128)(2,1)S(1)}, bf16[80,512]{1,0:T(8,128)(2,1)S(1)}, u32[]{:S(2)}, u32[]{:S(2)}) collective-permute-start(bf16[80,512]{1,0:T(8,128)(2,1)S(1)} %get-tuple-element.151), channel_id=1, source_target_pairs={{0,2},{1,3},{2,0},{3,1},{4,6},{5,7},{6,4},{7,5},{8,10},{9,11},{10,... | collective-permute-start | bytes 245768 | tf_op jit(solution)/shard_map/sum_mp/ppermute | solution.py:683
  99.6 4.9 %collective-permute-done.19 = bf16[80,512]{1,0:T(8,128)(2,1)S(1)} collective-permute-done((bf16[80,512]{1,0:T(8,128)(2,1)S(1)}, bf16[80,512]{1,0:T(8,128)(2,1)S(1)}, u32[]{:S(2)}, u32[]{:S(2)}) %collective-permute-start.19) | collective-permute-done | bytes 81952 | tf_op jit(solution)/shard_map/sum_mp/ppermute | solution.py:683
  104.6 1.5 %collective-permute-start.23 = (bf16[64,512]{1,0:T(8,128)(2,1)S(1)}, bf16[64,512]{1,0:T(8,128)(2,1)S(1)}, u32[]{:S(2)}, u32[]{:S(2)}) collective-permute-start(bf16[64,512]{1,0:T(8,128)(2,1)S(1)} %fusion.5), channel_id=1, source_target_pairs={{0,24},{4,28},{8,16},{12,20},{16,8},{20,12},{24,0},{28,4},{1,25},{... | collective-permute-start | bytes 196616 | tf_op jit(solution)/shard_map/spread_plane/ppermute | solution.py:680
  106.1 1.5 %collective-permute-start.22 = (bf16[64,512]{1,0:T(8,128)(2,1)S(1)}, bf16[64,512]{1,0:T(8,128)(2,1)S(1)}, u32[]{:S(2)}, u32[]{:S(2)}) collective-permute-start(bf16[64,512]{1,0:T(8,128)(2,1)S(1)} %fusion.5), channel_id=1, source_target_pairs={{0,16},{4,20},{8,24},{12,28},{16,0},{20,4},{24,8},{28,12},{1,17},{... | collective-permute-start | bytes 196616 | tf_op jit(solution)/shard_map/spread_plane/ppermute | solution.py:680
  108.2 1.7 %collective-permute-done.23 = bf16[64,512]{1,0:T(8,128)(2,1)S(1)} collective-permute-done((bf16[64,512]{1,0:T(8,128)(2,1)S(1)}, bf16[64,512]{1,0:T(8,128)(2,1)S(1)}, u32[]{:S(2)}, u32[]{:S(2)}) %collective-permute-start.23) | collective-permute-done | bytes 65568 | tf_op jit(solution)/shard_map/spread_plane/ppermute | solution.py:680
  (110 shorter events, 25.8 us)
Async XLA Ops:
  3.4 13.2 %collective-permute-start.2 = (bf16[80,512]{1,0:T(8,128)(2,1)S(1)}, bf16[80,512]{1,0:T(8,128)(2,1)S(1)}, u32[]{:S(2)}, u32[]{:S(2)}) collective-permute-start(bf16[80,512]{1,0:T(8,128)(2,1)S(1)} %fusion.6.refs_0_), channel_id=1, source_target_pairs={{0,3},{1,2},{2,1},{3,0},{4,7},{5,6},{6,5},{7,4},{8,11},{9,10},{10,... | collective-permute-start | bytes 245768 | tf_op jit(solution)/shard_map/gather_in/ppermute | solution.py:683
  8.6 8.1 %collective-permute-start.1 = (bf16[80,512]{1,0:T(8,128)(2,1)S(1)}, bf16[80,512]{1,0:T(8,128)(2,1)S(1)}, u32[]{:S(2)}, u32[]{:S(2)}) collective-permute-start(bf16[80,512]{1,0:T(8,128)(2,1)S(1)} %fusion.6.refs_0_), channel_id=1, source_target_pairs={{0,2},{1,3},{2,0},{3,1},{4,6},{5,7},{6,4},{7,5},{8,10},{9,11},{10,... | collective-permute-start | bytes 245768 | tf_op jit(solution)/shard_map/gather_in/ppermute | solution.py:683
  8.6 8.1 %collective-permute-start = (bf16[80,512]{1,0:T(8,128)(2,1)S(1)}, bf16[80,512]{1,0:T(8,128)(2,1)S(1)}, u32[]{:S(2)}, u32[]{:S(2)}) collective-permute-start(bf16[80,512]{1,0:T(8,128)(2,1)S(1)} %fusion.6.refs_0_), channel_id=1, source_target_pairs={{0,1},{1,0},{2,3},{3,2},{4,5},{5,4},{6,7},{7,6},{8,9},{9,8},{10,11... | collective-permute-start | bytes 245768 | tf_op jit(solution)/shard_map/gather_in/ppermute | solution.py:683
  17.2 8.4 %collective-permute-start.3 = (bf16[4,80,512]{2,1,0:T(8,128)(2,1)S(1)}, bf16[4,80,512]{2,1,0:T(8,128)(2,1)S(1)}, u32[]{:S(2)}, u32[]{:S(2)}) collective-permute-start(bf16[4,80,512]{2,1,0:T(8,128)(2,1)S(1)} %shard_map.212.own_ref), channel_id=1, source_target_pairs={{0,4},{4,0},{8,12},{12,8},{16,20},{20,16},{24,28},{28,24},{1,5},{5... | collective-permute-start | bytes 983048 | tf_op jit(solution)/shard_map/ppermute | solution.py:677
  17.3 14.9 %collective-permute-start.6 = (bf16[192,512]{1,0:T(8,128)(2,1)S(1)}, bf16[192,512]{1,0:T(8,128)(2,1)S(1)}, u32[]{:S(2)}, u32[]{:S(2)}) collective-permute-start(bf16[192,512]{1,0:T(8,128)(2,1)S(1)} %pad_maximum_fusion.4.refs_0_), channel_id=1, source_target_pairs={{0,3},{1,2},{2,1},{3,0},{4,7},{5,6},{6,5},{7,4},{8,11},{9,10},{10,... | collective-permute-start | bytes 589832 | tf_op jit(solution)/shard_map/gather_out_glu/ppermute | solution.py:683
  21.1 18.0 %collective-permute-start.5 = (bf16[192,512]{1,0:T(8,128)(2,1)S(1)}, bf16[192,512]{1,0:T(8,128)(2,1)S(1)}, u32[]{:S(2)}, u32[]{:S(2)}) collective-permute-start(bf16[192,512]{1,0:T(8,128)(2,1)S(1)} %pad_maximum_fusion.4.refs_0_), channel_id=1, source_target_pairs={{0,2},{1,3},{2,0},{3,1},{4,6},{5,7},{6,4},{7,5},{8,10},{9,11},{10,... | collective-permute-start | bytes 589832 | tf_op jit(solution)/shard_map/gather_out_glu/ppermute | solution.py:683
  21.1 18.0 %collective-permute-start.4 = (bf16[192,512]{1,0:T(8,128)(2,1)S(1)}, bf16[192,512]{1,0:T(8,128)(2,1)S(1)}, u32[]{:S(2)}, u32[]{:S(2)}) collective-permute-start(bf16[192,512]{1,0:T(8,128)(2,1)S(1)} %pad_maximum_fusion.4.refs_0_), channel_id=1, source_target_pairs={{0,1},{1,0},{2,3},{3,2},{4,5},{5,4},{6,7},{7,6},{8,9},{9,8},{10,11... | collective-permute-start | bytes 589832 | tf_op jit(solution)/shard_map/gather_out_glu/ppermute | solution.py:683
  28.4 10.7 %collective-permute-start.9 = (f32[8,512]{1,0:T(8,128)S(1)}, f32[8,512]{1,0:T(8,128)S(1)}, u32[]{:S(2)}, u32[]{:S(2)}) collective-permute-start(f32[8,512]{1,0:T(8,128)S(1)} %get-tuple-element.81), channel_id=1, source_target_pairs={{0,3},{1,2},{2,1},{3,0},{4,7},{5,6},{6,5},{7,4},{8,11},{9,10},{10,... | collective-permute-start | bytes 49160 | tf_op jit(solution)/shard_map/carry/ppermute | solution.py:683
  32.2 7.3 %collective-permute-start.8 = (f32[8,512]{1,0:T(8,128)S(1)}, f32[8,512]{1,0:T(8,128)S(1)}, u32[]{:S(2)}, u32[]{:S(2)}) collective-permute-start(f32[8,512]{1,0:T(8,128)S(1)} %get-tuple-element.81), channel_id=1, source_target_pairs={{0,2},{1,3},{2,0},{3,1},{4,6},{5,7},{6,4},{7,5},{8,10},{9,11},{10,... | collective-permute-start | bytes 49160 | tf_op jit(solution)/shard_map/carry/ppermute | solution.py:683
  32.2 7.3 %collective-permute-start.7 = (f32[8,512]{1,0:T(8,128)S(1)}, f32[8,512]{1,0:T(8,128)S(1)}, u32[]{:S(2)}, u32[]{:S(2)}) collective-permute-start(f32[8,512]{1,0:T(8,128)S(1)} %get-tuple-element.81), channel_id=1, source_target_pairs={{0,1},{1,0},{2,3},{3,2},{4,5},{5,4},{6,7},{7,6},{8,9},{9,8},{10,11... | collective-permute-start | bytes 49160 | tf_op jit(solution)/shard_map/carry/ppermute | solution.py:683
  40.1 2.4 %collective-permute-start.10 = (bf16[4,192,512]{2,1,0:T(8,128)(2,1)S(1)}, bf16[4,192,512]{2,1,0:T(8,128)(2,1)S(1)}, u32[]{:S(2)}, u32[]{:S(2)}) collective-permute-start(bf16[4,192,512]{2,1,0:T(8,128)(2,1)S(1)} %shard_map.215.own_ref), channel_id=1, source_target_pairs={{0,4},{4,0},{8,12},{12,8},{16,20},{20,16},{24,28},{28,24},{1,5},{5... | collective-permute-start | bytes 2359304 | tf_op jit(solution)/shard_map/ppermute | solution.py:677
  58.7 8.8 %collective-permute-start.11 = (f32[8,512]{1,0:T(8,128)S(1)}, f32[8,512]{1,0:T(8,128)S(1)}, u32[]{:S(2)}, u32[]{:S(2)}) collective-permute-start(f32[8,512]{1,0:T(8,128)S(1)} %get-tuple-element.92), channel_id=1, source_target_pairs={{0,1},{1,0},{2,3},{3,2},{4,5},{5,4},{6,7},{7,6},{8,9},{9,8},{10,11... | collective-permute-start | bytes 49160 | tf_op jit(solution)/shard_map/carry_back/ppermute | solution.py:683
  59.2 8.4 %collective-permute-start.13 = (f32[8,512]{1,0:T(8,128)S(1)}, f32[8,512]{1,0:T(8,128)S(1)}, u32[]{:S(2)}, u32[]{:S(2)}) collective-permute-start(f32[8,512]{1,0:T(8,128)S(1)} %get-tuple-element.92), channel_id=1, source_target_pairs={{0,3},{1,2},{2,1},{3,0},{4,7},{5,6},{6,5},{7,4},{8,11},{9,10},{10,... | collective-permute-start | bytes 49160 | tf_op jit(solution)/shard_map/carry_back/ppermute | solution.py:683
  61.5 6.0 %collective-permute-start.12 = (f32[8,512]{1,0:T(8,128)S(1)}, f32[8,512]{1,0:T(8,128)S(1)}, u32[]{:S(2)}, u32[]{:S(2)}) collective-permute-start(f32[8,512]{1,0:T(8,128)S(1)} %get-tuple-element.92), channel_id=1, source_target_pairs={{0,2},{1,3},{2,0},{3,1},{4,6},{5,7},{6,4},{7,5},{8,10},{9,11},{10,... | collective-permute-start | bytes 49160 | tf_op jit(solution)/shard_map/carry_back/ppermute | solution.py:683
  71.1 6.0 %collective-permute-start.14 = (bf16[1024,512]{1,0:T(8,128)(2,1)S(1)}, bf16[1024,512]{1,0:T(8,128)(2,1)S(1)}, u32[]{:S(2)}, u32[]{:S(2)}) collective-permute-start(bf16[1024,512]{1,0:T(8,128)(2,1)S(1)} %get-tuple-element.109), channel_id=1, source_target_pairs={{0,4},{4,0},{8,12},{12,8},{16,20},{20,16},{24,28},{28,24},{1,5},{5... | collective-permute-start | bytes 3145736 | tf_op jit(solution)/shard_map/sum_core/ppermute | solution.py:677
  77.8 9.6 %collective-permute-start.15 = (bf16[272,512]{1,0:T(8,128)(2,1)S(1)}, bf16[272,512]{1,0:T(8,128)(2,1)S(1)}, u32[]{:S(2)}, u32[]{:S(2)}) collective-permute-start(bf16[272,512]{1,0:T(8,128)(2,1)S(1)} %get-tuple-element.114), channel_id=1, source_target_pairs={{0,8},{4,12},{8,0},{12,4},{16,24},{20,28},{24,16},{28,20},{1,9},{5... | collective-permute-start | bytes 835592 | tf_op jit(solution)/shard_map/sum_plane/ppermute | solution.py:680
  79.4 14.7 %collective-permute-start.16 = (bf16[272,512]{1,0:T(8,128)(2,1)S(1)}, bf16[272,512]{1,0:T(8,128)(2,1)S(1)}, u32[]{:S(2)}, u32[]{:S(2)}) collective-permute-start(bf16[272,512]{1,0:T(8,128)(2,1)S(1)} %get-tuple-element.116), channel_id=1, source_target_pairs={{0,16},{4,20},{8,24},{12,28},{16,0},{20,4},{24,8},{28,12},{1,17},{... | collective-permute-start | bytes 835592 | tf_op jit(solution)/shard_map/sum_plane/ppermute | solution.py:680
  80.9 13.2 %collective-permute-start.17 = (bf16[272,512]{1,0:T(8,128)(2,1)S(1)}, bf16[272,512]{1,0:T(8,128)(2,1)S(1)}, u32[]{:S(2)}, u32[]{:S(2)}) collective-permute-start(bf16[272,512]{1,0:T(8,128)(2,1)S(1)} %get-tuple-element.117), channel_id=1, source_target_pairs={{0,24},{4,28},{8,16},{12,20},{16,8},{20,12},{24,0},{28,4},{1,25},{... | collective-permute-start | bytes 835592 | tf_op jit(solution)/shard_map/sum_plane/ppermute | solution.py:680
  94.4 5.2 %collective-permute-start.18 = (bf16[80,512]{1,0:T(8,128)(2,1)S(1)}, bf16[80,512]{1,0:T(8,128)(2,1)S(1)}, u32[]{:S(2)}, u32[]{:S(2)}) collective-permute-start(bf16[80,512]{1,0:T(8,128)(2,1)S(1)} %get-tuple-element.150), channel_id=1, source_target_pairs={{0,1},{1,0},{2,3},{3,2},{4,5},{5,4},{6,7},{7,6},{8,9},{9,8},{10,11... | collective-permute-start | bytes 245768 | tf_op jit(solution)/shard_map/sum_mp/ppermute | solution.py:683
  95.7 8.8 %collective-permute-start.19 = (bf16[80,512]{1,0:T(8,128)(2,1)S(1)}, bf16[80,512]{1,0:T(8,128)(2,1)S(1)}, u32[]{:S(2)}, u32[]{:S(2)}) collective-permute-start(bf16[80,512]{1,0:T(8,128)(2,1)S(1)} %get-tuple-element.151), channel_id=1, source_target_pairs={{0,2},{1,3},{2,0},{3,1},{4,6},{5,7},{6,4},{7,5},{8,10},{9,11},{10,... | collective-permute-start | bytes 245768 | tf_op jit(solution)/shard_map/sum_mp/ppermute | solution.py:683
  97.4 7.2 %collective-permute-start.20 = (bf16[80,512]{1,0:T(8,128)(2,1)S(1)}, bf16[80,512]{1,0:T(8,128)(2,1)S(1)}, u32[]{:S(2)}, u32[]{:S(2)}) collective-permute-start(bf16[80,512]{1,0:T(8,128)(2,1)S(1)} %get-tuple-element.152), channel_id=1, source_target_pairs={{0,3},{1,2},{2,1},{3,0},{4,7},{5,6},{6,5},{7,4},{8,11},{9,10},{10,... | collective-permute-start | bytes 245768 | tf_op jit(solution)/shard_map/sum_mp/ppermute | solution.py:683
  104.6 5.2 %collective-permute-start.23 = (bf16[64,512]{1,0:T(8,128)(2,1)S(1)}, bf16[64,512]{1,0:T(8,128)(2,1)S(1)}, u32[]{:S(2)}, u32[]{:S(2)}) collective-permute-start(bf16[64,512]{1,0:T(8,128)(2,1)S(1)} %fusion.5), channel_id=1, source_target_pairs={{0,24},{4,28},{8,16},{12,20},{16,8},{20,12},{24,0},{28,4},{1,25},{... | collective-permute-start | bytes 196616 | tf_op jit(solution)/shard_map/spread_plane/ppermute | solution.py:680
  106.1 4.4 %collective-permute-start.22 = (bf16[64,512]{1,0:T(8,128)(2,1)S(1)}, bf16[64,512]{1,0:T(8,128)(2,1)S(1)}, u32[]{:S(2)}, u32[]{:S(2)}) collective-permute-start(bf16[64,512]{1,0:T(8,128)(2,1)S(1)} %fusion.5), channel_id=1, source_target_pairs={{0,16},{4,20},{8,24},{12,28},{16,0},{20,4},{24,8},{28,12},{1,17},{... | collective-permute-start | bytes 196616 | tf_op jit(solution)/shard_map/spread_plane/ppermute | solution.py:680
  107.6 4.3 %collective-permute-start.21 = (bf16[64,512]{1,0:T(8,128)(2,1)S(1)}, bf16[64,512]{1,0:T(8,128)(2,1)S(1)}, u32[]{:S(2)}, u32[]{:S(2)}) collective-permute-start(bf16[64,512]{1,0:T(8,128)(2,1)S(1)} %fusion.5), channel_id=1, source_target_pairs={{0,8},{4,12},{8,0},{12,4},{16,24},{20,28},{24,16},{28,20},{1,9},{5... | collective-permute-start | bytes 196616 | tf_op jit(solution)/shard_map/spread_plane/ppermute | solution.py:680
  (11 other events, 85.6 us)

commit v3 on v2

--- a/solution.py
+++ b/solution.py
@@ -46,10 +46,14 @@
 
 
 def block_rows(step, block):
+    if isinstance(step, int):
+        return slice(block * BLOCK, (block + 1) * BLOCK)
     return pl.ds(pl.multiple_of(step * STEP_ROWS + block * BLOCK, BLOCK), BLOCK)
 
 
 def tile_rows(step, start):
+    if isinstance(step, int):
+        return slice(step * STEP_ROWS + start, step * STEP_ROWS + start + 16)
     return pl.ds(pl.multiple_of(step * STEP_ROWS + start, 16), 16)
 
 
@@ -133,39 +137,36 @@
     chunk, mp, idx, norm_ref, own_ref, other_ref,
     src_ref, wt_ref, par_ref, ends_ref, last_ref, h_ref, drive_a, drive_b,
 ):
-    step = pl.program_id(0)
+    step = 0
     width = norm_ref.shape[1]
     states = width // 2
     ns = states // mp
 
-    @pl.when(step == 0)
-    def _():
-        me, core = idx[0], idx[1]
-        assemble(wt_ref, own_ref, other_ref, 0, ns, me, core, mp, False)
-        total = own_ref[0, ns : ns + PARAM_ROWS, :].astype(F32)
-        for s in range(1, mp):
-            total = total + own_ref[s, ns : ns + PARAM_ROWS, :].astype(F32)
-        decay = total[0:1] + total[1:2] + total[2:3]
-        gam = jnp.exp(total[3:4] + total[4:5] + total[5:6])
-        radius = jnp.exp(-jnp.exp(decay[:, :states]))
-        turn = jnp.exp(decay[:, states:])
-        re, im = radius * jnp.cos(turn), radius * jnp.sin(turn)
-        lre, lim = cpower(re, im, log2_of(chunk))
-        tre, tim = cpower(lre, lim, log2_of(CHUNKS))
-        par_ref[0:1, :] = jnp.concatenate([re, im], 1)
-        par_ref[1:2, :] = gam
-        par_ref[2:3, :] = jnp.concatenate([lre, lim], 1)
-        par_ref[3:5, :] = total[6:8]
-        par_ref[5:8, :] = jnp.zeros((3, width), F32)
-        pre, pim = jnp.ones_like(tre), jnp.zeros_like(tim)
-        for s in range(mp):
-            par_ref[8 + s : 9 + s, :] = jnp.concatenate([pre, pim], 1)
-            pre, pim = cmul(pre, pim, tre, tim)
-        h_ref[...] = jnp.zeros_like(h_ref)
+    me, core = idx[0], idx[1]
+    assemble(wt_ref, own_ref, other_ref, 0, ns, me, core, mp, False)
+    total = own_ref[0, ns : ns + PARAM_ROWS, :].astype(F32)
+    for s in range(1, mp):
+        total = total + own_ref[s, ns : ns + PARAM_ROWS, :].astype(F32)
+    decay = total[0:1] + total[2:3] + total[4:5]
+    gamma = jnp.exp(total[1:2] + total[3:4] + total[5:6])
+    radius = jnp.exp(-jnp.exp(decay[:, :states]))
+    turn = jnp.exp(decay[:, states:])
+    re, im = radius * jnp.cos(turn), radius * jnp.sin(turn)
+    lre, lim = cpower(re, im, log2_of(chunk))
+    tre, tim = cpower(lre, lim, log2_of(CHUNKS))
+    par_ref[0:1, :] = jnp.concatenate([re, im], 1)
+    par_ref[1:2, :] = gamma
+    par_ref[2:3, :] = jnp.concatenate([lre, lim], 1)
+    par_ref[3:5, :] = total[6:8]
+    par_ref[5:8, :] = jnp.zeros((3, width), F32)
+    pre, pim = jnp.ones_like(tre), jnp.zeros_like(tim)
+    for s in range(mp):
+        par_ref[8 + s : 9 + s, :] = jnp.concatenate([pre, pim], 1)
+        pre, pim = cmul(pre, pim, tre, tim)
 
     gam = par_ref[1:2, :]
     lre, lim = par_ref[0:1, :states], par_ref[0:1, states:]
-    h = [h_ref[:, :states], h_ref[:, states:]]
+    h = [jnp.zeros((CHUNKS, states), F32)] * 2
 
     def drive_pieces(b, drive):
         return product_nt(drive, lambda: norm_ref[block_rows(step, b), :], wt_ref)
@@ -180,22 +181,20 @@
     def scan_pieces(b, drive):
         return [partial(scan_piece, b, drive, r) for r in range(0, BLOCK, CHUNKS)]
 
+    blocks = norm_ref.shape[0] // BLOCK
+    drives = (drive_a, drive_b)
     run(drive_pieces(0, drive_a))
-    alternate(drive_pieces(1, drive_b), scan_pieces(0, drive_a))
-    run(scan_pieces(1, drive_b))
-    hre, him = h
-    h_ref[:, :states] = hre
-    h_ref[:, states:] = him
-
-    @pl.when(step == pl.num_programs(0) - 1)
-    def _():
-        ends_ref[...] = h_ref[...]
-        pre, pim = par_ref[2:3, :states], par_ref[2:3, states:]
-        re, im = h_ref[0:1, :states], h_ref[0:1, states:]
-        for c in range(1, CHUNKS):
-            mre, mim = cmul(pre, pim, re, im)
-            re, im = mre + h_ref[c : c + 1, :states], mim + h_ref[c : c + 1, states:]
-        last_ref[...] = jnp.broadcast_to(jnp.concatenate([re, im], 1), last_ref.shape)
+    for b in range(blocks):
+        more = drive_pieces(b + 1, drives[(b + 1) % 2]) if b + 1 < blocks else []
+        alternate(more, scan_pieces(b, drives[b % 2]))
+    h_ref[:, :states], h_ref[:, states:] = h
+    ends_ref[...] = h_ref[...]
+    pre, pim = par_ref[2:3, :states], par_ref[2:3, states:]
+    re, im = h_ref[0:1, :states], h_ref[0:1, states:]
+    for c in range(1, CHUNKS):
+        mre, mim = cmul(pre, pim, re, im)
+        re, im = mre + h_ref[c : c + 1, :states], mim + h_ref[c : c + 1, states:]
+    last_ref[...] = jnp.broadcast_to(jnp.concatenate([re, im], 1), last_ref.shape)
 
 
 def gelu_parts(v):
@@ -207,29 +206,27 @@
 def readout(mp, idx, xhat_ref, src_ref, par_ref, ends_ref, gain_ref, bias_ref, skip_ref, own_ref, other_ref, *rest):
     others = rest[: mp - 1]
     (state_ref, act_ref, slope_ref, wc_ref, h_ref, low_a, low_b, mix_a, mix_b) = rest[mp - 1 :]
-    step = pl.program_id(0)
+    step = 0
     width = xhat_ref.shape[1]
     states = width // 2
     me, core = idx[0], idx[1]
 
-    @pl.when(step == 0)
-    def _():
-        assemble(wc_ref, own_ref, other_ref, 0, states // mp, me, core, mp, True)
-        re = jnp.zeros((1, states), F32)
-        im = jnp.zeros((1, states), F32)
-        for s in range(1, mp):
-            j = me ^ s
-            power = jnp.maximum(me - 1 - j, 0)
-            row = par_ref[pl.ds(8 + power, 1), :]
-            sre, sim = cmul(row[:, :states], row[:, states:], others[s - 1][0:1, :states], others[s - 1][0:1, states:])
-            keep = (j < me).astype(F32)
-            re, im = re + keep * sre, im + keep * sim
-        lre, lim = par_ref[2:3, :states], par_ref[2:3, states:]
-        for c in range(CHUNKS):
-            h_ref[c : c + 1, :states] = re
-            h_ref[c : c + 1, states:] = im
-            mre, mim = cmul(lre, lim, re, im)
-            re, im = mre + ends_ref[c : c + 1, :states], mim + ends_ref[c : c + 1, states:]
+    assemble(wc_ref, own_ref, other_ref, 0, states // mp, me, core, mp, True)
+    re = jnp.zeros((1, states), F32)
+    im = jnp.zeros((1, states), F32)
+    for s in range(1, mp):
+        j = me ^ s
+        power = jnp.maximum(me - 1 - j, 0)
+        row = par_ref[pl.ds(8 + power, 1), :]
+        sre, sim = cmul(row[:, :states], row[:, states:], others[s - 1][0:1, :states], others[s - 1][0:1, states:])
+        keep = (j < me).astype(F32)
+        re, im = re + keep * sre, im + keep * sim
+    lre, lim = par_ref[2:3, :states], par_ref[2:3, states:]
+    for c in range(CHUNKS):
+        h_ref[c : c + 1, :states] = re
+        h_ref[c : c + 1, states:] = im
+        mre, mim = cmul(lre, lim, re, im)
+        re, im = mre + ends_ref[c : c + 1, :states], mim + ends_ref[c : c + 1, states:]
 
     lre, lim = par_ref[0:1, :states], par_ref[0:1, states:]
     h = [h_ref[:, :states], h_ref[:, states:]]
@@ -265,12 +262,14 @@
     def gelus(b, mix):
         return [partial(gelu_piece, b, mix, r) for r in range(0, BLOCK, 16)]
 
+    blocks = src_ref.shape[0] // BLOCK
+    lows, mix_refs = (low_a, low_b), (mix_a, mix_b)
     run(scans(0, low_a))
-    alternate(mixes(low_a, mix_a), scans(1, low_b))
-    alternate(mixes(low_b, mix_b), gelus(0, mix_a))
-    run(gelus(1, mix_b))
-    h_ref[:, :states] = h[0]
-    h_ref[:, states:] = h[1]
+    for b in range(blocks):
+        other = scans(b + 1, lows[(b + 1) % 2]) if b + 1 < blocks else []
+        other = (gelus(b - 1, mix_refs[(b - 1) % 2]) if b else []) + other
+        alternate(mixes(lows[b % 2], mix_refs[b % 2]), other)
+    run(gelus(blocks - 1, mix_refs[(blocks - 1) % 2]))
 
 
 def add_branch(idx, x_ref, br_ref, y_ref):
@@ -282,55 +281,46 @@
 
 def gating(mp, idx, cotlow_ref, act_ref, par_ref, own_ref, other_ref,
            br_ref, gpre_ref, wg_ref, vec_ref, pre_a, pre_b):
-    step = pl.program_id(0)
     width = act_ref.shape[1]
     core = idx[1]
-
-    @pl.when(step == 0)
-    def _():
-        assemble(wg_ref, own_ref, other_ref, width // 2 // mp, width // mp, idx[0], core, mp, False)
-        vec_ref[...] = jnp.zeros_like(vec_ref)
-
-    def pre_pieces(block, pre):
-        rows = pl.ds(pl.multiple_of(block * BLOCK, BLOCK), BLOCK)
-        return product_nt(pre, lambda: act_ref[rows, :], wg_ref)
-
-    @pl.when(step == 0)
-    def _():
-        run(pre_pieces(0, pre_a))
+    assemble(wg_ref, own_ref, other_ref, width // 2 // mp, width // mp, idx[0], core, mp, False)
+    vec_ref[...] = jnp.zeros_like(vec_ref)
+    blocks = act_ref.shape[0] // BLOCK
+    buffers = (pre_a, pre_b)
+
+    def pre_pieces(b):
+        return product_nt(buffers[b % 2], lambda: act_ref[b * BLOCK : (b + 1) * BLOCK, :], wg_ref) if b < blocks else []
 
     sums = {}
 
-    def gate_piece(b, pre, start, c):
+    def gate_piece(b, start, c):
+        pre = buffers[b % 2]
         cols = slice(c, c + 128)
         gate_cols = slice(width + c, width + c + 128)
         for r in range(start, start + 64, 16):
-            rows = tile_rows(step, b * BLOCK + r)
+            rows = slice(b * BLOCK + r, b * BLOCK + r + 16)
             value = pre[r : r + 16, cols] + par_ref[3:4, cols]
             gate = pre[r : r + 16, gate_cols] + par_ref[4:5, cols]
             sig = 0.5 * jnp.tanh(0.5 * gate) + 0.5
             branch = value * sig
-            br_ref[b * BLOCK + r : b * BLOCK + r + 16, cols] = branch.astype(BF16)
+            br_ref[rows, cols] = branch.astype(BF16)
             g = cotlow_ref[rows, cols].astype(F32)
-            g_value = (g * sig).astype(BF16)
-            g_gate = (g * branch * (1.0 - sig)).astype(BF16)
-            gpre_ref[rows, cols] = g_value
-            gpre_ref[rows, gate_cols] = g_gate
+            g_value = g * sig
+            g_gate = g * branch * (1.0 - sig)
+            gpre_ref[rows, cols] = g_value.astype(BF16)
+            gpre_ref[rows, gate_cols] = g_gate.astype(BF16)
             for key, part in ((("value", c), g_value), (("gate", c), g_gate)):
-                part = part.astype(F32)
                 sums[key] = sums[key] + part if key in sums else part
 
-    def gate_pieces(b, pre):
-        return [
-            partial(gate_piece, b, pre, start, c) for start in range(0, BLOCK, 64) for c in range(0, width, 128)
-        ]
-
-    after = jnp.minimum(2 * step + 2, act_ref.shape[0] // BLOCK - 1)
-    alternate(pre_pieces(2 * step + 1, pre_b), gate_pieces(0, pre_a))
-    alternate(pre_pieces(after, pre_a), gate_pieces(1, pre_b))
-    for c in range(0, width, 128):
-        vec_ref[1:2, c : c + 128] += jnp.sum(sums["value", c], 0, keepdims=True)
-        vec_ref[2:3, c : c + 128] += jnp.sum(sums["gate", c], 0, keepdims=True)
+    def gate_pieces(b):
+        return [partial(gate_piece, b, start, c) for start in range(0, BLOCK, 64) for c in range(0, width, 128)]
+
+    run(pre_pieces(0))
+    for b in range(blocks):
+        alternate(pre_pieces(b + 1), gate_pieces(b))
+        for c in range(0, width, 128):
+            vec_ref[1:2, c : c + 128] += jnp.sum(sums.pop(("value", c)), 0, keepdims=True)
+            vec_ref[2:3, c : c + 128] += jnp.sum(sums.pop(("gate", c)), 0, keepdims=True)
 
 
 def weight_products(idx, gpre_ref, act_ref, state_ref, gmix_ref, keep_ref, send_ref):
@@ -356,19 +346,13 @@
 
 
 def unmix(idx, gpre_ref, slope_ref, norm_ref, wg_ref, wc_ref, par_ref,
-          gmix_ref, gs_ref, adj_ref, first_ref, vec_ref, p_ref, ga_a, ga_b, gmix_a, gmix_b, gs_a, gs_b):
-    step = pl.program_id(0)
+          gmix_ref, gs_ref, adj_ref, first_ref, vec_ref, ga_a, ga_b, gmix_a, gmix_b, gs_a, gs_b):
+    step = 0
     width = norm_ref.shape[1]
     states = width // 2
     core = idx[1]
 
-    @pl.when(step == 0)
-    def _():
-        p_ref[:, :states] = jnp.ones((8, states), F32)
-        p_ref[:, states:] = jnp.zeros((8, states), F32)
-        adj_ref[...] = jnp.zeros_like(adj_ref)
-        vec_ref[...] = jnp.zeros_like(vec_ref)
-
+    vec_ref[...] = jnp.zeros_like(vec_ref)
     sums = {}
 
     def act_pieces(b, ga):
@@ -392,9 +376,9 @@
         return product_nt(gs, lambda: gmix[...], wc_ref)
 
     lre, lim = par_ref[0:1, :states], par_ref[0:1, states:]
-    power = [p_ref[:, :states], p_ref[:, states:]]
-    are = [adj_ref[c : c + 8, :states] for c in range(0, CHUNKS, 8)]
-    aim = [adj_ref[c : c + 8, states:] for c in range(0, CHUNKS, 8)]
+    power = [jnp.ones((8, states), F32), jnp.zeros((8, states), F32)]
+    are = [jnp.zeros((8, states), F32) for _ in range(0, CHUNKS, 8)]
+    aim = [jnp.zeros((8, states), F32) for _ in range(0, CHUNKS, 8)]
 
     def end_piece(b, gs, r):
         pre, pim = power
@@ -408,28 +392,27 @@
     def end_pieces(b, gs):
         return [partial(end_piece, b, gs, r) for r in range(0, BLOCK, CHUNKS)]
 
+    blocks = gpre_ref.shape[0] // BLOCK
+    gas, gmixes, gss = (ga_a, ga_b), (gmix_a, gmix_b), (gs_a, gs_b)
     run(act_pieces(0, ga_a))
-    alternate(act_pieces(1, ga_b), lru_pieces(0, ga_a, gmix_a))
-    alternate(mix_pieces(0, gs_a, gmix_a), lru_pieces(1, ga_b, gmix_b))
-    alternate(mix_pieces(1, gs_b, gmix_b), end_pieces(0, gs_a))
-    run(end_pieces(1, gs_b))
+    for b in range(blocks + 2):
+        products = act_pieces(b + 1, gas[(b + 1) % 2]) if b + 1 < blocks else []
+        products += mix_pieces(b - 1, gss[(b - 1) % 2], gmixes[(b - 1) % 2]) if 0 <= b - 1 < blocks else []
+        other = lru_pieces(b, gas[b % 2], gmixes[b % 2]) if b < blocks else []
+        other += end_pieces(b - 2, gss[b % 2]) if b >= 2 else []
+        alternate(products, other)
     for c in range(0, width, 128):
         vec_ref[0:1, c : c + 128] += jnp.sum(sums[c], 0, keepdims=True)
     for n, c in enumerate(range(0, CHUNKS, 8)):
         adj_ref[c : c + 8, :states] = are[n]
         adj_ref[c : c + 8, states:] = aim[n]
-    p_ref[:, :states] = power[0]
-    p_ref[:, states:] = power[1]
-
-    @pl.when(step == pl.num_programs(0) - 1)
-    def _():
-        lre, lim = par_ref[2:3, :states], -par_ref[2:3, states:]
-        last = CHUNKS - 1
-        re, im = adj_ref[last : last + 1, :states], adj_ref[last : last + 1, states:]
-        for c in range(CHUNKS - 2, -1, -1):
-            mre, mim = cmul(lre, lim, re, im)
-            re, im = mre + adj_ref[c : c + 1, :states], mim + adj_ref[c : c + 1, states:]
-        first_ref[...] = jnp.broadcast_to(jnp.concatenate([re, im], 1), first_ref.shape)
+    lre, lim = par_ref[2:3, :states], -par_ref[2:3, states:]
+    last = CHUNKS - 1
+    re, im = adj_ref[last : last + 1, :states], adj_ref[last : last + 1, states:]
+    for c in range(CHUNKS - 2, -1, -1):
+        mre, mim = cmul(lre, lim, re, im)
+        re, im = mre + adj_ref[c : c + 1, :states], mim + adj_ref[c : c + 1, states:]
+    first_ref[...] = jnp.broadcast_to(jnp.concatenate([re, im], 1), first_ref.shape)
 
 
 def adjoint_scan(mp, idx, keep_in, send_in, gs_ref, state_ref, src_ref, norm_ref, par_ref, adj_ref, *rest):
@@ -554,7 +537,7 @@
 
 
 def split_pieces(slots, count, hid, ns, idx, keep_ref, got_ref, skip_ref, glu_ref, norm_ref, lam_ref,
-                 own_ref, vec_ref, *sends):
+                 own_ref, vec_ref, vec_send_ref, *sends):
     place = idx[2]
     height = (hid + 2 * ns) // count
     for slot in range(slots):
@@ -574,13 +557,12 @@
     high = vec.astype(BF16)
     low = (vec - high.astype(F32)).astype(BF16)
     vec_ref[...] = high.astype(F32) + low.astype(F32)
-    for send in sends:
-        send[slots * height :, :] = jnp.concatenate([high.astype(F32), low.astype(F32)], 0).astype(BF16)
-
-
-def call(kernel, steps, ins, outs, scratch, mib, flops, moved, in_place=None):
+    vec_send_ref[...] = jnp.concatenate([high.astype(F32), low.astype(F32)], 0).astype(BF16)
+
+
+def call(kernel, steps, ins, outs, scratch, mib, flops, moved, in_place=None, first=False):
     def in_hbm(array, block):
-        return array if block is None or array.size < 65536 else pltpu.with_memory_space_constraint(array, pltpu.HBM)
+        return array if block is None or (array.size < 65536 and not first) else pltpu.with_memory_space_constraint(array, pltpu.HBM)
 
     def spec(block):
         return pl.BlockSpec(memory_space=pltpu.VMEM) if block is None else block
@@ -621,24 +603,14 @@
     return high, lax.reduce_precision(v - high, 8, 7)
 
 
-def scatter_sum(rows, position, count, permute, vec=None):
-    width = rows.shape[-1]
-    own = lax.dynamic_index_in_dim(rows, position, 0, keepdims=False)
-    tail = []
-    if vec is not None:
-        high, low = high_low(vec)
-        tail = [high.astype(BF16), low.astype(BF16)]
-        vec = high + low
-    got, vecs = [own], [vec]
-    for s in range(1, count):
-        send = lax.dynamic_index_in_dim(rows, position ^ s, 0, keepdims=False).astype(BF16)
-        buffer = permute(jnp.concatenate([send.reshape(-1, width)] + tail) if tail else send, s)
-        if tail:
-            n = buffer.shape[0] - 2 * vec.shape[0]
-            vecs.append(buffer[n : n + vec.shape[0]].astype(F32) + buffer[n + vec.shape[0] :].astype(F32))
-            buffer = buffer[:n].reshape(own.shape)
-        got.append(buffer.astype(F32))
-    return tree_sum(got), (None if vec is None else tree_sum(vecs))
+def vector_rows(v):
+    high, low = high_low(v)
+    return high + low, jnp.concatenate([high, low]).astype(BF16)
+
+
+def vector_sum(rows):
+    n = rows.shape[0] // 2
+    return rows[:n].astype(F32) + rows[n:].astype(F32)
 
 
 def flip(stack, position):
@@ -691,10 +663,11 @@
         high, rest = high_low(v)
         return [high, rest, lax.reduce_precision(v - high - rest, 8, 7)]
 
-    decay_row = jnp.concatenate([placed(nu_log), placed(theta_log)])
-    gam_row = jnp.concatenate([placed(gamma_log), placed(gamma_log)])
-    bias_rows = [placed(glu_bias[p].astype(F32)) for p in range(2)]
-    params = jnp.stack(thirds(decay_row) + thirds(gam_row) + bias_rows).astype(BF16)
+    first_rows = [placed(nu_log), placed(gamma_log)], [placed(theta_log), placed(gamma_log)]
+    first_rows = jnp.concatenate([jnp.stack(v) for v in first_rows], 1)
+    bias_rows = jnp.stack([placed(glu_bias[p].astype(F32)) for p in range(2)])
+    first_rows, bias_rows = lax.optimization_barrier((first_rows, bias_rows))
+    params = jnp.concatenate(thirds(first_rows) + [bias_rows]).astype(BF16)
     params = jnp.pad(params, ((0, PARAM_ROWS - params.shape[0]), (0, 0)))
 
     def gathered(value, name):
@@ -716,7 +689,7 @@
     in_send = jnp.concatenate([in_part, params])
     both_part = jnp.concatenate([out_part, glu_part])
     x = tied(x, in_send, both_part)
-    in_own = gathered(in_send, "gather_in")
+    in_parts = gathered(in_send, "gather_in")
 
     chunked = pl.BlockSpec((CHUNKS, per, width), lambda i, idx: (0, i, 0))
     vector = pl.BlockSpec((1, width), lambda i, idx: (0, 0))
@@ -733,15 +706,16 @@
         prepare, steps,
         [(idx, None), (x, chunked), (gain, vector), (bias, vector)],
         [(big, F32, None), (big, BF16, None), ((tokens, 128), F32, None)],
-        [], 6, product, 12,
-    )
-    in_own = packed(in_own, norm)
+        [], 6, product, 12, None, True,
+    )
+    in_parts = list(lax.optimization_barrier(tuple(in_parts) + (norm,))[:-1])
+    both_own = gathered(tied(both_part, *in_parts[1:]), "gather_out_glu")
+    in_own = packed(in_parts, norm)
     in_other = over_core(in_own)
-    both_own = gathered(tied(both_part, in_own), "gather_out_glu")
     (cotlow,) = call(lower, steps, [(idx, None), (tied(cot, in_own), chunked)], [(big, BF16, None)], [], 5, 0, 8)
     norm = tied(norm, cotlow)
     src, wt, par, ends, last = call(
-        partial(first_scan, chunk, mp), steps,
+        partial(first_scan, chunk, mp), 1,
         [(idx, None), (norm, None), (in_own, None), (in_other, None)],
         [(big, F32, None), ((width, width), BF16, None), ((npar, width), F32, None), ((CHUNKS, width), F32, None), small],
         scratch((CHUNKS, width, F32), (BLOCK, width, F32), (BLOCK, width, F32)), 5, product, 8,
@@ -751,24 +725,24 @@
     both_own = packed(both_own, *lasts)
     both_other = over_core(both_own)
     state, act, slope, wc = call(
-        partial(readout, mp), steps,
+        partial(readout, mp), 1,
         [(idx, None), (xhat, None), (src, None), (par, None), (ends, None), (gain, vector), (bias, vector), (skp, vector),
          (both_own, None), (both_other, None)] + [(v, None) for v in lasts],
         [(big, BF16, None), (big, BF16, None), (big, F32, None), ((width, width), BF16, None)],
         scratch((CHUNKS, width, F32), (BLOCK, width, BF16), (BLOCK, width, BF16), (BLOCK, width, F32), (BLOCK, width, F32)), 8, product, 8,
     )
     branch, gpre, wg, vec_glu = call(
-        partial(gating, mp), steps,
+        partial(gating, mp), 1,
         [(idx, None), (cotlow, None), (act, None), (par, None), (both_own, None), (both_other, None)],
-        [(big, BF16, rowed), ((tokens, 2 * width), BF16, None), ((2 * width, width), BF16, None), small],
+        [(big, BF16, None), ((tokens, 2 * width), BF16, None), ((2 * width, width), BF16, None), small],
         scratch((BLOCK, 2 * width, F32), (BLOCK, 2 * width, F32)),
         10, 2 * product, 8,
     )
     gmix, gs, adj, first, vec_skip = call(
-        unmix, steps,
+        unmix, 1,
         [(idx, None), (gpre, None), (slope, None), (norm, None), (wg, None), (wc, None), (par, None)],
         [(big, BF16, None), (big, F32, None), ((CHUNKS, width), F32, None), small, small],
-        scratch((8, width, F32), (BLOCK, width, F32), (BLOCK, width, F32), (BLOCK, width, BF16),
+        scratch((BLOCK, width, F32), (BLOCK, width, F32), (BLOCK, width, BF16),
                 (BLOCK, width, BF16), (BLOCK, width, F32), (BLOCK, width, F32)),
         10, 4 * product, 8,
     )
@@ -807,38 +781,46 @@
     )[:6]
     height = mp * (hid + 2 * ns) // plane
     if ns // plane % 16 == 0 and hid // plane % 16 == 0:
-        own_piece, vec, *sends = call(
+        own_piece, vec, vec_rows, *sends = call(
             partial(split_pieces, mp, plane, hid, ns), 1,
             [(idx, None), (keep, None), (got, None), (vec_skip, None), (vec_glu, None), (vec_norm, None), (vec_lam, None)],
-            [((height, width), F32, None), small] + [((height + 16, width), BF16, None)] * (plane - 1), [], 4, 0, 0,
+            [((height, width), F32, None), small, ((16, width), BF16, None)] + [((height, width), BF16, None)] * (plane - 1),
+            [], 4, 0, 0,
         )
     else:
         vec = jnp.concatenate([vec_skip[0:1], vec_glu[1:3], vec_norm[0:2], vec_lam[0:2], jnp.zeros((1, width), F32)])
-        vec_high, vec_low = high_low(vec)
-        vec, vec_rows = vec_high + vec_low, jnp.concatenate([vec_high, vec_low]).astype(BF16)
+        vec, vec_rows = vector_rows(vec)
         both = keep + got.astype(F32)
         both = [both[: mp * hid], both[mp * hid : early_rows], both[early_rows:]]
         both = jnp.concatenate([v.reshape(mp, plane, -1, width) for v in both], 2).swapaxes(0, 1)
         sends = [lax.dynamic_index_in_dim(both, place ^ s, 0, keepdims=False) for s in range(plane)]
         sends = [v.reshape(-1, width) for v in sends]
-        own_piece, sends = sends[0], [jnp.concatenate([v.astype(BF16), vec_rows]) for v in sends[1:]]
+        own_piece, sends = sends[0], [v.astype(BF16) for v in sends[1:]]
+    with jax.named_scope("sum_vectors_core"):
+        vec = vec + vector_sum(over_core(vec_rows))
     with jax.named_scope("sum_plane"):
         pieces = [over_plane(v, s + 1) for s, v in enumerate(sends)]
     pieces[0] = tied(pieces[0], y)
-    vec = tree_sum(
-        [vec] + [p[height : height + 8].astype(F32) + p[height + 8 :].astype(F32) for p in pieces]
-    )
-    rows = tree_sum([own_piece] + [p[:height].astype(F32) for p in pieces]).reshape(mp, -1, width)
+    rows = tree_sum([own_piece] + [p.astype(F32) for p in pieces]).reshape(mp, -1, width)
     with jax.named_scope("sum_mp"):
-        piece, vec = scatter_sum(rows, me, mp, over_mp, vec)
-    high, low = high_low(vec)
+        vec, vec_rows = vector_rows(vec)
+        got, vecs = [lax.dynamic_index_in_dim(rows, me, 0, keepdims=False)], [vec]
+        n = got[0].shape[0]
+        for s in range(1, mp):
+            send = lax.dynamic_index_in_dim(rows, me ^ s, 0, keepdims=False).astype(BF16)
+            buffer = over_mp(jnp.concatenate([send, vec_rows]), s)
+            got.append(buffer[:n].astype(F32))
+            vecs.append(vector_sum(buffer[n:]))
+    piece, vec = tree_sum(got).astype(BF16), tree_sum(vecs)
     with jax.named_scope("spread_plane"):
-        piece = piece.astype(BF16)
-        stack = jnp.stack([piece] + [over_plane(piece, s) for s in range(1, plane)])
-    n = plane * piece.shape[0]
-    got = over_core(jnp.concatenate([stack.reshape(n, width), high.astype(BF16), low.astype(BF16)]))
-    vec = high + low + (got[n : n + 8].astype(F32) + got[n + 8 :].astype(F32))
-    total = jnp.stack([flip(stack, place), flip(got[:n].reshape(stack.shape), place)])
+        vec, vec_rows = vector_rows(vec)
+        piece = jnp.concatenate([piece, vec_rows])
+        stack = [piece] + [over_plane(piece, s) for s in range(1, plane)]
+    vec = tree_sum([vec] + [vector_sum(v[n:]) for v in stack[1:]])
+    stack = jnp.stack([v[:n] for v in stack])
+    with jax.named_scope("spread_core"):
+        got = over_core(stack)
+    total = jnp.stack([flip(stack, place), flip(got, place)])
     total = flip(total, core).astype(F32)
     nh, nr = hid // plane, ns // plane
 

time: 119 us -> 113 us (0.950)
  Pallas kernels: 50.1 us -> 46.4 us
  waiting for transfers between devices: 24.4 us -> 22.6 us
  local copies, waits for them, and re-layouts: 7.47 us -> 6.05 us
    pallas_call x13, Pallas kernels: 50.1 us -> 46.4 us  [call(): pl.pallas_call(kernel, grid_spec=pltpu.PrefetchScalarGridSpec(num_scalar_...]
    ppermute x4 -> x5, waiting for transfers between devices: 3.67 us -> 2.28 us  [over_core(): return lax.ppermute(v, 'dp', xor_pairs(dp, 1))]
    unnamed x23 -> x19, local copies, waits for them, and re-layouts: 2.42 us -> 1.05 us
  transfers between devices with their start and end apart: 25 -> 26, of which waited for: 10 -> 10; matrix products, arithmetic and copies ran while one was open for 1% -> 3% of each run, Pallas kernels for 24% -> 25%
where the time goes in v3:
time: 113 us
  Pallas kernels  46.4 us (41%)
  starting transfers between devices  32.6 us (29%)
  waiting for transfers between devices  22.6 us (20%)
  local copies, waits for them, and re-layouts  6.05 us (5%)
  other arithmetic  3.72 us (3%)
  between operations  1.26 us (1%)
    pallas_call x13, Pallas kernels, call(): pl.pallas_call(kernel, grid_spec=pltpu.PrefetchScalarGridSpec(num_scalar_...  46.4 us
    ppermute x15, starting transfers between devices, over_mp(): return lax.ppermute(v, 'mp', xor_pairs(mp, s))  25.2 us
    ppermute x15, waiting for transfers between devices, over_mp(): return lax.ppermute(v, 'mp', xor_pairs(mp, s))  10.5 us
    ppermute x6, waiting for transfers between devices, over_plane(): return lax.ppermute(v, 'dp', xor_pairs(dp, 2 * s))  9.81 us
    ppermute x6, starting transfers between devices, over_plane(): return lax.ppermute(v, 'dp', xor_pairs(dp, 2 * s))  7.11 us
    ppermute x5, waiting for transfers between devices, over_core(): return lax.ppermute(v, 'dp', xor_pairs(dp, 1))  2.28 us
  transfers between devices with their start and end apart: 26, of which 10 were waited for; matrix products, arithmetic and copies ran while one was open for 3% of the time, Pallas kernels for 25%

profile of v3, /device:TPU:0, one launch (start us, length us, event | category | flops | bytes accessed | tf_op | source)
XLA Modules:
  0.0 112.7 jit_solution(8509889202324910439)
XLA Ops:
  3.4 5.1 %collective-permute-start.2 = (bf16[80,512]{1,0:T(8,128)(2,1)S(1)}, bf16[80,512]{1,0:T(8,128)(2,1)S(1)}, u32[]{:S(2)}, u32[]{:S(2)}) collective-permute-start(bf16[80,512]{1,0:T(8,128)(2,1)S(1)} %pad_maximum_fusion.10.refs_0_), channel_id=1, source_target_pairs={{0,3},{1,2},{2,1},{3,0},{4,7},{5,6},{6,5},{7,4},{8,11},{9,10},{10,... | collective-permute-start | bytes 245768 | tf_op jit(solution)/shard_map/gather_in/ppermute | solution.py:655
  10.5 4.7 %shard_map.211 = (f32[2048,512]{1,0:T(8,128)S(1)}, bf16[2048,512]{1,0:T(8,128)(2,1)S(1)}, f32[2048,128]{1,0:T(8,128)S(1)}) custom-call(s32[3]{0:T(128)S(1)} %pad_add_fusion.idx, f32[16,128,512]{2,1,0:T(8,128)} %bitcast.107, f32[1,512]{1,0:T(1,128)} %bitcast.100, f32[1,512]{1,0:T(1,128)} %bitcast.103), custom_call_target="tpu_custom_call" | custom-call | flops 1073741824 | bytes 12582912 | tf_op jit(solution)/shard_map/pallas_call | solution.py:570
  16.0 3.7 %collective-permute-start.6 = (bf16[192,512]{1,0:T(8,128)(2,1)S(1)}, bf16[192,512]{1,0:T(8,128)(2,1)S(1)}, u32[]{:S(2)}, u32[]{:S(2)}) collective-permute-start(bf16[192,512]{1,0:T(8,128)(2,1)S(1)} %pad_maximum_fusion.3.refs_0_), channel_id=1, source_target_pairs={{0,3},{1,2},{2,1},{3,0},{4,7},{5,6},{6,5},{7,4},{8,11},{9,10},{10,... | collective-permute-start | bytes 589832 | tf_op jit(solution)/shard_map/gather_out_glu/ppermute | solution.py:655
  20.5 3.8 %shard_map.213.cotlow_ref = bf16[2048,512]{1,0:T(8,128)(2,1)S(1)} custom-call(s32[3]{0:T(128)S(1)} %pad_add_fusion.idx, f32[16,128,512]{2,1,0:T(8,128)} %bitcast.98), custom_call_target="tpu_custom_call" | custom-call | bytes 8388608 | tf_op jit(solution)/shard_map/pallas_call | solution.py:570
  24.4 2.1 %shard_map.214 = (f32[2048,512]{1,0:T(8,128)S(1)}, bf16[512,512]{1,0:T(8,128)(2,1)S(1)}, f32[12,512]{1,0:T(8,128)S(1)}, f32[16,512]{1,0:T(8,128)S(1)}, f32[8,512]{1,0:T(8,128)S(1)}) custom-call(s32[3]{0:T(128)S(1)} %pad_add_fusion.idx, bf16[2048,512]{1,0:T(8,128)(2,1)S(1)} %get-tuple-element.89.norm_ref, bf16[4,80,512]{2,1,0:T(8,128)(2,1)S(1)} %shard_map.212.own_ref, ...), custom_call_target="tpu_custom_call" | custom-call | flops 1073741824 | bytes 8388608 | tf_op jit(solution)/shard_map/pallas_call | solution.py:570
  26.5 3.7 %collective-permute-start.9 = (f32[8,512]{1,0:T(8,128)S(1)}, f32[8,512]{1,0:T(8,128)S(1)}, u32[]{:S(2)}, u32[]{:S(2)}) collective-permute-start(f32[8,512]{1,0:T(8,128)S(1)} %get-tuple-element.94), channel_id=1, source_target_pairs={{0,3},{1,2},{2,1},{3,0},{4,7},{5,6},{6,5},{7,4},{8,11},{9,10},{10,... | collective-permute-start | bytes 49160 | tf_op jit(solution)/shard_map/carry/ppermute | solution.py:655
  30.1 3.4 %collective-permute-start.7 = (f32[8,512]{1,0:T(8,128)S(1)}, f32[8,512]{1,0:T(8,128)S(1)}, u32[]{:S(2)}, u32[]{:S(2)}) collective-permute-start(f32[8,512]{1,0:T(8,128)S(1)} %get-tuple-element.94), channel_id=1, source_target_pairs={{0,1},{1,0},{2,3},{3,2},{4,5},{5,4},{6,7},{7,6},{8,9},{9,8},{10,11... | collective-permute-start | bytes 49160 | tf_op jit(solution)/shard_map/carry/ppermute | solution.py:655
  33.5 4.3 %collective-permute-done.5.refs_2_ = bf16[192,512]{1,0:T(8,128)(2,1)S(1)} collective-permute-done((bf16[192,512]{1,0:T(8,128)(2,1)S(1)}, bf16[192,512]{1,0:T(8,128)(2,1)S(1)}, u32[]{:S(2)}, u32[]{:S(2)}) %collective-permute-start.5) | collective-permute-done | bytes 196640 | tf_op jit(solution)/shard_map/gather_out_glu/ppermute | solution.py:655
  38.8 2.3 %collective-permute-done.10.other_ref = bf16[4,192,512]{2,1,0:T(8,128)(2,1)S(1)} collective-permute-done((bf16[4,192,512]{2,1,0:T(8,128)(2,1)S(1)}, bf16[4,192,512]{2,1,0:T(8,128)(2,1)S(1)}, u32[]{:S(2)}, u32[]{:S(2)}) %collective-permute-start.10) | collective-permute-done | bytes 786464 | tf_op jit(solution)/shard_map/ppermute | solution.py:649
  41.1 4.1 %shard_map.216 = (bf16[2048,512]{1,0:T(8,128)(2,1)S(1)}, bf16[2048,512]{1,0:T(8,128)(2,1)S(1)}, f32[2048,512]{1,0:T(8,128)S(1)}, bf16[512,512]{1,0:T(8,128)(2,1)S(1)}) custom-call(s32[3]{0:T(128)S(1)} %pad_add_fusion.idx, f32[2048,512]{1,0:T(8,128)S(1)} %get-tuple-element.88.xhat_ref, f32[2048,512]{1,0:T(8,128)S(1)} %get-tuple-element.90.src_ref, ...), custom_call_target="tpu_custom_call" | custom-call | flops 1073741824 | bytes 8388608 | tf_op jit(solution)/shard_map/pallas_call | solution.py:570
  45.2 4.7 %shard_map.217 = (bf16[2048,512]{1,0:T(8,128)(2,1)S(1)}, bf16[2048,1024]{1,0:T(8,128)(2,1)S(1)}, bf16[1024,512]{1,0:T(8,128)(2,1)S(1)}, f32[8,512]{1,0:T(8,128)S(1)}) custom-call(s32[3]{0:T(128)S(1)} %pad_add_fusion.idx, bf16[2048,512]{1,0:T(8,128)(2,1)S(1)} %shard_map.213.cotlow_ref, bf16[2048,512]{1,0:T(8,128)(2,1)S(1)} %get-tuple-element.99.act_ref, ...), custom_call_target="tpu_custom_call" | custom-call | flops 2147483648 | bytes 8388608 | tf_op jit(solution)/shard_map/pallas_call | solution.py:570
  49.9 4.4 %shard_map.218 = (bf16[2048,512]{1,0:T(8,128)(2,1)S(1)}, f32[2048,512]{1,0:T(8,128)S(1)}, f32[16,512]{1,0:T(8,128)S(1)}, f32[8,512]{1,0:T(8,128)S(1)}, f32[8,512]{1,0:T(8,128)S(1)}) custom-call(s32[3]{0:T(128)S(1)} %pad_add_fusion.idx, bf16[2048,1024]{1,0:T(8,128)(2,1)S(1)} %get-tuple-element.106.gpre_ref, f32[2048,512]{1,0:T(8,128)S(1)} %get-tuple-element.102.slope_ref, ...), custom_call_target="tpu_custom_call" | custom-call | flops 4294967296 | bytes 8388608 | tf_op jit(solution)/shard_map/pallas_call | solution.py:570
  55.0 2.4 %collective-permute-start.13 = (f32[8,512]{1,0:T(8,128)S(1)}, f32[8,512]{1,0:T(8,128)S(1)}, u32[]{:S(2)}, u32[]{:S(2)}) collective-permute-start(f32[8,512]{1,0:T(8,128)S(1)} %get-tuple-element.105), channel_id=1, source_target_pairs={{0,3},{1,2},{2,1},{3,0},{4,7},{5,6},{6,5},{7,4},{8,11},{9,10},{10,... | collective-permute-start | bytes 49160 | tf_op jit(solution)/shard_map/carry_back/ppermute | solution.py:655
  58.1 5.2 %shard_map.219 = (f32[1024,512]{1,0:T(8,128)S(1)}, bf16[1024,512]{1,0:T(8,128)(2,1)S(1)}) custom-call(s32[3]{0:T(128)S(1)} %pad_add_fusion.idx, bf16[2048,1024]{1,0:T(8,128)(2,1)S(1)} %get-tuple-element.106.gpre_ref, bf16[2048,512]{1,0:T(8,128)(2,1)S(1)} %get-tuple-element.99.act_ref, bf16[2048,512]{1,0:T(8,128)(2,1)S(1)} %get-tuple-element.107.state_ref, ...), custom_call_target="tpu_custom_call" | custom-call | tf_op jit(solution)/shard_map/pallas_call | solution.py:570
  63.3 3.5 %shard_map.220 = (bf16[2048,512]{1,0:T(8,128)(2,1)S(1)}, f32[1024,512]{1,0:T(8,128)S(1)}, bf16[1024,512]{1,0:T(8,128)(2,1)S(1)}, f32[8,512]{1,0:T(8,128)S(1)}) custom-call(s32[3]{0:T(128)S(1)} %pad_add_fusion.idx, f32[1024,512]{1,0:T(8,128)S(1)} %get-tuple-element.109.keep_in, ...), custom_call_target="tpu_custom_call", output_to_operand_aliasing={{1}: (1, {}), {2}: (2, {})} | custom-call | flops 1073741824 | bytes 8388608 | tf_op jit(solution)/shard_map/pallas_call | solution.py:570
  66.9 5.9 %shard_map.221 = (f32[16,128,512]{2,1,0:T(8,128)}, f32[8,512]{1,0:T(8,128)S(1)}) custom-call(s32[3]{0:T(128)S(1)} %pad_add_fusion.idx, f32[16,128,512]{2,1,0:T(8,128)S(1)} %bitcast.99, bf16[2048,512]{1,0:T(8,128)(2,1)S(1)} %get-tuple-element.114.gdrive_ref, bf16[512,512]{1,0:T(8,128)(2,1)S(1)} %get-tuple-element.115.wt_ref, ...), custom_call_target="tpu_custom_call" | custom-call | flops 1073741824 | bytes 8388608 | tf_op jit(solution)/shard_map/pallas_call | solution.py:570
  73.6 1.6 %collective-permute-start.16 = (bf16[256,512]{1,0:T(8,128)(2,1)S(1)}, bf16[256,512]{1,0:T(8,128)(2,1)S(1)}, u32[]{:S(2)}, u32[]{:S(2)}) collective-permute-start(bf16[256,512]{1,0:T(8,128)(2,1)S(1)} %get-tuple-element.129), channel_id=1, source_target_pairs={{0,8},{4,12},{8,0},{12,4},{16,24},{20,28},{24,16},{28,20},{1,9},{5... | collective-permute-start | bytes 786440 | tf_op jit(solution)/shard_map/sum_plane/ppermute | solution.py:652
  75.2 1.5 %collective-permute-start.17 = (bf16[256,512]{1,0:T(8,128)(2,1)S(1)}, bf16[256,512]{1,0:T(8,128)(2,1)S(1)}, u32[]{:S(2)}, u32[]{:S(2)}) collective-permute-start(bf16[256,512]{1,0:T(8,128)(2,1)S(1)} %get-tuple-element.131), channel_id=1, source_target_pairs={{0,16},{4,20},{8,24},{12,28},{16,0},{20,4},{24,8},{28,12},{1,17},{... | collective-permute-start | bytes 786440 | tf_op jit(solution)/shard_map/sum_plane/ppermute | solution.py:652
  77.2 6.0 %shard_map.222 = f32[16,128,512]{2,1,0:T(8,128)} custom-call(s32[3]{0:T(128)S(1)} %pad_add_fusion.idx, f32[16,128,512]{2,1,0:T(8,128)} %bitcast.108, bf16[2048,512]{1,0:T(8,128)(2,1)} %copy-done.3), custom_call_target="tpu_custom_call" | custom-call | tf_op jit(solution)/shard_map/pallas_call | solution.py:570
  83.2 5.9 %collective-permute-done.17 = bf16[256,512]{1,0:T(8,128)(2,1)S(1)} collective-permute-done((bf16[256,512]{1,0:T(8,128)(2,1)S(1)}, bf16[256,512]{1,0:T(8,128)(2,1)S(1)}, u32[]{:S(2)}, u32[]{:S(2)}) %collective-permute-start.17) | collective-permute-done | bytes 262176 | tf_op jit(solution)/shard_map/sum_plane/ppermute | solution.py:652
  90.8 1.6 %collective-permute-start.20 = (bf16[80,512]{1,0:T(8,128)(2,1)S(1)}, bf16[80,512]{1,0:T(8,128)(2,1)S(1)}, u32[]{:S(2)}, u32[]{:S(2)}) collective-permute-start(bf16[80,512]{1,0:T(8,128)(2,1)S(1)} %get-tuple-element.165), channel_id=1, source_target_pairs={{0,2},{1,3},{2,0},{3,1},{4,6},{5,7},{6,4},{7,5},{8,10},{9,11},{10,... | collective-permute-start | bytes 245768 | tf_op jit(solution)/shard_map/sum_mp/ppermute | solution.py:655
  94.6 5.0 %collective-permute-done.20 = bf16[80,512]{1,0:T(8,128)(2,1)S(1)} collective-permute-done((bf16[80,512]{1,0:T(8,128)(2,1)S(1)}, bf16[80,512]{1,0:T(8,128)(2,1)S(1)}, u32[]{:S(2)}, u32[]{:S(2)}) %collective-permute-start.20) | collective-permute-done | bytes 81952 | tf_op jit(solution)/shard_map/sum_mp/ppermute | solution.py:655
  99.7 1.5 %collective-permute-start.24 = (bf16[80,512]{1,0:T(8,128)(2,1)S(1)}, bf16[80,512]{1,0:T(8,128)(2,1)S(1)}, u32[]{:S(2)}, u32[]{:S(2)}) collective-permute-start(bf16[80,512]{1,0:T(8,128)(2,1)S(1)} %pad_maximum_fusion.11), channel_id=1, source_target_pairs={{0,24},{4,28},{8,16},{12,20},{16,8},{20,12},{24,0},{28,4},{1,25},{... | collective-permute-start | bytes 245768 | tf_op jit(solution)/shard_map/spread_plane/ppermute | solution.py:652
  103.3 1.9 %collective-permute-done.24 = bf16[80,512]{1,0:T(8,128)(2,1)S(1)} collective-permute-done((bf16[80,512]{1,0:T(8,128)(2,1)S(1)}, bf16[80,512]{1,0:T(8,128)(2,1)S(1)}, u32[]{:S(2)}, u32[]{:S(2)}) %collective-permute-start.24) | collective-permute-done | bytes 81952 | tf_op jit(solution)/shard_map/spread_plane/ppermute | solution.py:652
  (107 shorter events, 23.2 us)
Async XLA Ops:
  3.4 11.8 %collective-permute-start.2 = (bf16[80,512]{1,0:T(8,128)(2,1)S(1)}, bf16[80,512]{1,0:T(8,128)(2,1)S(1)}, u32[]{:S(2)}, u32[]{:S(2)}) collective-permute-start(bf16[80,512]{1,0:T(8,128)(2,1)S(1)} %pad_maximum_fusion.10.refs_0_), channel_id=1, source_target_pairs={{0,3},{1,2},{2,1},{3,0},{4,7},{5,6},{6,5},{7,4},{8,11},{9,10},{10,... | collective-permute-start | bytes 245768 | tf_op jit(solution)/shard_map/gather_in/ppermute | solution.py:655
  8.5 6.9 %collective-permute-start.1 = (bf16[80,512]{1,0:T(8,128)(2,1)S(1)}, bf16[80,512]{1,0:T(8,128)(2,1)S(1)}, u32[]{:S(2)}, u32[]{:S(2)}) collective-permute-start(bf16[80,512]{1,0:T(8,128)(2,1)S(1)} %pad_maximum_fusion.10.refs_0_), channel_id=1, source_target_pairs={{0,2},{1,3},{2,0},{3,1},{4,6},{5,7},{6,4},{7,5},{8,10},{9,11},{10,... | collective-permute-start | bytes 245768 | tf_op jit(solution)/shard_map/gather_in/ppermute | solution.py:655
  8.5 6.9 %collective-permute-start = (bf16[80,512]{1,0:T(8,128)(2,1)S(1)}, bf16[80,512]{1,0:T(8,128)(2,1)S(1)}, u32[]{:S(2)}, u32[]{:S(2)}) collective-permute-start(bf16[80,512]{1,0:T(8,128)(2,1)S(1)} %pad_maximum_fusion.10.refs_0_), channel_id=1, source_target_pairs={{0,1},{1,0},{2,3},{3,2},{4,5},{5,4},{6,7},{7,6},{8,9},{9,8},{10,11... | collective-permute-start | bytes 245768 | tf_op jit(solution)/shard_map/gather_in/ppermute | solution.py:655
  16.0 8.4 %collective-permute-start.3 = (bf16[4,80,512]{2,1,0:T(8,128)(2,1)S(1)}, bf16[4,80,512]{2,1,0:T(8,128)(2,1)S(1)}, u32[]{:S(2)}, u32[]{:S(2)}) collective-permute-start(bf16[4,80,512]{2,1,0:T(8,128)(2,1)S(1)} %shard_map.212.own_ref), channel_id=1, source_target_pairs={{0,4},{4,0},{8,12},{12,8},{16,20},{20,16},{24,28},{28,24},{1,5},{5... | collective-permute-start | bytes 983048 | tf_op jit(solution)/shard_map/ppermute | solution.py:649
  16.0 14.1 %collective-permute-start.6 = (bf16[192,512]{1,0:T(8,128)(2,1)S(1)}, bf16[192,512]{1,0:T(8,128)(2,1)S(1)}, u32[]{:S(2)}, u32[]{:S(2)}) collective-permute-start(bf16[192,512]{1,0:T(8,128)(2,1)S(1)} %pad_maximum_fusion.3.refs_0_), channel_id=1, source_target_pairs={{0,3},{1,2},{2,1},{3,0},{4,7},{5,6},{6,5},{7,4},{8,11},{9,10},{10,... | collective-permute-start | bytes 589832 | tf_op jit(solution)/shard_map/gather_out_glu/ppermute | solution.py:655
  19.7 18.0 %collective-permute-start.5 = (bf16[192,512]{1,0:T(8,128)(2,1)S(1)}, bf16[192,512]{1,0:T(8,128)(2,1)S(1)}, u32[]{:S(2)}, u32[]{:S(2)}) collective-permute-start(bf16[192,512]{1,0:T(8,128)(2,1)S(1)} %pad_maximum_fusion.3.refs_0_), channel_id=1, source_target_pairs={{0,2},{1,3},{2,0},{3,1},{4,6},{5,7},{6,4},{7,5},{8,10},{9,11},{10,... | collective-permute-start | bytes 589832 | tf_op jit(solution)/shard_map/gather_out_glu/ppermute | solution.py:655
  19.7 18.0 %collective-permute-start.4 = (bf16[192,512]{1,0:T(8,128)(2,1)S(1)}, bf16[192,512]{1,0:T(8,128)(2,1)S(1)}, u32[]{:S(2)}, u32[]{:S(2)}) collective-permute-start(bf16[192,512]{1,0:T(8,128)(2,1)S(1)} %pad_maximum_fusion.3.refs_0_), channel_id=1, source_target_pairs={{0,1},{1,0},{2,3},{3,2},{4,5},{5,4},{6,7},{7,6},{8,9},{9,8},{10,11... | collective-permute-start | bytes 589832 | tf_op jit(solution)/shard_map/gather_out_glu/ppermute | solution.py:655
  26.5 11.3 %collective-permute-start.9 = (f32[8,512]{1,0:T(8,128)S(1)}, f32[8,512]{1,0:T(8,128)S(1)}, u32[]{:S(2)}, u32[]{:S(2)}) collective-permute-start(f32[8,512]{1,0:T(8,128)S(1)} %get-tuple-element.94), channel_id=1, source_target_pairs={{0,3},{1,2},{2,1},{3,0},{4,7},{5,6},{6,5},{7,4},{8,11},{9,10},{10,... | collective-permute-start | bytes 49160 | tf_op jit(solution)/shard_map/carry/ppermute | solution.py:655
  30.1 8.0 %collective-permute-start.8 = (f32[8,512]{1,0:T(8,128)S(1)}, f32[8,512]{1,0:T(8,128)S(1)}, u32[]{:S(2)}, u32[]{:S(2)}) collective-permute-start(f32[8,512]{1,0:T(8,128)S(1)} %get-tuple-element.94), channel_id=1, source_target_pairs={{0,2},{1,3},{2,0},{3,1},{4,6},{5,7},{6,4},{7,5},{8,10},{9,11},{10,... | collective-permute-start | bytes 49160 | tf_op jit(solution)/shard_map/carry/ppermute | solution.py:655
  30.1 8.0 %collective-permute-start.7 = (f32[8,512]{1,0:T(8,128)S(1)}, f32[8,512]{1,0:T(8,128)S(1)}, u32[]{:S(2)}, u32[]{:S(2)}) collective-permute-start(f32[8,512]{1,0:T(8,128)S(1)} %get-tuple-element.94), channel_id=1, source_target_pairs={{0,1},{1,0},{2,3},{3,2},{4,5},{5,4},{6,7},{7,6},{8,9},{9,8},{10,11... | collective-permute-start | bytes 49160 | tf_op jit(solution)/shard_map/carry/ppermute | solution.py:655
  54.5 8.8 %collective-permute-start.11 = (f32[8,512]{1,0:T(8,128)S(1)}, f32[8,512]{1,0:T(8,128)S(1)}, u32[]{:S(2)}, u32[]{:S(2)}) collective-permute-start(f32[8,512]{1,0:T(8,128)S(1)} %get-tuple-element.105), channel_id=1, source_target_pairs={{0,1},{1,0},{2,3},{3,2},{4,5},{5,4},{6,7},{7,6},{8,9},{9,8},{10,11... | collective-permute-start | bytes 49160 | tf_op jit(solution)/shard_map/carry_back/ppermute | solution.py:655
  55.0 8.3 %collective-permute-start.13 = (f32[8,512]{1,0:T(8,128)S(1)}, f32[8,512]{1,0:T(8,128)S(1)}, u32[]{:S(2)}, u32[]{:S(2)}) collective-permute-start(f32[8,512]{1,0:T(8,128)S(1)} %get-tuple-element.105), channel_id=1, source_target_pairs={{0,3},{1,2},{2,1},{3,0},{4,7},{5,6},{6,5},{7,4},{8,11},{9,10},{10,... | collective-permute-start | bytes 49160 | tf_op jit(solution)/shard_map/carry_back/ppermute | solution.py:655
  57.4 6.0 %collective-permute-start.12 = (f32[8,512]{1,0:T(8,128)S(1)}, f32[8,512]{1,0:T(8,128)S(1)}, u32[]{:S(2)}, u32[]{:S(2)}) collective-permute-start(f32[8,512]{1,0:T(8,128)S(1)} %get-tuple-element.105), channel_id=1, source_target_pairs={{0,2},{1,3},{2,0},{3,1},{4,6},{5,7},{6,4},{7,5},{8,10},{9,11},{10,... | collective-permute-start | bytes 49160 | tf_op jit(solution)/shard_map/carry_back/ppermute | solution.py:655
  66.8 6.0 %collective-permute-start.14 = (bf16[1024,512]{1,0:T(8,128)(2,1)S(1)}, bf16[1024,512]{1,0:T(8,128)(2,1)S(1)}, u32[]{:S(2)}, u32[]{:S(2)}) collective-permute-start(bf16[1024,512]{1,0:T(8,128)(2,1)S(1)} %get-tuple-element.122), channel_id=1, source_target_pairs={{0,4},{4,0},{8,12},{12,8},{16,20},{20,16},{24,28},{28,24},{1,5},{5... | collective-permute-start | bytes 3145736 | tf_op jit(solution)/shard_map/sum_core/ppermute | solution.py:649
  73.6 9.6 %collective-permute-start.16 = (bf16[256,512]{1,0:T(8,128)(2,1)S(1)}, bf16[256,512]{1,0:T(8,128)(2,1)S(1)}, u32[]{:S(2)}, u32[]{:S(2)}) collective-permute-start(bf16[256,512]{1,0:T(8,128)(2,1)S(1)} %get-tuple-element.129), channel_id=1, source_target_pairs={{0,8},{4,12},{8,0},{12,4},{16,24},{20,28},{24,16},{28,20},{1,9},{5... | collective-permute-start | bytes 786440 | tf_op jit(solution)/shard_map/sum_plane/ppermute | solution.py:652
  75.2 14.0 %collective-permute-start.17 = (bf16[256,512]{1,0:T(8,128)(2,1)S(1)}, bf16[256,512]{1,0:T(8,128)(2,1)S(1)}, u32[]{:S(2)}, u32[]{:S(2)}) collective-permute-start(bf16[256,512]{1,0:T(8,128)(2,1)S(1)} %get-tuple-element.131), channel_id=1, source_target_pairs={{0,16},{4,20},{8,24},{12,28},{16,0},{20,4},{24,8},{28,12},{1,17},{... | collective-permute-start | bytes 786440 | tf_op jit(solution)/shard_map/sum_plane/ppermute | solution.py:652
  76.7 12.5 %collective-permute-start.18 = (bf16[256,512]{1,0:T(8,128)(2,1)S(1)}, bf16[256,512]{1,0:T(8,128)(2,1)S(1)}, u32[]{:S(2)}, u32[]{:S(2)}) collective-permute-start(bf16[256,512]{1,0:T(8,128)(2,1)S(1)} %get-tuple-element.132), channel_id=1, source_target_pairs={{0,24},{4,28},{8,16},{12,20},{16,8},{20,12},{24,0},{28,4},{1,25},{... | collective-permute-start | bytes 786440 | tf_op jit(solution)/shard_map/sum_plane/ppermute | solution.py:652
  77.2 6.1 %collective-permute-start.15 = (bf16[16,512]{1,0:T(8,128)(2,1)S(1)}, bf16[16,512]{1,0:T(8,128)(2,1)S(1)}, u32[]{:S(2)}, u32[]{:S(2)}) collective-permute-start(bf16[16,512]{1,0:T(8,128)(2,1)S(1)} %get-tuple-element.127), channel_id=1, source_target_pairs={{0,4},{4,0},{8,12},{12,8},{16,20},{20,16},{24,28},{28,24},{1,5},{5... | collective-permute-start | bytes 49160 | tf_op jit(solution)/shard_map/sum_vectors_core/ppermute | solution.py:649
  89.4 5.2 %collective-permute-start.19 = (bf16[80,512]{1,0:T(8,128)(2,1)S(1)}, bf16[80,512]{1,0:T(8,128)(2,1)S(1)}, u32[]{:S(2)}, u32[]{:S(2)}) collective-permute-start(bf16[80,512]{1,0:T(8,128)(2,1)S(1)} %get-tuple-element.164), channel_id=1, source_target_pairs={{0,1},{1,0},{2,3},{3,2},{4,5},{5,4},{6,7},{7,6},{8,9},{9,8},{10,11... | collective-permute-start | bytes 245768 | tf_op jit(solution)/shard_map/sum_mp/ppermute | solution.py:655
  90.8 8.8 %collective-permute-start.20 = (bf16[80,512]{1,0:T(8,128)(2,1)S(1)}, bf16[80,512]{1,0:T(8,128)(2,1)S(1)}, u32[]{:S(2)}, u32[]{:S(2)}) collective-permute-start(bf16[80,512]{1,0:T(8,128)(2,1)S(1)} %get-tuple-element.165), channel_id=1, source_target_pairs={{0,2},{1,3},{2,0},{3,1},{4,6},{5,7},{6,4},{7,5},{8,10},{9,11},{10,... | collective-permute-start | bytes 245768 | tf_op jit(solution)/shard_map/sum_mp/ppermute | solution.py:655
  92.4 7.2 %collective-permute-start.21 = (bf16[80,512]{1,0:T(8,128)(2,1)S(1)}, bf16[80,512]{1,0:T(8,128)(2,1)S(1)}, u32[]{:S(2)}, u32[]{:S(2)}) collective-permute-start(bf16[80,512]{1,0:T(8,128)(2,1)S(1)} %get-tuple-element.166), channel_id=1, source_target_pairs={{0,3},{1,2},{2,1},{3,0},{4,7},{5,6},{6,5},{7,4},{8,11},{9,10},{10,... | collective-permute-start | bytes 245768 | tf_op jit(solution)/shard_map/sum_mp/ppermute | solution.py:655
  99.7 5.4 %collective-permute-start.24 = (bf16[80,512]{1,0:T(8,128)(2,1)S(1)}, bf16[80,512]{1,0:T(8,128)(2,1)S(1)}, u32[]{:S(2)}, u32[]{:S(2)}) collective-permute-start(bf16[80,512]{1,0:T(8,128)(2,1)S(1)} %pad_maximum_fusion.11), channel_id=1, source_target_pairs={{0,24},{4,28},{8,16},{12,20},{16,8},{20,12},{24,0},{28,4},{1,25},{... | collective-permute-start | bytes 245768 | tf_op jit(solution)/shard_map/spread_plane/ppermute | solution.py:652
  101.2 4.8 %collective-permute-start.23 = (bf16[80,512]{1,0:T(8,128)(2,1)S(1)}, bf16[80,512]{1,0:T(8,128)(2,1)S(1)}, u32[]{:S(2)}, u32[]{:S(2)}) collective-permute-start(bf16[80,512]{1,0:T(8,128)(2,1)S(1)} %pad_maximum_fusion.11), channel_id=1, source_target_pairs={{0,16},{4,20},{8,24},{12,28},{16,0},{20,4},{24,8},{28,12},{1,17},{... | collective-permute-start | bytes 245768 | tf_op jit(solution)/shard_map/spread_plane/ppermute | solution.py:652
  102.7 4.4 %collective-permute-start.22 = (bf16[80,512]{1,0:T(8,128)(2,1)S(1)}, bf16[80,512]{1,0:T(8,128)(2,1)S(1)}, u32[]{:S(2)}, u32[]{:S(2)}) collective-permute-start(bf16[80,512]{1,0:T(8,128)(2,1)S(1)} %pad_maximum_fusion.11), channel_id=1, source_target_pairs={{0,8},{4,12},{8,0},{12,4},{16,24},{20,28},{24,16},{28,20},{1,9},{5... | collective-permute-start | bytes 245768 | tf_op jit(solution)/shard_map/spread_plane/ppermute | solution.py:652
  (11 other events, 125.5 us)

commit v4 on v3

--- a/solution.py
+++ b/solution.py
@@ -558,6 +558,46 @@
     low = (vec - high.astype(F32)).astype(BF16)
     vec_ref[...] = high.astype(F32) + low.astype(F32)
     vec_send_ref[...] = jnp.concatenate([high.astype(F32), low.astype(F32)], 0).astype(BF16)
+
+
+def finish(width, idx, own_ref, got_ref, in_ref, out_ref, glu_ref):
+    core, place = idx[1], idx[2]
+    count, height = own_ref.shape[0], own_ref.shape[1]
+    ns, hid = in_ref.shape[1], glu_ref.shape[1]
+    for part in range(2):
+        for i in range(count):
+            mine, theirs = own_ref[i ^ place], got_ref[i ^ place]
+            rows = jnp.where(core == part, mine, theirs).astype(F32)
+            low = 0
+            for ref, size in ((glu_ref, hid // count), (out_ref, ns // count), (in_ref, ns // count)):
+                value = rows[low : low + size]
+                ref[part, i * size : (i + 1) * size, :] = -value if ref is out_ref and part == 1 else value
+                low += size
+
+
+def small_outputs(hid, ns, idx, vec_ref, nu_ref, theta_ref, gain_ref, bias_ref, skip_ref, nu_out, theta_out, gamma_out, glu_ref):
+    me = idx[0]
+    width = vec_ref.shape[1]
+    states = width // 2
+    skip_ref[...] = vec_ref[0:1, :]
+    gain_ref[...] = vec_ref[3:4, :]
+    bias_ref[...] = vec_ref[4:5, :]
+
+    def share(rows, start, size, count):
+        total = jnp.zeros((rows.shape[0], size), F32)
+        for j in range(count):
+            total = total + jnp.where(me == j, rows[:, start + j * size : start + (j + 1) * size], 0.0)
+        return total
+
+    glu_ref[...] = share(vec_ref[1:3, :], 0, hid, width // hid)
+    re = share(vec_ref[5:6, :], 0, ns, states // ns)
+    im = share(vec_ref[5:6, :], states, ns, states // ns)
+    gamma_out[...] = share(vec_ref[6:7, :], 0, ns, states // ns)
+    speed, turn = jnp.exp(nu_ref[...]), jnp.exp(theta_ref[...])
+    radius = jnp.exp(-speed)
+    cos, sin = radius * jnp.cos(turn), radius * jnp.sin(turn)
+    nu_out[...] = -speed * (cos * re + sin * im)
+    theta_out[...] = turn * (cos * im - sin * re)
 
 
 def call(kernel, steps, ins, outs, scratch, mib, flops, moved, in_place=None, first=False):
@@ -820,40 +860,44 @@
     stack = jnp.stack([v[:n] for v in stack])
     with jax.named_scope("spread_core"):
         got = over_core(stack)
-    total = jnp.stack([flip(stack, place), flip(got, place)])
-    total = flip(total, core).astype(F32)
-    nh, nr = hid // plane, ns // plane
-
-    def part(start, size):
-        return total[:, :, start : start + size].reshape(2, -1, width)
-
-    grad_glu_weight = part(0, nh).transpose(2, 0, 1)
-    grad_out = part(nh, nr)
-    grad_out_weight = jnp.stack([grad_out[0], -grad_out[1]])
-    grad_in_weight = part(nh + nr, nr).transpose(2, 0, 1)
-
-    def decay(nu, theta):
-        radius = jnp.exp(-jnp.exp(nu))
-        turn = jnp.exp(theta)
-        return radius * jnp.cos(turn), radius * jnp.sin(turn)
-
-    _, decay_back = jax.vjp(decay, nu_log, theta_log)
-    grad_glu_bias = lax.dynamic_slice_in_dim(vec[1:3], me * hid, hid, 1)
-    grad_lam = lax.dynamic_slice_in_dim(vec[5].reshape(2, states), me * ns, ns, 1)
-    grad_nu_log, grad_theta_log = decay_back((grad_lam[0], grad_lam[1]))
-    grad_gamma_log = lax.dynamic_slice_in_dim(vec[6], me * ns, ns, 0)
+    line = pl.BlockSpec((1, width), lambda i, idx: (0, 0))
+    share = pl.BlockSpec((1, ns), lambda i, idx: (0, 0))
+    grad_ln_gain, grad_ln_bias, grad_skip, grad_nu, grad_theta, grad_gamma, grad_glu_bias = call(
+        partial(small_outputs, hid, ns), 1,
+        [(idx, None), (vec, None), (nu_log[None], None), (theta_log[None], None)],
+        [((1, width), F32, line)] * 3 + [((1, ns), F32, share)] * 3
+        + [((2, hid), F32, pl.BlockSpec((2, hid), lambda i, idx: (0, 0)))], [], 2, 0, 0,
+    )
+    if ns // plane % 16 == 0 and hid // plane % 16 == 0:
+        grad_in, grad_out_weight, grad_glu = call(
+            partial(finish, width), 1,
+            [(idx, None), (stack, None), (got, None)],
+            [((2, ns, width), F32, pl.BlockSpec((2, ns, width), lambda i, idx: (0, 0, 0))),
+             ((2, ns, width), F32, pl.BlockSpec((2, ns, width), lambda i, idx: (0, 0, 0))),
+             ((2, hid, width), F32, None)], [], 6, 0, 0,
+        )
+    else:
+        total = jnp.stack([flip(stack, place), flip(got, place)])
+        total = flip(total, core).astype(F32)
+        nh, nr = hid // plane, ns // plane
+
+        def part(start, size):
+            return total[:, :, start : start + size].reshape(2, -1, width)
+
+        grad_glu, grad_out, grad_in = part(0, nh), part(nh, nr), part(nh + nr, nr)
+        grad_out_weight = jnp.stack([grad_out[0], -grad_out[1]])
     return (
         y.reshape(block_input.shape),
         gx.reshape(block_input.shape),
-        vec[3],
-        vec[4],
-        grad_nu_log,
-        grad_theta_log,
-        grad_gamma_log,
-        grad_in_weight,
+        grad_ln_gain[0],
+        grad_ln_bias[0],
+        grad_nu[0],
+        grad_theta[0],
+        grad_gamma[0],
+        grad_in.transpose(2, 0, 1),
         grad_out_weight,
-        vec[0],
-        grad_glu_weight,
+        grad_skip[0],
+        grad_glu.transpose(2, 0, 1),
         grad_glu_bias,
     )
 

time: 113 us -> 112 us (level)
  local copies, waits for them, and re-layouts: 6.05 us -> 3.44 us
  Pallas kernels: 46.4 us -> 49 us
  other arithmetic: 3.72 us -> 2.03 us
    pallas_call x13 -> x15, Pallas kernels: 46.4 us -> 49 us  [call(): pl.pallas_call(kernel, grid_spec=pltpu.PrefetchScalarGridSpec(num_scalar_...]
    slice x4 -> x0, local copies, waits for them, and re-layouts: 1.37 us -> none  [the longest x2 0.77 us: part(): return total[:, :, start:start + size].reshape(2, -1, width)]
    dynamic_slice x3 -> x0, local copies, waits for them, and re-layouts: 1.23 us -> none  [the longest x1 0.58 us: on_device(): grad_gamma_log = lax.dynamic_slice_in_dim(vec[6], me * ns, ns, 0)]
  transfers between devices with their start and end apart: 26 -> 26, of which waited for: 10 -> 11; matrix products, arithmetic and copies ran while one was open for 3% -> 1% of each run, Pallas kernels for 25% -> 26%
where the time goes in v4:
time: 112 us; the launch traced here: 111 us
  Pallas kernels  49 us (44%)
  starting transfers between devices  32.6 us (29%)
  waiting for transfers between devices  22.9 us (20%)
  local copies, waits for them, and re-layouts  3.44 us (3%)
  other arithmetic  2.03 us (2%)
  between operations  1.2 us (1%)
    pallas_call x15, Pallas kernels, call(): pl.pallas_call(kernel, grid_spec=pltpu.PrefetchScalarGridSpec(num_scalar_...  49 us
    ppermute x15, starting transfers between devices, over_mp(): return lax.ppermute(v, 'mp', xor_pairs(mp, s))  25.2 us
    ppermute x15, waiting for transfers between devices, over_mp(): return lax.ppermute(v, 'mp', xor_pairs(mp, s))  10.5 us
    ppermute x6, waiting for transfers between devices, over_plane(): return lax.ppermute(v, 'dp', xor_pairs(dp, 2 * s))  9.79 us
    ppermute x6, starting transfers between devices, over_plane(): return lax.ppermute(v, 'dp', xor_pairs(dp, 2 * s))  7.11 us
    ppermute x5, waiting for transfers between devices, over_core(): return lax.ppermute(v, 'dp', xor_pairs(dp, 1))  2.57 us
  transfers between devices with their start and end apart: 26, of which 11 were waited for; matrix products, arithmetic and copies ran while one was open for 1% of the time, Pallas kernels for 26%

profile of v4, /device:TPU:0, one launch (start us, length us, event | category | flops | bytes accessed | tf_op | source)
XLA Modules:
  0.0 111.2 jit_solution(7598229449150306145)
XLA Ops:
  3.4 5.1 %collective-permute-start.2 = (bf16[80,512]{1,0:T(8,128)(2,1)S(1)}, bf16[80,512]{1,0:T(8,128)(2,1)S(1)}, u32[]{:S(2)}, u32[]{:S(2)}) collective-permute-start(bf16[80,512]{1,0:T(8,128)(2,1)S(1)} %pad_maximum_fusion.8.refs_0_), channel_id=1, source_target_pairs={{0,3},{1,2},{2,1},{3,0},{4,7},{5,6},{6,5},{7,4},{8,11},{9,10},{10,... | collective-permute-start | bytes 245768 | tf_op jit(solution)/shard_map/gather_in/ppermute | solution.py:695
  10.5 4.7 %shard_map.211 = (f32[2048,512]{1,0:T(8,128)S(1)}, bf16[2048,512]{1,0:T(8,128)(2,1)S(1)}, f32[2048,128]{1,0:T(8,128)S(1)}) custom-call(s32[3]{0:T(128)S(1)} %pad_add_fusion.idx, f32[16,128,512]{2,1,0:T(8,128)} %bitcast.69, f32[1,512]{1,0:T(1,128)} %bitcast.60, f32[1,512]{1,0:T(1,128)} %bitcast.63), custom_call_target="tpu_custom_call" | custom-call | flops 1073741824 | bytes 12582912 | tf_op jit(solution)/shard_map/pallas_call | solution.py:610
  16.0 3.7 %collective-permute-start.6 = (bf16[192,512]{1,0:T(8,128)(2,1)S(1)}, bf16[192,512]{1,0:T(8,128)(2,1)S(1)}, u32[]{:S(2)}, u32[]{:S(2)}) collective-permute-start(bf16[192,512]{1,0:T(8,128)(2,1)S(1)} %pad_maximum_fusion.1.refs_0_), channel_id=1, source_target_pairs={{0,3},{1,2},{2,1},{3,0},{4,7},{5,6},{6,5},{7,4},{8,11},{9,10},{10,... | collective-permute-start | bytes 589832 | tf_op jit(solution)/shard_map/gather_out_glu/ppermute | solution.py:695
  20.5 3.8 %shard_map.213.cotlow_ref = bf16[2048,512]{1,0:T(8,128)(2,1)S(1)} custom-call(s32[3]{0:T(128)S(1)} %pad_add_fusion.idx, f32[16,128,512]{2,1,0:T(8,128)} %bitcast.57), custom_call_target="tpu_custom_call" | custom-call | bytes 8388608 | tf_op jit(solution)/shard_map/pallas_call | solution.py:610
  24.4 2.1 %shard_map.214 = (f32[2048,512]{1,0:T(8,128)S(1)}, bf16[512,512]{1,0:T(8,128)(2,1)S(1)}, f32[12,512]{1,0:T(8,128)S(1)}, f32[16,512]{1,0:T(8,128)S(1)}, f32[8,512]{1,0:T(8,128)S(1)}) custom-call(s32[3]{0:T(128)S(1)} %pad_add_fusion.idx, bf16[2048,512]{1,0:T(8,128)(2,1)S(1)} %get-tuple-element.97.norm_ref, bf16[4,80,512]{2,1,0:T(8,128)(2,1)S(1)} %shard_map.212.own_ref, ...), custom_call_target="tpu_custom_call" | custom-call | flops 1073741824 | bytes 8388608 | tf_op jit(solution)/shard_map/pallas_call | solution.py:610
  26.5 3.7 %collective-permute-start.9 = (f32[8,512]{1,0:T(8,128)S(1)}, f32[8,512]{1,0:T(8,128)S(1)}, u32[]{:S(2)}, u32[]{:S(2)}) collective-permute-start(f32[8,512]{1,0:T(8,128)S(1)} %get-tuple-element.102), channel_id=1, source_target_pairs={{0,3},{1,2},{2,1},{3,0},{4,7},{5,6},{6,5},{7,4},{8,11},{9,10},{10,... | collective-permute-start | bytes 49160 | tf_op jit(solution)/shard_map/carry/ppermute | solution.py:695
  30.1 3.4 %collective-permute-start.7 = (f32[8,512]{1,0:T(8,128)S(1)}, f32[8,512]{1,0:T(8,128)S(1)}, u32[]{:S(2)}, u32[]{:S(2)}) collective-permute-start(f32[8,512]{1,0:T(8,128)S(1)} %get-tuple-element.102), channel_id=1, source_target_pairs={{0,1},{1,0},{2,3},{3,2},{4,5},{5,4},{6,7},{7,6},{8,9},{9,8},{10,11... | collective-permute-start | bytes 49160 | tf_op jit(solution)/shard_map/carry/ppermute | solution.py:695
  33.5 4.3 %collective-permute-done.5.refs_2_ = bf16[192,512]{1,0:T(8,128)(2,1)S(1)} collective-permute-done((bf16[192,512]{1,0:T(8,128)(2,1)S(1)}, bf16[192,512]{1,0:T(8,128)(2,1)S(1)}, u32[]{:S(2)}, u32[]{:S(2)}) %collective-permute-start.5) | collective-permute-done | bytes 196640 | tf_op jit(solution)/shard_map/gather_out_glu/ppermute | solution.py:695
  38.8 2.3 %collective-permute-done.10.other_ref = bf16[4,192,512]{2,1,0:T(8,128)(2,1)S(1)} collective-permute-done((bf16[4,192,512]{2,1,0:T(8,128)(2,1)S(1)}, bf16[4,192,512]{2,1,0:T(8,128)(2,1)S(1)}, u32[]{:S(2)}, u32[]{:S(2)}) %collective-permute-start.10) | collective-permute-done | bytes 786464 | tf_op jit(solution)/shard_map/ppermute | solution.py:689
  41.1 4.1 %shard_map.216 = (bf16[2048,512]{1,0:T(8,128)(2,1)S(1)}, bf16[2048,512]{1,0:T(8,128)(2,1)S(1)}, f32[2048,512]{1,0:T(8,128)S(1)}, bf16[512,512]{1,0:T(8,128)(2,1)S(1)}) custom-call(s32[3]{0:T(128)S(1)} %pad_add_fusion.idx, f32[2048,512]{1,0:T(8,128)S(1)} %get-tuple-element.96.xhat_ref, f32[2048,512]{1,0:T(8,128)S(1)} %get-tuple-element.98.src_ref, ...), custom_call_target="tpu_custom_call" | custom-call | flops 1073741824 | bytes 8388608 | tf_op jit(solution)/shard_map/pallas_call | solution.py:610
  45.2 4.7 %shard_map.217 = (bf16[2048,512]{1,0:T(8,128)(2,1)S(1)}, bf16[2048,1024]{1,0:T(8,128)(2,1)S(1)}, bf16[1024,512]{1,0:T(8,128)(2,1)S(1)}, f32[8,512]{1,0:T(8,128)S(1)}) custom-call(s32[3]{0:T(128)S(1)} %pad_add_fusion.idx, bf16[2048,512]{1,0:T(8,128)(2,1)S(1)} %shard_map.213.cotlow_ref, bf16[2048,512]{1,0:T(8,128)(2,1)S(1)} %get-tuple-element.107.act_ref, ...), custom_call_target="tpu_custom_call" | custom-call | flops 2147483648 | bytes 8388608 | tf_op jit(solution)/shard_map/pallas_call | solution.py:610
  49.9 4.4 %shard_map.218 = (bf16[2048,512]{1,0:T(8,128)(2,1)S(1)}, f32[2048,512]{1,0:T(8,128)S(1)}, f32[16,512]{1,0:T(8,128)S(1)}, f32[8,512]{1,0:T(8,128)S(1)}, f32[8,512]{1,0:T(8,128)S(1)}) custom-call(s32[3]{0:T(128)S(1)} %pad_add_fusion.idx, bf16[2048,1024]{1,0:T(8,128)(2,1)S(1)} %get-tuple-element.114.gpre_ref, f32[2048,512]{1,0:T(8,128)S(1)} %get-tuple-element.110.slope_ref, ...), custom_call_target="tpu_custom_call" | custom-call | flops 4294967296 | bytes 8388608 | tf_op jit(solution)/shard_map/pallas_call | solution.py:610
  55.0 2.4 %collective-permute-start.13 = (f32[8,512]{1,0:T(8,128)S(1)}, f32[8,512]{1,0:T(8,128)S(1)}, u32[]{:S(2)}, u32[]{:S(2)}) collective-permute-start(f32[8,512]{1,0:T(8,128)S(1)} %get-tuple-element.113), channel_id=1, source_target_pairs={{0,3},{1,2},{2,1},{3,0},{4,7},{5,6},{6,5},{7,4},{8,11},{9,10},{10,... | collective-permute-start | bytes 49160 | tf_op jit(solution)/shard_map/carry_back/ppermute | solution.py:695
  58.1 5.2 %shard_map.219 = (f32[1024,512]{1,0:T(8,128)S(1)}, bf16[1024,512]{1,0:T(8,128)(2,1)S(1)}) custom-call(s32[3]{0:T(128)S(1)} %pad_add_fusion.idx, bf16[2048,1024]{1,0:T(8,128)(2,1)S(1)} %get-tuple-element.114.gpre_ref, bf16[2048,512]{1,0:T(8,128)(2,1)S(1)} %get-tuple-element.107.act_ref, bf16[2048,512]{1,0:T(8,128)(2,1)S(1)} %get-tuple-element.115.state_ref, ...), custom_call_target="tpu_custom_call" | custom-call | tf_op jit(solution)/shard_map/pallas_call | solution.py:610
  63.3 3.5 %shard_map.220 = (bf16[2048,512]{1,0:T(8,128)(2,1)S(1)}, f32[1024,512]{1,0:T(8,128)S(1)}, bf16[1024,512]{1,0:T(8,128)(2,1)S(1)}, f32[8,512]{1,0:T(8,128)S(1)}) custom-call(s32[3]{0:T(128)S(1)} %pad_add_fusion.idx, f32[1024,512]{1,0:T(8,128)S(1)} %get-tuple-element.117.keep_in, ...), custom_call_target="tpu_custom_call", output_to_operand_aliasing={{1}: (1, {}), {2}: (2, {})} | custom-call | flops 1073741824 | bytes 8388608 | tf_op jit(solution)/shard_map/pallas_call | solution.py:610
  66.9 5.9 %shard_map.221 = (f32[16,128,512]{2,1,0:T(8,128)}, f32[8,512]{1,0:T(8,128)S(1)}) custom-call(s32[3]{0:T(128)S(1)} %pad_add_fusion.idx, f32[16,128,512]{2,1,0:T(8,128)S(1)} %bitcast.58, bf16[2048,512]{1,0:T(8,128)(2,1)S(1)} %get-tuple-element.122.gdrive_ref, bf16[512,512]{1,0:T(8,128)(2,1)S(1)} %get-tuple-element.123.wt_ref, ...), custom_call_target="tpu_custom_call" | custom-call | flops 1073741824 | bytes 8388608 | tf_op jit(solution)/shard_map/pallas_call | solution.py:610
  73.6 1.6 %collective-permute-start.16 = (bf16[256,512]{1,0:T(8,128)(2,1)S(1)}, bf16[256,512]{1,0:T(8,128)(2,1)S(1)}, u32[]{:S(2)}, u32[]{:S(2)}) collective-permute-start(bf16[256,512]{1,0:T(8,128)(2,1)S(1)} %get-tuple-element.137), channel_id=1, source_target_pairs={{0,8},{4,12},{8,0},{12,4},{16,24},{20,28},{24,16},{28,20},{1,9},{5... | collective-permute-start | bytes 786440 | tf_op jit(solution)/shard_map/sum_plane/ppermute | solution.py:692
  75.2 1.5 %collective-permute-start.17 = (bf16[256,512]{1,0:T(8,128)(2,1)S(1)}, bf16[256,512]{1,0:T(8,128)(2,1)S(1)}, u32[]{:S(2)}, u32[]{:S(2)}) collective-permute-start(bf16[256,512]{1,0:T(8,128)(2,1)S(1)} %get-tuple-element.139), channel_id=1, source_target_pairs={{0,16},{4,20},{8,24},{12,28},{16,0},{20,4},{24,8},{28,12},{1,17},{... | collective-permute-start | bytes 786440 | tf_op jit(solution)/shard_map/sum_plane/ppermute | solution.py:692
  77.2 6.0 %shard_map.222 = f32[16,128,512]{2,1,0:T(8,128)} custom-call(s32[3]{0:T(128)S(1)} %pad_add_fusion.idx, f32[16,128,512]{2,1,0:T(8,128)} %bitcast.70, bf16[2048,512]{1,0:T(8,128)(2,1)} %copy-done.3), custom_call_target="tpu_custom_call" | custom-call | tf_op jit(solution)/shard_map/pallas_call | solution.py:610
  83.2 5.9 %collective-permute-done.17 = bf16[256,512]{1,0:T(8,128)(2,1)S(1)} collective-permute-done((bf16[256,512]{1,0:T(8,128)(2,1)S(1)}, bf16[256,512]{1,0:T(8,128)(2,1)S(1)}, u32[]{:S(2)}, u32[]{:S(2)}) %collective-permute-start.17) | collective-permute-done | bytes 262176 | tf_op jit(solution)/shard_map/sum_plane/ppermute | solution.py:692
  90.8 1.6 %collective-permute-start.20 = (bf16[80,512]{1,0:T(8,128)(2,1)S(1)}, bf16[80,512]{1,0:T(8,128)(2,1)S(1)}, u32[]{:S(2)}, u32[]{:S(2)}) collective-permute-start(bf16[80,512]{1,0:T(8,128)(2,1)S(1)} %get-tuple-element.174), channel_id=1, source_target_pairs={{0,2},{1,3},{2,0},{3,1},{4,6},{5,7},{6,4},{7,5},{8,10},{9,11},{10,... | collective-permute-start | bytes 245768 | tf_op jit(solution)/shard_map/sum_mp/ppermute | solution.py:695
  94.6 5.0 %collective-permute-done.20 = bf16[80,512]{1,0:T(8,128)(2,1)S(1)} collective-permute-done((bf16[80,512]{1,0:T(8,128)(2,1)S(1)}, bf16[80,512]{1,0:T(8,128)(2,1)S(1)}, u32[]{:S(2)}, u32[]{:S(2)}) %collective-permute-start.20) | collective-permute-done | bytes 81952 | tf_op jit(solution)/shard_map/sum_mp/ppermute | solution.py:695
  99.7 1.5 %collective-permute-start.24 = (bf16[80,512]{1,0:T(8,128)(2,1)S(1)}, bf16[80,512]{1,0:T(8,128)(2,1)S(1)}, u32[]{:S(2)}, u32[]{:S(2)}) collective-permute-start(bf16[80,512]{1,0:T(8,128)(2,1)S(1)} %pad_maximum_fusion.9), channel_id=1, source_target_pairs={{0,24},{4,28},{8,16},{12,20},{16,8},{20,12},{24,0},{28,4},{1,25},{... | collective-permute-start | bytes 245768 | tf_op jit(solution)/shard_map/spread_plane/ppermute | solution.py:692
  103.3 1.9 %collective-permute-done.24 = bf16[80,512]{1,0:T(8,128)(2,1)S(1)} collective-permute-done((bf16[80,512]{1,0:T(8,128)(2,1)S(1)}, bf16[80,512]{1,0:T(8,128)(2,1)S(1)}, u32[]{:S(2)}, u32[]{:S(2)}) %collective-permute-start.24) | collective-permute-done | bytes 81952 | tf_op jit(solution)/shard_map/spread_plane/ppermute | solution.py:692
  (93 shorter events, 21.8 us)
Async XLA Ops:
  3.4 11.8 %collective-permute-start.2 = (bf16[80,512]{1,0:T(8,128)(2,1)S(1)}, bf16[80,512]{1,0:T(8,128)(2,1)S(1)}, u32[]{:S(2)}, u32[]{:S(2)}) collective-permute-start(bf16[80,512]{1,0:T(8,128)(2,1)S(1)} %pad_maximum_fusion.8.refs_0_), channel_id=1, source_target_pairs={{0,3},{1,2},{2,1},{3,0},{4,7},{5,6},{6,5},{7,4},{8,11},{9,10},{10,... | collective-permute-start | bytes 245768 | tf_op jit(solution)/shard_map/gather_in/ppermute | solution.py:695
  8.5 6.9 %collective-permute-start.1 = (bf16[80,512]{1,0:T(8,128)(2,1)S(1)}, bf16[80,512]{1,0:T(8,128)(2,1)S(1)}, u32[]{:S(2)}, u32[]{:S(2)}) collective-permute-start(bf16[80,512]{1,0:T(8,128)(2,1)S(1)} %pad_maximum_fusion.8.refs_0_), channel_id=1, source_target_pairs={{0,2},{1,3},{2,0},{3,1},{4,6},{5,7},{6,4},{7,5},{8,10},{9,11},{10,... | collective-permute-start | bytes 245768 | tf_op jit(solution)/shard_map/gather_in/ppermute | solution.py:695
  8.5 6.9 %collective-permute-start = (bf16[80,512]{1,0:T(8,128)(2,1)S(1)}, bf16[80,512]{1,0:T(8,128)(2,1)S(1)}, u32[]{:S(2)}, u32[]{:S(2)}) collective-permute-start(bf16[80,512]{1,0:T(8,128)(2,1)S(1)} %pad_maximum_fusion.8.refs_0_), channel_id=1, source_target_pairs={{0,1},{1,0},{2,3},{3,2},{4,5},{5,4},{6,7},{7,6},{8,9},{9,8},{10,11... | collective-permute-start | bytes 245768 | tf_op jit(solution)/shard_map/gather_in/ppermute | solution.py:695
  16.0 8.4 %collective-permute-start.3 = (bf16[4,80,512]{2,1,0:T(8,128)(2,1)S(1)}, bf16[4,80,512]{2,1,0:T(8,128)(2,1)S(1)}, u32[]{:S(2)}, u32[]{:S(2)}) collective-permute-start(bf16[4,80,512]{2,1,0:T(8,128)(2,1)S(1)} %shard_map.212.own_ref), channel_id=1, source_target_pairs={{0,4},{4,0},{8,12},{12,8},{16,20},{20,16},{24,28},{28,24},{1,5},{5... | collective-permute-start | bytes 983048 | tf_op jit(solution)/shard_map/ppermute | solution.py:689
  16.0 14.1 %collective-permute-start.6 = (bf16[192,512]{1,0:T(8,128)(2,1)S(1)}, bf16[192,512]{1,0:T(8,128)(2,1)S(1)}, u32[]{:S(2)}, u32[]{:S(2)}) collective-permute-start(bf16[192,512]{1,0:T(8,128)(2,1)S(1)} %pad_maximum_fusion.1.refs_0_), channel_id=1, source_target_pairs={{0,3},{1,2},{2,1},{3,0},{4,7},{5,6},{6,5},{7,4},{8,11},{9,10},{10,... | collective-permute-start | bytes 589832 | tf_op jit(solution)/shard_map/gather_out_glu/ppermute | solution.py:695
  19.7 18.0 %collective-permute-start.5 = (bf16[192,512]{1,0:T(8,128)(2,1)S(1)}, bf16[192,512]{1,0:T(8,128)(2,1)S(1)}, u32[]{:S(2)}, u32[]{:S(2)}) collective-permute-start(bf16[192,512]{1,0:T(8,128)(2,1)S(1)} %pad_maximum_fusion.1.refs_0_), channel_id=1, source_target_pairs={{0,2},{1,3},{2,0},{3,1},{4,6},{5,7},{6,4},{7,5},{8,10},{9,11},{10,... | collective-permute-start | bytes 589832 | tf_op jit(solution)/shard_map/gather_out_glu/ppermute | solution.py:695
  19.7 18.0 %collective-permute-start.4 = (bf16[192,512]{1,0:T(8,128)(2,1)S(1)}, bf16[192,512]{1,0:T(8,128)(2,1)S(1)}, u32[]{:S(2)}, u32[]{:S(2)}) collective-permute-start(bf16[192,512]{1,0:T(8,128)(2,1)S(1)} %pad_maximum_fusion.1.refs_0_), channel_id=1, source_target_pairs={{0,1},{1,0},{2,3},{3,2},{4,5},{5,4},{6,7},{7,6},{8,9},{9,8},{10,11... | collective-permute-start | bytes 589832 | tf_op jit(solution)/shard_map/gather_out_glu/ppermute | solution.py:695
  26.5 11.3 %collective-permute-start.9 = (f32[8,512]{1,0:T(8,128)S(1)}, f32[8,512]{1,0:T(8,128)S(1)}, u32[]{:S(2)}, u32[]{:S(2)}) collective-permute-start(f32[8,512]{1,0:T(8,128)S(1)} %get-tuple-element.102), channel_id=1, source_target_pairs={{0,3},{1,2},{2,1},{3,0},{4,7},{5,6},{6,5},{7,4},{8,11},{9,10},{10,... | collective-permute-start | bytes 49160 | tf_op jit(solution)/shard_map/carry/ppermute | solution.py:695
  30.1 8.0 %collective-permute-start.8 = (f32[8,512]{1,0:T(8,128)S(1)}, f32[8,512]{1,0:T(8,128)S(1)}, u32[]{:S(2)}, u32[]{:S(2)}) collective-permute-start(f32[8,512]{1,0:T(8,128)S(1)} %get-tuple-element.102), channel_id=1, source_target_pairs={{0,2},{1,3},{2,0},{3,1},{4,6},{5,7},{6,4},{7,5},{8,10},{9,11},{10,... | collective-permute-start | bytes 49160 | tf_op jit(solution)/shard_map/carry/ppermute | solution.py:695
  30.1 8.0 %collective-permute-start.7 = (f32[8,512]{1,0:T(8,128)S(1)}, f32[8,512]{1,0:T(8,128)S(1)}, u32[]{:S(2)}, u32[]{:S(2)}) collective-permute-start(f32[8,512]{1,0:T(8,128)S(1)} %get-tuple-element.102), channel_id=1, source_target_pairs={{0,1},{1,0},{2,3},{3,2},{4,5},{5,4},{6,7},{7,6},{8,9},{9,8},{10,11... | collective-permute-start | bytes 49160 | tf_op jit(solution)/shard_map/carry/ppermute | solution.py:695
  54.5 8.8 %collective-permute-start.11 = (f32[8,512]{1,0:T(8,128)S(1)}, f32[8,512]{1,0:T(8,128)S(1)}, u32[]{:S(2)}, u32[]{:S(2)}) collective-permute-start(f32[8,512]{1,0:T(8,128)S(1)} %get-tuple-element.113), channel_id=1, source_target_pairs={{0,1},{1,0},{2,3},{3,2},{4,5},{5,4},{6,7},{7,6},{8,9},{9,8},{10,11... | collective-permute-start | bytes 49160 | tf_op jit(solution)/shard_map/carry_back/ppermute | solution.py:695
  55.0 8.3 %collective-permute-start.13 = (f32[8,512]{1,0:T(8,128)S(1)}, f32[8,512]{1,0:T(8,128)S(1)}, u32[]{:S(2)}, u32[]{:S(2)}) collective-permute-start(f32[8,512]{1,0:T(8,128)S(1)} %get-tuple-element.113), channel_id=1, source_target_pairs={{0,3},{1,2},{2,1},{3,0},{4,7},{5,6},{6,5},{7,4},{8,11},{9,10},{10,... | collective-permute-start | bytes 49160 | tf_op jit(solution)/shard_map/carry_back/ppermute | solution.py:695
  57.4 6.0 %collective-permute-start.12 = (f32[8,512]{1,0:T(8,128)S(1)}, f32[8,512]{1,0:T(8,128)S(1)}, u32[]{:S(2)}, u32[]{:S(2)}) collective-permute-start(f32[8,512]{1,0:T(8,128)S(1)} %get-tuple-element.113), channel_id=1, source_target_pairs={{0,2},{1,3},{2,0},{3,1},{4,6},{5,7},{6,4},{7,5},{8,10},{9,11},{10,... | collective-permute-start | bytes 49160 | tf_op jit(solution)/shard_map/carry_back/ppermute | solution.py:695
  66.8 6.0 %collective-permute-start.14 = (bf16[1024,512]{1,0:T(8,128)(2,1)S(1)}, bf16[1024,512]{1,0:T(8,128)(2,1)S(1)}, u32[]{:S(2)}, u32[]{:S(2)}) collective-permute-start(bf16[1024,512]{1,0:T(8,128)(2,1)S(1)} %get-tuple-element.130), channel_id=1, source_target_pairs={{0,4},{4,0},{8,12},{12,8},{16,20},{20,16},{24,28},{28,24},{1,5},{5... | collective-permute-start | bytes 3145736 | tf_op jit(solution)/shard_map/sum_core/ppermute | solution.py:689
  73.6 9.6 %collective-permute-start.16 = (bf16[256,512]{1,0:T(8,128)(2,1)S(1)}, bf16[256,512]{1,0:T(8,128)(2,1)S(1)}, u32[]{:S(2)}, u32[]{:S(2)}) collective-permute-start(bf16[256,512]{1,0:T(8,128)(2,1)S(1)} %get-tuple-element.137), channel_id=1, source_target_pairs={{0,8},{4,12},{8,0},{12,4},{16,24},{20,28},{24,16},{28,20},{1,9},{5... | collective-permute-start | bytes 786440 | tf_op jit(solution)/shard_map/sum_plane/ppermute | solution.py:692
  75.2 14.0 %collective-permute-start.17 = (bf16[256,512]{1,0:T(8,128)(2,1)S(1)}, bf16[256,512]{1,0:T(8,128)(2,1)S(1)}, u32[]{:S(2)}, u32[]{:S(2)}) collective-permute-start(bf16[256,512]{1,0:T(8,128)(2,1)S(1)} %get-tuple-element.139), channel_id=1, source_target_pairs={{0,16},{4,20},{8,24},{12,28},{16,0},{20,4},{24,8},{28,12},{1,17},{... | collective-permute-start | bytes 786440 | tf_op jit(solution)/shard_map/sum_plane/ppermute | solution.py:692
  76.7 12.5 %collective-permute-start.18 = (bf16[256,512]{1,0:T(8,128)(2,1)S(1)}, bf16[256,512]{1,0:T(8,128)(2,1)S(1)}, u32[]{:S(2)}, u32[]{:S(2)}) collective-permute-start(bf16[256,512]{1,0:T(8,128)(2,1)S(1)} %get-tuple-element.140), channel_id=1, source_target_pairs={{0,24},{4,28},{8,16},{12,20},{16,8},{20,12},{24,0},{28,4},{1,25},{... | collective-permute-start | bytes 786440 | tf_op jit(solution)/shard_map/sum_plane/ppermute | solution.py:692
  77.2 6.1 %collective-permute-start.15 = (bf16[16,512]{1,0:T(8,128)(2,1)S(1)}, bf16[16,512]{1,0:T(8,128)(2,1)S(1)}, u32[]{:S(2)}, u32[]{:S(2)}) collective-permute-start(bf16[16,512]{1,0:T(8,128)(2,1)S(1)} %get-tuple-element.135), channel_id=1, source_target_pairs={{0,4},{4,0},{8,12},{12,8},{16,20},{20,16},{24,28},{28,24},{1,5},{5... | collective-permute-start | bytes 49160 | tf_op jit(solution)/shard_map/sum_vectors_core/ppermute | solution.py:689
  89.4 5.2 %collective-permute-start.19 = (bf16[80,512]{1,0:T(8,128)(2,1)S(1)}, bf16[80,512]{1,0:T(8,128)(2,1)S(1)}, u32[]{:S(2)}, u32[]{:S(2)}) collective-permute-start(bf16[80,512]{1,0:T(8,128)(2,1)S(1)} %get-tuple-element.173), channel_id=1, source_target_pairs={{0,1},{1,0},{2,3},{3,2},{4,5},{5,4},{6,7},{7,6},{8,9},{9,8},{10,11... | collective-permute-start | bytes 245768 | tf_op jit(solution)/shard_map/sum_mp/ppermute | solution.py:695
  90.8 8.8 %collective-permute-start.20 = (bf16[80,512]{1,0:T(8,128)(2,1)S(1)}, bf16[80,512]{1,0:T(8,128)(2,1)S(1)}, u32[]{:S(2)}, u32[]{:S(2)}) collective-permute-start(bf16[80,512]{1,0:T(8,128)(2,1)S(1)} %get-tuple-element.174), channel_id=1, source_target_pairs={{0,2},{1,3},{2,0},{3,1},{4,6},{5,7},{6,4},{7,5},{8,10},{9,11},{10,... | collective-permute-start | bytes 245768 | tf_op jit(solution)/shard_map/sum_mp/ppermute | solution.py:695
  92.4 7.2 %collective-permute-start.21 = (bf16[80,512]{1,0:T(8,128)(2,1)S(1)}, bf16[80,512]{1,0:T(8,128)(2,1)S(1)}, u32[]{:S(2)}, u32[]{:S(2)}) collective-permute-start(bf16[80,512]{1,0:T(8,128)(2,1)S(1)} %get-tuple-element.175), channel_id=1, source_target_pairs={{0,3},{1,2},{2,1},{3,0},{4,7},{5,6},{6,5},{7,4},{8,11},{9,10},{10,... | collective-permute-start | bytes 245768 | tf_op jit(solution)/shard_map/sum_mp/ppermute | solution.py:695
  99.7 5.4 %collective-permute-start.24 = (bf16[80,512]{1,0:T(8,128)(2,1)S(1)}, bf16[80,512]{1,0:T(8,128)(2,1)S(1)}, u32[]{:S(2)}, u32[]{:S(2)}) collective-permute-start(bf16[80,512]{1,0:T(8,128)(2,1)S(1)} %pad_maximum_fusion.9), channel_id=1, source_target_pairs={{0,24},{4,28},{8,16},{12,20},{16,8},{20,12},{24,0},{28,4},{1,25},{... | collective-permute-start | bytes 245768 | tf_op jit(solution)/shard_map/spread_plane/ppermute | solution.py:692
  101.2 4.8 %collective-permute-start.23 = (bf16[80,512]{1,0:T(8,128)(2,1)S(1)}, bf16[80,512]{1,0:T(8,128)(2,1)S(1)}, u32[]{:S(2)}, u32[]{:S(2)}) collective-permute-start(bf16[80,512]{1,0:T(8,128)(2,1)S(1)} %pad_maximum_fusion.9), channel_id=1, source_target_pairs={{0,16},{4,20},{8,24},{12,28},{16,0},{20,4},{24,8},{28,12},{1,17},{... | collective-permute-start | bytes 245768 | tf_op jit(solution)/shard_map/spread_plane/ppermute | solution.py:692
  102.7 4.4 %collective-permute-start.22 = (bf16[80,512]{1,0:T(8,128)(2,1)S(1)}, bf16[80,512]{1,0:T(8,128)(2,1)S(1)}, u32[]{:S(2)}, u32[]{:S(2)}) collective-permute-start(bf16[80,512]{1,0:T(8,128)(2,1)S(1)} %pad_maximum_fusion.9), channel_id=1, source_target_pairs={{0,8},{4,12},{8,0},{12,4},{16,24},{20,28},{24,16},{28,20},{1,9},{5... | collective-permute-start | bytes 245768 | tf_op jit(solution)/shard_map/spread_plane/ppermute | solution.py:692
  (11 other events, 153.6 us)

commit v5 on v4

--- a/solution.py
+++ b/solution.py
@@ -272,13 +272,6 @@
     run(gelus(blocks - 1, mix_refs[(blocks - 1) % 2]))
 
 
-def add_branch(idx, x_ref, br_ref, y_ref):
-    width = x_ref.shape[2]
-    for k in range(0, x_ref.shape[1], 8):
-        rows = br_ref[k * CHUNKS : (k + 8) * CHUNKS, :].astype(F32).reshape(8, CHUNKS, width)
-        y_ref[:, k : k + 8, :] = x_ref[:, k : k + 8, :] + jnp.swapaxes(rows, 0, 1)
-
-
 def gating(mp, idx, cotlow_ref, act_ref, par_ref, own_ref, other_ref,
            br_ref, gpre_ref, wg_ref, vec_ref, pre_a, pre_b):
     width = act_ref.shape[1]
@@ -482,8 +475,8 @@
     vec_ref[2:8, :] = jnp.zeros((6, width), F32)
 
 
-def norm_back(idx, cot_ref, gdrive_ref, wt_ref, gmix_ref, xhat_ref, rstd_ref, gain_ref, skip_ref,
-              gx_ref, vec_ref, gn_a, gn_b, dx_ref):
+def norm_back(idx, cot_ref, gdrive_ref, wt_ref, gmix_ref, xhat_ref, rstd_ref, gain_ref, skip_ref, x_ref, br_ref,
+              vec_skip_ref, vec_glu_ref, vec_lam_ref, gx_ref, y_ref, parts_ref, send_ref, gn_a, gn_b, dx_ref, vec_ref):
     step = pl.program_id(0)
     width = cot_ref.shape[2]
     per = STEP_ROWS // CHUNKS
@@ -522,13 +515,28 @@
         place = pl.ds(pl.multiple_of(step * per + k, 8), 8)
         gx_ref[:, k : k + 8, :] = cot_ref[:, place, :] + jnp.swapaxes(rows, 0, 1)
 
+    def branch_piece(k):
+        here = pl.ds(pl.multiple_of(step * STEP_ROWS + k * CHUNKS, 128), 8 * CHUNKS)
+        rows = br_ref[here, :].astype(F32).reshape(8, CHUNKS, width)
+        y_ref[:, k : k + 8, :] = x_ref[:, k : k + 8, :] + jnp.swapaxes(rows, 0, 1)
+
     after = jnp.minimum(2 * step + 2, gdrive_ref.shape[0] // BLOCK - 1)
     outputs = [partial(output_piece, k) for k in range(0, per, 8)]
+    run([partial(branch_piece, k) for k in range(0, per, 8)])
     alternate(normed_pieces(2 * step + 1, gn_b), norm_pieces(0, gn_a))
     alternate(normed_pieces(after, gn_a), outputs[: len(outputs) // 2] + norm_pieces(1, gn_b) + outputs[len(outputs) // 2 :])
     vec_ref[0:1, :] += jnp.sum(sums[0], 0, keepdims=True)
     vec_ref[1:2, :] += jnp.sum(sums[1], 0, keepdims=True)
 
+    @pl.when(step == pl.num_programs(0) - 1)
+    def _():
+        rows = [vec_skip_ref[0:1, :], vec_glu_ref[1:3, :], vec_ref[0:2, :], vec_lam_ref[0:2, :], jnp.zeros((1, width), F32)]
+        vec = jnp.concatenate(rows, 0)
+        high = vec.astype(BF16)
+        low = (vec - high.astype(F32)).astype(BF16)
+        parts_ref[...] = high.astype(F32) + low.astype(F32)
+        send_ref[...] = jnp.concatenate([high.astype(F32), low.astype(F32)], 0).astype(BF16)
+
 
 def pack_rows(idx, *refs):
     *parts, out = refs
@@ -536,52 +544,48 @@
         out[i] = part[...]
 
 
-def split_pieces(slots, count, hid, ns, idx, keep_ref, got_ref, skip_ref, glu_ref, norm_ref, lam_ref,
-                 own_ref, vec_ref, vec_send_ref, *sends):
+def split_pieces(slots, count, sizes, idx, keep_ref, got_ref, own_ref, *sends):
     place = idx[2]
+    height = sum(sizes) // count
+    for slot in range(slots):
+        for s in range(count):
+            base, low = 0, slot * height
+            for size in sizes:
+                rows = size // count
+                start = pl.multiple_of(base + slot * size + (place ^ s) * rows, rows)
+                piece = keep_ref[pl.ds(start, rows), :] + got_ref[pl.ds(start, rows), :].astype(F32)
+                if s == 0:
+                    own_ref[low : low + rows, :] = piece
+                else:
+                    sends[s - 1][low : low + rows, :] = piece.astype(BF16)
+                base, low = base + slots * size, low + rows
+
+
+def finish(hid, ns, count, idx, own_ref, got_ref, nu_ref, theta_ref, in_ref, out_ref, glu_ref, *rest):
+    core, place = idx[1], idx[2]
     height = (hid + 2 * ns) // count
-    for slot in range(slots):
-        parts = ((slot * hid, hid, 0), (slots * hid + slot * ns, ns, hid), (slots * (hid + ns) + slot * ns, ns, hid + ns))
-        for s in range(count):
-            for first, size, low in parts:
-                rows = size // count
-                start = pl.multiple_of(first + (place ^ s) * rows, rows)
-                piece = keep_ref[pl.ds(start, rows), :] + got_ref[pl.ds(start, rows), :].astype(F32)
-                begin = slot * height + low // count
-                if s == 0:
-                    own_ref[begin : begin + rows, :] = piece
-                else:
-                    sends[s - 1][begin : begin + rows, :] = piece.astype(BF16)
-    rows = [skip_ref[0:1, :], glu_ref[1:3, :], norm_ref[0:2, :], lam_ref[0:2, :], jnp.zeros((1, skip_ref.shape[1]), F32)]
-    vec = jnp.concatenate(rows, 0)
-    high = vec.astype(BF16)
-    low = (vec - high.astype(F32)).astype(BF16)
-    vec_ref[...] = high.astype(F32) + low.astype(F32)
-    vec_send_ref[...] = jnp.concatenate([high.astype(F32), low.astype(F32)], 0).astype(BF16)
-
-
-def finish(width, idx, own_ref, got_ref, in_ref, out_ref, glu_ref):
-    core, place = idx[1], idx[2]
-    count, height = own_ref.shape[0], own_ref.shape[1]
-    ns, hid = in_ref.shape[1], glu_ref.shape[1]
     for part in range(2):
         for i in range(count):
-            mine, theirs = own_ref[i ^ place], got_ref[i ^ place]
-            rows = jnp.where(core == part, mine, theirs).astype(F32)
+            here = pl.ds(pl.multiple_of((i ^ place) * height, 16), height)
+            rows = jnp.where(core == part, own_ref[here, :], got_ref[here, :]).astype(F32)
             low = 0
             for ref, size in ((glu_ref, hid // count), (out_ref, ns // count), (in_ref, ns // count)):
                 value = rows[low : low + size]
                 ref[part, i * size : (i + 1) * size, :] = -value if ref is out_ref and part == 1 else value
                 low += size
-
-
-def small_outputs(hid, ns, idx, vec_ref, nu_ref, theta_ref, gain_ref, bias_ref, skip_ref, nu_out, theta_out, gamma_out, glu_ref):
+    first = count * height
+    both = [ref[first : first + 16, :].astype(F32) for ref in (own_ref, got_ref)]
+    vec = (both[0][:8] + both[0][8:]) + (both[1][:8] + both[1][8:])
+    vector_outputs(hid, ns, idx, vec, nu_ref, theta_ref, *rest)
+
+
+def vector_outputs(hid, ns, idx, vec, nu_ref, theta_ref, gain_ref, bias_ref, skip_ref, nu_out, theta_out, gamma_out, glu_ref):
     me = idx[0]
-    width = vec_ref.shape[1]
+    width = vec.shape[1]
     states = width // 2
-    skip_ref[...] = vec_ref[0:1, :]
-    gain_ref[...] = vec_ref[3:4, :]
-    bias_ref[...] = vec_ref[4:5, :]
+    skip_ref[...] = vec[0:1, :]
+    gain_ref[...] = vec[3:4, :]
+    bias_ref[...] = vec[4:5, :]
 
     def share(rows, start, size, count):
         total = jnp.zeros((rows.shape[0], size), F32)
@@ -589,15 +593,19 @@
             total = total + jnp.where(me == j, rows[:, start + j * size : start + (j + 1) * size], 0.0)
         return total
 
-    glu_ref[...] = share(vec_ref[1:3, :], 0, hid, width // hid)
-    re = share(vec_ref[5:6, :], 0, ns, states // ns)
-    im = share(vec_ref[5:6, :], states, ns, states // ns)
-    gamma_out[...] = share(vec_ref[6:7, :], 0, ns, states // ns)
+    glu_ref[...] = share(vec[1:3, :], 0, hid, width // hid)
+    re = share(vec[5:6, :], 0, ns, states // ns)
+    im = share(vec[5:6, :], states, ns, states // ns)
+    gamma_out[...] = share(vec[6:7, :], 0, ns, states // ns)
     speed, turn = jnp.exp(nu_ref[...]), jnp.exp(theta_ref[...])
     radius = jnp.exp(-speed)
     cos, sin = radius * jnp.cos(turn), radius * jnp.sin(turn)
     nu_out[...] = -speed * (cos * re + sin * im)
     theta_out[...] = turn * (cos * im - sin * re)
+
+
+def small_outputs(hid, ns, idx, vec_ref, *rest):
+    vector_outputs(hid, ns, idx, vec_ref[...], *rest)
 
 
 def call(kernel, steps, ins, outs, scratch, mib, flops, moved, in_place=None, first=False):
@@ -807,43 +815,35 @@
     )
     with jax.named_scope("sum_core"):
         got = over_core(send)
-    gx, vec_norm = call(
-        norm_back, steps,
-        [(idx, None), (cot, None), (gdrive, None), (wt, None), (gmix, None), (xhat, None), (rstd, None),
-         (gain, vector), (skp, vector)],
-        [((CHUNKS, chunk, width), F32, chunked), small],
-        scratch((BLOCK, width, F32), (BLOCK, width, F32), (STEP_ROWS, width, F32)), 8, product, 8,
-    )
-    (y,) = call(add_branch, steps, [(idx, None), (x, chunked), (tied(branch, vec_norm), rowed)],
-                [((CHUNKS, chunk, width), F32, chunked)], [], 10, 0, 0)
-    keep, nu_log, theta_log, me, core, place = lax.optimization_barrier(
-        (keep, nu_log, theta_log, me, core, place, vec_norm)
-    )[:6]
     height = mp * (hid + 2 * ns) // plane
     if ns // plane % 16 == 0 and hid // plane % 16 == 0:
-        own_piece, vec, vec_rows, *sends = call(
-            partial(split_pieces, mp, plane, hid, ns), 1,
-            [(idx, None), (keep, None), (got, None), (vec_skip, None), (vec_glu, None), (vec_norm, None), (vec_lam, None)],
-            [((height, width), F32, None), small, ((16, width), BF16, None)] + [((height, width), BF16, None)] * (plane - 1),
-            [], 4, 0, 0,
+        own_piece, *sends = call(
+            partial(split_pieces, mp, plane, (hid, ns, ns)), 1,
+            [(idx, None), (keep, None), (got, None)],
+            [((height, width), F32, None)] + [((height, width), BF16, None)] * (plane - 1), [], 4, 0, 0,
         )
     else:
-        vec = jnp.concatenate([vec_skip[0:1], vec_glu[1:3], vec_norm[0:2], vec_lam[0:2], jnp.zeros((1, width), F32)])
-        vec, vec_rows = vector_rows(vec)
         both = keep + got.astype(F32)
         both = [both[: mp * hid], both[mp * hid : early_rows], both[early_rows:]]
         both = jnp.concatenate([v.reshape(mp, plane, -1, width) for v in both], 2).swapaxes(0, 1)
         sends = [lax.dynamic_index_in_dim(both, place ^ s, 0, keepdims=False) for s in range(plane)]
         sends = [v.reshape(-1, width) for v in sends]
         own_piece, sends = sends[0], [v.astype(BF16) for v in sends[1:]]
-    with jax.named_scope("sum_vectors_core"):
-        vec = vec + vector_sum(over_core(vec_rows))
     with jax.named_scope("sum_plane"):
         pieces = [over_plane(v, s + 1) for s, v in enumerate(sends)]
-    pieces[0] = tied(pieces[0], y)
+    gx, y, vec, vec_rows = call(
+        norm_back, steps,
+        [(idx, None), (cot, None), (tied(gdrive, own_piece), None), (wt, None), (gmix, None), (xhat, None), (rstd, None),
+         (gain, vector), (skp, vector), (x, chunked), (branch, None), (vec_skip, None), (vec_glu, None),
+         (vec_lam, None)],
+        [((CHUNKS, chunk, width), F32, chunked), ((CHUNKS, chunk, width), F32, chunked), small, ((16, width), BF16, None)],
+        scratch((BLOCK, width, F32), (BLOCK, width, F32), (STEP_ROWS, width, F32), (8, width, F32)), 18, product, 8,
+    )
+    pieces[0], own_piece, nu_log, theta_log, me, core, place = lax.optimization_barrier(
+        (pieces[0], own_piece, nu_log, theta_log, me, core, place, vec)
+    )[:7]
     rows = tree_sum([own_piece] + [p.astype(F32) for p in pieces]).reshape(mp, -1, width)
     with jax.named_scope("sum_mp"):
-        vec, vec_rows = vector_rows(vec)
         got, vecs = [lax.dynamic_index_in_dim(rows, me, 0, keepdims=False)], [vec]
         n = got[0].shape[0]
         for s in range(1, mp):
@@ -857,28 +857,28 @@
         piece = jnp.concatenate([piece, vec_rows])
         stack = [piece] + [over_plane(piece, s) for s in range(1, plane)]
     vec = tree_sum([vec] + [vector_sum(v[n:]) for v in stack[1:]])
-    stack = jnp.stack([v[:n] for v in stack])
+    vec, vec_rows = vector_rows(vec)
+    own = jnp.concatenate([v[:n] for v in stack] + [vec_rows])
     with jax.named_scope("spread_core"):
-        got = over_core(stack)
+        got = over_core(own)
     line = pl.BlockSpec((1, width), lambda i, idx: (0, 0))
     share = pl.BlockSpec((1, ns), lambda i, idx: (0, 0))
-    grad_ln_gain, grad_ln_bias, grad_skip, grad_nu, grad_theta, grad_gamma, grad_glu_bias = call(
-        partial(small_outputs, hid, ns), 1,
-        [(idx, None), (vec, None), (nu_log[None], None), (theta_log[None], None)],
-        [((1, width), F32, line)] * 3 + [((1, ns), F32, share)] * 3
-        + [((2, hid), F32, pl.BlockSpec((2, hid), lambda i, idx: (0, 0)))], [], 2, 0, 0,
-    )
+    shared = [((1, width), F32, line)] * 3 + [((1, ns), F32, share)] * 3
+    shared.append(((2, hid), F32, pl.BlockSpec((2, hid), lambda i, idx: (0, 0))))
+    logs = [(nu_log[None], None), (theta_log[None], None)]
     if ns // plane % 16 == 0 and hid // plane % 16 == 0:
-        grad_in, grad_out_weight, grad_glu = call(
-            partial(finish, width), 1,
-            [(idx, None), (stack, None), (got, None)],
-            [((2, ns, width), F32, pl.BlockSpec((2, ns, width), lambda i, idx: (0, 0, 0))),
-             ((2, ns, width), F32, pl.BlockSpec((2, ns, width), lambda i, idx: (0, 0, 0))),
-             ((2, hid, width), F32, None)], [], 6, 0, 0,
+        whole = pl.BlockSpec((2, ns, width), lambda i, idx: (0, 0, 0))
+        grad_in, grad_out_weight, grad_glu, *vectors = call(
+            partial(finish, hid, ns, plane), 1,
+            [(idx, None), (own, None), (got, None)] + logs,
+            [((2, ns, width), F32, whole), ((2, ns, width), F32, whole), ((2, hid, width), F32, None)] + shared,
+            [], 8, 0, 0,
         )
     else:
-        total = jnp.stack([flip(stack, place), flip(got, place)])
-        total = flip(total, core).astype(F32)
+        vec = vec + vector_sum(got[plane * n :])
+        vectors = call(partial(small_outputs, hid, ns), 1, [(idx, None), (vec, None)] + logs, shared, [], 2, 0, 0)
+        pieces = [flip(v[: plane * n].reshape(plane, n, width), place) for v in (own, got)]
+        total = flip(jnp.stack(pieces), core).astype(F32)
         nh, nr = hid // plane, ns // plane
 
         def part(start, size):
@@ -886,6 +886,7 @@
 
         grad_glu, grad_out, grad_in = part(0, nh), part(nh, nr), part(nh + nr, nr)
         grad_out_weight = jnp.stack([grad_out[0], -grad_out[1]])
+    grad_ln_gain, grad_ln_bias, grad_skip, grad_nu, grad_theta, grad_gamma, grad_glu_bias = vectors
     return (
         y.reshape(block_input.shape),
         gx.reshape(block_input.shape),

time: 112 us -> 108 us (0.964)
  Pallas kernels: 49 us -> 45.2 us
    ppermute x5 -> x4, waiting for transfers between devices: 2.57 us -> 6.47 us  [over_core(): return lax.ppermute(v, 'dp', xor_pairs(dp, 1))]
    pallas_call x15 -> x13, Pallas kernels: 49 us -> 45.2 us  [call(): pl.pallas_call(kernel, grid_spec=pltpu.PrefetchScalarGridSpec(num_scalar_...]
    ppermute x6, waiting for transfers between devices: 9.79 us -> 6.4 us  [over_plane(): return lax.ppermute(v, 'dp', xor_pairs(dp, 2 * s))]
  transfers between devices with their start and end apart: 26 -> 25, of which waited for: 11 -> 11; matrix products, arithmetic and copies ran while one was open for 1% -> 1% of each run, Pallas kernels for 26% -> 23%
where the time goes in v5:
time: 108 us; the launch traced here: 107 us
  Pallas kernels  45.2 us (42%)
  starting transfers between devices  32.8 us (30%)
  waiting for transfers between devices  23 us (21%)
  local copies, waits for them, and re-layouts  3.44 us (3%)
  other arithmetic  1.99 us (2%)
    pallas_call x13, Pallas kernels, call(): pl.pallas_call(kernel, grid_spec=pltpu.PrefetchScalarGridSpec(num_scalar_...  45.2 us
    ppermute x15, starting transfers between devices, over_mp(): return lax.ppermute(v, 'mp', xor_pairs(mp, s))  25.4 us
    ppermute x15, waiting for transfers between devices, over_mp(): return lax.ppermute(v, 'mp', xor_pairs(mp, s))  10.1 us
    ppermute x6, starting transfers between devices, over_plane(): return lax.ppermute(v, 'dp', xor_pairs(dp, 2 * s))  7.11 us
    ppermute x4, waiting for transfers between devices, over_core(): return lax.ppermute(v, 'dp', xor_pairs(dp, 1))  6.47 us
    ppermute x6, waiting for transfers between devices, over_plane(): return lax.ppermute(v, 'dp', xor_pairs(dp, 2 * s))  6.4 us
  transfers between devices with their start and end apart: 25, of which 11 were waited for; matrix products, arithmetic and copies ran while one was open for 1% of the time, Pallas kernels for 23%

profile of v5, /device:TPU:0, one launch (start us, length us, event | category | flops | bytes accessed | tf_op | source)
XLA Modules:
  0.0 107.5 jit_solution(15313388632409171994)
XLA Ops:
  3.4 5.1 %collective-permute-start.2 = (bf16[80,512]{1,0:T(8,128)(2,1)S(1)}, bf16[80,512]{1,0:T(8,128)(2,1)S(1)}, u32[]{:S(2)}, u32[]{:S(2)}) collective-permute-start(bf16[80,512]{1,0:T(8,128)(2,1)S(1)} %pad_maximum_fusion.4.refs_0_), channel_id=1, source_target_pairs={{0,3},{1,2},{2,1},{3,0},{4,7},{5,6},{6,5},{7,4},{8,11},{9,10},{10,... | collective-permute-start | bytes 245768 | tf_op jit(solution)/shard_map/gather_in/ppermute | solution.py:703
  10.5 4.7 %shard_map.211 = (f32[2048,512]{1,0:T(8,128)S(1)}, bf16[2048,512]{1,0:T(8,128)(2,1)S(1)}, f32[2048,128]{1,0:T(8,128)S(1)}) custom-call(s32[3]{0:T(128)S(1)} %pad_add_fusion.idx, f32[16,128,512]{2,1,0:T(8,128)} %bitcast.63, f32[1,512]{1,0:T(1,128)} %bitcast.54, f32[1,512]{1,0:T(1,128)} %bitcast.57), custom_call_target="tpu_custom_call" | custom-call | flops 1073741824 | bytes 12582912 | tf_op jit(solution)/shard_map/pallas_call | solution.py:618
  16.0 3.7 %collective-permute-start.6 = (bf16[192,512]{1,0:T(8,128)(2,1)S(1)}, bf16[192,512]{1,0:T(8,128)(2,1)S(1)}, u32[]{:S(2)}, u32[]{:S(2)}) collective-permute-start(bf16[192,512]{1,0:T(8,128)(2,1)S(1)} %pad_maximum_fusion.refs_0_), channel_id=1, source_target_pairs={{0,3},{1,2},{2,1},{3,0},{4,7},{5,6},{6,5},{7,4},{8,11},{9,10},{10,... | collective-permute-start | bytes 589832 | tf_op jit(solution)/shard_map/gather_out_glu/ppermute | solution.py:703
  20.5 3.8 %shard_map.213.cotlow_ref = bf16[2048,512]{1,0:T(8,128)(2,1)S(1)} custom-call(s32[3]{0:T(128)S(1)} %pad_add_fusion.idx, f32[16,128,512]{2,1,0:T(8,128)} %bitcast.51), custom_call_target="tpu_custom_call" | custom-call | bytes 8388608 | tf_op jit(solution)/shard_map/pallas_call | solution.py:618
  24.4 2.0 %shard_map.214 = (f32[2048,512]{1,0:T(8,128)S(1)}, bf16[512,512]{1,0:T(8,128)(2,1)S(1)}, f32[12,512]{1,0:T(8,128)S(1)}, f32[16,512]{1,0:T(8,128)S(1)}, f32[8,512]{1,0:T(8,128)S(1)}) custom-call(s32[3]{0:T(128)S(1)} %pad_add_fusion.idx, bf16[2048,512]{1,0:T(8,128)(2,1)S(1)} %get-tuple-element.97.norm_ref, bf16[4,80,512]{2,1,0:T(8,128)(2,1)S(1)} %shard_map.212.own_ref, ...), custom_call_target="tpu_custom_call" | custom-call | flops 1073741824 | bytes 8388608 | tf_op jit(solution)/shard_map/pallas_call | solution.py:618
  26.4 3.7 %collective-permute-start.9 = (f32[8,512]{1,0:T(8,128)S(1)}, f32[8,512]{1,0:T(8,128)S(1)}, u32[]{:S(2)}, u32[]{:S(2)}) collective-permute-start(f32[8,512]{1,0:T(8,128)S(1)} %get-tuple-element.102), channel_id=1, source_target_pairs={{0,3},{1,2},{2,1},{3,0},{4,7},{5,6},{6,5},{7,4},{8,11},{9,10},{10,... | collective-permute-start | bytes 49160 | tf_op jit(solution)/shard_map/carry/ppermute | solution.py:703
  30.1 3.4 %collective-permute-start.7 = (f32[8,512]{1,0:T(8,128)S(1)}, f32[8,512]{1,0:T(8,128)S(1)}, u32[]{:S(2)}, u32[]{:S(2)}) collective-permute-start(f32[8,512]{1,0:T(8,128)S(1)} %get-tuple-element.102), channel_id=1, source_target_pairs={{0,1},{1,0},{2,3},{3,2},{4,5},{5,4},{6,7},{7,6},{8,9},{9,8},{10,11... | collective-permute-start | bytes 49160 | tf_op jit(solution)/shard_map/carry/ppermute | solution.py:703
  33.5 4.3 %collective-permute-done.5.refs_2_ = bf16[192,512]{1,0:T(8,128)(2,1)S(1)} collective-permute-done((bf16[192,512]{1,0:T(8,128)(2,1)S(1)}, bf16[192,512]{1,0:T(8,128)(2,1)S(1)}, u32[]{:S(2)}, u32[]{:S(2)}) %collective-permute-start.5) | collective-permute-done | bytes 196640 | tf_op jit(solution)/shard_map/gather_out_glu/ppermute | solution.py:703
  38.8 2.3 %collective-permute-done.10.other_ref = bf16[4,192,512]{2,1,0:T(8,128)(2,1)S(1)} collective-permute-done((bf16[4,192,512]{2,1,0:T(8,128)(2,1)S(1)}, bf16[4,192,512]{2,1,0:T(8,128)(2,1)S(1)}, u32[]{:S(2)}, u32[]{:S(2)}) %collective-permute-start.10) | collective-permute-done | bytes 786464 | tf_op jit(solution)/shard_map/ppermute | solution.py:697
  41.1 4.1 %shard_map.216 = (bf16[2048,512]{1,0:T(8,128)(2,1)S(1)}, bf16[2048,512]{1,0:T(8,128)(2,1)S(1)}, f32[2048,512]{1,0:T(8,128)S(1)}, bf16[512,512]{1,0:T(8,128)(2,1)S(1)}) custom-call(s32[3]{0:T(128)S(1)} %pad_add_fusion.idx, f32[2048,512]{1,0:T(8,128)S(1)} %get-tuple-element.96.xhat_ref, f32[2048,512]{1,0:T(8,128)S(1)} %get-tuple-element.98.src_ref, ...), custom_call_target="tpu_custom_call" | custom-call | flops 1073741824 | bytes 8388608 | tf_op jit(solution)/shard_map/pallas_call | solution.py:618
  45.2 4.7 %shard_map.217 = (bf16[2048,512]{1,0:T(8,128)(2,1)S(1)}, bf16[2048,1024]{1,0:T(8,128)(2,1)S(1)}, bf16[1024,512]{1,0:T(8,128)(2,1)S(1)}, f32[8,512]{1,0:T(8,128)S(1)}) custom-call(s32[3]{0:T(128)S(1)} %pad_add_fusion.idx, bf16[2048,512]{1,0:T(8,128)(2,1)S(1)} %shard_map.213.cotlow_ref, bf16[2048,512]{1,0:T(8,128)(2,1)S(1)} %get-tuple-element.107.act_ref, ...), custom_call_target="tpu_custom_call" | custom-call | flops 2147483648 | bytes 8388608 | tf_op jit(solution)/shard_map/pallas_call | solution.py:618
  49.9 4.4 %shard_map.218 = (bf16[2048,512]{1,0:T(8,128)(2,1)S(1)}, f32[2048,512]{1,0:T(8,128)S(1)}, f32[16,512]{1,0:T(8,128)S(1)}, f32[8,512]{1,0:T(8,128)S(1)}, f32[8,512]{1,0:T(8,128)S(1)}) custom-call(s32[3]{0:T(128)S(1)} %pad_add_fusion.idx, bf16[2048,1024]{1,0:T(8,128)(2,1)S(1)} %get-tuple-element.113.gpre_ref, f32[2048,512]{1,0:T(8,128)S(1)} %get-tuple-element.109.slope_ref, ...), custom_call_target="tpu_custom_call" | custom-call | flops 4294967296 | bytes 8388608 | tf_op jit(solution)/shard_map/pallas_call | solution.py:618
  55.0 2.4 %collective-permute-start.13 = (f32[8,512]{1,0:T(8,128)S(1)}, f32[8,512]{1,0:T(8,128)S(1)}, u32[]{:S(2)}, u32[]{:S(2)}) collective-permute-start(f32[8,512]{1,0:T(8,128)S(1)} %get-tuple-element.112), channel_id=1, source_target_pairs={{0,3},{1,2},{2,1},{3,0},{4,7},{5,6},{6,5},{7,4},{8,11},{9,10},{10,... | collective-permute-start | bytes 49160 | tf_op jit(solution)/shard_map/carry_back/ppermute | solution.py:703
  58.1 5.1 %shard_map.219 = (f32[1024,512]{1,0:T(8,128)S(1)}, bf16[1024,512]{1,0:T(8,128)(2,1)S(1)}) custom-call(s32[3]{0:T(128)S(1)} %pad_add_fusion.idx, bf16[2048,1024]{1,0:T(8,128)(2,1)S(1)} %get-tuple-element.113.gpre_ref, bf16[2048,512]{1,0:T(8,128)(2,1)S(1)} %get-tuple-element.107.act_ref, bf16[2048,512]{1,0:T(8,128)(2,1)S(1)} %get-tuple-element.114.state_ref, ...), custom_call_target="tpu_custom_call" | custom-call | tf_op jit(solution)/shard_map/pallas_call | solution.py:618
  63.2 3.6 %shard_map.220 = (bf16[2048,512]{1,0:T(8,128)(2,1)S(1)}, f32[1024,512]{1,0:T(8,128)S(1)}, bf16[1024,512]{1,0:T(8,128)(2,1)S(1)}, f32[8,512]{1,0:T(8,128)S(1)}) custom-call(s32[3]{0:T(128)S(1)} %pad_add_fusion.idx, f32[1024,512]{1,0:T(8,128)S(1)} %get-tuple-element.116.keep_in, ...), custom_call_target="tpu_custom_call", output_to_operand_aliasing={{1}: (1, {}), {2}: (2, {})} | custom-call | flops 1073741824 | bytes 8388608 | tf_op jit(solution)/shard_map/pallas_call | solution.py:618
  66.9 2.6 %collective-permute-done.14.got_ref = bf16[1024,512]{1,0:T(8,128)(2,1)S(1)} collective-permute-done((bf16[1024,512]{1,0:T(8,128)(2,1)S(1)}, bf16[1024,512]{1,0:T(8,128)(2,1)S(1)}, u32[]{:S(2)}, u32[]{:S(2)}) %collective-permute-start.14) | collective-permute-done | bytes 1048608 | tf_op jit(solution)/shard_map/sum_core/ppermute | solution.py:697
  70.3 1.6 %collective-permute-start.15 = (bf16[256,512]{1,0:T(8,128)(2,1)S(1)}, bf16[256,512]{1,0:T(8,128)(2,1)S(1)}, u32[]{:S(2)}, u32[]{:S(2)}) collective-permute-start(bf16[256,512]{1,0:T(8,128)(2,1)S(1)} %get-tuple-element.134), channel_id=1, source_target_pairs={{0,8},{4,12},{8,0},{12,4},{16,24},{20,28},{24,16},{28,20},{1,9},{5... | collective-permute-start | bytes 786440 | tf_op jit(solution)/shard_map/sum_plane/ppermute | solution.py:700
  71.8 1.5 %collective-permute-start.16 = (bf16[256,512]{1,0:T(8,128)(2,1)S(1)}, bf16[256,512]{1,0:T(8,128)(2,1)S(1)}, u32[]{:S(2)}, u32[]{:S(2)}) collective-permute-start(bf16[256,512]{1,0:T(8,128)(2,1)S(1)} %get-tuple-element.138), channel_id=1, source_target_pairs={{0,16},{4,20},{8,24},{12,28},{16,0},{20,4},{24,8},{28,12},{1,17},{... | collective-permute-start | bytes 786440 | tf_op jit(solution)/shard_map/sum_plane/ppermute | solution.py:700
  73.9 9.4 %shard_map.222 = (f32[16,128,512]{2,1,0:T(8,128)}, f32[16,128,512]{2,1,0:T(8,128)}, f32[8,512]{1,0:T(8,128)S(1)}, bf16[16,512]{1,0:T(8,128)(2,1)S(1)}) custom-call(s32[3]{0:T(128)S(1)} %pad_add_fusion.idx, f32[16,128,512]{2,1,0:T(8,128)S(1)} %bitcast.52, bf16[2048,512]{1,0:T(8,128)(2,1)S(1)} %get-tuple-element.125.gdrive_ref, ...), custom_call_target="tpu_custom_call" | custom-call | flops 1073741824 | bytes 8388608 | tf_op jit(solution)/shard_map/pallas_call | solution.py:618
  83.3 2.2 %collective-permute-done.16 = bf16[256,512]{1,0:T(8,128)(2,1)S(1)} collective-permute-done((bf16[256,512]{1,0:T(8,128)(2,1)S(1)}, bf16[256,512]{1,0:T(8,128)(2,1)S(1)}, u32[]{:S(2)}, u32[]{:S(2)}) %collective-permute-start.16) | collective-permute-done | bytes 262176 | tf_op jit(solution)/shard_map/sum_plane/ppermute | solution.py:700
  87.1 1.6 %collective-permute-start.19 = (bf16[80,512]{1,0:T(8,128)(2,1)S(1)}, bf16[80,512]{1,0:T(8,128)(2,1)S(1)}, u32[]{:S(2)}, u32[]{:S(2)}) collective-permute-start(bf16[80,512]{1,0:T(8,128)(2,1)S(1)} %get-tuple-element.176), channel_id=1, source_target_pairs={{0,2},{1,3},{2,0},{3,1},{4,6},{5,7},{6,4},{7,5},{8,10},{9,11},{10,... | collective-permute-start | bytes 245768 | tf_op jit(solution)/shard_map/sum_mp/ppermute | solution.py:703
  91.0 4.6 %collective-permute-done.19 = bf16[80,512]{1,0:T(8,128)(2,1)S(1)} collective-permute-done((bf16[80,512]{1,0:T(8,128)(2,1)S(1)}, bf16[80,512]{1,0:T(8,128)(2,1)S(1)}, u32[]{:S(2)}, u32[]{:S(2)}) %collective-permute-start.19) | collective-permute-done | bytes 81952 | tf_op jit(solution)/shard_map/sum_mp/ppermute | solution.py:703
  100.2 3.2 %collective-permute-done.22 = bf16[80,512]{1,0:T(8,128)(2,1)S(1)} collective-permute-done((bf16[80,512]{1,0:T(8,128)(2,1)S(1)}, bf16[80,512]{1,0:T(8,128)(2,1)S(1)}, u32[]{:S(2)}, u32[]{:S(2)}) %collective-permute-start.22) | collective-permute-done | bytes 81952 | tf_op jit(solution)/shard_map/spread_plane/ppermute | solution.py:700
  103.5 1.5 %collective-permute-done.24.got_ref = bf16[272,512]{1,0:T(8,128)(2,1)S(1)} collective-permute-done((bf16[272,512]{1,0:T(8,128)(2,1)S(1)}, bf16[272,512]{1,0:T(8,128)(2,1)S(1)}, u32[]{:S(2)}, u32[]{:S(2)}) %collective-permute-start.24) | collective-permute-done | bytes 278560 | tf_op jit(solution)/shard_map/spread_core/ppermute | solution.py:697
  (86 shorter events, 20.8 us)
Async XLA Ops:
  3.4 11.8 %collective-permute-start.2 = (bf16[80,512]{1,0:T(8,128)(2,1)S(1)}, bf16[80,512]{1,0:T(8,128)(2,1)S(1)}, u32[]{:S(2)}, u32[]{:S(2)}) collective-permute-start(bf16[80,512]{1,0:T(8,128)(2,1)S(1)} %pad_maximum_fusion.4.refs_0_), channel_id=1, source_target_pairs={{0,3},{1,2},{2,1},{3,0},{4,7},{5,6},{6,5},{7,4},{8,11},{9,10},{10,... | collective-permute-start | bytes 245768 | tf_op jit(solution)/shard_map/gather_in/ppermute | solution.py:703
  8.5 6.9 %collective-permute-start.1 = (bf16[80,512]{1,0:T(8,128)(2,1)S(1)}, bf16[80,512]{1,0:T(8,128)(2,1)S(1)}, u32[]{:S(2)}, u32[]{:S(2)}) collective-permute-start(bf16[80,512]{1,0:T(8,128)(2,1)S(1)} %pad_maximum_fusion.4.refs_0_), channel_id=1, source_target_pairs={{0,2},{1,3},{2,0},{3,1},{4,6},{5,7},{6,4},{7,5},{8,10},{9,11},{10,... | collective-permute-start | bytes 245768 | tf_op jit(solution)/shard_map/gather_in/ppermute | solution.py:703
  8.5 6.9 %collective-permute-start = (bf16[80,512]{1,0:T(8,128)(2,1)S(1)}, bf16[80,512]{1,0:T(8,128)(2,1)S(1)}, u32[]{:S(2)}, u32[]{:S(2)}) collective-permute-start(bf16[80,512]{1,0:T(8,128)(2,1)S(1)} %pad_maximum_fusion.4.refs_0_), channel_id=1, source_target_pairs={{0,1},{1,0},{2,3},{3,2},{4,5},{5,4},{6,7},{7,6},{8,9},{9,8},{10,11... | collective-permute-start | bytes 245768 | tf_op jit(solution)/shard_map/gather_in/ppermute | solution.py:703
  16.0 8.4 %collective-permute-start.3 = (bf16[4,80,512]{2,1,0:T(8,128)(2,1)S(1)}, bf16[4,80,512]{2,1,0:T(8,128)(2,1)S(1)}, u32[]{:S(2)}, u32[]{:S(2)}) collective-permute-start(bf16[4,80,512]{2,1,0:T(8,128)(2,1)S(1)} %shard_map.212.own_ref), channel_id=1, source_target_pairs={{0,4},{4,0},{8,12},{12,8},{16,20},{20,16},{24,28},{28,24},{1,5},{5... | collective-permute-start | bytes 983048 | tf_op jit(solution)/shard_map/ppermute | solution.py:697
  16.0 14.1 %collective-permute-start.6 = (bf16[192,512]{1,0:T(8,128)(2,1)S(1)}, bf16[192,512]{1,0:T(8,128)(2,1)S(1)}, u32[]{:S(2)}, u32[]{:S(2)}) collective-permute-start(bf16[192,512]{1,0:T(8,128)(2,1)S(1)} %pad_maximum_fusion.refs_0_), channel_id=1, source_target_pairs={{0,3},{1,2},{2,1},{3,0},{4,7},{5,6},{6,5},{7,4},{8,11},{9,10},{10,... | collective-permute-start | bytes 589832 | tf_op jit(solution)/shard_map/gather_out_glu/ppermute | solution.py:703
  19.7 18.0 %collective-permute-start.5 = (bf16[192,512]{1,0:T(8,128)(2,1)S(1)}, bf16[192,512]{1,0:T(8,128)(2,1)S(1)}, u32[]{:S(2)}, u32[]{:S(2)}) collective-permute-start(bf16[192,512]{1,0:T(8,128)(2,1)S(1)} %pad_maximum_fusion.refs_0_), channel_id=1, source_target_pairs={{0,2},{1,3},{2,0},{3,1},{4,6},{5,7},{6,4},{7,5},{8,10},{9,11},{10,... | collective-permute-start | bytes 589832 | tf_op jit(solution)/shard_map/gather_out_glu/ppermute | solution.py:703
  19.7 18.0 %collective-permute-start.4 = (bf16[192,512]{1,0:T(8,128)(2,1)S(1)}, bf16[192,512]{1,0:T(8,128)(2,1)S(1)}, u32[]{:S(2)}, u32[]{:S(2)}) collective-permute-start(bf16[192,512]{1,0:T(8,128)(2,1)S(1)} %pad_maximum_fusion.refs_0_), channel_id=1, source_target_pairs={{0,1},{1,0},{2,3},{3,2},{4,5},{5,4},{6,7},{7,6},{8,9},{9,8},{10,11... | collective-permute-start | bytes 589832 | tf_op jit(solution)/shard_map/gather_out_glu/ppermute | solution.py:703
  26.4 11.3 %collective-permute-start.9 = (f32[8,512]{1,0:T(8,128)S(1)}, f32[8,512]{1,0:T(8,128)S(1)}, u32[]{:S(2)}, u32[]{:S(2)}) collective-permute-start(f32[8,512]{1,0:T(8,128)S(1)} %get-tuple-element.102), channel_id=1, source_target_pairs={{0,3},{1,2},{2,1},{3,0},{4,7},{5,6},{6,5},{7,4},{8,11},{9,10},{10,... | collective-permute-start | bytes 49160 | tf_op jit(solution)/shard_map/carry/ppermute | solution.py:703
  30.1 8.0 %collective-permute-start.8 = (f32[8,512]{1,0:T(8,128)S(1)}, f32[8,512]{1,0:T(8,128)S(1)}, u32[]{:S(2)}, u32[]{:S(2)}) collective-permute-start(f32[8,512]{1,0:T(8,128)S(1)} %get-tuple-element.102), channel_id=1, source_target_pairs={{0,2},{1,3},{2,0},{3,1},{4,6},{5,7},{6,4},{7,5},{8,10},{9,11},{10,... | collective-permute-start | bytes 49160 | tf_op jit(solution)/shard_map/carry/ppermute | solution.py:703
  30.1 8.0 %collective-permute-start.7 = (f32[8,512]{1,0:T(8,128)S(1)}, f32[8,512]{1,0:T(8,128)S(1)}, u32[]{:S(2)}, u32[]{:S(2)}) collective-permute-start(f32[8,512]{1,0:T(8,128)S(1)} %get-tuple-element.102), channel_id=1, source_target_pairs={{0,1},{1,0},{2,3},{3,2},{4,5},{5,4},{6,7},{7,6},{8,9},{9,8},{10,11... | collective-permute-start | bytes 49160 | tf_op jit(solution)/shard_map/carry/ppermute | solution.py:703
  38.7 2.4 %collective-permute-start.10 = (bf16[4,192,512]{2,1,0:T(8,128)(2,1)S(1)}, bf16[4,192,512]{2,1,0:T(8,128)(2,1)S(1)}, u32[]{:S(2)}, u32[]{:S(2)}) collective-permute-start(bf16[4,192,512]{2,1,0:T(8,128)(2,1)S(1)} %shard_map.215.own_ref), channel_id=1, source_target_pairs={{0,4},{4,0},{8,12},{12,8},{16,20},{20,16},{24,28},{28,24},{1,5},{5... | collective-permute-start | bytes 2359304 | tf_op jit(solution)/shard_map/ppermute | solution.py:697
  54.4 8.8 %collective-permute-start.11 = (f32[8,512]{1,0:T(8,128)S(1)}, f32[8,512]{1,0:T(8,128)S(1)}, u32[]{:S(2)}, u32[]{:S(2)}) collective-permute-start(f32[8,512]{1,0:T(8,128)S(1)} %get-tuple-element.112), channel_id=1, source_target_pairs={{0,1},{1,0},{2,3},{3,2},{4,5},{5,4},{6,7},{7,6},{8,9},{9,8},{10,11... | collective-permute-start | bytes 49160 | tf_op jit(solution)/shard_map/carry_back/ppermute | solution.py:703
  55.0 8.2 %collective-permute-start.13 = (f32[8,512]{1,0:T(8,128)S(1)}, f32[8,512]{1,0:T(8,128)S(1)}, u32[]{:S(2)}, u32[]{:S(2)}) collective-permute-start(f32[8,512]{1,0:T(8,128)S(1)} %get-tuple-element.112), channel_id=1, source_target_pairs={{0,3},{1,2},{2,1},{3,0},{4,7},{5,6},{6,5},{7,4},{8,11},{9,10},{10,... | collective-permute-start | bytes 49160 | tf_op jit(solution)/shard_map/carry_back/ppermute | solution.py:703
  57.4 5.8 %collective-permute-start.12 = (f32[8,512]{1,0:T(8,128)S(1)}, f32[8,512]{1,0:T(8,128)S(1)}, u32[]{:S(2)}, u32[]{:S(2)}) collective-permute-start(f32[8,512]{1,0:T(8,128)S(1)} %get-tuple-element.112), channel_id=1, source_target_pairs={{0,2},{1,3},{2,0},{3,1},{4,6},{5,7},{6,4},{7,5},{8,10},{9,11},{10,... | collective-permute-start | bytes 49160 | tf_op jit(solution)/shard_map/carry_back/ppermute | solution.py:703
  66.8 2.7 %collective-permute-start.14 = (bf16[1024,512]{1,0:T(8,128)(2,1)S(1)}, bf16[1024,512]{1,0:T(8,128)(2,1)S(1)}, u32[]{:S(2)}, u32[]{:S(2)}) collective-permute-start(bf16[1024,512]{1,0:T(8,128)(2,1)S(1)} %get-tuple-element.123), channel_id=1, source_target_pairs={{0,4},{4,0},{8,12},{12,8},{16,20},{20,16},{24,28},{28,24},{1,5},{5... | collective-permute-start | bytes 3145736 | tf_op jit(solution)/shard_map/sum_core/ppermute | solution.py:697
  70.3 13.0 %collective-permute-start.15 = (bf16[256,512]{1,0:T(8,128)(2,1)S(1)}, bf16[256,512]{1,0:T(8,128)(2,1)S(1)}, u32[]{:S(2)}, u32[]{:S(2)}) collective-permute-start(bf16[256,512]{1,0:T(8,128)(2,1)S(1)} %get-tuple-element.134), channel_id=1, source_target_pairs={{0,8},{4,12},{8,0},{12,4},{16,24},{20,28},{24,16},{28,20},{1,9},{5... | collective-permute-start | bytes 786440 | tf_op jit(solution)/shard_map/sum_plane/ppermute | solution.py:700
  71.8 13.7 %collective-permute-start.16 = (bf16[256,512]{1,0:T(8,128)(2,1)S(1)}, bf16[256,512]{1,0:T(8,128)(2,1)S(1)}, u32[]{:S(2)}, u32[]{:S(2)}) collective-permute-start(bf16[256,512]{1,0:T(8,128)(2,1)S(1)} %get-tuple-element.138), channel_id=1, source_target_pairs={{0,16},{4,20},{8,24},{12,28},{16,0},{20,4},{24,8},{28,12},{1,17},{... | collective-permute-start | bytes 786440 | tf_op jit(solution)/shard_map/sum_plane/ppermute | solution.py:700
  73.4 12.2 %collective-permute-start.17 = (bf16[256,512]{1,0:T(8,128)(2,1)S(1)}, bf16[256,512]{1,0:T(8,128)(2,1)S(1)}, u32[]{:S(2)}, u32[]{:S(2)}) collective-permute-start(bf16[256,512]{1,0:T(8,128)(2,1)S(1)} %get-tuple-element.139), channel_id=1, source_target_pairs={{0,24},{4,28},{8,16},{12,20},{16,8},{20,12},{24,0},{28,4},{1,25},{... | collective-permute-start | bytes 786440 | tf_op jit(solution)/shard_map/sum_plane/ppermute | solution.py:700
  85.8 5.2 %collective-permute-start.18 = (bf16[80,512]{1,0:T(8,128)(2,1)S(1)}, bf16[80,512]{1,0:T(8,128)(2,1)S(1)}, u32[]{:S(2)}, u32[]{:S(2)}) collective-permute-start(bf16[80,512]{1,0:T(8,128)(2,1)S(1)} %get-tuple-element.175), channel_id=1, source_target_pairs={{0,1},{1,0},{2,3},{3,2},{4,5},{5,4},{6,7},{7,6},{8,9},{9,8},{10,11... | collective-permute-start | bytes 245768 | tf_op jit(solution)/shard_map/sum_mp/ppermute | solution.py:703
  87.1 8.4 %collective-permute-start.19 = (bf16[80,512]{1,0:T(8,128)(2,1)S(1)}, bf16[80,512]{1,0:T(8,128)(2,1)S(1)}, u32[]{:S(2)}, u32[]{:S(2)}) collective-permute-start(bf16[80,512]{1,0:T(8,128)(2,1)S(1)} %get-tuple-element.176), channel_id=1, source_target_pairs={{0,2},{1,3},{2,0},{3,1},{4,6},{5,7},{6,4},{7,5},{8,10},{9,11},{10,... | collective-permute-start | bytes 245768 | tf_op jit(solution)/shard_map/sum_mp/ppermute | solution.py:703
  88.8 6.8 %collective-permute-start.20 = (bf16[80,512]{1,0:T(8,128)(2,1)S(1)}, bf16[80,512]{1,0:T(8,128)(2,1)S(1)}, u32[]{:S(2)}, u32[]{:S(2)}) collective-permute-start(bf16[80,512]{1,0:T(8,128)(2,1)S(1)} %get-tuple-element.177), channel_id=1, source_target_pairs={{0,3},{1,2},{2,1},{3,0},{4,7},{5,6},{6,5},{7,4},{8,11},{9,10},{10,... | collective-permute-start | bytes 245768 | tf_op jit(solution)/shard_map/sum_mp/ppermute | solution.py:703
  95.7 4.5 %collective-permute-start.21 = (bf16[80,512]{1,0:T(8,128)(2,1)S(1)}, bf16[80,512]{1,0:T(8,128)(2,1)S(1)}, u32[]{:S(2)}, u32[]{:S(2)}) collective-permute-start(bf16[80,512]{1,0:T(8,128)(2,1)S(1)} %pad_maximum_fusion.5), channel_id=1, source_target_pairs={{0,8},{4,12},{8,0},{12,4},{16,24},{20,28},{24,16},{28,20},{1,9},{5... | collective-permute-start | bytes 245768 | tf_op jit(solution)/shard_map/spread_plane/ppermute | solution.py:700
  97.2 6.2 %collective-permute-start.23 = (bf16[80,512]{1,0:T(8,128)(2,1)S(1)}, bf16[80,512]{1,0:T(8,128)(2,1)S(1)}, u32[]{:S(2)}, u32[]{:S(2)}) collective-permute-start(bf16[80,512]{1,0:T(8,128)(2,1)S(1)} %pad_maximum_fusion.5), channel_id=1, source_target_pairs={{0,24},{4,28},{8,16},{12,20},{16,8},{20,12},{24,0},{28,4},{1,25},{... | collective-permute-start | bytes 245768 | tf_op jit(solution)/shard_map/spread_plane/ppermute | solution.py:700
  98.6 4.8 %collective-permute-start.22 = (bf16[80,512]{1,0:T(8,128)(2,1)S(1)}, bf16[80,512]{1,0:T(8,128)(2,1)S(1)}, u32[]{:S(2)}, u32[]{:S(2)}) collective-permute-start(bf16[80,512]{1,0:T(8,128)(2,1)S(1)} %pad_maximum_fusion.5), channel_id=1, source_target_pairs={{0,16},{4,20},{8,24},{12,28},{16,0},{20,4},{24,8},{28,12},{1,17},{... | collective-permute-start | bytes 245768 | tf_op jit(solution)/shard_map/spread_plane/ppermute | solution.py:700
  (9 other events, 167.8 us)

commit v6 on v5

--- a/solution.py
+++ b/solution.py
@@ -134,7 +134,7 @@
 
 
 def first_scan(
-    chunk, mp, idx, norm_ref, own_ref, other_ref,
+    chunk, mp, idx, norm_ref, own_ref, other_ref, glu_bias_ref,
     src_ref, wt_ref, par_ref, ends_ref, last_ref, h_ref, drive_a, drive_b,
 ):
     step = 0
@@ -157,8 +157,7 @@
     par_ref[0:1, :] = jnp.concatenate([re, im], 1)
     par_ref[1:2, :] = gamma
     par_ref[2:3, :] = jnp.concatenate([lre, lim], 1)
-    par_ref[3:5, :] = total[6:8]
-    par_ref[5:8, :] = jnp.zeros((3, width), F32)
+    par_ref[3:8, :] = jnp.zeros((5, width), F32)
     pre, pim = jnp.ones_like(tre), jnp.zeros_like(tim)
     for s in range(mp):
         par_ref[8 + s : 9 + s, :] = jnp.concatenate([pre, pim], 1)
@@ -194,7 +193,12 @@
     for c in range(1, CHUNKS):
         mre, mim = cmul(pre, pim, re, im)
         re, im = mre + h_ref[c : c + 1, :states], mim + h_ref[c : c + 1, states:]
-    last_ref[...] = jnp.broadcast_to(jnp.concatenate([re, im], 1), last_ref.shape)
+    last_ref[...] = jnp.zeros_like(last_ref)
+    last_ref[0:1, :] = jnp.concatenate([re, im], 1)
+    hid = glu_bias_ref.shape[1]
+    biases = glu_bias_ref[...].astype(F32)
+    for j in range(mp):
+        last_ref[1:3, j * hid : (j + 1) * hid] = jnp.where(me == j, biases, 0.0)
 
 
 def gelu_parts(v):
@@ -204,14 +208,18 @@
 
 
 def readout(mp, idx, xhat_ref, src_ref, par_ref, ends_ref, gain_ref, bias_ref, skip_ref, own_ref, other_ref, *rest):
-    others = rest[: mp - 1]
-    (state_ref, act_ref, slope_ref, wc_ref, h_ref, low_a, low_b, mix_a, mix_b) = rest[mp - 1 :]
+    others, mine = rest[: mp - 1], rest[mp - 1]
+    (state_ref, act_ref, slope_ref, wc_ref, rows_ref, h_ref, low_a, low_b, mix_a, mix_b) = rest[mp:]
     step = 0
     width = xhat_ref.shape[1]
     states = width // 2
     me, core = idx[0], idx[1]
 
     assemble(wc_ref, own_ref, other_ref, 0, states // mp, me, core, mp, True)
+    total = mine[...]
+    for other in others:
+        total = total + other[...]
+    rows_ref[...] = total
     re = jnp.zeros((1, states), F32)
     im = jnp.zeros((1, states), F32)
     for s in range(1, mp):
@@ -272,7 +280,7 @@
     run(gelus(blocks - 1, mix_refs[(blocks - 1) % 2]))
 
 
-def gating(mp, idx, cotlow_ref, act_ref, par_ref, own_ref, other_ref,
+def gating(mp, idx, cotlow_ref, act_ref, rows_ref, own_ref, other_ref,
            br_ref, gpre_ref, wg_ref, vec_ref, pre_a, pre_b):
     width = act_ref.shape[1]
     core = idx[1]
@@ -292,8 +300,8 @@
         gate_cols = slice(width + c, width + c + 128)
         for r in range(start, start + 64, 16):
             rows = slice(b * BLOCK + r, b * BLOCK + r + 16)
-            value = pre[r : r + 16, cols] + par_ref[3:4, cols]
-            gate = pre[r : r + 16, gate_cols] + par_ref[4:5, cols]
+            value = pre[r : r + 16, cols] + rows_ref[1:2, cols]
+            gate = pre[r : r + 16, gate_cols] + rows_ref[2:3, cols]
             sig = 0.5 * jnp.tanh(0.5 * gate) + 0.5
             branch = value * sig
             br_ref[rows, cols] = branch.astype(BF16)
@@ -408,7 +416,7 @@
     first_ref[...] = jnp.broadcast_to(jnp.concatenate([re, im], 1), first_ref.shape)
 
 
-def adjoint_scan(mp, idx, keep_in, send_in, gs_ref, state_ref, src_ref, norm_ref, par_ref, adj_ref, *rest):
+def adjoint_scan(mp, idx, gs_ref, state_ref, src_ref, norm_ref, par_ref, adj_ref, *rest):
     others = rest[: mp - 1]
     (gdrive_ref, keep_ref, send_ref, vec_ref, acc_ref, h_ref, gdrive_a, gdrive_b) = rest[mp - 1 :]
     step = 0
@@ -466,9 +474,8 @@
     for b in range(last - 1, -1, -1):
         alternate(weight_pieces(b + 1, buffers[(b + 1) % 2]), scans(b, buffers[b % 2]))
     run(weight_pieces(0, buffers[0]))
-    first = keep_ref.shape[0] - states
-    keep_ref[first:, :] = acc_ref[pl.ds(core * states, states), :]
-    send_ref[first:, :] = acc_ref[pl.ds((1 - core) * states, states), :].astype(BF16)
+    keep_ref[...] = acc_ref[pl.ds(core * states, states), :]
+    send_ref[...] = acc_ref[pl.ds((1 - core) * states, states), :].astype(BF16)
     sre, sim, sgam = [jnp.sum(v, 0, keepdims=True) for v in sums]
     vec_ref[0:1, :] = jnp.concatenate([sre, sim], 1)
     vec_ref[1:2, :] = jnp.concatenate([sgam, jnp.zeros((1, states), F32)], 1)
@@ -544,21 +551,22 @@
         out[i] = part[...]
 
 
-def split_pieces(slots, count, sizes, idx, keep_ref, got_ref, own_ref, *sends):
+def split_pieces(slots, count, hid, ns, idx, keep_ref, got_ref, in_keep_ref, in_got_ref, own_ref, *sends):
     place = idx[2]
-    height = sum(sizes) // count
+    parts = ((keep_ref, got_ref, 0, hid), (keep_ref, got_ref, slots * hid, ns), (in_keep_ref, in_got_ref, 0, ns))
+    height = (hid + 2 * ns) // count
     for slot in range(slots):
         for s in range(count):
-            base, low = 0, slot * height
-            for size in sizes:
+            low = slot * height
+            for keep, got, base, size in parts:
                 rows = size // count
                 start = pl.multiple_of(base + slot * size + (place ^ s) * rows, rows)
-                piece = keep_ref[pl.ds(start, rows), :] + got_ref[pl.ds(start, rows), :].astype(F32)
+                piece = keep[pl.ds(start, rows), :] + got[pl.ds(start, rows), :].astype(F32)
                 if s == 0:
                     own_ref[low : low + rows, :] = piece
                 else:
                     sends[s - 1][low : low + rows, :] = piece.astype(BF16)
-                base, low = base + slots * size, low + rows
+                low += rows
 
 
 def finish(hid, ns, count, idx, own_ref, got_ref, nu_ref, theta_ref, in_ref, out_ref, glu_ref, *rest):
@@ -713,9 +721,8 @@
 
     first_rows = [placed(nu_log), placed(gamma_log)], [placed(theta_log), placed(gamma_log)]
     first_rows = jnp.concatenate([jnp.stack(v) for v in first_rows], 1)
-    bias_rows = jnp.stack([placed(glu_bias[p].astype(F32)) for p in range(2)])
-    first_rows, bias_rows = lax.optimization_barrier((first_rows, bias_rows))
-    params = jnp.concatenate(thirds(first_rows) + [bias_rows]).astype(BF16)
+    first_rows = lax.optimization_barrier(first_rows)
+    params = jnp.concatenate(thirds(first_rows)).astype(BF16)
     params = jnp.pad(params, ((0, PARAM_ROWS - params.shape[0]), (0, 0)))
 
     def gathered(value, name):
@@ -764,7 +771,7 @@
     norm = tied(norm, cotlow)
     src, wt, par, ends, last = call(
         partial(first_scan, chunk, mp), 1,
-        [(idx, None), (norm, None), (in_own, None), (in_other, None)],
+        [(idx, None), (norm, None), (in_own, None), (in_other, None), (glu_bias, None)],
         [(big, F32, None), ((width, width), BF16, None), ((npar, width), F32, None), ((CHUNKS, width), F32, None), small],
         scratch((CHUNKS, width, F32), (BLOCK, width, F32), (BLOCK, width, F32)), 5, product, 8,
     )
@@ -772,16 +779,16 @@
         lasts = [over_mp(last, s) for s in range(1, mp)]
     both_own = packed(both_own, *lasts)
     both_other = over_core(both_own)
-    state, act, slope, wc = call(
+    state, act, slope, wc, bias_rows = call(
         partial(readout, mp), 1,
         [(idx, None), (xhat, None), (src, None), (par, None), (ends, None), (gain, vector), (bias, vector), (skp, vector),
-         (both_own, None), (both_other, None)] + [(v, None) for v in lasts],
-        [(big, BF16, None), (big, BF16, None), (big, F32, None), ((width, width), BF16, None)],
+         (both_own, None), (both_other, None)] + [(v, None) for v in lasts + [last]],
+        [(big, BF16, None), (big, BF16, None), (big, F32, None), ((width, width), BF16, None), small],
         scratch((CHUNKS, width, F32), (BLOCK, width, BF16), (BLOCK, width, BF16), (BLOCK, width, F32), (BLOCK, width, F32)), 8, product, 8,
     )
     branch, gpre, wg, vec_glu = call(
         partial(gating, mp), 1,
-        [(idx, None), (cotlow, None), (act, None), (par, None), (both_own, None), (both_other, None)],
+        [(idx, None), (cotlow, None), (act, None), (bias_rows, None), (both_own, None), (both_other, None)],
         [(big, BF16, None), ((tokens, 2 * width), BF16, None), ((2 * width, width), BF16, None), small],
         scratch((BLOCK, 2 * width, F32), (BLOCK, 2 * width, F32)),
         10, 2 * product, 8,
@@ -797,34 +804,36 @@
     with jax.named_scope("carry_back"):
         firsts = [over_mp(first, s) for s in range(1, mp)]
     early_rows = mp * (hid + ns)
-    half_rows = early_rows + states
-    sums = [((half_rows, width), F32, None), ((half_rows, width), BF16, None)]
+    sums = [((early_rows, width), F32, None), ((early_rows, width), BF16, None)]
     keep, send = call(
         weight_products, 1,
         [(idx, None), (tied(gpre, first), None), (act, None), (state, None), (gmix, None)],
         sums, [], 12, 0, 0,
     )
     firsts[0] = tied(firsts[0], send)
-    gdrive, keep, send, vec_lam = call(
+    with jax.named_scope("sum_early_core"):
+        got = over_core(tied(send, *firsts))
+    gdrive, in_keep, in_send, vec_lam = call(
         partial(adjoint_scan, mp), 1,
-        [(idx, None), (keep, None), (send, None), (gs, None), (state, None), (src, None), (norm, None), (par, None),
+        [(idx, None), (gs, None), (state, None), (src, None), (norm, None), (par, None),
          (adj, None)] + [(v, None) for v in firsts],
-        [(big, BF16, None)] + sums + [small],
+        [(big, BF16, None), ((states, width), F32, None), ((states, width), BF16, None), small],
         scratch((width, width, F32), (CHUNKS, width, F32), (BLOCK, width, BF16),
-                (BLOCK, width, BF16)), 8, product, 8, {1: 1, 2: 2},
-    )
-    with jax.named_scope("sum_core"):
-        got = over_core(send)
+                (BLOCK, width, BF16)), 8, product, 8,
+    )
+    with jax.named_scope("sum_in_core"):
+        in_got = over_core(in_send)
+    got = tied(got, gdrive)
     height = mp * (hid + 2 * ns) // plane
     if ns // plane % 16 == 0 and hid // plane % 16 == 0:
         own_piece, *sends = call(
-            partial(split_pieces, mp, plane, (hid, ns, ns)), 1,
-            [(idx, None), (keep, None), (got, None)],
+            partial(split_pieces, mp, plane, hid, ns), 1,
+            [(idx, None), (keep, None), (got, None), (in_keep, None), (in_got, None)],
             [((height, width), F32, None)] + [((height, width), BF16, None)] * (plane - 1), [], 4, 0, 0,
         )
     else:
         both = keep + got.astype(F32)
-        both = [both[: mp * hid], both[mp * hid : early_rows], both[early_rows:]]
+        both = [both[: mp * hid], both[mp * hid :], in_keep + in_got.astype(F32)]
         both = jnp.concatenate([v.reshape(mp, plane, -1, width) for v in both], 2).swapaxes(0, 1)
         sends = [lax.dynamic_index_in_dim(both, place ^ s, 0, keepdims=False) for s in range(plane)]
         sends = [v.reshape(-1, width) for v in sends]

time: 108 us -> 107 us (level)
    ppermute x4 -> x5, waiting for transfers between devices: 6.47 us -> 4.98 us  [over_core(): return lax.ppermute(v, 'dp', xor_pairs(dp, 1))]
  transfers between devices with their start and end apart: 25 -> 26, of which waited for: 11 -> 11; matrix products, arithmetic and copies ran while one was open for 1% -> 1% of each run, Pallas kernels for 23% -> 27%
where the time goes in v6:
time: 107 us; the launch traced here: 106 us
  Pallas kernels  45.4 us (42%)
  starting transfers between devices  33.2 us (31%)
  waiting for transfers between devices  22 us (21%)
  local copies, waits for them, and re-layouts  3.45 us (3%)
  other arithmetic  1.21 us (1%)
    pallas_call x13, Pallas kernels, call(): pl.pallas_call(kernel, grid_spec=pltpu.PrefetchScalarGridSpec(num_scalar_...  45.4 us
    ppermute x15, starting transfers between devices, over_mp(): return lax.ppermute(v, 'mp', xor_pairs(mp, s))  25.3 us
    ppermute x15, waiting for transfers between devices, over_mp(): return lax.ppermute(v, 'mp', xor_pairs(mp, s))  10.4 us
    ppermute x6, starting transfers between devices, over_plane(): return lax.ppermute(v, 'dp', xor_pairs(dp, 2 * s))  7.12 us
    ppermute x6, waiting for transfers between devices, over_plane(): return lax.ppermute(v, 'dp', xor_pairs(dp, 2 * s))  6.62 us
    ppermute x5, waiting for transfers between devices, over_core(): return lax.ppermute(v, 'dp', xor_pairs(dp, 1))  4.98 us
  transfers between devices with their start and end apart: 26, of which 11 were waited for; matrix products, arithmetic and copies ran while one was open for 1% of the time, Pallas kernels for 27%

profile of v6, /device:TPU:0, one launch (start us, length us, event | category | flops | bytes accessed | tf_op | source)
XLA Modules:
  0.0 106.2 jit_solution(10300499530755264202)
XLA Ops:
  2.6 5.1 %collective-permute-start.2 = (bf16[80,512]{1,0:T(8,128)(2,1)S(1)}, bf16[80,512]{1,0:T(8,128)(2,1)S(1)}, u32[]{:S(2)}, u32[]{:S(2)}) collective-permute-start(bf16[80,512]{1,0:T(8,128)(2,1)S(1)} %pad_maximum_fusion.4.refs_0_), channel_id=1, source_target_pairs={{0,3},{1,2},{2,1},{3,0},{4,7},{5,6},{6,5},{7,4},{8,11},{9,10},{10,... | collective-permute-start | bytes 245768 | tf_op jit(solution)/shard_map/gather_in/ppermute | solution.py:711
  9.8 4.7 %shard_map.211 = (f32[2048,512]{1,0:T(8,128)S(1)}, bf16[2048,512]{1,0:T(8,128)(2,1)S(1)}, f32[2048,128]{1,0:T(8,128)S(1)}) custom-call(s32[3]{0:T(128)S(1)} %pad_add_fusion.idx, f32[16,128,512]{2,1,0:T(8,128)} %bitcast.55, f32[1,512]{1,0:T(1,128)} %bitcast.46, f32[1,512]{1,0:T(1,128)} %bitcast.49), custom_call_target="tpu_custom_call" | custom-call | flops 1073741824 | bytes 12582912 | tf_op jit(solution)/shard_map/pallas_call | solution.py:626
  15.3 3.7 %collective-permute-start.6 = (bf16[192,512]{1,0:T(8,128)(2,1)S(1)}, bf16[192,512]{1,0:T(8,128)(2,1)S(1)}, u32[]{:S(2)}, u32[]{:S(2)}) collective-permute-start(bf16[192,512]{1,0:T(8,128)(2,1)S(1)} %pad_maximum_fusion.refs_0_), channel_id=1, source_target_pairs={{0,3},{1,2},{2,1},{3,0},{4,7},{5,6},{6,5},{7,4},{8,11},{9,10},{10,... | collective-permute-start | bytes 589832 | tf_op jit(solution)/shard_map/gather_out_glu/ppermute | solution.py:711
  19.7 3.8 %shard_map.213.cotlow_ref = bf16[2048,512]{1,0:T(8,128)(2,1)S(1)} custom-call(s32[3]{0:T(128)S(1)} %pad_add_fusion.idx, f32[16,128,512]{2,1,0:T(8,128)} %bitcast.43), custom_call_target="tpu_custom_call" | custom-call | bytes 8388608 | tf_op jit(solution)/shard_map/pallas_call | solution.py:626
  23.6 2.0 %shard_map.214 = (f32[2048,512]{1,0:T(8,128)S(1)}, bf16[512,512]{1,0:T(8,128)(2,1)S(1)}, f32[12,512]{1,0:T(8,128)S(1)}, f32[16,512]{1,0:T(8,128)S(1)}, f32[8,512]{1,0:T(8,128)S(1)}) custom-call(s32[3]{0:T(128)S(1)} %pad_add_fusion.idx, bf16[2048,512]{1,0:T(8,128)(2,1)S(1)} %get-tuple-element.96.norm_ref, bf16[4,80,512]{2,1,0:T(8,128)(2,1)S(1)} %shard_map.212.own_ref, ...), custom_call_target="tpu_custom_call" | custom-call | flops 1073741824 | bytes 8388608 | tf_op jit(solution)/shard_map/pallas_call | solution.py:626
  25.7 3.7 %collective-permute-start.9 = (f32[8,512]{1,0:T(8,128)S(1)}, f32[8,512]{1,0:T(8,128)S(1)}, u32[]{:S(2)}, u32[]{:S(2)}) collective-permute-start(f32[8,512]{1,0:T(8,128)S(1)} %get-tuple-element.101.rest_3_), channel_id=1, source_target_pairs={{0,3},{1,2},{2,1},{3,0},{4,7},{5,6},{6,5},{7,4},{8,11},{9,10},{10,... | collective-permute-start | bytes 49160 | tf_op jit(solution)/shard_map/carry/ppermute | solution.py:711
  29.4 3.4 %collective-permute-start.7 = (f32[8,512]{1,0:T(8,128)S(1)}, f32[8,512]{1,0:T(8,128)S(1)}, u32[]{:S(2)}, u32[]{:S(2)}) collective-permute-start(f32[8,512]{1,0:T(8,128)S(1)} %get-tuple-element.101.rest_3_), channel_id=1, source_target_pairs={{0,1},{1,0},{2,3},{3,2},{4,5},{5,4},{6,7},{7,6},{8,9},{9,8},{10,11... | collective-permute-start | bytes 49160 | tf_op jit(solution)/shard_map/carry/ppermute | solution.py:711
  32.7 4.3 %collective-permute-done.5.refs_2_ = bf16[192,512]{1,0:T(8,128)(2,1)S(1)} collective-permute-done((bf16[192,512]{1,0:T(8,128)(2,1)S(1)}, bf16[192,512]{1,0:T(8,128)(2,1)S(1)}, u32[]{:S(2)}, u32[]{:S(2)}) %collective-permute-start.5) | collective-permute-done | bytes 196640 | tf_op jit(solution)/shard_map/gather_out_glu/ppermute | solution.py:711
  38.0 2.3 %collective-permute-done.10.other_ref = bf16[4,192,512]{2,1,0:T(8,128)(2,1)S(1)} collective-permute-done((bf16[4,192,512]{2,1,0:T(8,128)(2,1)S(1)}, bf16[4,192,512]{2,1,0:T(8,128)(2,1)S(1)}, u32[]{:S(2)}, u32[]{:S(2)}) %collective-permute-start.10) | collective-permute-done | bytes 786464 | tf_op jit(solution)/shard_map/ppermute | solution.py:705
  40.3 4.1 %shard_map.216 = (bf16[2048,512]{1,0:T(8,128)(2,1)S(1)}, bf16[2048,512]{1,0:T(8,128)(2,1)S(1)}, f32[2048,512]{1,0:T(8,128)S(1)}, bf16[512,512]{1,0:T(8,128)(2,1)S(1)}, f32[8,512]{1,0:T(8,128)S(1)}) custom-call(s32[3]{0:T(128)S(1)} %pad_add_fusion.idx, f32[2048,512]{1,0:T(8,128)S(1)} %get-tuple-element.95.xhat_ref, ...), custom_call_target="tpu_custom_call" | custom-call | flops 1073741824 | bytes 8388608 | tf_op jit(solution)/shard_map/pallas_call | solution.py:626
  44.4 4.7 %shard_map.217 = (bf16[2048,512]{1,0:T(8,128)(2,1)S(1)}, bf16[2048,1024]{1,0:T(8,128)(2,1)S(1)}, bf16[1024,512]{1,0:T(8,128)(2,1)S(1)}, f32[8,512]{1,0:T(8,128)S(1)}) custom-call(s32[3]{0:T(128)S(1)} %pad_add_fusion.idx, bf16[2048,512]{1,0:T(8,128)(2,1)S(1)} %shard_map.213.cotlow_ref, bf16[2048,512]{1,0:T(8,128)(2,1)S(1)} %get-tuple-element.106.act_ref, ...), custom_call_target="tpu_custom_call" | custom-call | flops 2147483648 | bytes 8388608 | tf_op jit(solution)/shard_map/pallas_call | solution.py:626
  49.1 4.6 %shard_map.218 = (bf16[2048,512]{1,0:T(8,128)(2,1)S(1)}, f32[2048,512]{1,0:T(8,128)S(1)}, f32[16,512]{1,0:T(8,128)S(1)}, f32[8,512]{1,0:T(8,128)S(1)}, f32[8,512]{1,0:T(8,128)S(1)}) custom-call(s32[3]{0:T(128)S(1)} %pad_add_fusion.idx, bf16[2048,1024]{1,0:T(8,128)(2,1)S(1)} %get-tuple-element.116.gpre_ref, f32[2048,512]{1,0:T(8,128)S(1)} %get-tuple-element.109.slope_ref, ...), custom_call_target="tpu_custom_call" | custom-call | flops 4294967296 | bytes 8388608 | tf_op jit(solution)/shard_map/pallas_call | solution.py:626
  54.2 2.3 %collective-permute-start.13 = (f32[8,512]{1,0:T(8,128)S(1)}, f32[8,512]{1,0:T(8,128)S(1)}, u32[]{:S(2)}, u32[]{:S(2)}) collective-permute-start(f32[8,512]{1,0:T(8,128)S(1)} %get-tuple-element.115), channel_id=1, source_target_pairs={{0,3},{1,2},{2,1},{3,0},{4,7},{5,6},{6,5},{7,4},{8,11},{9,10},{10,... | collective-permute-start | bytes 49160 | tf_op jit(solution)/shard_map/carry_back/ppermute | solution.py:711
  57.3 5.1 %shard_map.219 = (f32[768,512]{1,0:T(8,128)S(1)}, bf16[768,512]{1,0:T(8,128)(2,1)S(1)}) custom-call(s32[3]{0:T(128)S(1)} %pad_add_fusion.idx, bf16[2048,1024]{1,0:T(8,128)(2,1)S(1)} %get-tuple-element.116.gpre_ref, bf16[2048,512]{1,0:T(8,128)(2,1)S(1)} %get-tuple-element.106.act_ref, bf16[2048,512]{1,0:T(8,128)(2,1)S(1)} %get-tuple-element.113.state_ref, ...), custom_call_target="tpu_custom_call" | custom-call | tf_op jit(solution)/shard_map/pallas_call | solution.py:626
  62.5 3.6 %shard_map.220 = (bf16[2048,512]{1,0:T(8,128)(2,1)S(1)}, f32[256,512]{1,0:T(8,128)S(1)}, bf16[256,512]{1,0:T(8,128)(2,1)S(1)}, f32[8,512]{1,0:T(8,128)S(1)}) custom-call(s32[3]{0:T(128)S(1)} %pad_add_fusion.idx, f32[2048,512]{1,0:T(8,128)S(1)} %get-tuple-element.112.gs_ref, bf16[2048,512]{1,0:T(8,128)(2,1)S(1)} %get-tuple-element.113.state_ref, ...), custom_call_target="tpu_custom_call" | custom-call | flops 1073741824 | bytes 8388608 | tf_op jit(solution)/shard_map/pallas_call | solution.py:626
  68.6 1.6 %collective-permute-start.16 = (bf16[256,512]{1,0:T(8,128)(2,1)S(1)}, bf16[256,512]{1,0:T(8,128)(2,1)S(1)}, u32[]{:S(2)}, u32[]{:S(2)}) collective-permute-start(bf16[256,512]{1,0:T(8,128)(2,1)S(1)} %get-tuple-element.136), channel_id=1, source_target_pairs={{0,8},{4,12},{8,0},{12,4},{16,24},{20,28},{24,16},{28,20},{1,9},{5... | collective-permute-start | bytes 786440 | tf_op jit(solution)/shard_map/sum_plane/ppermute | solution.py:708
  70.2 1.5 %collective-permute-start.17 = (bf16[256,512]{1,0:T(8,128)(2,1)S(1)}, bf16[256,512]{1,0:T(8,128)(2,1)S(1)}, u32[]{:S(2)}, u32[]{:S(2)}) collective-permute-start(bf16[256,512]{1,0:T(8,128)(2,1)S(1)} %get-tuple-element.140), channel_id=1, source_target_pairs={{0,16},{4,20},{8,24},{12,28},{16,0},{20,4},{24,8},{28,12},{1,17},{... | collective-permute-start | bytes 786440 | tf_op jit(solution)/shard_map/sum_plane/ppermute | solution.py:708
  72.2 9.4 %shard_map.222 = (f32[16,128,512]{2,1,0:T(8,128)}, f32[16,128,512]{2,1,0:T(8,128)}, f32[8,512]{1,0:T(8,128)S(1)}, bf16[16,512]{1,0:T(8,128)(2,1)S(1)}) custom-call(s32[3]{0:T(128)S(1)} %pad_add_fusion.idx, f32[16,128,512]{2,1,0:T(8,128)S(1)} %bitcast.44, bf16[2048,512]{1,0:T(8,128)(2,1)S(1)} %get-tuple-element.127.gdrive_ref, ...), custom_call_target="tpu_custom_call" | custom-call | flops 1073741824 | bytes 8388608 | tf_op jit(solution)/shard_map/pallas_call | solution.py:626
  81.6 2.5 %collective-permute-done.17 = bf16[256,512]{1,0:T(8,128)(2,1)S(1)} collective-permute-done((bf16[256,512]{1,0:T(8,128)(2,1)S(1)}, bf16[256,512]{1,0:T(8,128)(2,1)S(1)}, u32[]{:S(2)}, u32[]{:S(2)}) %collective-permute-start.17) | collective-permute-done | bytes 262176 | tf_op jit(solution)/shard_map/sum_plane/ppermute | solution.py:708
  85.6 1.6 %collective-permute-start.20 = (bf16[80,512]{1,0:T(8,128)(2,1)S(1)}, bf16[80,512]{1,0:T(8,128)(2,1)S(1)}, u32[]{:S(2)}, u32[]{:S(2)}) collective-permute-start(bf16[80,512]{1,0:T(8,128)(2,1)S(1)} %get-tuple-element.178), channel_id=1, source_target_pairs={{0,2},{1,3},{2,0},{3,1},{4,6},{5,7},{6,4},{7,5},{8,10},{9,11},{10,... | collective-permute-start | bytes 245768 | tf_op jit(solution)/shard_map/sum_mp/ppermute | solution.py:711
  89.5 4.8 %collective-permute-done.20 = bf16[80,512]{1,0:T(8,128)(2,1)S(1)} collective-permute-done((bf16[80,512]{1,0:T(8,128)(2,1)S(1)}, bf16[80,512]{1,0:T(8,128)(2,1)S(1)}, u32[]{:S(2)}, u32[]{:S(2)}) %collective-permute-start.20) | collective-permute-done | bytes 81952 | tf_op jit(solution)/shard_map/sum_mp/ppermute | solution.py:711
  94.4 1.5 %collective-permute-start.22 = (bf16[80,512]{1,0:T(8,128)(2,1)S(1)}, bf16[80,512]{1,0:T(8,128)(2,1)S(1)}, u32[]{:S(2)}, u32[]{:S(2)}) collective-permute-start(bf16[80,512]{1,0:T(8,128)(2,1)S(1)} %pad_maximum_fusion.5), channel_id=1, source_target_pairs={{0,8},{4,12},{8,0},{12,4},{16,24},{20,28},{24,16},{28,20},{1,9},{5... | collective-permute-start | bytes 245768 | tf_op jit(solution)/shard_map/spread_plane/ppermute | solution.py:708
  99.0 3.2 %collective-permute-done.23 = bf16[80,512]{1,0:T(8,128)(2,1)S(1)} collective-permute-done((bf16[80,512]{1,0:T(8,128)(2,1)S(1)}, bf16[80,512]{1,0:T(8,128)(2,1)S(1)}, u32[]{:S(2)}, u32[]{:S(2)}) %collective-permute-start.23) | collective-permute-done | bytes 81952 | tf_op jit(solution)/shard_map/spread_plane/ppermute | solution.py:708
  102.3 1.5 %collective-permute-done.25.got_ref = bf16[272,512]{1,0:T(8,128)(2,1)S(1)} collective-permute-done((bf16[272,512]{1,0:T(8,128)(2,1)S(1)}, bf16[272,512]{1,0:T(8,128)(2,1)S(1)}, u32[]{:S(2)}, u32[]{:S(2)}) %collective-permute-start.25) | collective-permute-done | bytes 278560 | tf_op jit(solution)/shard_map/spread_core/ppermute | solution.py:705
  (87 shorter events, 20.1 us)
Async XLA Ops:
  2.6 11.8 %collective-permute-start.2 = (bf16[80,512]{1,0:T(8,128)(2,1)S(1)}, bf16[80,512]{1,0:T(8,128)(2,1)S(1)}, u32[]{:S(2)}, u32[]{:S(2)}) collective-permute-start(bf16[80,512]{1,0:T(8,128)(2,1)S(1)} %pad_maximum_fusion.4.refs_0_), channel_id=1, source_target_pairs={{0,3},{1,2},{2,1},{3,0},{4,7},{5,6},{6,5},{7,4},{8,11},{9,10},{10,... | collective-permute-start | bytes 245768 | tf_op jit(solution)/shard_map/gather_in/ppermute | solution.py:711
  7.7 6.9 %collective-permute-start.1 = (bf16[80,512]{1,0:T(8,128)(2,1)S(1)}, bf16[80,512]{1,0:T(8,128)(2,1)S(1)}, u32[]{:S(2)}, u32[]{:S(2)}) collective-permute-start(bf16[80,512]{1,0:T(8,128)(2,1)S(1)} %pad_maximum_fusion.4.refs_0_), channel_id=1, source_target_pairs={{0,2},{1,3},{2,0},{3,1},{4,6},{5,7},{6,4},{7,5},{8,10},{9,11},{10,... | collective-permute-start | bytes 245768 | tf_op jit(solution)/shard_map/gather_in/ppermute | solution.py:711
  7.7 6.9 %collective-permute-start = (bf16[80,512]{1,0:T(8,128)(2,1)S(1)}, bf16[80,512]{1,0:T(8,128)(2,1)S(1)}, u32[]{:S(2)}, u32[]{:S(2)}) collective-permute-start(bf16[80,512]{1,0:T(8,128)(2,1)S(1)} %pad_maximum_fusion.4.refs_0_), channel_id=1, source_target_pairs={{0,1},{1,0},{2,3},{3,2},{4,5},{5,4},{6,7},{7,6},{8,9},{9,8},{10,11... | collective-permute-start | bytes 245768 | tf_op jit(solution)/shard_map/gather_in/ppermute | solution.py:711
  15.2 8.4 %collective-permute-start.3 = (bf16[4,80,512]{2,1,0:T(8,128)(2,1)S(1)}, bf16[4,80,512]{2,1,0:T(8,128)(2,1)S(1)}, u32[]{:S(2)}, u32[]{:S(2)}) collective-permute-start(bf16[4,80,512]{2,1,0:T(8,128)(2,1)S(1)} %shard_map.212.own_ref), channel_id=1, source_target_pairs={{0,4},{4,0},{8,12},{12,8},{16,20},{20,16},{24,28},{28,24},{1,5},{5... | collective-permute-start | bytes 983048 | tf_op jit(solution)/shard_map/ppermute | solution.py:705
  15.3 14.1 %collective-permute-start.6 = (bf16[192,512]{1,0:T(8,128)(2,1)S(1)}, bf16[192,512]{1,0:T(8,128)(2,1)S(1)}, u32[]{:S(2)}, u32[]{:S(2)}) collective-permute-start(bf16[192,512]{1,0:T(8,128)(2,1)S(1)} %pad_maximum_fusion.refs_0_), channel_id=1, source_target_pairs={{0,3},{1,2},{2,1},{3,0},{4,7},{5,6},{6,5},{7,4},{8,11},{9,10},{10,... | collective-permute-start | bytes 589832 | tf_op jit(solution)/shard_map/gather_out_glu/ppermute | solution.py:711
  18.9 18.0 %collective-permute-start.5 = (bf16[192,512]{1,0:T(8,128)(2,1)S(1)}, bf16[192,512]{1,0:T(8,128)(2,1)S(1)}, u32[]{:S(2)}, u32[]{:S(2)}) collective-permute-start(bf16[192,512]{1,0:T(8,128)(2,1)S(1)} %pad_maximum_fusion.refs_0_), channel_id=1, source_target_pairs={{0,2},{1,3},{2,0},{3,1},{4,6},{5,7},{6,4},{7,5},{8,10},{9,11},{10,... | collective-permute-start | bytes 589832 | tf_op jit(solution)/shard_map/gather_out_glu/ppermute | solution.py:711
  18.9 18.0 %collective-permute-start.4 = (bf16[192,512]{1,0:T(8,128)(2,1)S(1)}, bf16[192,512]{1,0:T(8,128)(2,1)S(1)}, u32[]{:S(2)}, u32[]{:S(2)}) collective-permute-start(bf16[192,512]{1,0:T(8,128)(2,1)S(1)} %pad_maximum_fusion.refs_0_), channel_id=1, source_target_pairs={{0,1},{1,0},{2,3},{3,2},{4,5},{5,4},{6,7},{7,6},{8,9},{9,8},{10,11... | collective-permute-start | bytes 589832 | tf_op jit(solution)/shard_map/gather_out_glu/ppermute | solution.py:711
  25.7 11.3 %collective-permute-start.9 = (f32[8,512]{1,0:T(8,128)S(1)}, f32[8,512]{1,0:T(8,128)S(1)}, u32[]{:S(2)}, u32[]{:S(2)}) collective-permute-start(f32[8,512]{1,0:T(8,128)S(1)} %get-tuple-element.101.rest_3_), channel_id=1, source_target_pairs={{0,3},{1,2},{2,1},{3,0},{4,7},{5,6},{6,5},{7,4},{8,11},{9,10},{10,... | collective-permute-start | bytes 49160 | tf_op jit(solution)/shard_map/carry/ppermute | solution.py:711
  29.4 8.0 %collective-permute-start.8 = (f32[8,512]{1,0:T(8,128)S(1)}, f32[8,512]{1,0:T(8,128)S(1)}, u32[]{:S(2)}, u32[]{:S(2)}) collective-permute-start(f32[8,512]{1,0:T(8,128)S(1)} %get-tuple-element.101.rest_3_), channel_id=1, source_target_pairs={{0,2},{1,3},{2,0},{3,1},{4,6},{5,7},{6,4},{7,5},{8,10},{9,11},{10,... | collective-permute-start | bytes 49160 | tf_op jit(solution)/shard_map/carry/ppermute | solution.py:711
  29.4 8.0 %collective-permute-start.7 = (f32[8,512]{1,0:T(8,128)S(1)}, f32[8,512]{1,0:T(8,128)S(1)}, u32[]{:S(2)}, u32[]{:S(2)}) collective-permute-start(f32[8,512]{1,0:T(8,128)S(1)} %get-tuple-element.101.rest_3_), channel_id=1, source_target_pairs={{0,1},{1,0},{2,3},{3,2},{4,5},{5,4},{6,7},{7,6},{8,9},{9,8},{10,11... | collective-permute-start | bytes 49160 | tf_op jit(solution)/shard_map/carry/ppermute | solution.py:711
  37.9 2.4 %collective-permute-start.10 = (bf16[4,192,512]{2,1,0:T(8,128)(2,1)S(1)}, bf16[4,192,512]{2,1,0:T(8,128)(2,1)S(1)}, u32[]{:S(2)}, u32[]{:S(2)}) collective-permute-start(bf16[4,192,512]{2,1,0:T(8,128)(2,1)S(1)} %shard_map.215.own_ref), channel_id=1, source_target_pairs={{0,4},{4,0},{8,12},{12,8},{16,20},{20,16},{24,28},{28,24},{1,5},{5... | collective-permute-start | bytes 2359304 | tf_op jit(solution)/shard_map/ppermute | solution.py:705
  53.8 8.7 %collective-permute-start.11 = (f32[8,512]{1,0:T(8,128)S(1)}, f32[8,512]{1,0:T(8,128)S(1)}, u32[]{:S(2)}, u32[]{:S(2)}) collective-permute-start(f32[8,512]{1,0:T(8,128)S(1)} %get-tuple-element.115), channel_id=1, source_target_pairs={{0,1},{1,0},{2,3},{3,2},{4,5},{5,4},{6,7},{7,6},{8,9},{9,8},{10,11... | collective-permute-start | bytes 49160 | tf_op jit(solution)/shard_map/carry_back/ppermute | solution.py:711
  54.2 8.2 %collective-permute-start.13 = (f32[8,512]{1,0:T(8,128)S(1)}, f32[8,512]{1,0:T(8,128)S(1)}, u32[]{:S(2)}, u32[]{:S(2)}) collective-permute-start(f32[8,512]{1,0:T(8,128)S(1)} %get-tuple-element.115), channel_id=1, source_target_pairs={{0,3},{1,2},{2,1},{3,0},{4,7},{5,6},{6,5},{7,4},{8,11},{9,10},{10,... | collective-permute-start | bytes 49160 | tf_op jit(solution)/shard_map/carry_back/ppermute | solution.py:711
  56.6 5.9 %collective-permute-start.12 = (f32[8,512]{1,0:T(8,128)S(1)}, f32[8,512]{1,0:T(8,128)S(1)}, u32[]{:S(2)}, u32[]{:S(2)}) collective-permute-start(f32[8,512]{1,0:T(8,128)S(1)} %get-tuple-element.115), channel_id=1, source_target_pairs={{0,2},{1,3},{2,0},{3,1},{4,6},{5,7},{6,4},{7,5},{8,10},{9,11},{10,... | collective-permute-start | bytes 49160 | tf_op jit(solution)/shard_map/carry_back/ppermute | solution.py:711
  62.4 4.3 %collective-permute-start.14 = (bf16[768,512]{1,0:T(8,128)(2,1)S(1)}, bf16[768,512]{1,0:T(8,128)(2,1)S(1)}, u32[]{:S(2)}, u32[]{:S(2)}) collective-permute-start(bf16[768,512]{1,0:T(8,128)(2,1)S(1)} %get-tuple-element.122), channel_id=1, source_target_pairs={{0,4},{4,0},{8,12},{12,8},{16,20},{20,16},{24,28},{28,24},{1,5},{5... | collective-permute-start | bytes 2359304 | tf_op jit(solution)/shard_map/sum_early_core/ppermute | solution.py:705
  68.6 13.0 %collective-permute-start.16 = (bf16[256,512]{1,0:T(8,128)(2,1)S(1)}, bf16[256,512]{1,0:T(8,128)(2,1)S(1)}, u32[]{:S(2)}, u32[]{:S(2)}) collective-permute-start(bf16[256,512]{1,0:T(8,128)(2,1)S(1)} %get-tuple-element.136), channel_id=1, source_target_pairs={{0,8},{4,12},{8,0},{12,4},{16,24},{20,28},{24,16},{28,20},{1,9},{5... | collective-permute-start | bytes 786440 | tf_op jit(solution)/shard_map/sum_plane/ppermute | solution.py:708
  70.2 13.9 %collective-permute-start.17 = (bf16[256,512]{1,0:T(8,128)(2,1)S(1)}, bf16[256,512]{1,0:T(8,128)(2,1)S(1)}, u32[]{:S(2)}, u32[]{:S(2)}) collective-permute-start(bf16[256,512]{1,0:T(8,128)(2,1)S(1)} %get-tuple-element.140), channel_id=1, source_target_pairs={{0,16},{4,20},{8,24},{12,28},{16,0},{20,4},{24,8},{28,12},{1,17},{... | collective-permute-start | bytes 786440 | tf_op jit(solution)/shard_map/sum_plane/ppermute | solution.py:708
  71.7 12.4 %collective-permute-start.18 = (bf16[256,512]{1,0:T(8,128)(2,1)S(1)}, bf16[256,512]{1,0:T(8,128)(2,1)S(1)}, u32[]{:S(2)}, u32[]{:S(2)}) collective-permute-start(bf16[256,512]{1,0:T(8,128)(2,1)S(1)} %get-tuple-element.141), channel_id=1, source_target_pairs={{0,24},{4,28},{8,16},{12,20},{16,8},{20,12},{24,0},{28,4},{1,25},{... | collective-permute-start | bytes 786440 | tf_op jit(solution)/shard_map/sum_plane/ppermute | solution.py:708
  84.3 5.2 %collective-permute-start.19 = (bf16[80,512]{1,0:T(8,128)(2,1)S(1)}, bf16[80,512]{1,0:T(8,128)(2,1)S(1)}, u32[]{:S(2)}, u32[]{:S(2)}) collective-permute-start(bf16[80,512]{1,0:T(8,128)(2,1)S(1)} %get-tuple-element.177), channel_id=1, source_target_pairs={{0,1},{1,0},{2,3},{3,2},{4,5},{5,4},{6,7},{7,6},{8,9},{9,8},{10,11... | collective-permute-start | bytes 245768 | tf_op jit(solution)/shard_map/sum_mp/ppermute | solution.py:711
  85.6 8.7 %collective-permute-start.20 = (bf16[80,512]{1,0:T(8,128)(2,1)S(1)}, bf16[80,512]{1,0:T(8,128)(2,1)S(1)}, u32[]{:S(2)}, u32[]{:S(2)}) collective-permute-start(bf16[80,512]{1,0:T(8,128)(2,1)S(1)} %get-tuple-element.178), channel_id=1, source_target_pairs={{0,2},{1,3},{2,0},{3,1},{4,6},{5,7},{6,4},{7,5},{8,10},{9,11},{10,... | collective-permute-start | bytes 245768 | tf_op jit(solution)/shard_map/sum_mp/ppermute | solution.py:711
  87.3 7.1 %collective-permute-start.21 = (bf16[80,512]{1,0:T(8,128)(2,1)S(1)}, bf16[80,512]{1,0:T(8,128)(2,1)S(1)}, u32[]{:S(2)}, u32[]{:S(2)}) collective-permute-start(bf16[80,512]{1,0:T(8,128)(2,1)S(1)} %get-tuple-element.179), channel_id=1, source_target_pairs={{0,3},{1,2},{2,1},{3,0},{4,7},{5,6},{6,5},{7,4},{8,11},{9,10},{10,... | collective-permute-start | bytes 245768 | tf_op jit(solution)/shard_map/sum_mp/ppermute | solution.py:711
  94.4 4.5 %collective-permute-start.22 = (bf16[80,512]{1,0:T(8,128)(2,1)S(1)}, bf16[80,512]{1,0:T(8,128)(2,1)S(1)}, u32[]{:S(2)}, u32[]{:S(2)}) collective-permute-start(bf16[80,512]{1,0:T(8,128)(2,1)S(1)} %pad_maximum_fusion.5), channel_id=1, source_target_pairs={{0,8},{4,12},{8,0},{12,4},{16,24},{20,28},{24,16},{28,20},{1,9},{5... | collective-permute-start | bytes 245768 | tf_op jit(solution)/shard_map/spread_plane/ppermute | solution.py:708
  95.9 6.2 %collective-permute-start.24 = (bf16[80,512]{1,0:T(8,128)(2,1)S(1)}, bf16[80,512]{1,0:T(8,128)(2,1)S(1)}, u32[]{:S(2)}, u32[]{:S(2)}) collective-permute-start(bf16[80,512]{1,0:T(8,128)(2,1)S(1)} %pad_maximum_fusion.5), channel_id=1, source_target_pairs={{0,24},{4,28},{8,16},{12,20},{16,8},{20,12},{24,0},{28,4},{1,25},{... | collective-permute-start | bytes 245768 | tf_op jit(solution)/shard_map/spread_plane/ppermute | solution.py:708
  97.4 4.8 %collective-permute-start.23 = (bf16[80,512]{1,0:T(8,128)(2,1)S(1)}, bf16[80,512]{1,0:T(8,128)(2,1)S(1)}, u32[]{:S(2)}, u32[]{:S(2)}) collective-permute-start(bf16[80,512]{1,0:T(8,128)(2,1)S(1)} %pad_maximum_fusion.5), channel_id=1, source_target_pairs={{0,16},{4,20},{8,24},{12,28},{16,0},{20,4},{24,8},{28,12},{1,17},{... | collective-permute-start | bytes 245768 | tf_op jit(solution)/shard_map/spread_plane/ppermute | solution.py:708
  (11 other events, 178.3 us)

commit v7 on v6

--- a/solution.py
+++ b/solution.py
@@ -570,6 +570,7 @@
 
 
 def finish(hid, ns, count, idx, own_ref, got_ref, nu_ref, theta_ref, in_ref, out_ref, glu_ref, *rest):
+    *rest, rows_ref = rest
     core, place = idx[1], idx[2]
     height = (hid + 2 * ns) // count
     for part in range(2):
@@ -577,10 +578,11 @@
             here = pl.ds(pl.multiple_of((i ^ place) * height, 16), height)
             rows = jnp.where(core == part, own_ref[here, :], got_ref[here, :]).astype(F32)
             low = 0
-            for ref, size in ((glu_ref, hid // count), (out_ref, ns // count), (in_ref, ns // count)):
+            for ref, size in ((rows_ref, hid // count), (out_ref, ns // count), (in_ref, ns // count)):
                 value = rows[low : low + size]
                 ref[part, i * size : (i + 1) * size, :] = -value if ref is out_ref and part == 1 else value
                 low += size
+        glu_ref[:, part, :] = rows_ref[part].T
     first = count * height
     both = [ref[first : first + 16, :].astype(F32) for ref in (own_ref, got_ref)]
     vec = (both[0][:8] + both[0][8:]) + (both[1][:8] + both[1][8:])
@@ -880,8 +882,8 @@
         grad_in, grad_out_weight, grad_glu, *vectors = call(
             partial(finish, hid, ns, plane), 1,
             [(idx, None), (own, None), (got, None)] + logs,
-            [((2, ns, width), F32, whole), ((2, ns, width), F32, whole), ((2, hid, width), F32, None)] + shared,
-            [], 8, 0, 0,
+            [((2, ns, width), F32, whole), ((2, ns, width), F32, whole), ((width, 2, hid), F32, pl.BlockSpec((width, 2, hid), lambda i, idx: (0, 0, 0)))] + shared,
+            [((2, hid, width), F32)], 8, 0, 0,
         )
     else:
         vec = vec + vector_sum(got[plane * n :])
@@ -893,7 +895,7 @@
         def part(start, size):
             return total[:, :, start : start + size].reshape(2, -1, width)
 
-        grad_glu, grad_out, grad_in = part(0, nh), part(nh, nr), part(nh + nr, nr)
+        grad_glu, grad_out, grad_in = part(0, nh).transpose(2, 0, 1), part(nh, nr), part(nh + nr, nr)
         grad_out_weight = jnp.stack([grad_out[0], -grad_out[1]])
     grad_ln_gain, grad_ln_bias, grad_skip, grad_nu, grad_theta, grad_gamma, grad_glu_bias = vectors
     return (
@@ -907,7 +909,7 @@
         grad_in.transpose(2, 0, 1),
         grad_out_weight,
         grad_skip[0],
-        grad_glu.transpose(2, 0, 1),
+        grad_glu,
         grad_glu_bias,
     )
 

time: 107 us -> 106 us (level)
  no operation moved by 1% of the time
where the time goes in v7:
time: 106 us
  Pallas kernels  46 us (43%)
  starting transfers between devices  33.2 us (31%)
  waiting for transfers between devices  22 us (21%)
  local copies, waits for them, and re-layouts  2.45 us (2%)
  other arithmetic  1.21 us (1%)
  between operations  1.15 us (1%)
    pallas_call x13, Pallas kernels, call(): pl.pallas_call(kernel, grid_spec=pltpu.PrefetchScalarGridSpec(num_scalar_...  46 us
    ppermute x15, starting transfers between devices, over_mp(): return lax.ppermute(v, 'mp', xor_pairs(mp, s))  25.3 us
    ppermute x15, waiting for transfers between devices, over_mp(): return lax.ppermute(v, 'mp', xor_pairs(mp, s))  10.4 us
    ppermute x6, starting transfers between devices, over_plane(): return lax.ppermute(v, 'dp', xor_pairs(dp, 2 * s))  7.12 us
    ppermute x6, waiting for transfers between devices, over_plane(): return lax.ppermute(v, 'dp', xor_pairs(dp, 2 * s))  6.62 us
    ppermute x5, waiting for transfers between devices, over_core(): return lax.ppermute(v, 'dp', xor_pairs(dp, 1))  4.98 us
  transfers between devices with their start and end apart: 26, of which 11 were waited for; matrix products, arithmetic and copies ran while one was open for 1% of the time, Pallas kernels for 27%

profile of v7, /device:TPU:0, one launch (start us, length us, event | category | flops | bytes accessed | tf_op | source)
XLA Modules:
  0.0 105.9 jit_solution(978524596532960552)
XLA Ops:
  2.6 5.1 %collective-permute-start.2 = (bf16[80,512]{1,0:T(8,128)(2,1)S(1)}, bf16[80,512]{1,0:T(8,128)(2,1)S(1)}, u32[]{:S(2)}, u32[]{:S(2)}) collective-permute-start(bf16[80,512]{1,0:T(8,128)(2,1)S(1)} %pad_maximum_fusion.4.refs_0_), channel_id=1, source_target_pairs={{0,3},{1,2},{2,1},{3,0},{4,7},{5,6},{6,5},{7,4},{8,11},{9,10},{10,... | collective-permute-start | bytes 245768 | tf_op jit(solution)/shard_map/gather_in/ppermute | solution.py:713
  9.8 4.7 %shard_map.211 = (f32[2048,512]{1,0:T(8,128)S(1)}, bf16[2048,512]{1,0:T(8,128)(2,1)S(1)}, f32[2048,128]{1,0:T(8,128)S(1)}) custom-call(s32[3]{0:T(128)S(1)} %pad_add_fusion.idx, f32[16,128,512]{2,1,0:T(8,128)} %bitcast.53, f32[1,512]{1,0:T(1,128)} %bitcast.44, f32[1,512]{1,0:T(1,128)} %bitcast.47), custom_call_target="tpu_custom_call" | custom-call | flops 1073741824 | bytes 12582912 | tf_op jit(solution)/shard_map/pallas_call | solution.py:628
  15.3 3.7 %collective-permute-start.6 = (bf16[192,512]{1,0:T(8,128)(2,1)S(1)}, bf16[192,512]{1,0:T(8,128)(2,1)S(1)}, u32[]{:S(2)}, u32[]{:S(2)}) collective-permute-start(bf16[192,512]{1,0:T(8,128)(2,1)S(1)} %pad_maximum_fusion.refs_0_), channel_id=1, source_target_pairs={{0,3},{1,2},{2,1},{3,0},{4,7},{5,6},{6,5},{7,4},{8,11},{9,10},{10,... | collective-permute-start | bytes 589832 | tf_op jit(solution)/shard_map/gather_out_glu/ppermute | solution.py:713
  19.7 3.8 %shard_map.213.cotlow_ref = bf16[2048,512]{1,0:T(8,128)(2,1)S(1)} custom-call(s32[3]{0:T(128)S(1)} %pad_add_fusion.idx, f32[16,128,512]{2,1,0:T(8,128)} %bitcast.42), custom_call_target="tpu_custom_call" | custom-call | bytes 8388608 | tf_op jit(solution)/shard_map/pallas_call | solution.py:628
  23.6 2.0 %shard_map.214 = (f32[2048,512]{1,0:T(8,128)S(1)}, bf16[512,512]{1,0:T(8,128)(2,1)S(1)}, f32[12,512]{1,0:T(8,128)S(1)}, f32[16,512]{1,0:T(8,128)S(1)}, f32[8,512]{1,0:T(8,128)S(1)}) custom-call(s32[3]{0:T(128)S(1)} %pad_add_fusion.idx, bf16[2048,512]{1,0:T(8,128)(2,1)S(1)} %get-tuple-element.96.norm_ref, bf16[4,80,512]{2,1,0:T(8,128)(2,1)S(1)} %shard_map.212.own_ref, ...), custom_call_target="tpu_custom_call" | custom-call | flops 1073741824 | bytes 8388608 | tf_op jit(solution)/shard_map/pallas_call | solution.py:628
  25.7 3.7 %collective-permute-start.9 = (f32[8,512]{1,0:T(8,128)S(1)}, f32[8,512]{1,0:T(8,128)S(1)}, u32[]{:S(2)}, u32[]{:S(2)}) collective-permute-start(f32[8,512]{1,0:T(8,128)S(1)} %get-tuple-element.101.rest_3_), channel_id=1, source_target_pairs={{0,3},{1,2},{2,1},{3,0},{4,7},{5,6},{6,5},{7,4},{8,11},{9,10},{10,... | collective-permute-start | bytes 49160 | tf_op jit(solution)/shard_map/carry/ppermute | solution.py:713
  29.4 3.4 %collective-permute-start.7 = (f32[8,512]{1,0:T(8,128)S(1)}, f32[8,512]{1,0:T(8,128)S(1)}, u32[]{:S(2)}, u32[]{:S(2)}) collective-permute-start(f32[8,512]{1,0:T(8,128)S(1)} %get-tuple-element.101.rest_3_), channel_id=1, source_target_pairs={{0,1},{1,0},{2,3},{3,2},{4,5},{5,4},{6,7},{7,6},{8,9},{9,8},{10,11... | collective-permute-start | bytes 49160 | tf_op jit(solution)/shard_map/carry/ppermute | solution.py:713
  32.7 4.3 %collective-permute-done.5.refs_2_ = bf16[192,512]{1,0:T(8,128)(2,1)S(1)} collective-permute-done((bf16[192,512]{1,0:T(8,128)(2,1)S(1)}, bf16[192,512]{1,0:T(8,128)(2,1)S(1)}, u32[]{:S(2)}, u32[]{:S(2)}) %collective-permute-start.5) | collective-permute-done | bytes 196640 | tf_op jit(solution)/shard_map/gather_out_glu/ppermute | solution.py:713
  38.0 2.3 %collective-permute-done.10.other_ref = bf16[4,192,512]{2,1,0:T(8,128)(2,1)S(1)} collective-permute-done((bf16[4,192,512]{2,1,0:T(8,128)(2,1)S(1)}, bf16[4,192,512]{2,1,0:T(8,128)(2,1)S(1)}, u32[]{:S(2)}, u32[]{:S(2)}) %collective-permute-start.10) | collective-permute-done | bytes 786464 | tf_op jit(solution)/shard_map/ppermute | solution.py:707
  40.3 4.1 %shard_map.216 = (bf16[2048,512]{1,0:T(8,128)(2,1)S(1)}, bf16[2048,512]{1,0:T(8,128)(2,1)S(1)}, f32[2048,512]{1,0:T(8,128)S(1)}, bf16[512,512]{1,0:T(8,128)(2,1)S(1)}, f32[8,512]{1,0:T(8,128)S(1)}) custom-call(s32[3]{0:T(128)S(1)} %pad_add_fusion.idx, f32[2048,512]{1,0:T(8,128)S(1)} %get-tuple-element.95.xhat_ref, ...), custom_call_target="tpu_custom_call" | custom-call | flops 1073741824 | bytes 8388608 | tf_op jit(solution)/shard_map/pallas_call | solution.py:628
  44.4 4.7 %shard_map.217 = (bf16[2048,512]{1,0:T(8,128)(2,1)S(1)}, bf16[2048,1024]{1,0:T(8,128)(2,1)S(1)}, bf16[1024,512]{1,0:T(8,128)(2,1)S(1)}, f32[8,512]{1,0:T(8,128)S(1)}) custom-call(s32[3]{0:T(128)S(1)} %pad_add_fusion.idx, bf16[2048,512]{1,0:T(8,128)(2,1)S(1)} %shard_map.213.cotlow_ref, bf16[2048,512]{1,0:T(8,128)(2,1)S(1)} %get-tuple-element.106.act_ref, ...), custom_call_target="tpu_custom_call" | custom-call | flops 2147483648 | bytes 8388608 | tf_op jit(solution)/shard_map/pallas_call | solution.py:628
  49.1 4.6 %shard_map.218 = (bf16[2048,512]{1,0:T(8,128)(2,1)S(1)}, f32[2048,512]{1,0:T(8,128)S(1)}, f32[16,512]{1,0:T(8,128)S(1)}, f32[8,512]{1,0:T(8,128)S(1)}, f32[8,512]{1,0:T(8,128)S(1)}) custom-call(s32[3]{0:T(128)S(1)} %pad_add_fusion.idx, bf16[2048,1024]{1,0:T(8,128)(2,1)S(1)} %get-tuple-element.116.gpre_ref, f32[2048,512]{1,0:T(8,128)S(1)} %get-tuple-element.109.slope_ref, ...), custom_call_target="tpu_custom_call" | custom-call | flops 4294967296 | bytes 8388608 | tf_op jit(solution)/shard_map/pallas_call | solution.py:628
  54.2 2.3 %collective-permute-start.13 = (f32[8,512]{1,0:T(8,128)S(1)}, f32[8,512]{1,0:T(8,128)S(1)}, u32[]{:S(2)}, u32[]{:S(2)}) collective-permute-start(f32[8,512]{1,0:T(8,128)S(1)} %get-tuple-element.115), channel_id=1, source_target_pairs={{0,3},{1,2},{2,1},{3,0},{4,7},{5,6},{6,5},{7,4},{8,11},{9,10},{10,... | collective-permute-start | bytes 49160 | tf_op jit(solution)/shard_map/carry_back/ppermute | solution.py:713
  57.3 5.1 %shard_map.219 = (f32[768,512]{1,0:T(8,128)S(1)}, bf16[768,512]{1,0:T(8,128)(2,1)S(1)}) custom-call(s32[3]{0:T(128)S(1)} %pad_add_fusion.idx, bf16[2048,1024]{1,0:T(8,128)(2,1)S(1)} %get-tuple-element.116.gpre_ref, bf16[2048,512]{1,0:T(8,128)(2,1)S(1)} %get-tuple-element.106.act_ref, bf16[2048,512]{1,0:T(8,128)(2,1)S(1)} %get-tuple-element.113.state_ref, ...), custom_call_target="tpu_custom_call" | custom-call | tf_op jit(solution)/shard_map/pallas_call | solution.py:628
  62.5 3.6 %shard_map.220 = (bf16[2048,512]{1,0:T(8,128)(2,1)S(1)}, f32[256,512]{1,0:T(8,128)S(1)}, bf16[256,512]{1,0:T(8,128)(2,1)S(1)}, f32[8,512]{1,0:T(8,128)S(1)}) custom-call(s32[3]{0:T(128)S(1)} %pad_add_fusion.idx, f32[2048,512]{1,0:T(8,128)S(1)} %get-tuple-element.112.gs_ref, bf16[2048,512]{1,0:T(8,128)(2,1)S(1)} %get-tuple-element.113.state_ref, ...), custom_call_target="tpu_custom_call" | custom-call | flops 1073741824 | bytes 8388608 | tf_op jit(solution)/shard_map/pallas_call | solution.py:628
  68.6 1.6 %collective-permute-start.16 = (bf16[256,512]{1,0:T(8,128)(2,1)S(1)}, bf16[256,512]{1,0:T(8,128)(2,1)S(1)}, u32[]{:S(2)}, u32[]{:S(2)}) collective-permute-start(bf16[256,512]{1,0:T(8,128)(2,1)S(1)} %get-tuple-element.136), channel_id=1, source_target_pairs={{0,8},{4,12},{8,0},{12,4},{16,24},{20,28},{24,16},{28,20},{1,9},{5... | collective-permute-start | bytes 786440 | tf_op jit(solution)/shard_map/sum_plane/ppermute | solution.py:710
  70.2 1.5 %collective-permute-start.17 = (bf16[256,512]{1,0:T(8,128)(2,1)S(1)}, bf16[256,512]{1,0:T(8,128)(2,1)S(1)}, u32[]{:S(2)}, u32[]{:S(2)}) collective-permute-start(bf16[256,512]{1,0:T(8,128)(2,1)S(1)} %get-tuple-element.140), channel_id=1, source_target_pairs={{0,16},{4,20},{8,24},{12,28},{16,0},{20,4},{24,8},{28,12},{1,17},{... | collective-permute-start | bytes 786440 | tf_op jit(solution)/shard_map/sum_plane/ppermute | solution.py:710
  72.2 9.4 %shard_map.222 = (f32[16,128,512]{2,1,0:T(8,128)}, f32[16,128,512]{2,1,0:T(8,128)}, f32[8,512]{1,0:T(8,128)S(1)}, bf16[16,512]{1,0:T(8,128)(2,1)S(1)}) custom-call(s32[3]{0:T(128)S(1)} %pad_add_fusion.idx, f32[16,128,512]{2,1,0:T(8,128)S(1)} %bitcast.43, bf16[2048,512]{1,0:T(8,128)(2,1)S(1)} %get-tuple-element.127.gdrive_ref, ...), custom_call_target="tpu_custom_call" | custom-call | flops 1073741824 | bytes 8388608 | tf_op jit(solution)/shard_map/pallas_call | solution.py:628
  81.6 2.5 %collective-permute-done.17 = bf16[256,512]{1,0:T(8,128)(2,1)S(1)} collective-permute-done((bf16[256,512]{1,0:T(8,128)(2,1)S(1)}, bf16[256,512]{1,0:T(8,128)(2,1)S(1)}, u32[]{:S(2)}, u32[]{:S(2)}) %collective-permute-start.17) | collective-permute-done | bytes 262176 | tf_op jit(solution)/shard_map/sum_plane/ppermute | solution.py:710
  85.6 1.6 %collective-permute-start.20 = (bf16[80,512]{1,0:T(8,128)(2,1)S(1)}, bf16[80,512]{1,0:T(8,128)(2,1)S(1)}, u32[]{:S(2)}, u32[]{:S(2)}) collective-permute-start(bf16[80,512]{1,0:T(8,128)(2,1)S(1)} %get-tuple-element.166), channel_id=1, source_target_pairs={{0,2},{1,3},{2,0},{3,1},{4,6},{5,7},{6,4},{7,5},{8,10},{9,11},{10,... | collective-permute-start | bytes 245768 | tf_op jit(solution)/shard_map/sum_mp/ppermute | solution.py:713
  89.5 4.8 %collective-permute-done.20 = bf16[80,512]{1,0:T(8,128)(2,1)S(1)} collective-permute-done((bf16[80,512]{1,0:T(8,128)(2,1)S(1)}, bf16[80,512]{1,0:T(8,128)(2,1)S(1)}, u32[]{:S(2)}, u32[]{:S(2)}) %collective-permute-start.20) | collective-permute-done | bytes 81952 | tf_op jit(solution)/shard_map/sum_mp/ppermute | solution.py:713
  99.0 3.2 %collective-permute-done.23 = bf16[80,512]{1,0:T(8,128)(2,1)S(1)} collective-permute-done((bf16[80,512]{1,0:T(8,128)(2,1)S(1)}, bf16[80,512]{1,0:T(8,128)(2,1)S(1)}, u32[]{:S(2)}, u32[]{:S(2)}) %collective-permute-start.23) | collective-permute-done | bytes 81952 | tf_op jit(solution)/shard_map/spread_plane/ppermute | solution.py:710
  102.3 1.5 %collective-permute-done.25.got_ref = bf16[272,512]{1,0:T(8,128)(2,1)S(1)} collective-permute-done((bf16[272,512]{1,0:T(8,128)(2,1)S(1)}, bf16[272,512]{1,0:T(8,128)(2,1)S(1)}, u32[]{:S(2)}, u32[]{:S(2)}) %collective-permute-start.25) | collective-permute-done | bytes 278560 | tf_op jit(solution)/shard_map/spread_core/ppermute | solution.py:707
  103.9 1.9 %shard_map.223 = (f32[2,64,512]{2,1,0:T(8,128)}, f32[2,64,512]{2,1,0:T(8,128)}, f32[512,2,128]{2,1,0:T(2,128)}, f32[1,512]{1,0:T(1,128)}, f32[1,512]{1,0:T(1,128...) custom-call(s32[3]{0:T(128)S(1)} %pad_add_fusion.idx, ...), custom_call_target="tpu_custom_call" | custom-call | tf_op jit(solution)/shard_map/pallas_call | solution.py:628
  (86 shorter events, 19.2 us)
Async XLA Ops:
  2.6 11.8 %collective-permute-start.2 = (bf16[80,512]{1,0:T(8,128)(2,1)S(1)}, bf16[80,512]{1,0:T(8,128)(2,1)S(1)}, u32[]{:S(2)}, u32[]{:S(2)}) collective-permute-start(bf16[80,512]{1,0:T(8,128)(2,1)S(1)} %pad_maximum_fusion.4.refs_0_), channel_id=1, source_target_pairs={{0,3},{1,2},{2,1},{3,0},{4,7},{5,6},{6,5},{7,4},{8,11},{9,10},{10,... | collective-permute-start | bytes 245768 | tf_op jit(solution)/shard_map/gather_in/ppermute | solution.py:713
  7.7 6.9 %collective-permute-start.1 = (bf16[80,512]{1,0:T(8,128)(2,1)S(1)}, bf16[80,512]{1,0:T(8,128)(2,1)S(1)}, u32[]{:S(2)}, u32[]{:S(2)}) collective-permute-start(bf16[80,512]{1,0:T(8,128)(2,1)S(1)} %pad_maximum_fusion.4.refs_0_), channel_id=1, source_target_pairs={{0,2},{1,3},{2,0},{3,1},{4,6},{5,7},{6,4},{7,5},{8,10},{9,11},{10,... | collective-permute-start | bytes 245768 | tf_op jit(solution)/shard_map/gather_in/ppermute | solution.py:713
  7.7 6.9 %collective-permute-start = (bf16[80,512]{1,0:T(8,128)(2,1)S(1)}, bf16[80,512]{1,0:T(8,128)(2,1)S(1)}, u32[]{:S(2)}, u32[]{:S(2)}) collective-permute-start(bf16[80,512]{1,0:T(8,128)(2,1)S(1)} %pad_maximum_fusion.4.refs_0_), channel_id=1, source_target_pairs={{0,1},{1,0},{2,3},{3,2},{4,5},{5,4},{6,7},{7,6},{8,9},{9,8},{10,11... | collective-permute-start | bytes 245768 | tf_op jit(solution)/shard_map/gather_in/ppermute | solution.py:713
  15.2 8.4 %collective-permute-start.3 = (bf16[4,80,512]{2,1,0:T(8,128)(2,1)S(1)}, bf16[4,80,512]{2,1,0:T(8,128)(2,1)S(1)}, u32[]{:S(2)}, u32[]{:S(2)}) collective-permute-start(bf16[4,80,512]{2,1,0:T(8,128)(2,1)S(1)} %shard_map.212.own_ref), channel_id=1, source_target_pairs={{0,4},{4,0},{8,12},{12,8},{16,20},{20,16},{24,28},{28,24},{1,5},{5... | collective-permute-start | bytes 983048 | tf_op jit(solution)/shard_map/ppermute | solution.py:707
  15.3 14.1 %collective-permute-start.6 = (bf16[192,512]{1,0:T(8,128)(2,1)S(1)}, bf16[192,512]{1,0:T(8,128)(2,1)S(1)}, u32[]{:S(2)}, u32[]{:S(2)}) collective-permute-start(bf16[192,512]{1,0:T(8,128)(2,1)S(1)} %pad_maximum_fusion.refs_0_), channel_id=1, source_target_pairs={{0,3},{1,2},{2,1},{3,0},{4,7},{5,6},{6,5},{7,4},{8,11},{9,10},{10,... | collective-permute-start | bytes 589832 | tf_op jit(solution)/shard_map/gather_out_glu/ppermute | solution.py:713
  18.9 18.0 %collective-permute-start.5 = (bf16[192,512]{1,0:T(8,128)(2,1)S(1)}, bf16[192,512]{1,0:T(8,128)(2,1)S(1)}, u32[]{:S(2)}, u32[]{:S(2)}) collective-permute-start(bf16[192,512]{1,0:T(8,128)(2,1)S(1)} %pad_maximum_fusion.refs_0_), channel_id=1, source_target_pairs={{0,2},{1,3},{2,0},{3,1},{4,6},{5,7},{6,4},{7,5},{8,10},{9,11},{10,... | collective-permute-start | bytes 589832 | tf_op jit(solution)/shard_map/gather_out_glu/ppermute | solution.py:713
  18.9 18.0 %collective-permute-start.4 = (bf16[192,512]{1,0:T(8,128)(2,1)S(1)}, bf16[192,512]{1,0:T(8,128)(2,1)S(1)}, u32[]{:S(2)}, u32[]{:S(2)}) collective-permute-start(bf16[192,512]{1,0:T(8,128)(2,1)S(1)} %pad_maximum_fusion.refs_0_), channel_id=1, source_target_pairs={{0,1},{1,0},{2,3},{3,2},{4,5},{5,4},{6,7},{7,6},{8,9},{9,8},{10,11... | collective-permute-start | bytes 589832 | tf_op jit(solution)/shard_map/gather_out_glu/ppermute | solution.py:713
  25.7 11.3 %collective-permute-start.9 = (f32[8,512]{1,0:T(8,128)S(1)}, f32[8,512]{1,0:T(8,128)S(1)}, u32[]{:S(2)}, u32[]{:S(2)}) collective-permute-start(f32[8,512]{1,0:T(8,128)S(1)} %get-tuple-element.101.rest_3_), channel_id=1, source_target_pairs={{0,3},{1,2},{2,1},{3,0},{4,7},{5,6},{6,5},{7,4},{8,11},{9,10},{10,... | collective-permute-start | bytes 49160 | tf_op jit(solution)/shard_map/carry/ppermute | solution.py:713
  29.4 8.0 %collective-permute-start.8 = (f32[8,512]{1,0:T(8,128)S(1)}, f32[8,512]{1,0:T(8,128)S(1)}, u32[]{:S(2)}, u32[]{:S(2)}) collective-permute-start(f32[8,512]{1,0:T(8,128)S(1)} %get-tuple-element.101.rest_3_), channel_id=1, source_target_pairs={{0,2},{1,3},{2,0},{3,1},{4,6},{5,7},{6,4},{7,5},{8,10},{9,11},{10,... | collective-permute-start | bytes 49160 | tf_op jit(solution)/shard_map/carry/ppermute | solution.py:713
  29.4 8.0 %collective-permute-start.7 = (f32[8,512]{1,0:T(8,128)S(1)}, f32[8,512]{1,0:T(8,128)S(1)}, u32[]{:S(2)}, u32[]{:S(2)}) collective-permute-start(f32[8,512]{1,0:T(8,128)S(1)} %get-tuple-element.101.rest_3_), channel_id=1, source_target_pairs={{0,1},{1,0},{2,3},{3,2},{4,5},{5,4},{6,7},{7,6},{8,9},{9,8},{10,11... | collective-permute-start | bytes 49160 | tf_op jit(solution)/shard_map/carry/ppermute | solution.py:713
  37.9 2.4 %collective-permute-start.10 = (bf16[4,192,512]{2,1,0:T(8,128)(2,1)S(1)}, bf16[4,192,512]{2,1,0:T(8,128)(2,1)S(1)}, u32[]{:S(2)}, u32[]{:S(2)}) collective-permute-start(bf16[4,192,512]{2,1,0:T(8,128)(2,1)S(1)} %shard_map.215.own_ref), channel_id=1, source_target_pairs={{0,4},{4,0},{8,12},{12,8},{16,20},{20,16},{24,28},{28,24},{1,5},{5... | collective-permute-start | bytes 2359304 | tf_op jit(solution)/shard_map/ppermute | solution.py:707
  53.8 8.7 %collective-permute-start.11 = (f32[8,512]{1,0:T(8,128)S(1)}, f32[8,512]{1,0:T(8,128)S(1)}, u32[]{:S(2)}, u32[]{:S(2)}) collective-permute-start(f32[8,512]{1,0:T(8,128)S(1)} %get-tuple-element.115), channel_id=1, source_target_pairs={{0,1},{1,0},{2,3},{3,2},{4,5},{5,4},{6,7},{7,6},{8,9},{9,8},{10,11... | collective-permute-start | bytes 49160 | tf_op jit(solution)/shard_map/carry_back/ppermute | solution.py:713
  54.2 8.2 %collective-permute-start.13 = (f32[8,512]{1,0:T(8,128)S(1)}, f32[8,512]{1,0:T(8,128)S(1)}, u32[]{:S(2)}, u32[]{:S(2)}) collective-permute-start(f32[8,512]{1,0:T(8,128)S(1)} %get-tuple-element.115), channel_id=1, source_target_pairs={{0,3},{1,2},{2,1},{3,0},{4,7},{5,6},{6,5},{7,4},{8,11},{9,10},{10,... | collective-permute-start | bytes 49160 | tf_op jit(solution)/shard_map/carry_back/ppermute | solution.py:713
  56.6 5.9 %collective-permute-start.12 = (f32[8,512]{1,0:T(8,128)S(1)}, f32[8,512]{1,0:T(8,128)S(1)}, u32[]{:S(2)}, u32[]{:S(2)}) collective-permute-start(f32[8,512]{1,0:T(8,128)S(1)} %get-tuple-element.115), channel_id=1, source_target_pairs={{0,2},{1,3},{2,0},{3,1},{4,6},{5,7},{6,4},{7,5},{8,10},{9,11},{10,... | collective-permute-start | bytes 49160 | tf_op jit(solution)/shard_map/carry_back/ppermute | solution.py:713
  62.4 4.3 %collective-permute-start.14 = (bf16[768,512]{1,0:T(8,128)(2,1)S(1)}, bf16[768,512]{1,0:T(8,128)(2,1)S(1)}, u32[]{:S(2)}, u32[]{:S(2)}) collective-permute-start(bf16[768,512]{1,0:T(8,128)(2,1)S(1)} %get-tuple-element.122), channel_id=1, source_target_pairs={{0,4},{4,0},{8,12},{12,8},{16,20},{20,16},{24,28},{28,24},{1,5},{5... | collective-permute-start | bytes 2359304 | tf_op jit(solution)/shard_map/sum_early_core/ppermute | solution.py:707
  68.6 13.0 %collective-permute-start.16 = (bf16[256,512]{1,0:T(8,128)(2,1)S(1)}, bf16[256,512]{1,0:T(8,128)(2,1)S(1)}, u32[]{:S(2)}, u32[]{:S(2)}) collective-permute-start(bf16[256,512]{1,0:T(8,128)(2,1)S(1)} %get-tuple-element.136), channel_id=1, source_target_pairs={{0,8},{4,12},{8,0},{12,4},{16,24},{20,28},{24,16},{28,20},{1,9},{5... | collective-permute-start | bytes 786440 | tf_op jit(solution)/shard_map/sum_plane/ppermute | solution.py:710
  70.2 13.9 %collective-permute-start.17 = (bf16[256,512]{1,0:T(8,128)(2,1)S(1)}, bf16[256,512]{1,0:T(8,128)(2,1)S(1)}, u32[]{:S(2)}, u32[]{:S(2)}) collective-permute-start(bf16[256,512]{1,0:T(8,128)(2,1)S(1)} %get-tuple-element.140), channel_id=1, source_target_pairs={{0,16},{4,20},{8,24},{12,28},{16,0},{20,4},{24,8},{28,12},{1,17},{... | collective-permute-start | bytes 786440 | tf_op jit(solution)/shard_map/sum_plane/ppermute | solution.py:710
  71.7 12.4 %collective-permute-start.18 = (bf16[256,512]{1,0:T(8,128)(2,1)S(1)}, bf16[256,512]{1,0:T(8,128)(2,1)S(1)}, u32[]{:S(2)}, u32[]{:S(2)}) collective-permute-start(bf16[256,512]{1,0:T(8,128)(2,1)S(1)} %get-tuple-element.141), channel_id=1, source_target_pairs={{0,24},{4,28},{8,16},{12,20},{16,8},{20,12},{24,0},{28,4},{1,25},{... | collective-permute-start | bytes 786440 | tf_op jit(solution)/shard_map/sum_plane/ppermute | solution.py:710
  84.3 5.2 %collective-permute-start.19 = (bf16[80,512]{1,0:T(8,128)(2,1)S(1)}, bf16[80,512]{1,0:T(8,128)(2,1)S(1)}, u32[]{:S(2)}, u32[]{:S(2)}) collective-permute-start(bf16[80,512]{1,0:T(8,128)(2,1)S(1)} %get-tuple-element.165), channel_id=1, source_target_pairs={{0,1},{1,0},{2,3},{3,2},{4,5},{5,4},{6,7},{7,6},{8,9},{9,8},{10,11... | collective-permute-start | bytes 245768 | tf_op jit(solution)/shard_map/sum_mp/ppermute | solution.py:713
  85.6 8.7 %collective-permute-start.20 = (bf16[80,512]{1,0:T(8,128)(2,1)S(1)}, bf16[80,512]{1,0:T(8,128)(2,1)S(1)}, u32[]{:S(2)}, u32[]{:S(2)}) collective-permute-start(bf16[80,512]{1,0:T(8,128)(2,1)S(1)} %get-tuple-element.166), channel_id=1, source_target_pairs={{0,2},{1,3},{2,0},{3,1},{4,6},{5,7},{6,4},{7,5},{8,10},{9,11},{10,... | collective-permute-start | bytes 245768 | tf_op jit(solution)/shard_map/sum_mp/ppermute | solution.py:713
  87.3 7.1 %collective-permute-start.21 = (bf16[80,512]{1,0:T(8,128)(2,1)S(1)}, bf16[80,512]{1,0:T(8,128)(2,1)S(1)}, u32[]{:S(2)}, u32[]{:S(2)}) collective-permute-start(bf16[80,512]{1,0:T(8,128)(2,1)S(1)} %get-tuple-element.167), channel_id=1, source_target_pairs={{0,3},{1,2},{2,1},{3,0},{4,7},{5,6},{6,5},{7,4},{8,11},{9,10},{10,... | collective-permute-start | bytes 245768 | tf_op jit(solution)/shard_map/sum_mp/ppermute | solution.py:713
  94.4 4.5 %collective-permute-start.22 = (bf16[80,512]{1,0:T(8,128)(2,1)S(1)}, bf16[80,512]{1,0:T(8,128)(2,1)S(1)}, u32[]{:S(2)}, u32[]{:S(2)}) collective-permute-start(bf16[80,512]{1,0:T(8,128)(2,1)S(1)} %pad_maximum_fusion.5), channel_id=1, source_target_pairs={{0,8},{4,12},{8,0},{12,4},{16,24},{20,28},{24,16},{28,20},{1,9},{5... | collective-permute-start | bytes 245768 | tf_op jit(solution)/shard_map/spread_plane/ppermute | solution.py:710
  95.9 6.2 %collective-permute-start.24 = (bf16[80,512]{1,0:T(8,128)(2,1)S(1)}, bf16[80,512]{1,0:T(8,128)(2,1)S(1)}, u32[]{:S(2)}, u32[]{:S(2)}) collective-permute-start(bf16[80,512]{1,0:T(8,128)(2,1)S(1)} %pad_maximum_fusion.5), channel_id=1, source_target_pairs={{0,24},{4,28},{8,16},{12,20},{16,8},{20,12},{24,0},{28,4},{1,25},{... | collective-permute-start | bytes 245768 | tf_op jit(solution)/shard_map/spread_plane/ppermute | solution.py:710
  97.4 4.8 %collective-permute-start.23 = (bf16[80,512]{1,0:T(8,128)(2,1)S(1)}, bf16[80,512]{1,0:T(8,128)(2,1)S(1)}, u32[]{:S(2)}, u32[]{:S(2)}) collective-permute-start(bf16[80,512]{1,0:T(8,128)(2,1)S(1)} %pad_maximum_fusion.5), channel_id=1, source_target_pairs={{0,16},{4,20},{8,24},{12,28},{16,0},{20,4},{24,8},{28,12},{1,17},{... | collective-permute-start | bytes 245768 | tf_op jit(solution)/shard_map/spread_plane/ppermute | solution.py:710
  (11 other events, 177.8 us)

commit v8 on v7

--- a/solution.py
+++ b/solution.py
@@ -529,8 +529,8 @@
 
     after = jnp.minimum(2 * step + 2, gdrive_ref.shape[0] // BLOCK - 1)
     outputs = [partial(output_piece, k) for k in range(0, per, 8)]
-    run([partial(branch_piece, k) for k in range(0, per, 8)])
-    alternate(normed_pieces(2 * step + 1, gn_b), norm_pieces(0, gn_a))
+    branches = [partial(branch_piece, k) for k in range(0, per, 8)]
+    alternate(normed_pieces(2 * step + 1, gn_b), branches + norm_pieces(0, gn_a))
     alternate(normed_pieces(after, gn_a), outputs[: len(outputs) // 2] + norm_pieces(1, gn_b) + outputs[len(outputs) // 2 :])
     vec_ref[0:1, :] += jnp.sum(sums[0], 0, keepdims=True)
     vec_ref[1:2, :] += jnp.sum(sums[1], 0, keepdims=True)

time: 106 us -> 106 us (level)
  no operation moved by 1% of the time
where the time goes in v8:
time: 106 us
  Pallas kernels  46 us (43%)
  starting transfers between devices  33.2 us (31%)
  waiting for transfers between devices  21.9 us (21%)
  local copies, waits for them, and re-layouts  2.45 us (2%)
  other arithmetic  1.21 us (1%)
  between operations  1.15 us (1%)
    pallas_call x13, Pallas kernels, call(): pl.pallas_call(kernel, grid_spec=pltpu.PrefetchScalarGridSpec(num_scalar_...  46 us
    ppermute x15, starting transfers between devices, over_mp(): return lax.ppermute(v, 'mp', xor_pairs(mp, s))  25.3 us
    ppermute x15, waiting for transfers between devices, over_mp(): return lax.ppermute(v, 'mp', xor_pairs(mp, s))  10.4 us
    ppermute x6, starting transfers between devices, over_plane(): return lax.ppermute(v, 'dp', xor_pairs(dp, 2 * s))  7.12 us
    ppermute x6, waiting for transfers between devices, over_plane(): return lax.ppermute(v, 'dp', xor_pairs(dp, 2 * s))  6.6 us
    ppermute x5, waiting for transfers between devices, over_core(): return lax.ppermute(v, 'dp', xor_pairs(dp, 1))  4.98 us
  transfers between devices with their start and end apart: 26, of which 11 were waited for; matrix products, arithmetic and copies ran while one was open for 1% of the time, Pallas kernels for 27%

profile of v8, /device:TPU:0, one launch (start us, length us, event | category | flops | bytes accessed | tf_op | source)
XLA Modules:
  0.0 105.9 jit_solution(17157410567679862380)
XLA Ops:
  2.6 5.1 %collective-permute-start.2 = (bf16[80,512]{1,0:T(8,128)(2,1)S(1)}, bf16[80,512]{1,0:T(8,128)(2,1)S(1)}, u32[]{:S(2)}, u32[]{:S(2)}) collective-permute-start(bf16[80,512]{1,0:T(8,128)(2,1)S(1)} %pad_maximum_fusion.4.refs_0_), channel_id=1, source_target_pairs={{0,3},{1,2},{2,1},{3,0},{4,7},{5,6},{6,5},{7,4},{8,11},{9,10},{10,... | collective-permute-start | bytes 245768 | tf_op jit(solution)/shard_map/gather_in/ppermute | solution.py:713
  9.8 4.7 %shard_map.211 = (f32[2048,512]{1,0:T(8,128)S(1)}, bf16[2048,512]{1,0:T(8,128)(2,1)S(1)}, f32[2048,128]{1,0:T(8,128)S(1)}) custom-call(s32[3]{0:T(128)S(1)} %pad_add_fusion.idx, f32[16,128,512]{2,1,0:T(8,128)} %bitcast.53, f32[1,512]{1,0:T(1,128)} %bitcast.44, f32[1,512]{1,0:T(1,128)} %bitcast.47), custom_call_target="tpu_custom_call" | custom-call | flops 1073741824 | bytes 12582912 | tf_op jit(solution)/shard_map/pallas_call | solution.py:628
  15.3 3.7 %collective-permute-start.6 = (bf16[192,512]{1,0:T(8,128)(2,1)S(1)}, bf16[192,512]{1,0:T(8,128)(2,1)S(1)}, u32[]{:S(2)}, u32[]{:S(2)}) collective-permute-start(bf16[192,512]{1,0:T(8,128)(2,1)S(1)} %pad_maximum_fusion.refs_0_), channel_id=1, source_target_pairs={{0,3},{1,2},{2,1},{3,0},{4,7},{5,6},{6,5},{7,4},{8,11},{9,10},{10,... | collective-permute-start | bytes 589832 | tf_op jit(solution)/shard_map/gather_out_glu/ppermute | solution.py:713
  19.7 3.8 %shard_map.213.cotlow_ref = bf16[2048,512]{1,0:T(8,128)(2,1)S(1)} custom-call(s32[3]{0:T(128)S(1)} %pad_add_fusion.idx, f32[16,128,512]{2,1,0:T(8,128)} %bitcast.42), custom_call_target="tpu_custom_call" | custom-call | bytes 8388608 | tf_op jit(solution)/shard_map/pallas_call | solution.py:628
  23.6 2.0 %shard_map.214 = (f32[2048,512]{1,0:T(8,128)S(1)}, bf16[512,512]{1,0:T(8,128)(2,1)S(1)}, f32[12,512]{1,0:T(8,128)S(1)}, f32[16,512]{1,0:T(8,128)S(1)}, f32[8,512]{1,0:T(8,128)S(1)}) custom-call(s32[3]{0:T(128)S(1)} %pad_add_fusion.idx, bf16[2048,512]{1,0:T(8,128)(2,1)S(1)} %get-tuple-element.96.norm_ref, bf16[4,80,512]{2,1,0:T(8,128)(2,1)S(1)} %shard_map.212.own_ref, ...), custom_call_target="tpu_custom_call" | custom-call | flops 1073741824 | bytes 8388608 | tf_op jit(solution)/shard_map/pallas_call | solution.py:628
  25.7 3.7 %collective-permute-start.9 = (f32[8,512]{1,0:T(8,128)S(1)}, f32[8,512]{1,0:T(8,128)S(1)}, u32[]{:S(2)}, u32[]{:S(2)}) collective-permute-start(f32[8,512]{1,0:T(8,128)S(1)} %get-tuple-element.101.rest_3_), channel_id=1, source_target_pairs={{0,3},{1,2},{2,1},{3,0},{4,7},{5,6},{6,5},{7,4},{8,11},{9,10},{10,... | collective-permute-start | bytes 49160 | tf_op jit(solution)/shard_map/carry/ppermute | solution.py:713
  29.4 3.4 %collective-permute-start.7 = (f32[8,512]{1,0:T(8,128)S(1)}, f32[8,512]{1,0:T(8,128)S(1)}, u32[]{:S(2)}, u32[]{:S(2)}) collective-permute-start(f32[8,512]{1,0:T(8,128)S(1)} %get-tuple-element.101.rest_3_), channel_id=1, source_target_pairs={{0,1},{1,0},{2,3},{3,2},{4,5},{5,4},{6,7},{7,6},{8,9},{9,8},{10,11... | collective-permute-start | bytes 49160 | tf_op jit(solution)/shard_map/carry/ppermute | solution.py:713
  32.7 4.3 %collective-permute-done.5.refs_2_ = bf16[192,512]{1,0:T(8,128)(2,1)S(1)} collective-permute-done((bf16[192,512]{1,0:T(8,128)(2,1)S(1)}, bf16[192,512]{1,0:T(8,128)(2,1)S(1)}, u32[]{:S(2)}, u32[]{:S(2)}) %collective-permute-start.5) | collective-permute-done | bytes 196640 | tf_op jit(solution)/shard_map/gather_out_glu/ppermute | solution.py:713
  38.0 2.3 %collective-permute-done.10.other_ref = bf16[4,192,512]{2,1,0:T(8,128)(2,1)S(1)} collective-permute-done((bf16[4,192,512]{2,1,0:T(8,128)(2,1)S(1)}, bf16[4,192,512]{2,1,0:T(8,128)(2,1)S(1)}, u32[]{:S(2)}, u32[]{:S(2)}) %collective-permute-start.10) | collective-permute-done | bytes 786464 | tf_op jit(solution)/shard_map/ppermute | solution.py:707
  40.3 4.1 %shard_map.216 = (bf16[2048,512]{1,0:T(8,128)(2,1)S(1)}, bf16[2048,512]{1,0:T(8,128)(2,1)S(1)}, f32[2048,512]{1,0:T(8,128)S(1)}, bf16[512,512]{1,0:T(8,128)(2,1)S(1)}, f32[8,512]{1,0:T(8,128)S(1)}) custom-call(s32[3]{0:T(128)S(1)} %pad_add_fusion.idx, f32[2048,512]{1,0:T(8,128)S(1)} %get-tuple-element.95.xhat_ref, ...), custom_call_target="tpu_custom_call" | custom-call | flops 1073741824 | bytes 8388608 | tf_op jit(solution)/shard_map/pallas_call | solution.py:628
  44.4 4.7 %shard_map.217 = (bf16[2048,512]{1,0:T(8,128)(2,1)S(1)}, bf16[2048,1024]{1,0:T(8,128)(2,1)S(1)}, bf16[1024,512]{1,0:T(8,128)(2,1)S(1)}, f32[8,512]{1,0:T(8,128)S(1)}) custom-call(s32[3]{0:T(128)S(1)} %pad_add_fusion.idx, bf16[2048,512]{1,0:T(8,128)(2,1)S(1)} %shard_map.213.cotlow_ref, bf16[2048,512]{1,0:T(8,128)(2,1)S(1)} %get-tuple-element.106.act_ref, ...), custom_call_target="tpu_custom_call" | custom-call | flops 2147483648 | bytes 8388608 | tf_op jit(solution)/shard_map/pallas_call | solution.py:628
  49.1 4.6 %shard_map.218 = (bf16[2048,512]{1,0:T(8,128)(2,1)S(1)}, f32[2048,512]{1,0:T(8,128)S(1)}, f32[16,512]{1,0:T(8,128)S(1)}, f32[8,512]{1,0:T(8,128)S(1)}, f32[8,512]{1,0:T(8,128)S(1)}) custom-call(s32[3]{0:T(128)S(1)} %pad_add_fusion.idx, bf16[2048,1024]{1,0:T(8,128)(2,1)S(1)} %get-tuple-element.116.gpre_ref, f32[2048,512]{1,0:T(8,128)S(1)} %get-tuple-element.109.slope_ref, ...), custom_call_target="tpu_custom_call" | custom-call | flops 4294967296 | bytes 8388608 | tf_op jit(solution)/shard_map/pallas_call | solution.py:628
  54.2 2.3 %collective-permute-start.13 = (f32[8,512]{1,0:T(8,128)S(1)}, f32[8,512]{1,0:T(8,128)S(1)}, u32[]{:S(2)}, u32[]{:S(2)}) collective-permute-start(f32[8,512]{1,0:T(8,128)S(1)} %get-tuple-element.115), channel_id=1, source_target_pairs={{0,3},{1,2},{2,1},{3,0},{4,7},{5,6},{6,5},{7,4},{8,11},{9,10},{10,... | collective-permute-start | bytes 49160 | tf_op jit(solution)/shard_map/carry_back/ppermute | solution.py:713
  57.3 5.1 %shard_map.219 = (f32[768,512]{1,0:T(8,128)S(1)}, bf16[768,512]{1,0:T(8,128)(2,1)S(1)}) custom-call(s32[3]{0:T(128)S(1)} %pad_add_fusion.idx, bf16[2048,1024]{1,0:T(8,128)(2,1)S(1)} %get-tuple-element.116.gpre_ref, bf16[2048,512]{1,0:T(8,128)(2,1)S(1)} %get-tuple-element.106.act_ref, bf16[2048,512]{1,0:T(8,128)(2,1)S(1)} %get-tuple-element.113.state_ref, ...), custom_call_target="tpu_custom_call" | custom-call | tf_op jit(solution)/shard_map/pallas_call | solution.py:628
  62.5 3.6 %shard_map.220 = (bf16[2048,512]{1,0:T(8,128)(2,1)S(1)}, f32[256,512]{1,0:T(8,128)S(1)}, bf16[256,512]{1,0:T(8,128)(2,1)S(1)}, f32[8,512]{1,0:T(8,128)S(1)}) custom-call(s32[3]{0:T(128)S(1)} %pad_add_fusion.idx, f32[2048,512]{1,0:T(8,128)S(1)} %get-tuple-element.112.gs_ref, bf16[2048,512]{1,0:T(8,128)(2,1)S(1)} %get-tuple-element.113.state_ref, ...), custom_call_target="tpu_custom_call" | custom-call | flops 1073741824 | bytes 8388608 | tf_op jit(solution)/shard_map/pallas_call | solution.py:628
  68.6 1.6 %collective-permute-start.16 = (bf16[256,512]{1,0:T(8,128)(2,1)S(1)}, bf16[256,512]{1,0:T(8,128)(2,1)S(1)}, u32[]{:S(2)}, u32[]{:S(2)}) collective-permute-start(bf16[256,512]{1,0:T(8,128)(2,1)S(1)} %get-tuple-element.136), channel_id=1, source_target_pairs={{0,8},{4,12},{8,0},{12,4},{16,24},{20,28},{24,16},{28,20},{1,9},{5... | collective-permute-start | bytes 786440 | tf_op jit(solution)/shard_map/sum_plane/ppermute | solution.py:710
  70.2 1.5 %collective-permute-start.17 = (bf16[256,512]{1,0:T(8,128)(2,1)S(1)}, bf16[256,512]{1,0:T(8,128)(2,1)S(1)}, u32[]{:S(2)}, u32[]{:S(2)}) collective-permute-start(bf16[256,512]{1,0:T(8,128)(2,1)S(1)} %get-tuple-element.140), channel_id=1, source_target_pairs={{0,16},{4,20},{8,24},{12,28},{16,0},{20,4},{24,8},{28,12},{1,17},{... | collective-permute-start | bytes 786440 | tf_op jit(solution)/shard_map/sum_plane/ppermute | solution.py:710
  72.2 9.5 %shard_map.222 = (f32[16,128,512]{2,1,0:T(8,128)}, f32[16,128,512]{2,1,0:T(8,128)}, f32[8,512]{1,0:T(8,128)S(1)}, bf16[16,512]{1,0:T(8,128)(2,1)S(1)}) custom-call(s32[3]{0:T(128)S(1)} %pad_add_fusion.idx, f32[16,128,512]{2,1,0:T(8,128)S(1)} %bitcast.43, bf16[2048,512]{1,0:T(8,128)(2,1)S(1)} %get-tuple-element.127.gdrive_ref, ...), custom_call_target="tpu_custom_call" | custom-call | flops 1073741824 | bytes 8388608 | tf_op jit(solution)/shard_map/pallas_call | solution.py:628
  81.6 2.4 %collective-permute-done.17 = bf16[256,512]{1,0:T(8,128)(2,1)S(1)} collective-permute-done((bf16[256,512]{1,0:T(8,128)(2,1)S(1)}, bf16[256,512]{1,0:T(8,128)(2,1)S(1)}, u32[]{:S(2)}, u32[]{:S(2)}) %collective-permute-start.17) | collective-permute-done | bytes 262176 | tf_op jit(solution)/shard_map/sum_plane/ppermute | solution.py:710
  85.6 1.6 %collective-permute-start.20 = (bf16[80,512]{1,0:T(8,128)(2,1)S(1)}, bf16[80,512]{1,0:T(8,128)(2,1)S(1)}, u32[]{:S(2)}, u32[]{:S(2)}) collective-permute-start(bf16[80,512]{1,0:T(8,128)(2,1)S(1)} %get-tuple-element.166), channel_id=1, source_target_pairs={{0,2},{1,3},{2,0},{3,1},{4,6},{5,7},{6,4},{7,5},{8,10},{9,11},{10,... | collective-permute-start | bytes 245768 | tf_op jit(solution)/shard_map/sum_mp/ppermute | solution.py:713
  89.5 4.8 %collective-permute-done.20 = bf16[80,512]{1,0:T(8,128)(2,1)S(1)} collective-permute-done((bf16[80,512]{1,0:T(8,128)(2,1)S(1)}, bf16[80,512]{1,0:T(8,128)(2,1)S(1)}, u32[]{:S(2)}, u32[]{:S(2)}) %collective-permute-start.20) | collective-permute-done | bytes 81952 | tf_op jit(solution)/shard_map/sum_mp/ppermute | solution.py:713
  99.0 3.2 %collective-permute-done.23 = bf16[80,512]{1,0:T(8,128)(2,1)S(1)} collective-permute-done((bf16[80,512]{1,0:T(8,128)(2,1)S(1)}, bf16[80,512]{1,0:T(8,128)(2,1)S(1)}, u32[]{:S(2)}, u32[]{:S(2)}) %collective-permute-start.23) | collective-permute-done | bytes 81952 | tf_op jit(solution)/shard_map/spread_plane/ppermute | solution.py:710
  102.3 1.5 %collective-permute-done.25.got_ref = bf16[272,512]{1,0:T(8,128)(2,1)S(1)} collective-permute-done((bf16[272,512]{1,0:T(8,128)(2,1)S(1)}, bf16[272,512]{1,0:T(8,128)(2,1)S(1)}, u32[]{:S(2)}, u32[]{:S(2)}) %collective-permute-start.25) | collective-permute-done | bytes 278560 | tf_op jit(solution)/shard_map/spread_core/ppermute | solution.py:707
  103.9 1.9 %shard_map.223 = (f32[2,64,512]{2,1,0:T(8,128)}, f32[2,64,512]{2,1,0:T(8,128)}, f32[512,2,128]{2,1,0:T(2,128)}, f32[1,512]{1,0:T(1,128)}, f32[1,512]{1,0:T(1,128...) custom-call(s32[3]{0:T(128)S(1)} %pad_add_fusion.idx, ...), custom_call_target="tpu_custom_call" | custom-call | tf_op jit(solution)/shard_map/pallas_call | solution.py:628
  (86 shorter events, 19.2 us)
Async XLA Ops:
  2.6 11.8 %collective-permute-start.2 = (bf16[80,512]{1,0:T(8,128)(2,1)S(1)}, bf16[80,512]{1,0:T(8,128)(2,1)S(1)}, u32[]{:S(2)}, u32[]{:S(2)}) collective-permute-start(bf16[80,512]{1,0:T(8,128)(2,1)S(1)} %pad_maximum_fusion.4.refs_0_), channel_id=1, source_target_pairs={{0,3},{1,2},{2,1},{3,0},{4,7},{5,6},{6,5},{7,4},{8,11},{9,10},{10,... | collective-permute-start | bytes 245768 | tf_op jit(solution)/shard_map/gather_in/ppermute | solution.py:713
  7.7 6.9 %collective-permute-start.1 = (bf16[80,512]{1,0:T(8,128)(2,1)S(1)}, bf16[80,512]{1,0:T(8,128)(2,1)S(1)}, u32[]{:S(2)}, u32[]{:S(2)}) collective-permute-start(bf16[80,512]{1,0:T(8,128)(2,1)S(1)} %pad_maximum_fusion.4.refs_0_), channel_id=1, source_target_pairs={{0,2},{1,3},{2,0},{3,1},{4,6},{5,7},{6,4},{7,5},{8,10},{9,11},{10,... | collective-permute-start | bytes 245768 | tf_op jit(solution)/shard_map/gather_in/ppermute | solution.py:713
  7.7 6.9 %collective-permute-start = (bf16[80,512]{1,0:T(8,128)(2,1)S(1)}, bf16[80,512]{1,0:T(8,128)(2,1)S(1)}, u32[]{:S(2)}, u32[]{:S(2)}) collective-permute-start(bf16[80,512]{1,0:T(8,128)(2,1)S(1)} %pad_maximum_fusion.4.refs_0_), channel_id=1, source_target_pairs={{0,1},{1,0},{2,3},{3,2},{4,5},{5,4},{6,7},{7,6},{8,9},{9,8},{10,11... | collective-permute-start | bytes 245768 | tf_op jit(solution)/shard_map/gather_in/ppermute | solution.py:713
  15.2 8.4 %collective-permute-start.3 = (bf16[4,80,512]{2,1,0:T(8,128)(2,1)S(1)}, bf16[4,80,512]{2,1,0:T(8,128)(2,1)S(1)}, u32[]{:S(2)}, u32[]{:S(2)}) collective-permute-start(bf16[4,80,512]{2,1,0:T(8,128)(2,1)S(1)} %shard_map.212.own_ref), channel_id=1, source_target_pairs={{0,4},{4,0},{8,12},{12,8},{16,20},{20,16},{24,28},{28,24},{1,5},{5... | collective-permute-start | bytes 983048 | tf_op jit(solution)/shard_map/ppermute | solution.py:707
  15.3 14.1 %collective-permute-start.6 = (bf16[192,512]{1,0:T(8,128)(2,1)S(1)}, bf16[192,512]{1,0:T(8,128)(2,1)S(1)}, u32[]{:S(2)}, u32[]{:S(2)}) collective-permute-start(bf16[192,512]{1,0:T(8,128)(2,1)S(1)} %pad_maximum_fusion.refs_0_), channel_id=1, source_target_pairs={{0,3},{1,2},{2,1},{3,0},{4,7},{5,6},{6,5},{7,4},{8,11},{9,10},{10,... | collective-permute-start | bytes 589832 | tf_op jit(solution)/shard_map/gather_out_glu/ppermute | solution.py:713
  18.9 18.0 %collective-permute-start.5 = (bf16[192,512]{1,0:T(8,128)(2,1)S(1)}, bf16[192,512]{1,0:T(8,128)(2,1)S(1)}, u32[]{:S(2)}, u32[]{:S(2)}) collective-permute-start(bf16[192,512]{1,0:T(8,128)(2,1)S(1)} %pad_maximum_fusion.refs_0_), channel_id=1, source_target_pairs={{0,2},{1,3},{2,0},{3,1},{4,6},{5,7},{6,4},{7,5},{8,10},{9,11},{10,... | collective-permute-start | bytes 589832 | tf_op jit(solution)/shard_map/gather_out_glu/ppermute | solution.py:713
  18.9 18.0 %collective-permute-start.4 = (bf16[192,512]{1,0:T(8,128)(2,1)S(1)}, bf16[192,512]{1,0:T(8,128)(2,1)S(1)}, u32[]{:S(2)}, u32[]{:S(2)}) collective-permute-start(bf16[192,512]{1,0:T(8,128)(2,1)S(1)} %pad_maximum_fusion.refs_0_), channel_id=1, source_target_pairs={{0,1},{1,0},{2,3},{3,2},{4,5},{5,4},{6,7},{7,6},{8,9},{9,8},{10,11... | collective-permute-start | bytes 589832 | tf_op jit(solution)/shard_map/gather_out_glu/ppermute | solution.py:713
  25.7 11.3 %collective-permute-start.9 = (f32[8,512]{1,0:T(8,128)S(1)}, f32[8,512]{1,0:T(8,128)S(1)}, u32[]{:S(2)}, u32[]{:S(2)}) collective-permute-start(f32[8,512]{1,0:T(8,128)S(1)} %get-tuple-element.101.rest_3_), channel_id=1, source_target_pairs={{0,3},{1,2},{2,1},{3,0},{4,7},{5,6},{6,5},{7,4},{8,11},{9,10},{10,... | collective-permute-start | bytes 49160 | tf_op jit(solution)/shard_map/carry/ppermute | solution.py:713
  29.4 8.0 %collective-permute-start.8 = (f32[8,512]{1,0:T(8,128)S(1)}, f32[8,512]{1,0:T(8,128)S(1)}, u32[]{:S(2)}, u32[]{:S(2)}) collective-permute-start(f32[8,512]{1,0:T(8,128)S(1)} %get-tuple-element.101.rest_3_), channel_id=1, source_target_pairs={{0,2},{1,3},{2,0},{3,1},{4,6},{5,7},{6,4},{7,5},{8,10},{9,11},{10,... | collective-permute-start | bytes 49160 | tf_op jit(solution)/shard_map/carry/ppermute | solution.py:713
  29.4 8.0 %collective-permute-start.7 = (f32[8,512]{1,0:T(8,128)S(1)}, f32[8,512]{1,0:T(8,128)S(1)}, u32[]{:S(2)}, u32[]{:S(2)}) collective-permute-start(f32[8,512]{1,0:T(8,128)S(1)} %get-tuple-element.101.rest_3_), channel_id=1, source_target_pairs={{0,1},{1,0},{2,3},{3,2},{4,5},{5,4},{6,7},{7,6},{8,9},{9,8},{10,11... | collective-permute-start | bytes 49160 | tf_op jit(solution)/shard_map/carry/ppermute | solution.py:713
  37.9 2.4 %collective-permute-start.10 = (bf16[4,192,512]{2,1,0:T(8,128)(2,1)S(1)}, bf16[4,192,512]{2,1,0:T(8,128)(2,1)S(1)}, u32[]{:S(2)}, u32[]{:S(2)}) collective-permute-start(bf16[4,192,512]{2,1,0:T(8,128)(2,1)S(1)} %shard_map.215.own_ref), channel_id=1, source_target_pairs={{0,4},{4,0},{8,12},{12,8},{16,20},{20,16},{24,28},{28,24},{1,5},{5... | collective-permute-start | bytes 2359304 | tf_op jit(solution)/shard_map/ppermute | solution.py:707
  53.8 8.7 %collective-permute-start.11 = (f32[8,512]{1,0:T(8,128)S(1)}, f32[8,512]{1,0:T(8,128)S(1)}, u32[]{:S(2)}, u32[]{:S(2)}) collective-permute-start(f32[8,512]{1,0:T(8,128)S(1)} %get-tuple-element.115), channel_id=1, source_target_pairs={{0,1},{1,0},{2,3},{3,2},{4,5},{5,4},{6,7},{7,6},{8,9},{9,8},{10,11... | collective-permute-start | bytes 49160 | tf_op jit(solution)/shard_map/carry_back/ppermute | solution.py:713
  54.2 8.2 %collective-permute-start.13 = (f32[8,512]{1,0:T(8,128)S(1)}, f32[8,512]{1,0:T(8,128)S(1)}, u32[]{:S(2)}, u32[]{:S(2)}) collective-permute-start(f32[8,512]{1,0:T(8,128)S(1)} %get-tuple-element.115), channel_id=1, source_target_pairs={{0,3},{1,2},{2,1},{3,0},{4,7},{5,6},{6,5},{7,4},{8,11},{9,10},{10,... | collective-permute-start | bytes 49160 | tf_op jit(solution)/shard_map/carry_back/ppermute | solution.py:713
  56.6 5.9 %collective-permute-start.12 = (f32[8,512]{1,0:T(8,128)S(1)}, f32[8,512]{1,0:T(8,128)S(1)}, u32[]{:S(2)}, u32[]{:S(2)}) collective-permute-start(f32[8,512]{1,0:T(8,128)S(1)} %get-tuple-element.115), channel_id=1, source_target_pairs={{0,2},{1,3},{2,0},{3,1},{4,6},{5,7},{6,4},{7,5},{8,10},{9,11},{10,... | collective-permute-start | bytes 49160 | tf_op jit(solution)/shard_map/carry_back/ppermute | solution.py:713
  62.4 4.3 %collective-permute-start.14 = (bf16[768,512]{1,0:T(8,128)(2,1)S(1)}, bf16[768,512]{1,0:T(8,128)(2,1)S(1)}, u32[]{:S(2)}, u32[]{:S(2)}) collective-permute-start(bf16[768,512]{1,0:T(8,128)(2,1)S(1)} %get-tuple-element.122), channel_id=1, source_target_pairs={{0,4},{4,0},{8,12},{12,8},{16,20},{20,16},{24,28},{28,24},{1,5},{5... | collective-permute-start | bytes 2359304 | tf_op jit(solution)/shard_map/sum_early_core/ppermute | solution.py:707
  68.6 13.0 %collective-permute-start.16 = (bf16[256,512]{1,0:T(8,128)(2,1)S(1)}, bf16[256,512]{1,0:T(8,128)(2,1)S(1)}, u32[]{:S(2)}, u32[]{:S(2)}) collective-permute-start(bf16[256,512]{1,0:T(8,128)(2,1)S(1)} %get-tuple-element.136), channel_id=1, source_target_pairs={{0,8},{4,12},{8,0},{12,4},{16,24},{20,28},{24,16},{28,20},{1,9},{5... | collective-permute-start | bytes 786440 | tf_op jit(solution)/shard_map/sum_plane/ppermute | solution.py:710
  70.2 13.9 %collective-permute-start.17 = (bf16[256,512]{1,0:T(8,128)(2,1)S(1)}, bf16[256,512]{1,0:T(8,128)(2,1)S(1)}, u32[]{:S(2)}, u32[]{:S(2)}) collective-permute-start(bf16[256,512]{1,0:T(8,128)(2,1)S(1)} %get-tuple-element.140), channel_id=1, source_target_pairs={{0,16},{4,20},{8,24},{12,28},{16,0},{20,4},{24,8},{28,12},{1,17},{... | collective-permute-start | bytes 786440 | tf_op jit(solution)/shard_map/sum_plane/ppermute | solution.py:710
  71.7 12.4 %collective-permute-start.18 = (bf16[256,512]{1,0:T(8,128)(2,1)S(1)}, bf16[256,512]{1,0:T(8,128)(2,1)S(1)}, u32[]{:S(2)}, u32[]{:S(2)}) collective-permute-start(bf16[256,512]{1,0:T(8,128)(2,1)S(1)} %get-tuple-element.141), channel_id=1, source_target_pairs={{0,24},{4,28},{8,16},{12,20},{16,8},{20,12},{24,0},{28,4},{1,25},{... | collective-permute-start | bytes 786440 | tf_op jit(solution)/shard_map/sum_plane/ppermute | solution.py:710
  84.3 5.2 %collective-permute-start.19 = (bf16[80,512]{1,0:T(8,128)(2,1)S(1)}, bf16[80,512]{1,0:T(8,128)(2,1)S(1)}, u32[]{:S(2)}, u32[]{:S(2)}) collective-permute-start(bf16[80,512]{1,0:T(8,128)(2,1)S(1)} %get-tuple-element.165), channel_id=1, source_target_pairs={{0,1},{1,0},{2,3},{3,2},{4,5},{5,4},{6,7},{7,6},{8,9},{9,8},{10,11... | collective-permute-start | bytes 245768 | tf_op jit(solution)/shard_map/sum_mp/ppermute | solution.py:713
  85.6 8.7 %collective-permute-start.20 = (bf16[80,512]{1,0:T(8,128)(2,1)S(1)}, bf16[80,512]{1,0:T(8,128)(2,1)S(1)}, u32[]{:S(2)}, u32[]{:S(2)}) collective-permute-start(bf16[80,512]{1,0:T(8,128)(2,1)S(1)} %get-tuple-element.166), channel_id=1, source_target_pairs={{0,2},{1,3},{2,0},{3,1},{4,6},{5,7},{6,4},{7,5},{8,10},{9,11},{10,... | collective-permute-start | bytes 245768 | tf_op jit(solution)/shard_map/sum_mp/ppermute | solution.py:713
  87.3 7.1 %collective-permute-start.21 = (bf16[80,512]{1,0:T(8,128)(2,1)S(1)}, bf16[80,512]{1,0:T(8,128)(2,1)S(1)}, u32[]{:S(2)}, u32[]{:S(2)}) collective-permute-start(bf16[80,512]{1,0:T(8,128)(2,1)S(1)} %get-tuple-element.167), channel_id=1, source_target_pairs={{0,3},{1,2},{2,1},{3,0},{4,7},{5,6},{6,5},{7,4},{8,11},{9,10},{10,... | collective-permute-start | bytes 245768 | tf_op jit(solution)/shard_map/sum_mp/ppermute | solution.py:713
  94.4 4.5 %collective-permute-start.22 = (bf16[80,512]{1,0:T(8,128)(2,1)S(1)}, bf16[80,512]{1,0:T(8,128)(2,1)S(1)}, u32[]{:S(2)}, u32[]{:S(2)}) collective-permute-start(bf16[80,512]{1,0:T(8,128)(2,1)S(1)} %pad_maximum_fusion.5), channel_id=1, source_target_pairs={{0,8},{4,12},{8,0},{12,4},{16,24},{20,28},{24,16},{28,20},{1,9},{5... | collective-permute-start | bytes 245768 | tf_op jit(solution)/shard_map/spread_plane/ppermute | solution.py:710
  95.9 6.2 %collective-permute-start.24 = (bf16[80,512]{1,0:T(8,128)(2,1)S(1)}, bf16[80,512]{1,0:T(8,128)(2,1)S(1)}, u32[]{:S(2)}, u32[]{:S(2)}) collective-permute-start(bf16[80,512]{1,0:T(8,128)(2,1)S(1)} %pad_maximum_fusion.5), channel_id=1, source_target_pairs={{0,24},{4,28},{8,16},{12,20},{16,8},{20,12},{24,0},{28,4},{1,25},{... | collective-permute-start | bytes 245768 | tf_op jit(solution)/shard_map/spread_plane/ppermute | solution.py:710
  97.4 4.8 %collective-permute-start.23 = (bf16[80,512]{1,0:T(8,128)(2,1)S(1)}, bf16[80,512]{1,0:T(8,128)(2,1)S(1)}, u32[]{:S(2)}, u32[]{:S(2)}) collective-permute-start(bf16[80,512]{1,0:T(8,128)(2,1)S(1)} %pad_maximum_fusion.5), channel_id=1, source_target_pairs={{0,16},{4,20},{8,24},{12,28},{16,0},{20,4},{24,8},{28,12},{1,17},{... | collective-permute-start | bytes 245768 | tf_op jit(solution)/shard_map/spread_plane/ppermute | solution.py:710
  (11 other events, 177.8 us)
